TPU v7x, 32 devices: a whole 2x2x4 slice. The times are simulated.
32 devices in a mesh: dp: 4 (over z), ctx: 8 (over y, x, core).
Axes of the slice: x: 2, y: 2, z: 4, core: 2. Of those that a mesh axis runs over, the one named last changes fastest.
Arguments:
- normed_input: bfloat16 [4, 1024, 8192], P('dp', 'ctx'), may hold values from -6 to 6
- queries: bfloat16 [4, 1024, 1024], P('dp', 'ctx'), may hold values from -6 to 6
- keys_values: bfloat16 [4, 1024, 256], P('dp', 'ctx'), may hold values from -6 to 6
- grad_output: bfloat16 [4, 1024, 1024], P('dp', 'ctx'), may hold values from -6 to 6
- doc_lengths: int32 [4, 3], P('dp'), may hold values from 1 to 5, 8 in all within a row
Outputs:
- grad_queries: bfloat16 [4, 1024, 1024], P('dp', 'ctx')
- grad_keys_values: bfloat16 [4, 1024, 256], P('dp', 'ctx')
- grad_weights: float32 [8192, 1280], P(('ctx', 'dp'))
Inputs may be any that keep to these rules, and one draw needn't show every extreme that they name: `doc_lengths`: the lengths of a window sum to 8 shards; in every window the longest document spans exactly 5 shards.
All inputs are finite; a program needn't handle non-finite values.
Results may differ from a plain program's by a relative error of at most 0.012.
Values may be sent and summed in bfloat16 or wider, within the bound.
No kernel may reach another device: no remote copies, remote signals or barrier semaphores. Data moves between devices by JAX's collectives and lax.ppermute only.
A program may use at most 64 MiB of HBM per device.

v0:
```python
import jax
import jax.numpy as jnp
from jax import lax
from jax.sharding import PartitionSpec as P


def shard_grads(query_rows, kv_rows, grad_rows, allowed, head_size, group_heads):
    shard_rows = query_rows.shape[0]
    softmax_scale = head_size ** (-0.5)
    query_heads = query_rows.reshape(shard_rows, group_heads, head_size)
    grad_heads = grad_rows.reshape(shard_rows, group_heads, head_size)
    key_rows = kv_rows[:, :head_size]
    value_rows = kv_rows[:, head_size:]
    scores = (
        jnp.einsum("sgh,kh->gsk", query_heads, key_rows, preferred_element_type=jnp.float32)
        * softmax_scale
    )
    masked = jnp.where(allowed[None], scores, -1e30)
    row_max = jnp.max(masked, axis=-1, keepdims=True)
    exps_kept = jnp.where(allowed[None], jnp.exp(masked - row_max), 0.0)
    probs = exps_kept / jnp.sum(exps_kept, axis=-1, keepdims=True)
    probs_half = probs.astype(jnp.bfloat16)
    attended = jnp.einsum("gsk,kh->gsh", probs_half, value_rows, preferred_element_type=jnp.float32)
    grad_wide = jnp.transpose(grad_heads.astype(jnp.float32), (1, 0, 2))
    row_dots = jnp.sum(grad_wide * attended, axis=-1)
    dprobs = jnp.einsum("sgh,kh->gsk", grad_heads, value_rows, preferred_element_type=jnp.float32)
    dscores_half = (probs * (dprobs - row_dots[..., None])).astype(jnp.bfloat16)
    grad_query = (
        jnp.einsum("gsk,kh->sgh", dscores_half, key_rows, preferred_element_type=jnp.float32)
        * softmax_scale
    )
    grad_key = (
        jnp.einsum("gsk,sgh->kh", dscores_half, query_heads, preferred_element_type=jnp.float32)
        * softmax_scale
    )
    grad_value = jnp.einsum(
        "gsk,sgh->kh", probs_half, grad_heads, preferred_element_type=jnp.float32
    )
    grad_query = grad_query.reshape(shard_rows, group_heads * head_size).astype(jnp.bfloat16)
    return (grad_query, jnp.concatenate([grad_key, grad_value], axis=1).astype(jnp.bfloat16))


def fold_rows(features, piece_rows):
    return lax.dot_general(
        features, piece_rows, (((0,), (0,)), ((), ())), preferred_element_type=jnp.float32
    )


def shards(normed_input, queries, keys_values, grad_output, doc_lengths):
    ctx_count = lax.axis_size("ctx")
    doc_span = ctx_count // 2 + 1
    shard_rows = queries.shape[1]
    head_size = keys_values.shape[2] // 2
    group_heads = queries.shape[2] // head_size
    model_width = normed_input.shape[2]
    own_index = lax.axis_index("ctx")
    doc_lens = doc_lengths[0]
    doc_ends = jnp.cumsum(doc_lens)
    doc_starts = doc_ends - doc_lens
    doc_first = jnp.max(jnp.where(doc_starts <= own_index, doc_starts, 0))
    own_kv = keys_values[0]
    whole_kv = lax.all_gather(own_kv, "ctx", axis=0, tiled=True)
    padded = jnp.concatenate(
        [jnp.zeros(((doc_span - 1) * shard_rows, 2 * head_size), own_kv.dtype), whole_kv], axis=0
    )
    kv_window = lax.dynamic_slice_in_dim(padded, own_index * shard_rows, doc_span * shard_rows, 0)
    query_pos = jnp.arange(shard_rows, dtype=jnp.int32)[:, None]
    key_pos = jnp.arange(doc_span * shard_rows, dtype=jnp.int32)[None, :]
    key_slot = key_pos // shard_rows
    key_shard = own_index - (doc_span - 1) + key_slot
    allowed = (key_shard >= doc_first) & (
        (key_slot < doc_span - 1) | (key_pos % shard_rows <= query_pos)
    )
    grad_query, kv_partial = shard_grads(
        queries[0], kv_window, grad_output[0], allowed, head_size, group_heads
    )
    spread = jnp.zeros(((ctx_count + doc_span - 1) * shard_rows, 2 * head_size), jnp.float32)
    spread = lax.dynamic_update_slice_in_dim(
        spread, kv_partial.astype(jnp.float32), own_index * shard_rows, 0
    )
    kv_terms = spread[(doc_span - 1) * shard_rows :]
    kv_summed = lax.psum_scatter(
        kv_terms.astype(jnp.bfloat16), "ctx", scatter_dimension=0, tiled=True
    )
    grad_cols = jnp.concatenate([grad_query, kv_summed], axis=1)
    part_width = model_width // ctx_count
    pieces = normed_input[0].reshape(shard_rows, ctx_count, part_width)
    my_features = lax.all_to_all(pieces, "ctx", split_axis=1, concat_axis=0, tiled=True).reshape(
        ctx_count * shard_rows, part_width
    )
    partial_weights = fold_rows(my_features, lax.all_gather(grad_cols, "ctx", axis=0, tiled=True))
    grad_weights = lax.psum_scatter(
        partial_weights.astype(jnp.bfloat16), "dp", scatter_dimension=0, tiled=True
    ).astype(jnp.float32)
    return (grad_query[None], kv_summed[None], grad_weights)


def solution(mesh):
    placed = (
        P("dp", "ctx", None),
        P("dp", "ctx", None),
        P("dp", "ctx", None),
        P("dp", "ctx", None),
        P("dp", None),
    )
    return jax.shard_map(
        shards,
        mesh=mesh,
        in_specs=placed,
        out_specs=(P("dp", "ctx", None), P("dp", "ctx", None), P(("ctx", "dp"), None)),
        check_vma=False,
    )
```

profile of v0, /device:TPU:0, one launch (start us, length us, event | category | flops | bytes accessed | tf_op | source)
XLA Modules:
  0.0 184.1 jit_solution(8641733345254680219)
XLA Ops:
  7.2 0.0 reduce-scatter.3.cloned.1.call-start
  7.2 0.8 reduce-window.9
  8.1 1.3 fusion.39
  9.3 11.6 %all-gather = bf16[1,1024,256]{2,1,0:T(8,128)(2,1)S(1)} all-gather(bf16[1,128,256]{2,1,0:T(8,128)(2,1)} %param.7), channel_id=2, replica_groups=mesh['dp'=4,'ctx'=8] {'ctx'}, dimensions={1}, use_global_device_ids=true | all-gather | bytes 589824 | tf_op jit(solution)/shard_map/all_gather | solution.py:62
  20.9 1.8 copy.61
  22.7 1.1 copy.37
  23.9 0.7 fusion.36
  24.5 0.3 fusion.15
  24.8 2.2 %fusion.52 = (f32[8,128]{1,0:T(8,128)S(1)}, f32[8,128,640]{1,2,0:T(8,128)S(1)}) fusion(pred[128,640]{0,1:T(8,128)(4,1)S(1)} %fusion.15, bf16[128,8,128]{0,2,1:T(8,128)(2,1)} %bitcast.86, s32[]{:T(128)S(6)} %select_n.42, bf16[1024,256]{1,0:T(8,128)(2,1)S(1)} %bitcast.76), kind=kOutput, calls=%fused_computation.63 | convolution fusion | flops 171049600 | bytes 3575812 | tf_op jit(solution)/shard_map/sub | solution.py:20
  27.1 0.0 copy-start
  27.1 0.2 fusion.13
  27.3 0.5 fusion.11
  27.8 0.7 copy-done
  28.6 0.6 fusion.10
  29.1 0.0 copy-start.1
  29.2 2.4 %fusion.3 = bf16[8,128,640]{1,2,0:T(8,128)(2,1)S(1)} fusion(bf16[128,8,128]{0,2,1:T(8,128)(2,1)S(1)} %bitcast.84, f32[8,128]{1,0:T(8,128)S(1)} %fusion.10, f32[8,128,640]{1,2,0:T(8,128)} %copy-done, f32[8,128]{1,0:T(8,128)S(1)} %get-tuple-element.12, s32[]{:T(128)S(6)} %select_n.42, s32[]{:T(128)S(6)} %add.46, bf16[1024,256]{1,0:T(8,128)(2,1)S(1)} %bitcast.78), kind=kOutput, calls=%fused_computation.5 | convolution fusion | flops 170393600 | bytes 4726792 | tf_op jit(solution)/shard_map/sgh,kh->gsk/dot_general | solution.py:26
  31.6 0.0 copy-done.1
  31.6 0.5 fusion.12
  32.2 0.2 copy.46
  32.3 0.1 broadcast_in_dim.41
  32.4 0.8 slice.15
  33.3 0.0 reduce-scatter.3.cloned.1.call-update
  33.3 0.0 all-gather.3.cloned.1.call-start
  33.3 0.6 fusion.8
  33.9 33.9 %reduce-scatter.3.cloned.1.call-done = bf16[128,256]{1,0:T(8,128)(2,1)} async-done(((bf16[1024,256]{1,0:T(8,128)(2,1)}), bf16[128,256]{1,0:T(8,128)(2,1)}) %reduce-scatter.3.cloned.1.call-update) | async-done | bytes 65552 | tf_op jit(solution)/shard_map/reduce_scatter | solution.py:82
  67.9 0.9 copy.47
  68.8 0.8 pad_maximum_fusion
  69.6 0.0 all-gather.3.cloned.1.call-update
  69.6 0.0 reduce-scatter.5.cloned.1.call-start
  69.7 4.1 %copy.48 = bf16[1,128,8192]{1,2,0:T(8,128)(2,1)} copy(bf16[1,128,8192]{2,1,0:T(8,128)(2,1)} %param.5) | data formatting | bytes 4194304 | tf_op args[0]
  73.7 40.6 %all_to_all.15 = bf16[128,8,1024]{0,2,1:T(8,128)(2,1)S(1)} all-to-all(bf16[128,8,1024]{0,2,1:T(8,128)(2,1)} %bitcast.75), channel_id=1, replica_groups=mesh['dp'=4,'ctx'=8] {'ctx'}, dimensions={1} | all-to-all | bytes 4194304 | tf_op jit(solution)/shard_map/all_to_all | solution.py:88
  114.4 2.6 %copy.49 = bf16[8,128,1,1024]{3,1,0,2:T(8,128)(2,1)} copy(bf16[8,128,1,1024]{1,3,0,2:T(8,128)(2,1)S(1)} %bitcast.74) | data formatting | bytes 4194304 | tf_op jit(solution)/shard_map/all_to_all | solution.py:88
  117.0 0.0 all-gather.3.cloned.1.call-done
  117.0 6.8 %fusion.1 = bf16[1024,1280]{0,1:T(8,128)(2,1)} fusion(bf16[1024,1280]{0,1:T(8,128)(2,1)} %all-gather.3.cloned.1.call-done, bf16[1024,1024]{1,0:T(8,128)(2,1)} %bitcast.85), kind=kOutput, calls=%fused_computation.2 | convolution fusion | flops 2685665280 | bytes 7340032 | tf_op jit(solution)/shard_map/dot_general | solution.py:44
  123.8 0.0 reduce-scatter.5.cloned.1.call-update
  123.8 0.9 copy.50
  124.7 50.5 %reduce-scatter.5.cloned.1.call-done = bf16[256,1280]{0,1:T(8,128)(2,1)} async-done(((bf16[1024,1280]{0,1:T(8,128)(2,1)}), bf16[256,1280]{0,1:T(8,128)(2,1)}) %reduce-scatter.5.cloned.1.call-update) | async-done | bytes 655376 | tf_op jit(solution)/shard_map/reduce_scatter | solution.py:92
  175.2 2.4 %copy.51 = f32[256,1280]{1,0:T(8,128)} copy(bf16[256,1280]{0,1:T(8,128)(2,1)} %reduce-scatter.5.cloned.1.call-done) | data formatting | bytes 1966080
  (3 shorter events, 0.1 us)
Async XLA Ops:
  7.2 60.7 %reduce-scatter.3.cloned.1.call-start = ((), (), s32[]{:S(2)}) async-start(), calls=%async_computation.3 | async-start | bytes 589824 | tf_op jit(solution)/shard_map/reduce_scatter | solution.py:82
  27.1 1.5 copy-start
  29.1 2.4 %copy-start.1 = (bf16[1,128,1024]{1,2,0:T(8,128)(2,1)S(1)}, bf16[1,128,1024]{1,2,0:T(8,128)(2,1)}, u32[]{:S(2)}) copy-start(bf16[1,128,1024]{1,2,0:T(8,128)(2,1)} %copy.61) | copy-start | bytes 786436
  33.3 83.7 %all-gather.3.cloned.1.call-start = ((), (), s32[]{:S(2)}) async-start(), calls=%async_computation.4 | async-start | bytes 2949120 | tf_op jit(solution)/shard_map/all_gather | solution.py:91
  69.6 105.6 %reduce-scatter.5.cloned.1.call-start = ((), (), s32[]{:S(2)}) async-start(), calls=%async_computation.5 | async-start | bytes 3276800 | tf_op jit(solution)/shard_map/reduce_scatter | solution.py:92
Sparse Core Ops, SparseCore 0:
  33.4 34.4 reduce-scatter.2
  70.5 44.5 all-gather.2
  124.0 51.1 reduce-scatter.4
where the time goes:
time: 185 us; the launch traced here: 184 us
  waiting for transfers between devices  84.5 us (46%)
  blocking collectives  52.2 us (28%)
  local copies, waits for them, and re-layouts  15.6 us (8%)
  between operations  13.9 us (8%)
  matrix products  13.6 us (7%)
  other arithmetic  4.11 us (2%)
    reduce_scatter x1, waiting for transfers between devices, shards(): lax.psum_scatter(partial_weights.astype(jnp.bfloat16), 'dp', scatter_dime...  50.5 us
    all_to_all x1, blocking collectives, shards(): lax.all_to_all(pieces, 'ctx', split_axis=1, concat_axis=0, tiled=True)  40.6 us
    reduce_scatter x1, waiting for transfers between devices, shards(): lax.psum_scatter(kv_terms.astype(jnp.bfloat16), 'ctx', scatter_dimension=...  33.9 us
    all_gather x1, blocking collectives, shards(): whole_kv = lax.all_gather(own_kv, 'ctx', axis=0, tiled=True)  11.6 us
    unnamed x8, local copies, waits for them, and re-layouts  9.17 us
    dot_general x1, matrix products, fold_rows(): lax.dot_general(features, piece_rows, (((0,), (0,)), ((), ())), preferred...  6.8 us
  transfers between devices with their start and end apart: 3, of which 2 were waited for; matrix products, arithmetic and copies ran while one was open for 4% of the time, Pallas kernels for 0%

commit v1 on v0

v1 whole, which is shorter than its diff:
```python
import functools

import jax
import jax.numpy as jnp
from jax import lax
from jax.experimental import pallas as pl
from jax.experimental.pallas import tpu as pltpu
from jax.sharding import PartitionSpec as P

F32 = jnp.float32
BF16 = jnp.bfloat16
VMEM_LIMIT = 48 * 1024 * 1024


def dot(a, b, ca, cb):
    return lax.dot_general(a, b, (((ca,), (cb,)), ((), ())), preferred_element_type=F32)


def attention_kernel(own_ref, lens_ref, q_ref, do_ref, *refs, span, head, group, docs):
    kv_refs, (gq_ref, terms_ref) = refs[:span], refs[span:]
    rows = q_ref.shape[0]
    scale = head ** (-0.5)
    own = own_ref[0]
    first = jnp.int32(0)
    start = jnp.int32(0)
    for d in range(docs):
        first = jnp.where(start <= own, jnp.maximum(first, start), first)
        start = start + lens_ref[0, d]
    kv = jnp.concatenate([r[...] for r in kv_refs], axis=0)
    keys, values = kv[:, :head], kv[:, head:]
    keys_t = keys.T
    width = 2 * rows
    key_at = lax.broadcasted_iota(jnp.int32, (span * rows, width), 0)
    query_at = lax.broadcasted_iota(jnp.int32, (span * rows, width), 1) % rows
    low = (first - own + span - 1) * rows
    allowed = (key_at >= low) & (key_at <= query_at + (span - 1) * rows)
    dk = jnp.zeros((span * rows, head), F32)
    dv = jnp.zeros((span * rows, head), F32)
    for pair in range(group // 2):
        at = [2 * pair * head, (2 * pair + 1) * head]
        q2 = jnp.concatenate([q_ref[:, a : a + head] for a in at], axis=0)
        do2 = jnp.concatenate([do_ref[:, a : a + head] for a in at], axis=0)
        scores = jnp.where(allowed, dot(keys, q2, 1, 1) * scale, -1e30)
        exps = jnp.exp(scores - jnp.max(scores, axis=0, keepdims=True))
        probs = exps * (1.0 / jnp.sum(exps, axis=0, keepdims=True))
        probs_half = probs.astype(BF16)
        dprobs = dot(values, do2, 1, 1)
        row_dots = jnp.sum(probs_half.astype(F32) * dprobs, axis=0, keepdims=True)
        dscores_half = (probs * (dprobs - row_dots)).astype(BF16)
        dk = dk + dot(dscores_half, q2, 1, 0)
        dv = dv + dot(probs_half, do2, 1, 0)
        gq_t = dot(keys_t, dscores_half, 1, 0) * scale
        for i, a in enumerate(at):
            gq_ref[:, a : a + head] = gq_t[:, i * rows : (i + 1) * rows].T.astype(BF16)
    terms_ref[:, :, :head] = (dk * scale).astype(BF16).reshape(span, rows, head)
    terms_ref[:, :, head:] = dv.astype(BF16).reshape(span, rows, head)


def attention(own, lens, q, do, slots, head):
    span, rows = len(slots), q.shape[0]
    group = q.shape[1] // head
    smem = pl.BlockSpec(memory_space=pltpu.SMEM)
    vmem = pl.BlockSpec(memory_space=pltpu.VMEM)
    return pl.pallas_call(
        functools.partial(
            attention_kernel, span=span, head=head, group=group, docs=lens.shape[1]
        ),
        out_shape=(
            jax.ShapeDtypeStruct(q.shape, BF16),
            jax.ShapeDtypeStruct((span, rows, 2 * head), BF16),
        ),
        in_specs=[smem, smem] + [vmem] * (2 + span),
        out_specs=(vmem, vmem),
        compiler_params=pltpu.CompilerParams(vmem_limit_bytes=VMEM_LIMIT),
        cost_estimate=pl.CostEstimate(
            flops=12 * group * rows * rows * span * head,
            bytes_accessed=6 * q.size + 4 * span * rows * 2 * head,
            transcendentals=group * rows * rows * span,
        ),
        name="attention",
    )(own, lens, q, do, *slots)


def spread_kernel(place_ref, x_ref, *refs, ctx, dp, part):
    outs, sem = refs[:-1], refs[-1]
    z, c = place_ref[0], place_ref[1]
    core = c % 2
    first = 2 + 2 * core
    chips = (0, first, 6 - first, 6)
    copies = []
    for far in range(2):
        for at, flip in enumerate(chips):
            for other in range(2):
                dest = c ^ flip ^ other
                for high in range(2):
                    plane = 2 * high + (z % 2) ^ far
                    src = pl.multiple_of((dest * dp + plane) * part, part)
                    copies.append(
                        pltpu.make_async_copy(
                            x_ref.at[:, pl.ds(src, part)],
                            outs[4 * far + at].at[other, :, pl.ds(high * part, part)],
                            sem.at[len(copies)],
                        )
                    )
    for copy in copies:
        copy.start()
    for copy in copies:
        copy.wait()


def spread(place, x, ctx, dp):
    rows, width = x.shape
    part = width // (ctx * dp)
    piece = jax.ShapeDtypeStruct((2, rows, 2 * part), BF16)
    hbm = pl.BlockSpec(memory_space=pl.ANY)
    return pl.pallas_call(
        functools.partial(spread_kernel, ctx=ctx, dp=dp, part=part),
        out_shape=(piece,) * 8,
        in_specs=[pl.BlockSpec(memory_space=pltpu.SMEM), hbm],
        out_specs=(hbm,) * 8,
        scratch_shapes=[pltpu.SemaphoreType.DMA((32,))],
        cost_estimate=pl.CostEstimate(flops=0, bytes_accessed=4 * x.size, transcendentals=0),
        name="spread",
    )(place, x)


def turn_kernel(*refs):
    kept, siblings, out = refs[:8], refs[8:10], refs[10]
    rows = kept[0].shape[1]
    for at in range(4):
        for far in range(2):
            j = 2 * at + far
            out[:, j * rows : (j + 1) * rows] = kept[4 * far + at][0].T
            out[:, (8 + j) * rows : (9 + j) * rows] = siblings[far][at].T


def turn(kept, siblings):
    _, rows, width = kept[0].shape
    vmem = pl.BlockSpec(memory_space=pltpu.VMEM)
    half = pl.BlockSpec((1, rows, width), lambda i: (0, 0, 0))
    whole = pl.BlockSpec((4, rows, width), lambda i: (0, 0, 0))
    return pl.pallas_call(
        turn_kernel,
        grid=(1,),
        out_shape=jax.ShapeDtypeStruct((width, 16 * rows), BF16),
        in_specs=[half] * 8 + [whole] * 2,
        out_specs=pl.BlockSpec((width, 16 * rows), lambda i: (0, 0)),
        compiler_params=pltpu.CompilerParams(vmem_limit_bytes=VMEM_LIMIT),
        cost_estimate=pl.CostEstimate(
            flops=0, bytes_accessed=64 * rows * width, transcendentals=0
        ),
        name="turn",
    )(*kept, *siblings)


def fold_kernel(side_ref, x_ref, *refs):
    cols, out = refs[:-1], refs[-1]
    depth = cols[0].shape[0] * cols[0].shape[1]
    total = None
    for j, col in enumerate(cols):
        block = col[...].reshape(depth, col.shape[2])
        term = dot(x_ref[:, j * depth : (j + 1) * depth], block, 1, 0)
        total = term if total is None else total + term
    out[...] = total.astype(out.dtype)


def fold(side, turned, cols, dtype):
    width, depth = turned.shape
    half = width // 2
    n = cols[0].shape[2]
    return pl.pallas_call(
        fold_kernel,
        grid_spec=pltpu.PrefetchScalarGridSpec(
            num_scalar_prefetch=1,
            grid=(1,),
            in_specs=[pl.BlockSpec((half, depth), lambda i, side: (side[0], 0))]
            + [pl.BlockSpec(c.shape, lambda i, side: (0, 0, 0)) for c in cols],
            out_specs=pl.BlockSpec((half, n), lambda i, side: (0, 0)),
        ),
        out_shape=jax.ShapeDtypeStruct((half, n), dtype),
        compiler_params=pltpu.CompilerParams(vmem_limit_bytes=VMEM_LIMIT),
        cost_estimate=pl.CostEstimate(
            flops=2 * half * depth * n,
            bytes_accessed=2 * half * depth + 2 * depth * n + 4 * half * n,
            transcendentals=0,
        ),
        name="fold",
    )(side, turned, *cols)


def fold_rows(features, piece_rows):
    return lax.dot_general(
        features, piece_rows, (((0,), (0,)), ((), ())), preferred_element_type=F32
    )


def attend(own_index, queries, keys_values, grad_output, doc_lengths):
    ctx = lax.axis_size("ctx")
    span = ctx // 2 + 1
    own_kv = keys_values[0]
    slots = [own_kv]
    for d in range(1, span):
        moved = lax.ppermute(own_kv, "ctx", [(i, (i + d) % ctx) for i in range(ctx)])
        slots.insert(0, moved)
    head = keys_values.shape[2] // 2
    return attention(
        own_index[None], doc_lengths, queries[0], grad_output[0], slots, head
    )


def sum_terms(terms):
    ctx = lax.axis_size("ctx")
    span = terms.shape[0]
    total = terms[span - 1].astype(F32)
    for d in range(1, span):
        moved = lax.ppermute(
            terms[span - 1 - d], "ctx", [(i, (i - d) % ctx) for i in range(ctx)]
        )
        total = total + moved.astype(F32)
    return total.astype(BF16)


def hop(value, dz, of_core):
    pairs = [
        (8 * z + c, 8 * (z ^ dz) + (c ^ of_core[c % 2])) for z in range(4) for c in range(8)
    ]
    return lax.ppermute(value, ("dp", "ctx"), pairs)


FIRST, SECOND, DIAGONAL, STAY, SIBLING = (2, 4), (4, 2), (6, 6), (0, 0), (1, 1)


def gather_pairs(cols):
    both = jnp.stack([cols, hop(cols, 1, STAY)])
    from_first = hop(both, 0, FIRST)
    from_second = hop(both, 0, SECOND)
    from_diagonal = hop(from_first, 0, SECOND)
    kept = [both, from_first, from_second, from_diagonal]
    return kept + [hop(k, 0, SIBLING) for k in kept]


def shards_cube(normed_input, queries, keys_values, grad_output, doc_lengths):
    ctx, dp = lax.axis_size("ctx"), lax.axis_size("dp")
    own, z = lax.axis_index("ctx"), lax.axis_index("dp")
    pieces = spread(jnp.stack([z, own]), normed_input[0], ctx, dp)
    grad_query, terms = attend(own, queries, keys_values, grad_output, doc_lengths)
    chips = (STAY, FIRST, SECOND, DIAGONAL)
    kept = [pieces[0]] + [hop(pieces[i], 0, chips[i]) for i in range(1, 4)]
    kept += [hop(pieces[4 + i], 1, chips[i]) for i in range(4)]
    siblings = [
        hop(jnp.stack([k[1] for k in kept[4 * far : 4 * far + 4]]), 0, SIBLING)
        for far in range(2)
    ]
    turned = turn(kept, siblings)
    side = (z // 2)[None]
    grad_kv = sum_terms(terms)
    totals = []
    for cols in (grad_query, grad_kv):
        gathered = gather_pairs(cols)
        sent = hop(fold(1 - side, turned, gathered, BF16), 2, STAY)
        totals.append(fold(side, turned, gathered, F32) + sent.astype(F32))
    return grad_query[None], grad_kv[None], jnp.concatenate(totals, axis=1)


def shards(normed_input, queries, keys_values, grad_output, doc_lengths):
    ctx = lax.axis_size("ctx")
    own = lax.axis_index("ctx")
    shard_rows, model_width = normed_input.shape[1:]
    grad_query, terms = attend(own, queries, keys_values, grad_output, doc_lengths)
    grad_kv = sum_terms(terms)
    grad_cols = jnp.concatenate([grad_query, grad_kv], axis=1)
    part = model_width // ctx
    pieces = normed_input[0].reshape(shard_rows, ctx, part)
    my_features = lax.all_to_all(pieces, "ctx", split_axis=1, concat_axis=0, tiled=True)
    my_features = my_features.reshape(ctx * shard_rows, part)
    partial = fold_rows(my_features, lax.all_gather(grad_cols, "ctx", axis=0, tiled=True))
    grad_weights = lax.psum_scatter(
        partial.astype(BF16), "dp", scatter_dimension=0, tiled=True
    ).astype(F32)
    return grad_query[None], grad_kv[None], grad_weights


def solution(mesh):
    cube = mesh.shape["dp"] == 4 and mesh.shape["ctx"] == 8
    spec = P("dp", "ctx", None)
    return jax.shard_map(
        shards_cube if cube else shards,
        mesh=mesh,
        in_specs=(spec, spec, spec, spec, P("dp", None)),
        out_specs=(spec, spec, P(("ctx", "dp"), None)),
        check_vma=False,
    )
```

time: 185 us -> 207 us (1.12)
  Pallas kernels: 0 us -> 79.5 us
  blocking collectives: 52.2 us -> 0 us
  starting transfers between devices: 0.12 us -> 39.8 us
  waiting for transfers between devices: 84.5 us -> 67.4 us
  matrix products: 13.6 us -> 0 us
  between operations: 13.9 us -> 1.01 us
    reduce_scatter x2 -> x0, waiting for transfers between devices: 84.5 us -> none  [the longest x1 50.5 us: shards(): lax.psum_scatter(partial_weights.astype(jnp.bfloat16), 'dp', scatter_dime...]
    pallas_call x0 -> x7, Pallas kernels: none -> 79.5 us  [the longest x1 65.6 us: spread(): pl.pallas_call(functools.partial(spread_kernel, ctx=ctx, dp=dp, part=part...]
    ppermute x0 -> x35, waiting for transfers between devices: none -> 67.4 us  [the longest x27 56.6 us: hop(): return lax.ppermute(value, ('dp', 'ctx'), pairs)]
    all_to_all x1 -> x0, blocking collectives: 40.6 us -> none  [shards(): lax.all_to_all(pieces, 'ctx', split_axis=1, concat_axis=0, tiled=True)]
    ppermute x0 -> x35, starting transfers between devices: none -> 39.8 us  [the longest x27 22.9 us: hop(): return lax.ppermute(value, ('dp', 'ctx'), pairs)]
    all_gather x1 -> x0, blocking collectives: 11.6 us -> none  [shards(): whole_kv = lax.all_gather(own_kv, 'ctx', axis=0, tiled=True)]
    dot_general x6 -> x0, matrix products: 11.4 us -> none  [the longest x1 6.8 us: fold_rows(): lax.dot_general(features, piece_rows, (((0,), (0,)), ((), ())), preferred...]
    unnamed x8 -> x70, local copies, waits for them, and re-layouts: 9.17 us -> 15.9 us
  transfers between devices with their start and end apart: 3 -> 35, of which waited for: 2 -> 14; matrix products, arithmetic and copies ran while one was open for 4% -> 0% of each run, Pallas kernels for 0% -> 36%
where the time goes in v1:
time: 207 us; the launch traced here: 206 us
  Pallas kernels  79.5 us (38%)
  waiting for transfers between devices  67.4 us (33%)
  starting transfers between devices  39.8 us (19%)
  local copies, waits for them, and re-layouts  16 us (8%)
  other arithmetic  2.16 us (1%)
    pallas_call x1, Pallas kernels, spread(): pl.pallas_call(functools.partial(spread_kernel, ctx=ctx, dp=dp, part=part...  65.6 us
    ppermute x27, waiting for transfers between devices, hop(): return lax.ppermute(value, ('dp', 'ctx'), pairs)  56.6 us
    ppermute x27, starting transfers between devices, hop(): return lax.ppermute(value, ('dp', 'ctx'), pairs)  22.9 us
    unnamed x70, local copies, waits for them, and re-layouts  15.9 us
    ppermute x4, starting transfers between devices, sum_terms(): lax.ppermute(terms[span - 1 - d], 'ctx', [(i, (i - d) % ctx) for i in ran...  12 us
    pallas_call x4, Pallas kernels, fold(): pl.pallas_call(fold_kernel, grid_spec=pltpu.PrefetchScalarGridSpec(num_sc...  8.74 us
    ppermute x4, waiting for transfers between devices, sum_terms(): lax.ppermute(terms[span - 1 - d], 'ctx', [(i, (i - d) % ctx) for i in ran...  5.89 us
    ppermute x4, waiting for transfers between devices, attend(): lax.ppermute(own_kv, 'ctx', [(i, (i + d) % ctx) for i in range(ctx)])  4.89 us
  transfers between devices with their start and end apart: 35, of which 14 were waited for; matrix products, arithmetic and copies ran while one was open for 0% of the time, Pallas kernels for 36%

profile of v1, /device:TPU:0, one launch (start us, length us, event | category | flops | bytes accessed | tf_op | source)
XLA Modules:
  0.0 206.0 jit_solution(7331738853127507702)
XLA Ops:
  0.6 3.0 %collective-permute-start = (bf16[128,256]{1,0:T(8,128)(2,1)}, bf16[128,256]{1,0:T(8,128)(2,1)S(1)}, u32[]{:S(2)}, u32[]{:S(2)}) collective-permute-start(bf16[128,256]{1,0:T(8,128)(2,1)} %bitcast.24), channel_id=1, source_target_pairs={{0,4},{1,5},{2,6},{3,7},{4,0},{5,1},{6,2},{7,3},{8,12},{9,13},{10,... | collective-permute-start | bytes 196616 | tf_op jit(solution)/shard_map/ppermute | solution.py:203
  4.3 0.8 collective-permute-start.2
  6.2 1.3 collective-permute-done.1.refs_1_
  7.6 2.5 %collective-permute-done.2.refs_2_ = bf16[128,256]{1,0:T(8,128)(2,1)S(1)} collective-permute-done((bf16[128,256]{1,0:T(8,128)(2,1)}, bf16[128,256]{1,0:T(8,128)(2,1)S(1)}, u32[]{:S(2)}, u32[]{:S(2)}) %collective-permute-start.2) | collective-permute-done | bytes 65568 | tf_op jit(solution)/shard_map/ppermute | solution.py:203
  10.4 0.9 copy-done.23
  11.3 0.9 copy-done.24
  12.3 0.8 copy-done.25
  13.8 4.5 %attention.1 = (bf16[128,1024]{1,0:T(8,128)(2,1)}, bf16[5,128,256]{2,1,0:T(8,128)(2,1)S(1)}) custom-call(s32[1]{0:T(128)} %bitcast.own_ref, s32[1,3]{1,0:T(1,128)S(1)} %copy-done.26, bf16[128,1024]{1,0:T(8,128)(2,1)S(1)} %bitcast.22, bf16[128,1024]{1,0:T(8,128)(2,1)S(1)} %bitcast.23, bf16[128,256]{1,0:T(8,128)(2,1)S(1)} %collective-permute-done.refs_0_, ...), custom_call_target="tpu_custom_call" | custom-call | flops 1006632960 | bytes 1441792 | tf_op jit(solution)/shard_map/attention/pallas_call | solution.py:64
  18.3 1.6 collective-permute-start.17
  20.5 65.6 %spread.1 = (bf16[2,128,512]{2,1,0:T(8,128)(2,1)}, bf16[2,128,512]{2,1,0:T(8,128)(2,1)}, bf16[2,128,512]{2,1,0:T(8,128)(2,1)}, bf16[2,128,512]{2,1,0:T(8,128)(2,...) custom-call(s32[2]{0:T(128)} %pad_add_fusion.place_ref, ...), custom_call_target="tpu_custom_call" | custom-call | bytes 4194304 | tf_op jit(solution)/shard_map/spread/pallas_call | solution.py:116
  86.2 1.3 collective-permute-start.10
  87.5 1.5 collective-permute-start.18
  89.0 0.9 collective-permute-start.7
  89.9 1.3 collective-permute-start.5
  91.2 4.0 %collective-permute-done.7 = bf16[128,256]{1,0:T(8,128)(2,1)S(1)} collective-permute-done((bf16[128,256]{1,0:T(8,128)(2,1)S(1)}, bf16[128,256]{1,0:T(8,128)(2,1)S(1)}, u32[]{:S(2)}, u32[]{:S(2)}) %collective-permute-start.7) | collective-permute-done | bytes 65568 | tf_op jit(solution)/shard_map/ppermute | solution.py:216
  95.2 9.9 %collective-permute-start.4 = (bf16[128,256]{1,0:T(8,128)(2,1)S(1)}, bf16[128,256]{1,0:T(8,128)(2,1)S(1)}, u32[]{:S(2)}, u32[]{:S(2)}) collective-permute-start(bf16[128,256]{1,0:T(8,128)(2,1)S(1)} %get-tuple-element.23), channel_id=1, source_target_pairs={{0,7},{1,0},{2,1},{3,2},{4,3},{5,4},{6,5},{7,6},{8,15},{9,8},{10,9... | collective-permute-start | bytes 196616 | tf_op jit(solution)/shard_map/ppermute | solution.py:216
  105.7 1.9 collective-permute-done.4
  108.0 1.2 collective-permute-start.12
  109.4 4.5 %collective-permute-done.9.refs_2_ = bf16[2,128,512]{2,1,0:T(8,128)(2,1)S(1)} collective-permute-done((bf16[2,128,512]{2,1,0:T(8,128)(2,1)S(1)}, bf16[2,128,512]{2,1,0:T(8,128)(2,1)S(1)}, u32[]{:S(2)}, u32[]{:S(2)}) %collective-permute-start.9) | collective-permute-done | bytes 262176 | tf_op jit(solution)/shard_map/ppermute | solution.py:227
  113.9 1.7 collective-permute-start.13
  115.6 1.6 collective-permute-start.26
  117.4 9.1 %collective-permute-done.26 = bf16[128,256]{1,0:T(8,128)(2,1)S(1)} collective-permute-done((bf16[128,256]{1,0:T(8,128)(2,1)S(1)}, bf16[128,256]{1,0:T(8,128)(2,1)S(1)}, u32[]{:S(2)}, u32[]{:S(2)}) %collective-permute-start.26) | collective-permute-done | bytes 65568 | tf_op jit(solution)/shard_map/ppermute | solution.py:227
  127.3 1.3 collective-permute-start.20
  128.6 3.7 %collective-permute-start.14 = (bf16[2,128,512]{2,1,0:T(8,128)(2,1)S(1)}, bf16[2,128,512]{2,1,0:T(8,128)(2,1)S(1)}, u32[]{:S(2)}, u32[]{:S(2)}) collective-permute-start(bf16[2,128,512]{2,1,0:T(8,128)(2,1)S(1)} %copy-done.29), channel_id=1, source_target_pairs={{0,14},{1,15},{2,12},{3,13},{4,10},{5,11},{6,8},{7,9},{8,6},{9,7},... | collective-permute-start | bytes 786440 | tf_op jit(solution)/shard_map/ppermute | solution.py:227
  132.5 7.1 %collective-permute-done.14.refs_7_ = bf16[2,128,512]{2,1,0:T(8,128)(2,1)S(1)} collective-permute-done((bf16[2,128,512]{2,1,0:T(8,128)(2,1)S(1)}, bf16[2,128,512]{2,1,0:T(8,128)(2,1)S(1)}, u32[]{:S(2)}, u32[]{:S(2)}) %collective-permute-start.14) | collective-permute-done | bytes 262176 | tf_op jit(solution)/shard_map/ppermute | solution.py:227
  140.1 1.9 collective-permute-done.27.refs_1_
  142.0 1.1 collective-permute-start.29
  143.2 6.7 %collective-permute-done.28.refs_2_ = bf16[2,128,256]{2,1,0:T(8,128)(2,1)} collective-permute-done((bf16[2,128,256]{2,1,0:T(8,128)(2,1)S(1)}, bf16[2,128,256]{2,1,0:T(8,128)(2,1)}, u32[]{:S(2)}, u32[]{:S(2)}) %collective-permute-start.28) | collective-permute-done | bytes 131104 | tf_op jit(solution)/shard_map/ppermute | solution.py:227
  150.2 1.1 collective-permute-done.29.refs_3_
  153.2 0.8 copy-done.21
  154.6 1.1 collective-permute-done.23.refs_6_
  156.8 0.9 copy-done.6
  157.8 0.9 copy-done.8
  158.7 0.9 copy-done.10
  159.7 0.9 copy-done.12
  160.6 0.9 copy-done.14
  161.6 0.9 copy-done.16
  162.5 0.9 copy-done.18
  163.5 1.0 copy-done.20
  164.5 1.0 copy-done.22
  166.3 1.3 copy-done
  167.6 2.8 %fold.5 = bf16[256,1024]{1,0:T(8,128)(2,1)S(1)} custom-call(s32[1]{0:T(128)S(6)} %sub.9.side_ref, bf16[512,2048]{1,0:T(8,128)(2,1)} %copy-done, bf16[2,128,1024]{2,1,0:T(8,128)(2,1)S(1)} %pad_maximum_fusion.3.refs_0_, bf16[2,128,1024]{2,1,0:T(8,128)(2,1)S(1)} %collective-permute-done.18.refs_1_, bf16[2,128,1024]{2,1,0:T(8,128)(2,1)S(1)} %collective-permute-done.19.refs_2_, ...), custom_call_target="tpu_custom_call" | custom-call | flops 1073741824 | bytes 6291456 | tf_op jit(solution)/shard_map/fold/pallas_call | solution.py:171
  170.4 2.7 %collective-permute-start.25 = (bf16[256,1024]{1,0:T(8,128)(2,1)S(1)}, bf16[256,1024]{1,0:T(8,128)(2,1)S(1)}, u32[]{:S(2)}, u32[]{:S(2)}) collective-permute-start(bf16[256,1024]{1,0:T(8,128)(2,1)S(1)} %fold.5), channel_id=1, source_target_pairs={{0,16},{1,17},{2,18},{3,19},{4,20},{5,21},{6,22},{7,23},{8,24},{9,... | collective-permute-start | bytes 1572872 | tf_op jit(solution)/shard_map/ppermute | solution.py:227
  173.0 1.7 fold.7
  175.2 1.7 fold.6
  176.8 25.2 %collective-permute-done.34 = bf16[256,256]{1,0:T(8,128)(2,1)S(1)} collective-permute-done((bf16[256,256]{1,0:T(8,128)(2,1)S(1)}, bf16[256,256]{1,0:T(8,128)(2,1)S(1)}, u32[]{:S(2)}, u32[]{:S(2)}) %collective-permute-start.34) | collective-permute-done | bytes 131104 | tf_op jit(solution)/shard_map/ppermute | solution.py:227
  202.1 2.6 %fold.4 = f32[256,1024]{1,0:T(8,128)S(1)} custom-call(s32[1]{0:T(128)} %bitcast.11.side_ref, bf16[512,2048]{1,0:T(8,128)(2,1)} %copy-done, bf16[2,128,1024]{2,1,0:T(8,128)(2,1)S(1)} %pad_maximum_fusion.3.refs_0_, bf16[2,128,1024]{2,1,0:T(8,128)(2,1)S(1)} %collective-permute-done.18.refs_1_, bf16[2,128,1024]{2,1,0:T(8,128)(2,1)S(1)} %collective-permute-done.19.refs_2_, ...), custom_call_target="tpu_custom_call" | custom-call | flops 1073741824 | bytes 6291456 | tf_op jit(solution)/shard_map/fold/pallas_call | solution.py:171
  204.8 1.2 pad_maximum_fusion
  (117 shorter events, 11.3 us)
Async XLA Ops:
  0.6 5.6 %collective-permute-start = (bf16[128,256]{1,0:T(8,128)(2,1)}, bf16[128,256]{1,0:T(8,128)(2,1)S(1)}, u32[]{:S(2)}, u32[]{:S(2)}) collective-permute-start(bf16[128,256]{1,0:T(8,128)(2,1)} %bitcast.24), channel_id=1, source_target_pairs={{0,4},{1,5},{2,6},{3,7},{4,0},{5,1},{6,2},{7,3},{8,12},{9,13},{10,... | collective-permute-start | bytes 196616 | tf_op jit(solution)/shard_map/ppermute | solution.py:203
  3.7 3.9 %collective-permute-start.1 = (bf16[128,256]{1,0:T(8,128)(2,1)}, bf16[128,256]{1,0:T(8,128)(2,1)S(1)}, u32[]{:S(2)}, u32[]{:S(2)}) collective-permute-start(bf16[128,256]{1,0:T(8,128)(2,1)} %bitcast.25), channel_id=1, source_target_pairs={{0,3},{1,4},{2,5},{3,6},{4,7},{5,0},{6,1},{7,2},{8,11},{9,12},{10,... | collective-permute-start | bytes 196616 | tf_op jit(solution)/shard_map/ppermute | solution.py:203
  4.3 5.8 %collective-permute-start.2 = (bf16[128,256]{1,0:T(8,128)(2,1)}, bf16[128,256]{1,0:T(8,128)(2,1)S(1)}, u32[]{:S(2)}, u32[]{:S(2)}) collective-permute-start(bf16[128,256]{1,0:T(8,128)(2,1)} %bitcast.26), channel_id=1, source_target_pairs={{0,2},{1,3},{2,4},{3,5},{4,6},{5,7},{6,0},{7,1},{8,10},{9,11},{10,... | collective-permute-start | bytes 196616 | tf_op jit(solution)/shard_map/ppermute | solution.py:203
  5.2 5.2 %collective-permute-start.3 = (bf16[128,256]{1,0:T(8,128)(2,1)}, bf16[128,256]{1,0:T(8,128)(2,1)S(1)}, u32[]{:S(2)}, u32[]{:S(2)}) collective-permute-start(bf16[128,256]{1,0:T(8,128)(2,1)} %bitcast.27), channel_id=1, source_target_pairs={{0,1},{1,2},{2,3},{3,4},{4,5},{5,6},{6,7},{7,0},{8,9},{9,10},{10,1... | collective-permute-start | bytes 196616 | tf_op jit(solution)/shard_map/ppermute | solution.py:203
  18.3 69.1 %copy-start.27 = (bf16[128,1024]{1,0:T(8,128)(2,1)S(1)}, bf16[128,1024]{1,0:T(8,128)(2,1)}, u32[]{:S(2)}) copy-start(bf16[128,1024]{1,0:T(8,128)(2,1)} %get-tuple-element.13) | copy-start | bytes 786436
  18.3 69.1 %collective-permute-start.17 = (bf16[128,1024]{1,0:T(8,128)(2,1)}, bf16[128,1024]{1,0:T(8,128)(2,1)S(1)}, u32[]{:S(2)}, u32[]{:S(2)}) collective-permute-start(bf16[128,1024]{1,0:T(8,128)(2,1)} %get-tuple-element.13), channel_id=1, source_target_pairs={{0,8},{1,9},{2,10},{3,11},{4,12},{5,13},{6,14},{7,15},{8,0},{9,1},... | collective-permute-start | bytes 786440 | tf_op jit(solution)/shard_map/ppermute | solution.py:227
  86.1 19.0 %copy-start.34 = (bf16[2,128,512]{2,1,0:T(8,128)(2,1)S(1)}, bf16[2,128,512]{2,1,0:T(8,128)(2,1)}, u32[]{:S(2)}) copy-start(bf16[2,128,512]{2,1,0:T(8,128)(2,1)} %get-tuple-element.17) | copy-start | bytes 786436
  86.1 19.5 %copy-start.33 = (bf16[2,128,512]{2,1,0:T(8,128)(2,1)S(1)}, bf16[2,128,512]{2,1,0:T(8,128)(2,1)}, u32[]{:S(2)}) copy-start(bf16[2,128,512]{2,1,0:T(8,128)(2,1)} %get-tuple-element.16) | copy-start | bytes 786436
  86.1 19.5 %copy-start.4 = (bf16[2,128,512]{2,1,0:T(8,128)(2,1)S(1)}, bf16[2,128,512]{2,1,0:T(8,128)(2,1)}, u32[]{:S(2)}) copy-start(bf16[2,128,512]{2,1,0:T(8,128)(2,1)} %get-tuple-element.15.refs_0_) | copy-start | bytes 786436
  86.1 21.5 %copy-start.32 = (bf16[2,128,512]{2,1,0:T(8,128)(2,1)S(1)}, bf16[2,128,512]{2,1,0:T(8,128)(2,1)}, u32[]{:S(2)}) copy-start(bf16[2,128,512]{2,1,0:T(8,128)(2,1)} %get-tuple-element.19) | copy-start | bytes 786436
  86.1 21.9 %copy-start.31 = (bf16[2,128,512]{2,1,0:T(8,128)(2,1)S(1)}, bf16[2,128,512]{2,1,0:T(8,128)(2,1)}, u32[]{:S(2)}) copy-start(bf16[2,128,512]{2,1,0:T(8,128)(2,1)} %get-tuple-element.20) | copy-start | bytes 786436
  86.1 27.7 %copy-start.30 = (bf16[2,128,512]{2,1,0:T(8,128)(2,1)S(1)}, bf16[2,128,512]{2,1,0:T(8,128)(2,1)}, u32[]{:S(2)}) copy-start(bf16[2,128,512]{2,1,0:T(8,128)(2,1)} %get-tuple-element.21) | copy-start | bytes 786436
  86.2 21.9 %collective-permute-start.10 = (bf16[2,128,512]{2,1,0:T(8,128)(2,1)}, bf16[2,128,512]{2,1,0:T(8,128)(2,1)S(1)}, u32[]{:S(2)}, u32[]{:S(2)}) collective-permute-start(bf16[2,128,512]{2,1,0:T(8,128)(2,1)} %get-tuple-element.18), channel_id=1, source_target_pairs={{0,6},{1,7},{2,4},{3,5},{4,2},{5,3},{6,0},{7,1},{8,14},{9,15},{10,... | collective-permute-start | bytes 786440 | tf_op jit(solution)/shard_map/ppermute | solution.py:227
  87.5 39.8 %collective-permute-start.18 = (bf16[2,128,1024]{2,1,0:T(8,128)(2,1)S(1)}, bf16[2,128,1024]{2,1,0:T(8,128)(2,1)S(1)}, u32[]{:S(2)}, u32[]{:S(2)}) collective-permute-start(bf16[2,128,1024]{2,1,0:T(8,128)(2,1)S(1)} %pad_maximum_fusion.3.refs_0_), channel_id=1, source_target_pairs={{0,2},{1,5},{2,0},{3,7},{4,6},{5,1},{6,4},{7,3},{8,10},{9,13},{10,... | collective-permute-start | bytes 1572872 | tf_op jit(solution)/shard_map/ppermute | solution.py:227
  89.0 39.6 %copy-start.29 = (bf16[2,128,512]{2,1,0:T(8,128)(2,1)S(1)}, bf16[2,128,512]{2,1,0:T(8,128)(2,1)}, u32[]{:S(2)}) copy-start(bf16[2,128,512]{2,1,0:T(8,128)(2,1)} %get-tuple-element.22) | copy-start | bytes 786436
  89.0 6.1 %collective-permute-start.7 = (bf16[128,256]{1,0:T(8,128)(2,1)S(1)}, bf16[128,256]{1,0:T(8,128)(2,1)S(1)}, u32[]{:S(2)}, u32[]{:S(2)}) collective-permute-start(bf16[128,256]{1,0:T(8,128)(2,1)S(1)} %get-tuple-element.24), channel_id=1, source_target_pairs={{0,4},{1,5},{2,6},{3,7},{4,0},{5,1},{6,2},{7,3},{8,12},{9,13},{10,... | collective-permute-start | bytes 196616 | tf_op jit(solution)/shard_map/ppermute | solution.py:216
  89.9 15.1 %collective-permute-start.6 = (bf16[128,256]{1,0:T(8,128)(2,1)S(1)}, bf16[128,256]{1,0:T(8,128)(2,1)S(1)}, u32[]{:S(2)}, u32[]{:S(2)}) collective-permute-start(bf16[128,256]{1,0:T(8,128)(2,1)S(1)} %get-tuple-element.25), channel_id=1, source_target_pairs={{0,5},{1,6},{2,7},{3,0},{4,1},{5,2},{6,3},{7,4},{8,13},{9,14},{10,... | collective-permute-start | bytes 196616 | tf_op jit(solution)/shard_map/ppermute | solution.py:216
  89.9 15.7 %collective-permute-start.5 = (bf16[128,256]{1,0:T(8,128)(2,1)S(1)}, bf16[128,256]{1,0:T(8,128)(2,1)S(1)}, u32[]{:S(2)}, u32[]{:S(2)}) collective-permute-start(bf16[128,256]{1,0:T(8,128)(2,1)S(1)} %get-tuple-element.26), channel_id=1, source_target_pairs={{0,6},{1,7},{2,0},{3,1},{4,2},{5,3},{6,4},{7,5},{8,14},{9,15},{10,... | collective-permute-start | bytes 196616 | tf_op jit(solution)/shard_map/ppermute | solution.py:216
  95.2 12.4 %collective-permute-start.4 = (bf16[128,256]{1,0:T(8,128)(2,1)S(1)}, bf16[128,256]{1,0:T(8,128)(2,1)S(1)}, u32[]{:S(2)}, u32[]{:S(2)}) collective-permute-start(bf16[128,256]{1,0:T(8,128)(2,1)S(1)} %get-tuple-element.23), channel_id=1, source_target_pairs={{0,7},{1,0},{2,1},{3,2},{4,3},{5,4},{6,5},{7,6},{8,15},{9,8},{10,9... | collective-permute-start | bytes 196616 | tf_op jit(solution)/shard_map/ppermute | solution.py:216
  105.1 8.8 %collective-permute-start.9 = (bf16[2,128,512]{2,1,0:T(8,128)(2,1)S(1)}, bf16[2,128,512]{2,1,0:T(8,128)(2,1)S(1)}, u32[]{:S(2)}, u32[]{:S(2)}) collective-permute-start(bf16[2,128,512]{2,1,0:T(8,128)(2,1)S(1)} %copy-done.34), channel_id=1, source_target_pairs={{0,4},{1,3},{2,6},{3,1},{4,0},{5,7},{6,2},{7,5},{8,12},{9,11},{10,... | collective-permute-start | bytes 786440 | tf_op jit(solution)/shard_map/ppermute | solution.py:227
  105.6 10.0 %collective-permute-start.8 = (bf16[2,128,512]{2,1,0:T(8,128)(2,1)S(1)}, bf16[2,128,512]{2,1,0:T(8,128)(2,1)S(1)}, u32[]{:S(2)}, u32[]{:S(2)}) collective-permute-start(bf16[2,128,512]{2,1,0:T(8,128)(2,1)S(1)} %copy-done.33), channel_id=1, source_target_pairs={{0,2},{1,5},{2,0},{3,7},{4,6},{5,1},{6,4},{7,3},{8,10},{9,13},{10,... | collective-permute-start | bytes 786440 | tf_op jit(solution)/shard_map/ppermute | solution.py:227
  107.6 18.9 %collective-permute-start.11 = (bf16[2,128,512]{2,1,0:T(8,128)(2,1)S(1)}, bf16[2,128,512]{2,1,0:T(8,128)(2,1)S(1)}, u32[]{:S(2)}, u32[]{:S(2)}) collective-permute-start(bf16[2,128,512]{2,1,0:T(8,128)(2,1)S(1)} %copy-done.32), channel_id=1, source_target_pairs={{0,8},{1,9},{2,10},{3,11},{4,12},{5,13},{6,14},{7,15},{8,0},{9,1},... | collective-permute-start | bytes 786440 | tf_op jit(solution)/shard_map/ppermute | solution.py:227
  108.0 18.5 %copy-start.5 = (bf16[2,128,512]{2,1,0:T(8,128)(2,1)}, bf16[2,128,512]{2,1,0:T(8,128)(2,1)S(1)}, u32[]{:S(2)}) copy-start(bf16[2,128,512]{2,1,0:T(8,128)(2,1)S(1)} %collective-permute-done.10.refs_3_) | copy-start | bytes 786436
  108.0 20.6 %collective-permute-start.12 = (bf16[2,128,512]{2,1,0:T(8,128)(2,1)S(1)}, bf16[2,128,512]{2,1,0:T(8,128)(2,1)S(1)}, u32[]{:S(2)}, u32[]{:S(2)}) collective-permute-start(bf16[2,128,512]{2,1,0:T(8,128)(2,1)S(1)} %copy-done.31), channel_id=1, source_target_pairs={{0,10},{1,13},{2,8},{3,15},{4,14},{5,9},{6,12},{7,11},{8,2},{9,5},... | collective-permute-start | bytes 786440 | tf_op jit(solution)/shard_map/ppermute | solution.py:227
  109.3 33.7 %copy-start.28 = (bf16[128,256]{1,0:T(8,128)(2,1)}, bf16[128,256]{1,0:T(8,128)(2,1)S(1)}, u32[]{:S(2)}) copy-start(bf16[128,256]{1,0:T(8,128)(2,1)S(1)} %fusion.3) | copy-start | bytes 196612
  113.9 18.5 %collective-permute-start.13 = (bf16[2,128,512]{2,1,0:T(8,128)(2,1)S(1)}, bf16[2,128,512]{2,1,0:T(8,128)(2,1)S(1)}, u32[]{:S(2)}, u32[]{:S(2)}) collective-permute-start(bf16[2,128,512]{2,1,0:T(8,128)(2,1)S(1)} %copy-done.30), channel_id=1, source_target_pairs={{0,12},{1,11},{2,14},{3,9},{4,8},{5,15},{6,10},{7,13},{8,4},{9,3},... | collective-permute-start | bytes 786440 | tf_op jit(solution)/shard_map/ppermute | solution.py:227
  115.6 10.8 %collective-permute-start.26 = (bf16[128,256]{1,0:T(8,128)(2,1)S(1)}, bf16[128,256]{1,0:T(8,128)(2,1)S(1)}, u32[]{:S(2)}, u32[]{:S(2)}) collective-permute-start(bf16[128,256]{1,0:T(8,128)(2,1)S(1)} %fusion.3), channel_id=1, source_target_pairs={{0,8},{1,9},{2,10},{3,11},{4,12},{5,13},{6,14},{7,15},{8,0},{9,1},... | collective-permute-start | bytes 196616 | tf_op jit(solution)/shard_map/ppermute | solution.py:227
  126.5 25.0 %collective-permute-start.15 = (bf16[4,128,512]{2,1,0:T(8,128)(2,1)S(1)}, bf16[4,128,512]{2,1,0:T(8,128)(2,1)S(1)}, u32[]{:S(2)}, u32[]{:S(2)}) collective-permute-start(bf16[4,128,512]{2,1,0:T(8,128)(2,1)S(1)} %pad_maximum_fusion.1), channel_id=1, source_target_pairs={{0,1},{1,0},{2,3},{3,2},{4,5},{5,4},{6,7},{7,6},{8,9},{9,8},{10,11... | collective-permute-start | bytes 1572872 | tf_op jit(solution)/shard_map/ppermute | solution.py:227
  126.5 23.7 %copy-start.11 = (bf16[2,128,512]{2,1,0:T(8,128)(2,1)}, bf16[2,128,512]{2,1,0:T(8,128)(2,1)S(1)}, u32[]{:S(2)}) copy-start(bf16[2,128,512]{2,1,0:T(8,128)(2,1)S(1)} %collective-permute-done.11.refs_4_) | copy-start | bytes 786436
  126.5 26.1 %collective-permute-start.19 = (bf16[2,128,1024]{2,1,0:T(8,128)(2,1)S(1)}, bf16[2,128,1024]{2,1,0:T(8,128)(2,1)S(1)}, u32[]{:S(2)}, u32[]{:S(2)}) collective-permute-start(bf16[2,128,1024]{2,1,0:T(8,128)(2,1)S(1)} %pad_maximum_fusion.3.refs_0_), channel_id=1, source_target_pairs={{0,4},{1,3},{2,6},{3,1},{4,0},{5,7},{6,2},{7,5},{8,12},{9,11},{10,... | collective-permute-start | bytes 1572872 | tf_op jit(solution)/shard_map/ppermute | solution.py:227
  127.3 25.5 %collective-permute-start.20 = (bf16[2,128,1024]{2,1,0:T(8,128)(2,1)S(1)}, bf16[2,128,1024]{2,1,0:T(8,128)(2,1)S(1)}, u32[]{:S(2)}, u32[]{:S(2)}) collective-permute-start(bf16[2,128,1024]{2,1,0:T(8,128)(2,1)S(1)} %collective-permute-done.18.refs_1_), channel_id=1, source_target_pairs={{0,4},{1,3},{2,6},{3,1},{4,0},{5,7},{6,2},{7,5},{8,12},{9,11},{10,... | collective-permute-start | bytes 1572872 | tf_op jit(solution)/shard_map/ppermute | solution.py:227
  128.6 21.6 %copy-start.13 = (bf16[2,128,512]{2,1,0:T(8,128)(2,1)}, bf16[2,128,512]{2,1,0:T(8,128)(2,1)S(1)}, u32[]{:S(2)}) copy-start(bf16[2,128,512]{2,1,0:T(8,128)(2,1)S(1)} %collective-permute-done.12.refs_5_) | copy-start | bytes 786436
  128.6 10.9 %collective-permute-start.14 = (bf16[2,128,512]{2,1,0:T(8,128)(2,1)S(1)}, bf16[2,128,512]{2,1,0:T(8,128)(2,1)S(1)}, u32[]{:S(2)}, u32[]{:S(2)}) collective-permute-start(bf16[2,128,512]{2,1,0:T(8,128)(2,1)S(1)} %copy-done.29), channel_id=1, source_target_pairs={{0,14},{1,15},{2,12},{3,13},{4,10},{5,11},{6,8},{7,9},{8,6},{9,7},... | collective-permute-start | bytes 786440 | tf_op jit(solution)/shard_map/ppermute | solution.py:227
  132.4 19.0 %copy-start.15 = (bf16[2,128,512]{2,1,0:T(8,128)(2,1)}, bf16[2,128,512]{2,1,0:T(8,128)(2,1)S(1)}, u32[]{:S(2)}) copy-start(bf16[2,128,512]{2,1,0:T(8,128)(2,1)S(1)} %collective-permute-done.13.refs_6_) | copy-start | bytes 786436
  132.4 9.6 %collective-permute-start.27 = (bf16[2,128,256]{2,1,0:T(8,128)(2,1)S(1)}, bf16[2,128,256]{2,1,0:T(8,128)(2,1)}, u32[]{:S(2)}, u32[]{:S(2)}) collective-permute-start(bf16[2,128,256]{2,1,0:T(8,128)(2,1)S(1)} %pad_maximum_fusion.4.refs_0_), channel_id=1, source_target_pairs={{0,2},{1,5},{2,0},{3,7},{4,6},{5,1},{6,4},{7,3},{8,10},{9,13},{10,... | collective-permute-start | bytes 393224 | tf_op jit(solution)/shard_map/ppermute | solution.py:227
  139.6 10.4 %collective-permute-start.28 = (bf16[2,128,256]{2,1,0:T(8,128)(2,1)S(1)}, bf16[2,128,256]{2,1,0:T(8,128)(2,1)}, u32[]{:S(2)}, u32[]{:S(2)}) collective-permute-start(bf16[2,128,256]{2,1,0:T(8,128)(2,1)S(1)} %pad_maximum_fusion.4.refs_0_), channel_id=1, source_target_pairs={{0,4},{1,3},{2,6},{3,1},{4,0},{5,7},{6,2},{7,5},{8,12},{9,11},{10,... | collective-permute-start | bytes 393224 | tf_op jit(solution)/shard_map/ppermute | solution.py:227
  142.0 9.3 %collective-permute-start.29 = (bf16[2,128,256]{2,1,0:T(8,128)(2,1)}, bf16[2,128,256]{2,1,0:T(8,128)(2,1)}, u32[]{:S(2)}, u32[]{:S(2)}) collective-permute-start(bf16[2,128,256]{2,1,0:T(8,128)(2,1)} %collective-permute-done.27.refs_1_), channel_id=1, source_target_pairs={{0,4},{1,3},{2,6},{3,1},{4,0},{5,7},{6,2},{7,5},{8,12},{9,11},{10,... | collective-permute-start | bytes 393224 | tf_op jit(solution)/shard_map/ppermute | solution.py:227
  149.9 3.2 %collective-permute-start.16 = (bf16[4,128,512]{2,1,0:T(8,128)(2,1)S(1)}, bf16[4,128,512]{2,1,0:T(8,128)(2,1)S(1)}, u32[]{:S(2)}, u32[]{:S(2)}) collective-permute-start(bf16[4,128,512]{2,1,0:T(8,128)(2,1)S(1)} %pad_maximum_fusion.2), channel_id=1, source_target_pairs={{0,1},{1,0},{2,3},{3,2},{4,5},{5,4},{6,7},{7,6},{8,9},{9,8},{10,11... | collective-permute-start | bytes 1572872 | tf_op jit(solution)/shard_map/ppermute | solution.py:227
  151.3 2.8 %collective-permute-start.21 = (bf16[2,128,1024]{2,1,0:T(8,128)(2,1)S(1)}, bf16[2,128,1024]{2,1,0:T(8,128)(2,1)S(1)}, u32[]{:S(2)}, u32[]{:S(2)}) collective-permute-start(bf16[2,128,1024]{2,1,0:T(8,128)(2,1)S(1)} %pad_maximum_fusion.3.refs_0_), channel_id=1, source_target_pairs={{0,1},{1,0},{2,3},{3,2},{4,5},{5,4},{6,7},{7,6},{8,9},{9,8},{10,11... | collective-permute-start | bytes 1572872 | tf_op jit(solution)/shard_map/ppermute | solution.py:227
  152.2 2.2 %collective-permute-start.22 = (bf16[2,128,1024]{2,1,0:T(8,128)(2,1)S(1)}, bf16[2,128,1024]{2,1,0:T(8,128)(2,1)S(1)}, u32[]{:S(2)}, u32[]{:S(2)}) collective-permute-start(bf16[2,128,1024]{2,1,0:T(8,128)(2,1)S(1)} %collective-permute-done.18.refs_1_), channel_id=1, source_target_pairs={{0,1},{1,0},{2,3},{3,2},{4,5},{5,4},{6,7},{7,6},{8,9},{9,8},{10,11... | collective-permute-start | bytes 1572872 | tf_op jit(solution)/shard_map/ppermute | solution.py:227
  152.6 3.0 %collective-permute-start.23 = (bf16[2,128,1024]{2,1,0:T(8,128)(2,1)S(1)}, bf16[2,128,1024]{2,1,0:T(8,128)(2,1)S(1)}, u32[]{:S(2)}, u32[]{:S(2)}) collective-permute-start(bf16[2,128,1024]{2,1,0:T(8,128)(2,1)S(1)} %collective-permute-done.19.refs_2_), channel_id=1, source_target_pairs={{0,1},{1,0},{2,3},{3,2},{4,5},{5,4},{6,7},{7,6},{8,9},{9,8},{10,11... | collective-permute-start | bytes 1572872 | tf_op jit(solution)/shard_map/ppermute | solution.py:227
  152.8 14.8 %collective-permute-start.24 = (bf16[2,128,1024]{2,1,0:T(8,128)(2,1)S(1)}, bf16[2,128,1024]{2,1,0:T(8,128)(2,1)}, u32[]{:S(2)}, u32[]{:S(2)}) collective-permute-start(bf16[2,128,1024]{2,1,0:T(8,128)(2,1)S(1)} %collective-permute-done.20.refs_3_), channel_id=1, source_target_pairs={{0,1},{1,0},{2,3},{3,2},{4,5},{5,4},{6,7},{7,6},{8,9},{9,8},{10,11... | collective-permute-start | bytes 1572872 | tf_op jit(solution)/shard_map/ppermute | solution.py:227
  154.0 19.0 %collective-permute-start.30 = (bf16[2,128,256]{2,1,0:T(8,128)(2,1)S(1)}, bf16[2,128,256]{2,1,0:T(8,128)(2,1)}, u32[]{:S(2)}, u32[]{:S(2)}) collective-permute-start(bf16[2,128,256]{2,1,0:T(8,128)(2,1)S(1)} %pad_maximum_fusion.4.refs_0_), channel_id=1, source_target_pairs={{0,1},{1,0},{2,3},{3,2},{4,5},{5,4},{6,7},{7,6},{8,9},{9,8},{10,11... | collective-permute-start | bytes 393224 | tf_op jit(solution)/shard_map/ppermute | solution.py:227
  154.1 18.9 %collective-permute-start.31 = (bf16[2,128,256]{2,1,0:T(8,128)(2,1)}, bf16[2,128,256]{2,1,0:T(8,128)(2,1)}, u32[]{:S(2)}, u32[]{:S(2)}) collective-permute-start(bf16[2,128,256]{2,1,0:T(8,128)(2,1)} %collective-permute-done.27.refs_1_), channel_id=1, source_target_pairs={{0,1},{1,0},{2,3},{3,2},{4,5},{5,4},{6,7},{7,6},{8,9},{9,8},{10,11... | collective-permute-start | bytes 393224 | tf_op jit(solution)/shard_map/ppermute | solution.py:227
  154.5 18.5 %collective-permute-start.32 = (bf16[2,128,256]{2,1,0:T(8,128)(2,1)}, bf16[2,128,256]{2,1,0:T(8,128)(2,1)}, u32[]{:S(2)}, u32[]{:S(2)}) collective-permute-start(bf16[2,128,256]{2,1,0:T(8,128)(2,1)} %collective-permute-done.28.refs_2_), channel_id=1, source_target_pairs={{0,1},{1,0},{2,3},{3,2},{4,5},{5,4},{6,7},{7,6},{8,9},{9,8},{10,11... | collective-permute-start | bytes 393224 | tf_op jit(solution)/shard_map/ppermute | solution.py:227
  156.5 16.6 %collective-permute-start.33 = (bf16[2,128,256]{2,1,0:T(8,128)(2,1)}, bf16[2,128,256]{2,1,0:T(8,128)(2,1)}, u32[]{:S(2)}, u32[]{:S(2)}) collective-permute-start(bf16[2,128,256]{2,1,0:T(8,128)(2,1)} %collective-permute-done.29.refs_3_), channel_id=1, source_target_pairs={{0,1},{1,0},{2,3},{3,2},{4,5},{5,4},{6,7},{7,6},{8,9},{9,8},{10,11... | collective-permute-start | bytes 393224 | tf_op jit(solution)/shard_map/ppermute | solution.py:227
  170.4 34.3 %collective-permute-start.25 = (bf16[256,1024]{1,0:T(8,128)(2,1)S(1)}, bf16[256,1024]{1,0:T(8,128)(2,1)S(1)}, u32[]{:S(2)}, u32[]{:S(2)}) collective-permute-start(bf16[256,1024]{1,0:T(8,128)(2,1)S(1)} %fold.5), channel_id=1, source_target_pairs={{0,16},{1,17},{2,18},{3,19},{4,20},{5,21},{6,22},{7,23},{8,24},{9,... | collective-permute-start | bytes 1572872 | tf_op jit(solution)/shard_map/ppermute | solution.py:227
  174.8 27.3 %collective-permute-start.34 = (bf16[256,256]{1,0:T(8,128)(2,1)S(1)}, bf16[256,256]{1,0:T(8,128)(2,1)S(1)}, u32[]{:S(2)}, u32[]{:S(2)}) collective-permute-start(bf16[256,256]{1,0:T(8,128)(2,1)S(1)} %fold.7), channel_id=1, source_target_pairs={{0,16},{1,17},{2,18},{3,19},{4,20},{5,21},{6,22},{7,23},{8,24},{9,... | collective-permute-start | bytes 393224 | tf_op jit(solution)/shard_map/ppermute | solution.py:227
  (22 other events, 59.5 us)

commit v2 on v1

--- a/solution.py
+++ b/solution.py
@@ -9,7 +9,7 @@
 
 F32 = jnp.float32
 BF16 = jnp.bfloat16
-VMEM_LIMIT = 48 * 1024 * 1024
+VMEM_LIMIT = 16 * 1024 * 1024
 
 
 def dot(a, b, ca, cb):
@@ -81,44 +81,33 @@
     )(own, lens, q, do, *slots)
 
 
-def spread_kernel(place_ref, x_ref, *refs, ctx, dp, part):
-    outs, sem = refs[:-1], refs[-1]
+def spread_kernel(place_ref, x_ref, *outs, dp, part):
     z, c = place_ref[0], place_ref[1]
-    core = c % 2
-    first = 2 + 2 * core
+    first = 2 + 2 * (c % 2)
     chips = (0, first, 6 - first, 6)
-    copies = []
     for far in range(2):
         for at, flip in enumerate(chips):
             for other in range(2):
                 dest = c ^ flip ^ other
                 for high in range(2):
-                    plane = 2 * high + (z % 2) ^ far
+                    plane = (2 * high + z % 2) ^ far
                     src = pl.multiple_of((dest * dp + plane) * part, part)
-                    copies.append(
-                        pltpu.make_async_copy(
-                            x_ref.at[:, pl.ds(src, part)],
-                            outs[4 * far + at].at[other, :, pl.ds(high * part, part)],
-                            sem.at[len(copies)],
-                        )
-                    )
-    for copy in copies:
-        copy.start()
-    for copy in copies:
-        copy.wait()
+                    outs[4 * far + at][other, :, high * part : (high + 1) * part] = x_ref[
+                        :, pl.ds(src, part)
+                    ]
 
 
 def spread(place, x, ctx, dp):
     rows, width = x.shape
     part = width // (ctx * dp)
     piece = jax.ShapeDtypeStruct((2, rows, 2 * part), BF16)
-    hbm = pl.BlockSpec(memory_space=pl.ANY)
-    return pl.pallas_call(
-        functools.partial(spread_kernel, ctx=ctx, dp=dp, part=part),
+    vmem = pl.BlockSpec(memory_space=pltpu.VMEM)
+    return pl.pallas_call(
+        functools.partial(spread_kernel, dp=dp, part=part),
         out_shape=(piece,) * 8,
-        in_specs=[pl.BlockSpec(memory_space=pltpu.SMEM), hbm],
-        out_specs=(hbm,) * 8,
-        scratch_shapes=[pltpu.SemaphoreType.DMA((32,))],
+        in_specs=[pl.BlockSpec(memory_space=pltpu.SMEM), vmem],
+        out_specs=(vmem,) * 8,
+        compiler_params=pltpu.CompilerParams(vmem_limit_bytes=VMEM_LIMIT),
         cost_estimate=pl.CostEstimate(flops=0, bytes_accessed=4 * x.size, transcendentals=0),
         name="spread",
     )(place, x)
@@ -137,14 +126,11 @@
 def turn(kept, siblings):
     _, rows, width = kept[0].shape
     vmem = pl.BlockSpec(memory_space=pltpu.VMEM)
-    half = pl.BlockSpec((1, rows, width), lambda i: (0, 0, 0))
-    whole = pl.BlockSpec((4, rows, width), lambda i: (0, 0, 0))
     return pl.pallas_call(
         turn_kernel,
-        grid=(1,),
         out_shape=jax.ShapeDtypeStruct((width, 16 * rows), BF16),
-        in_specs=[half] * 8 + [whole] * 2,
-        out_specs=pl.BlockSpec((width, 16 * rows), lambda i: (0, 0)),
+        in_specs=[vmem] * 10,
+        out_specs=vmem,
         compiler_params=pltpu.CompilerParams(vmem_limit_bytes=VMEM_LIMIT),
         cost_estimate=pl.CostEstimate(
             flops=0, bytes_accessed=64 * rows * width, transcendentals=0
@@ -156,10 +142,12 @@
 def fold_kernel(side_ref, x_ref, *refs):
     cols, out = refs[:-1], refs[-1]
     depth = cols[0].shape[0] * cols[0].shape[1]
+    half = out.shape[0]
+    at = pl.multiple_of(side_ref[0] * half, half)
     total = None
     for j, col in enumerate(cols):
         block = col[...].reshape(depth, col.shape[2])
-        term = dot(x_ref[:, j * depth : (j + 1) * depth], block, 1, 0)
+        term = dot(x_ref[pl.ds(at, half), j * depth : (j + 1) * depth], block, 1, 0)
         total = term if total is None else total + term
     out[...] = total.astype(out.dtype)
 
@@ -168,15 +156,11 @@
     width, depth = turned.shape
     half = width // 2
     n = cols[0].shape[2]
+    vmem = pl.BlockSpec(memory_space=pltpu.VMEM)
     return pl.pallas_call(
         fold_kernel,
-        grid_spec=pltpu.PrefetchScalarGridSpec(
-            num_scalar_prefetch=1,
-            grid=(1,),
-            in_specs=[pl.BlockSpec((half, depth), lambda i, side: (side[0], 0))]
-            + [pl.BlockSpec(c.shape, lambda i, side: (0, 0, 0)) for c in cols],
-            out_specs=pl.BlockSpec((half, n), lambda i, side: (0, 0)),
-        ),
+        in_specs=[pl.BlockSpec(memory_space=pltpu.SMEM)] + [vmem] * (1 + len(cols)),
+        out_specs=vmem,
         out_shape=jax.ShapeDtypeStruct((half, n), dtype),
         compiler_params=pltpu.CompilerParams(vmem_limit_bytes=VMEM_LIMIT),
         cost_estimate=pl.CostEstimate(
@@ -255,7 +239,8 @@
     side = (z // 2)[None]
     grad_kv = sum_terms(terms)
     totals = []
-    for cols in (grad_query, grad_kv):
+    half = grad_query.shape[1] // 2
+    for cols in (grad_query[:, :half], grad_query[:, half:], grad_kv):
         gathered = gather_pairs(cols)
         sent = hop(fold(1 - side, turned, gathered, BF16), 2, STAY)
         totals.append(fold(side, turned, gathered, F32) + sent.astype(F32))

time: 207 us -> 125 us (0.60)
  Pallas kernels: 79.5 us -> 9.76 us
  waiting for transfers between devices: 67.4 us -> 56.4 us
    pallas_call x6 -> x8, Pallas kernels: 75 us -> 5.24 us  [the longest x6 3.73 us: fold(): pl.pallas_call(fold_kernel, in_specs=[pl.BlockSpec(memory_space=pltpu.SME...]
    ppermute x27 -> x36, starting transfers between devices: 22.9 us -> 32 us  [hop(): return lax.ppermute(value, ('dp', 'ctx'), pairs)]
    ppermute x4, starting transfers between devices: 12 us -> 4.23 us  [sum_terms(): lax.ppermute(terms[span - 1 - d], 'ctx', [(i, (i - d) % ctx) for i in ran...]
    ppermute x4, waiting for transfers between devices: 5.89 us -> 0.01 us  [sum_terms(): lax.ppermute(terms[span - 1 - d], 'ctx', [(i, (i - d) % ctx) for i in ran...]
    ppermute x4, waiting for transfers between devices: 4.89 us -> 0.84 us  [attend(): lax.ppermute(own_kv, 'ctx', [(i, (i + d) % ctx) for i in range(ctx)])]
    unnamed x70 -> x76, local copies, waits for them, and re-layouts: 15.9 us -> 13.8 us
    ppermute x27 -> x36, waiting for transfers between devices: 56.6 us -> 55.6 us  [hop(): return lax.ppermute(value, ('dp', 'ctx'), pairs)]
  transfers between devices with their start and end apart: 35 -> 44, of which waited for: 14 -> 13; matrix products, arithmetic and copies ran while one was open for 0% -> 1% of each run, Pallas kernels for 36% -> 8%
where the time goes in v2:
time: 125 us
  waiting for transfers between devices  56.4 us (45%)
  starting transfers between devices  41.1 us (33%)
  local copies, waits for them, and re-layouts  14.9 us (12%)
  Pallas kernels  9.76 us (8%)
  other arithmetic  1.63 us (1%)
    ppermute x36, waiting for transfers between devices, hop(): return lax.ppermute(value, ('dp', 'ctx'), pairs)  55.6 us
    ppermute x36, starting transfers between devices, hop(): return lax.ppermute(value, ('dp', 'ctx'), pairs)  32 us
    unnamed x76, local copies, waits for them, and re-layouts  13.8 us
    ppermute x4, starting transfers between devices, attend(): lax.ppermute(own_kv, 'ctx', [(i, (i + d) % ctx) for i in range(ctx)])  4.86 us
    pallas_call x1, Pallas kernels, attention(): pl.pallas_call(functools.partial(attention_kernel, span=span, head=head,...  4.53 us
    ppermute x4, starting transfers between devices, sum_terms(): lax.ppermute(terms[span - 1 - d], 'ctx', [(i, (i - d) % ctx) for i in ran...  4.23 us
    pallas_call x6, Pallas kernels, fold(): pl.pallas_call(fold_kernel, in_specs=[pl.BlockSpec(memory_space=pltpu.SME...  3.73 us
  transfers between devices with their start and end apart: 44, of which 13 were waited for; matrix products, arithmetic and copies ran while one was open for 1% of the time, Pallas kernels for 8%

profile of v2, /device:TPU:0, one launch (start us, length us, event | category | flops | bytes accessed | tf_op | source)
XLA Modules:
  0.0 124.9 jit_solution(6682866887002532741)
XLA Ops:
  0.6 3.0 %collective-permute-start = (bf16[128,256]{1,0:T(8,128)(2,1)}, bf16[128,256]{1,0:T(8,128)(2,1)S(1)}, u32[]{:S(2)}, u32[]{:S(2)}) collective-permute-start(bf16[128,256]{1,0:T(8,128)(2,1)} %bitcast.30), channel_id=1, source_target_pairs={{0,4},{1,5},{2,6},{3,7},{4,0},{5,1},{6,2},{7,3},{8,12},{9,13},{10,... | collective-permute-start | bytes 196616 | tf_op jit(solution)/shard_map/ppermute | solution.py:187
  4.3 0.8 collective-permute-start.2
  5.6 1.6 %copy-done = bf16[1,128,8192]{2,1,0:T(8,128)(2,1)S(1)} copy-done((bf16[1,128,8192]{2,1,0:T(8,128)(2,1)S(1)}, bf16[1,128,8192]{2,1,0:T(8,128)(2,1)}, u32[]{:S(2)}) %copy-start) | copy-done | bytes 2097176
  7.2 0.8 spread.1
  8.0 1.6 %collective-permute-start.8 = (bf16[2,128,512]{2,1,0:T(8,128)(2,1)S(1)}, bf16[2,128,512]{2,1,0:T(8,128)(2,1)S(1)}, u32[]{:S(2)}, u32[]{:S(2)}) collective-permute-start(bf16[2,128,512]{2,1,0:T(8,128)(2,1)S(1)} %get-tuple-element.16), channel_id=1, source_target_pairs={{0,2},{1,5},{2,0},{3,7},{4,6},{5,1},{6,4},{7,3},{8,10},{9,13},{10,... | collective-permute-start | bytes 786440 | tf_op jit(solution)/shard_map/ppermute | solution.py:211
  10.4 4.5 %attention.1 = (bf16[128,1024]{1,0:T(8,128)(2,1)}, bf16[5,128,256]{2,1,0:T(8,128)(2,1)S(1)}) custom-call(s32[1]{0:T(128)} %bitcast.own_ref, s32[1,3]{1,0:T(1,128)S(1)} %copy-done.36, bf16[128,1024]{1,0:T(8,128)(2,1)S(1)} %bitcast.28, bf16[128,1024]{1,0:T(8,128)(2,1)S(1)} %bitcast.29, bf16[128,256]{1,0:T(8,128)(2,1)S(1)} %collective-permute-done.refs_0_, ...), custom_call_target="tpu_custom_call" | custom-call | flops 1006632960 | bytes 1441792 | tf_op jit(solution)/shard_map/attention/pallas_call | solution.py:64
  15.0 1.3 %collective-permute-start.7 = (bf16[128,256]{1,0:T(8,128)(2,1)S(1)}, bf16[128,256]{1,0:T(8,128)(2,1)S(1)}, u32[]{:S(2)}, u32[]{:S(2)}) collective-permute-start(bf16[128,256]{1,0:T(8,128)(2,1)S(1)} %get-tuple-element.24), channel_id=1, source_target_pairs={{0,4},{1,5},{2,6},{3,7},{4,0},{5,1},{6,2},{7,3},{8,12},{9,13},{10,... | collective-permute-start | bytes 196616 | tf_op jit(solution)/shard_map/ppermute | solution.py:200
  16.3 1.4 %collective-permute-start.5 = (bf16[128,256]{1,0:T(8,128)(2,1)S(1)}, bf16[128,256]{1,0:T(8,128)(2,1)S(1)}, u32[]{:S(2)}, u32[]{:S(2)}) collective-permute-start(bf16[128,256]{1,0:T(8,128)(2,1)S(1)} %get-tuple-element.26), channel_id=1, source_target_pairs={{0,6},{1,7},{2,0},{3,1},{4,2},{5,3},{6,4},{7,5},{8,14},{9,15},{10,... | collective-permute-start | bytes 196616 | tf_op jit(solution)/shard_map/ppermute | solution.py:200
  17.7 1.5 %collective-permute-start.4 = (bf16[128,256]{1,0:T(8,128)(2,1)S(1)}, bf16[128,256]{1,0:T(8,128)(2,1)S(1)}, u32[]{:S(2)}, u32[]{:S(2)}) collective-permute-start(bf16[128,256]{1,0:T(8,128)(2,1)S(1)} %get-tuple-element.23), channel_id=1, source_target_pairs={{0,7},{1,0},{2,1},{3,2},{4,3},{5,4},{6,5},{7,6},{8,15},{9,8},{10,9... | collective-permute-start | bytes 196616 | tf_op jit(solution)/shard_map/ppermute | solution.py:200
  19.2 1.0 slice_bitcast_fusion.5
  20.2 0.8 collective-permute-start.9
  21.0 1.6 %collective-permute-start.26 = (bf16[128,512]{1,0:T(8,128)(2,1)S(1)}, bf16[128,512]{1,0:T(8,128)(2,1)S(1)}, u32[]{:S(2)}, u32[]{:S(2)}) collective-permute-start(bf16[128,512]{1,0:T(8,128)(2,1)S(1)} %get-tuple-element.29), channel_id=1, source_target_pairs={{0,8},{1,9},{2,10},{3,11},{4,12},{5,13},{6,14},{7,15},{8,0},{9,1},... | collective-permute-start | bytes 393224 | tf_op jit(solution)/shard_map/ppermute | solution.py:211
  23.4 1.8 %collective-permute-start.10 = (bf16[2,128,512]{2,1,0:T(8,128)(2,1)S(1)}, bf16[2,128,512]{2,1,0:T(8,128)(2,1)S(1)}, u32[]{:S(2)}, u32[]{:S(2)}) collective-permute-start(bf16[2,128,512]{2,1,0:T(8,128)(2,1)S(1)} %get-tuple-element.18), channel_id=1, source_target_pairs={{0,6},{1,7},{2,4},{3,5},{4,2},{5,3},{6,0},{7,1},{8,14},{9,15},{10,... | collective-permute-start | bytes 786440 | tf_op jit(solution)/shard_map/ppermute | solution.py:211
  25.2 2.1 %collective-permute-done.35 = bf16[128,256]{1,0:T(8,128)(2,1)S(1)} collective-permute-done((bf16[128,256]{1,0:T(8,128)(2,1)S(1)}, bf16[128,256]{1,0:T(8,128)(2,1)S(1)}, u32[]{:S(2)}, u32[]{:S(2)}) %collective-permute-start.35) | collective-permute-done | bytes 65568 | tf_op jit(solution)/shard_map/ppermute | solution.py:211
  27.4 1.6 %collective-permute-start.11 = (bf16[2,128,512]{2,1,0:T(8,128)(2,1)S(1)}, bf16[2,128,512]{2,1,0:T(8,128)(2,1)S(1)}, u32[]{:S(2)}, u32[]{:S(2)}) collective-permute-start(bf16[2,128,512]{2,1,0:T(8,128)(2,1)S(1)} %get-tuple-element.19), channel_id=1, source_target_pairs={{0,8},{1,9},{2,10},{3,11},{4,12},{5,13},{6,14},{7,15},{8,0},{9,1},... | collective-permute-start | bytes 786440 | tf_op jit(solution)/shard_map/ppermute | solution.py:211
  29.0 1.2 collective-permute-start.12
  30.2 1.6 %collective-permute-start.13 = (bf16[2,128,512]{2,1,0:T(8,128)(2,1)S(1)}, bf16[2,128,512]{2,1,0:T(8,128)(2,1)S(1)}, u32[]{:S(2)}, u32[]{:S(2)}) collective-permute-start(bf16[2,128,512]{2,1,0:T(8,128)(2,1)S(1)} %get-tuple-element.21), channel_id=1, source_target_pairs={{0,12},{1,11},{2,14},{3,9},{4,8},{5,15},{6,10},{7,13},{8,4},{9,3},... | collective-permute-start | bytes 786440 | tf_op jit(solution)/shard_map/ppermute | solution.py:211
  31.7 1.5 %collective-permute-start.14 = (bf16[2,128,512]{2,1,0:T(8,128)(2,1)S(1)}, bf16[2,128,512]{2,1,0:T(8,128)(2,1)S(1)}, u32[]{:S(2)}, u32[]{:S(2)}) collective-permute-start(bf16[2,128,512]{2,1,0:T(8,128)(2,1)S(1)} %get-tuple-element.22), channel_id=1, source_target_pairs={{0,14},{1,15},{2,12},{3,13},{4,10},{5,11},{6,8},{7,9},{8,6},{9,7},... | collective-permute-start | bytes 786440 | tf_op jit(solution)/shard_map/ppermute | solution.py:211
  33.3 1.4 %collective-permute-start.36 = (bf16[2,128,256]{2,1,0:T(8,128)(2,1)S(1)}, bf16[2,128,256]{2,1,0:T(8,128)(2,1)S(1)}, u32[]{:S(2)}, u32[]{:S(2)}) collective-permute-start(bf16[2,128,256]{2,1,0:T(8,128)(2,1)S(1)} %pad_maximum_fusion.5.refs_0_), channel_id=1, source_target_pairs={{0,2},{1,5},{2,0},{3,7},{4,6},{5,1},{6,4},{7,3},{8,10},{9,13},{10,... | collective-permute-start | bytes 393224 | tf_op jit(solution)/shard_map/ppermute | solution.py:211
  34.7 2.0 %collective-permute-done.11.refs_4_ = bf16[2,128,512]{2,1,0:T(8,128)(2,1)S(1)} collective-permute-done((bf16[2,128,512]{2,1,0:T(8,128)(2,1)S(1)}, bf16[2,128,512]{2,1,0:T(8,128)(2,1)S(1)}, u32[]{:S(2)}, u32[]{:S(2)}) %collective-permute-start.11) | collective-permute-done | bytes 262176 | tf_op jit(solution)/shard_map/ppermute | solution.py:211
  36.6 1.6 %collective-permute-start.17 = (bf16[128,512]{1,0:T(8,128)(2,1)S(1)}, bf16[128,512]{1,0:T(8,128)(2,1)S(1)}, u32[]{:S(2)}, u32[]{:S(2)}) collective-permute-start(bf16[128,512]{1,0:T(8,128)(2,1)S(1)} %get-tuple-element.30), channel_id=1, source_target_pairs={{0,8},{1,9},{2,10},{3,11},{4,12},{5,13},{6,14},{7,15},{8,0},{9,1},... | collective-permute-start | bytes 393224 | tf_op jit(solution)/shard_map/ppermute | solution.py:211
  38.2 4.8 %collective-permute-done.12.refs_5_ = bf16[2,128,512]{2,1,0:T(8,128)(2,1)S(1)} collective-permute-done((bf16[2,128,512]{2,1,0:T(8,128)(2,1)S(1)}, bf16[2,128,512]{2,1,0:T(8,128)(2,1)S(1)}, u32[]{:S(2)}, u32[]{:S(2)}) %collective-permute-start.12) | collective-permute-done | bytes 262176 | tf_op jit(solution)/shard_map/ppermute | solution.py:211
  43.0 1.0 collective-permute-start.37
  44.0 4.8 %collective-permute-done.13.refs_6_ = bf16[2,128,512]{2,1,0:T(8,128)(2,1)S(1)} collective-permute-done((bf16[2,128,512]{2,1,0:T(8,128)(2,1)S(1)}, bf16[2,128,512]{2,1,0:T(8,128)(2,1)S(1)}, u32[]{:S(2)}, u32[]{:S(2)}) %collective-permute-start.13) | collective-permute-done | bytes 262176 | tf_op jit(solution)/shard_map/ppermute | solution.py:211
  49.7 4.9 %collective-permute-done.14.refs_7_ = bf16[2,128,512]{2,1,0:T(8,128)(2,1)S(1)} collective-permute-done((bf16[2,128,512]{2,1,0:T(8,128)(2,1)S(1)}, bf16[2,128,512]{2,1,0:T(8,128)(2,1)S(1)}, u32[]{:S(2)}, u32[]{:S(2)}) %collective-permute-start.14) | collective-permute-done | bytes 262176 | tf_op jit(solution)/shard_map/ppermute | solution.py:211
  54.8 1.1 collective-permute-start.27
  55.9 1.6 %collective-permute-start.28 = (bf16[2,128,512]{2,1,0:T(8,128)(2,1)S(1)}, bf16[2,128,512]{2,1,0:T(8,128)(2,1)S(1)}, u32[]{:S(2)}, u32[]{:S(2)}) collective-permute-start(bf16[2,128,512]{2,1,0:T(8,128)(2,1)S(1)} %pad_maximum_fusion.4.refs_0_), channel_id=1, source_target_pairs={{0,4},{1,3},{2,6},{3,1},{4,0},{5,7},{6,2},{7,5},{8,12},{9,11},{10,... | collective-permute-start | bytes 786440 | tf_op jit(solution)/shard_map/ppermute | solution.py:211
  59.7 4.2 %collective-permute-done.27.refs_1_ = bf16[2,128,512]{2,1,0:T(8,128)(2,1)S(1)} collective-permute-done((bf16[2,128,512]{2,1,0:T(8,128)(2,1)S(1)}, bf16[2,128,512]{2,1,0:T(8,128)(2,1)S(1)}, u32[]{:S(2)}, u32[]{:S(2)}) %collective-permute-start.27) | collective-permute-done | bytes 262176 | tf_op jit(solution)/shard_map/ppermute | solution.py:211
  63.9 0.8 collective-permute-start.18
  64.7 1.2 collective-permute-start.29
  65.9 7.1 %collective-permute-done.18.refs_1_ = bf16[2,128,512]{2,1,0:T(8,128)(2,1)S(1)} collective-permute-done((bf16[2,128,512]{2,1,0:T(8,128)(2,1)S(1)}, bf16[2,128,512]{2,1,0:T(8,128)(2,1)S(1)}, u32[]{:S(2)}, u32[]{:S(2)}) %collective-permute-start.18) | collective-permute-done | bytes 262176 | tf_op jit(solution)/shard_map/ppermute | solution.py:211
  75.8 1.3 %collective-permute-start.20 = (bf16[2,128,512]{2,1,0:T(8,128)(2,1)S(1)}, bf16[2,128,512]{2,1,0:T(8,128)(2,1)S(1)}, u32[]{:S(2)}, u32[]{:S(2)}) collective-permute-start(bf16[2,128,512]{2,1,0:T(8,128)(2,1)S(1)} %collective-permute-done.18.refs_1_), channel_id=1, source_target_pairs={{0,4},{1,3},{2,6},{3,1},{4,0},{5,7},{6,2},{7,5},{8,12},{9,11},{10,... | collective-permute-start | bytes 786440 | tf_op jit(solution)/shard_map/ppermute | solution.py:211
  77.1 0.8 copy-done.17
  77.9 0.9 copy-done.2
  78.8 0.9 copy-done.4
  79.8 0.9 copy-done.6
  80.7 0.9 copy-done.8
  81.7 0.9 copy-done.10
  82.6 0.9 copy-done.12
  83.6 0.9 copy-done.14
  84.5 1.0 copy-done.16
  85.6 1.0 copy-done.18
  88.3 2.7 %collective-permute-start.43 = (bf16[256,256]{1,0:T(8,128)(2,1)S(1)}, bf16[256,256]{1,0:T(8,128)(2,1)S(1)}, u32[]{:S(2)}, u32[]{:S(2)}) collective-permute-start(bf16[256,256]{1,0:T(8,128)(2,1)S(1)} %fold.11), channel_id=1, source_target_pairs={{0,16},{1,17},{2,18},{3,19},{4,20},{5,21},{6,22},{7,23},{8,24},{9,... | collective-permute-start | bytes 393224 | tf_op jit(solution)/shard_map/ppermute | solution.py:211
  93.3 4.7 %collective-permute-done.43 = bf16[256,256]{1,0:T(8,128)(2,1)S(1)} collective-permute-done((bf16[256,256]{1,0:T(8,128)(2,1)S(1)}, bf16[256,256]{1,0:T(8,128)(2,1)S(1)}, u32[]{:S(2)}, u32[]{:S(2)}) %collective-permute-start.43) | collective-permute-done | bytes 131104 | tf_op jit(solution)/shard_map/ppermute | solution.py:211
  98.8 3.0 %collective-permute-start.25 = (bf16[256,512]{1,0:T(8,128)(2,1)S(1)}, bf16[256,512]{1,0:T(8,128)(2,1)S(1)}, u32[]{:S(2)}, u32[]{:S(2)}) collective-permute-start(bf16[256,512]{1,0:T(8,128)(2,1)S(1)} %fold.7), channel_id=1, source_target_pairs={{0,16},{1,17},{2,18},{3,19},{4,20},{5,21},{6,22},{7,23},{8,24},{9,... | collective-permute-start | bytes 786440 | tf_op jit(solution)/shard_map/ppermute | solution.py:211
  103.2 15.0 %collective-permute-done.34 = bf16[256,512]{1,0:T(8,128)(2,1)S(1)} collective-permute-done((bf16[256,512]{1,0:T(8,128)(2,1)S(1)}, bf16[256,512]{1,0:T(8,128)(2,1)S(1)}, u32[]{:S(2)}, u32[]{:S(2)}) %collective-permute-start.34) | collective-permute-done | bytes 262176 | tf_op jit(solution)/shard_map/ppermute | solution.py:211
  118.3 5.4 %collective-permute-done.25 = bf16[256,512]{1,0:T(8,128)(2,1)S(1)} collective-permute-done((bf16[256,512]{1,0:T(8,128)(2,1)S(1)}, bf16[256,512]{1,0:T(8,128)(2,1)S(1)}, u32[]{:S(2)}, u32[]{:S(2)}) %collective-permute-start.25) | collective-permute-done | bytes 262176 | tf_op jit(solution)/shard_map/ppermute | solution.py:211
  123.8 1.1 pad_maximum_fusion
  (146 shorter events, 15.0 us)
Async XLA Ops:
  0.6 8.9 %collective-permute-start = (bf16[128,256]{1,0:T(8,128)(2,1)}, bf16[128,256]{1,0:T(8,128)(2,1)S(1)}, u32[]{:S(2)}, u32[]{:S(2)}) collective-permute-start(bf16[128,256]{1,0:T(8,128)(2,1)} %bitcast.30), channel_id=1, source_target_pairs={{0,4},{1,5},{2,6},{3,7},{4,0},{5,1},{6,2},{7,3},{8,12},{9,13},{10,... | collective-permute-start | bytes 196616 | tf_op jit(solution)/shard_map/ppermute | solution.py:187
  3.7 5.9 %collective-permute-start.1 = (bf16[128,256]{1,0:T(8,128)(2,1)}, bf16[128,256]{1,0:T(8,128)(2,1)S(1)}, u32[]{:S(2)}, u32[]{:S(2)}) collective-permute-start(bf16[128,256]{1,0:T(8,128)(2,1)} %bitcast.31), channel_id=1, source_target_pairs={{0,3},{1,4},{2,5},{3,6},{4,7},{5,0},{6,1},{7,2},{8,11},{9,12},{10,... | collective-permute-start | bytes 196616 | tf_op jit(solution)/shard_map/ppermute | solution.py:187
  4.3 5.8 %collective-permute-start.2 = (bf16[128,256]{1,0:T(8,128)(2,1)}, bf16[128,256]{1,0:T(8,128)(2,1)S(1)}, u32[]{:S(2)}, u32[]{:S(2)}) collective-permute-start(bf16[128,256]{1,0:T(8,128)(2,1)} %bitcast.32), channel_id=1, source_target_pairs={{0,2},{1,3},{2,4},{3,5},{4,6},{5,7},{6,0},{7,1},{8,10},{9,11},{10,... | collective-permute-start | bytes 196616 | tf_op jit(solution)/shard_map/ppermute | solution.py:187
  5.2 5.2 %collective-permute-start.3 = (bf16[128,256]{1,0:T(8,128)(2,1)}, bf16[128,256]{1,0:T(8,128)(2,1)S(1)}, u32[]{:S(2)}, u32[]{:S(2)}) collective-permute-start(bf16[128,256]{1,0:T(8,128)(2,1)} %bitcast.33), channel_id=1, source_target_pairs={{0,1},{1,2},{2,3},{3,4},{4,5},{5,6},{6,7},{7,0},{8,9},{9,10},{10,1... | collective-permute-start | bytes 196616 | tf_op jit(solution)/shard_map/ppermute | solution.py:187
  8.0 22.2 %collective-permute-start.8 = (bf16[2,128,512]{2,1,0:T(8,128)(2,1)S(1)}, bf16[2,128,512]{2,1,0:T(8,128)(2,1)S(1)}, u32[]{:S(2)}, u32[]{:S(2)}) collective-permute-start(bf16[2,128,512]{2,1,0:T(8,128)(2,1)S(1)} %get-tuple-element.16), channel_id=1, source_target_pairs={{0,2},{1,5},{2,0},{3,7},{4,6},{5,1},{6,4},{7,3},{8,10},{9,13},{10,... | collective-permute-start | bytes 786440 | tf_op jit(solution)/shard_map/ppermute | solution.py:211
  15.0 5.2 %collective-permute-start.7 = (bf16[128,256]{1,0:T(8,128)(2,1)S(1)}, bf16[128,256]{1,0:T(8,128)(2,1)S(1)}, u32[]{:S(2)}, u32[]{:S(2)}) collective-permute-start(bf16[128,256]{1,0:T(8,128)(2,1)S(1)} %get-tuple-element.24), channel_id=1, source_target_pairs={{0,4},{1,5},{2,6},{3,7},{4,0},{5,1},{6,2},{7,3},{8,12},{9,13},{10,... | collective-permute-start | bytes 196616 | tf_op jit(solution)/shard_map/ppermute | solution.py:200
  16.3 4.7 %collective-permute-start.6 = (bf16[128,256]{1,0:T(8,128)(2,1)S(1)}, bf16[128,256]{1,0:T(8,128)(2,1)S(1)}, u32[]{:S(2)}, u32[]{:S(2)}) collective-permute-start(bf16[128,256]{1,0:T(8,128)(2,1)S(1)} %get-tuple-element.25), channel_id=1, source_target_pairs={{0,5},{1,6},{2,7},{3,0},{4,1},{5,2},{6,3},{7,4},{8,13},{9,14},{10,... | collective-permute-start | bytes 196616 | tf_op jit(solution)/shard_map/ppermute | solution.py:200
  16.3 6.3 %collective-permute-start.5 = (bf16[128,256]{1,0:T(8,128)(2,1)S(1)}, bf16[128,256]{1,0:T(8,128)(2,1)S(1)}, u32[]{:S(2)}, u32[]{:S(2)}) collective-permute-start(bf16[128,256]{1,0:T(8,128)(2,1)S(1)} %get-tuple-element.26), channel_id=1, source_target_pairs={{0,6},{1,7},{2,0},{3,1},{4,2},{5,3},{6,4},{7,5},{8,14},{9,15},{10,... | collective-permute-start | bytes 196616 | tf_op jit(solution)/shard_map/ppermute | solution.py:200
  17.7 4.9 %collective-permute-start.4 = (bf16[128,256]{1,0:T(8,128)(2,1)S(1)}, bf16[128,256]{1,0:T(8,128)(2,1)S(1)}, u32[]{:S(2)}, u32[]{:S(2)}) collective-permute-start(bf16[128,256]{1,0:T(8,128)(2,1)S(1)} %get-tuple-element.23), channel_id=1, source_target_pairs={{0,7},{1,0},{2,1},{3,2},{4,3},{5,4},{6,5},{7,6},{8,15},{9,8},{10,9... | collective-permute-start | bytes 196616 | tf_op jit(solution)/shard_map/ppermute | solution.py:200
  20.2 11.5 %collective-permute-start.9 = (bf16[2,128,512]{2,1,0:T(8,128)(2,1)S(1)}, bf16[2,128,512]{2,1,0:T(8,128)(2,1)S(1)}, u32[]{:S(2)}, u32[]{:S(2)}) collective-permute-start(bf16[2,128,512]{2,1,0:T(8,128)(2,1)S(1)} %get-tuple-element.17), channel_id=1, source_target_pairs={{0,4},{1,3},{2,6},{3,1},{4,0},{5,7},{6,2},{7,5},{8,12},{9,11},{10,... | collective-permute-start | bytes 786440 | tf_op jit(solution)/shard_map/ppermute | solution.py:211
  21.0 8.0 %collective-permute-start.26 = (bf16[128,512]{1,0:T(8,128)(2,1)S(1)}, bf16[128,512]{1,0:T(8,128)(2,1)S(1)}, u32[]{:S(2)}, u32[]{:S(2)}) collective-permute-start(bf16[128,512]{1,0:T(8,128)(2,1)S(1)} %get-tuple-element.29), channel_id=1, source_target_pairs={{0,8},{1,9},{2,10},{3,11},{4,12},{5,13},{6,14},{7,15},{8,0},{9,1},... | collective-permute-start | bytes 393224 | tf_op jit(solution)/shard_map/ppermute | solution.py:211
  22.7 4.7 %collective-permute-start.35 = (bf16[128,256]{1,0:T(8,128)(2,1)S(1)}, bf16[128,256]{1,0:T(8,128)(2,1)S(1)}, u32[]{:S(2)}, u32[]{:S(2)}) collective-permute-start(bf16[128,256]{1,0:T(8,128)(2,1)S(1)} %fusion.3), channel_id=1, source_target_pairs={{0,8},{1,9},{2,10},{3,11},{4,12},{5,13},{6,14},{7,15},{8,0},{9,1},... | collective-permute-start | bytes 196616 | tf_op jit(solution)/shard_map/ppermute | solution.py:211
  23.4 9.8 %collective-permute-start.10 = (bf16[2,128,512]{2,1,0:T(8,128)(2,1)S(1)}, bf16[2,128,512]{2,1,0:T(8,128)(2,1)S(1)}, u32[]{:S(2)}, u32[]{:S(2)}) collective-permute-start(bf16[2,128,512]{2,1,0:T(8,128)(2,1)S(1)} %get-tuple-element.18), channel_id=1, source_target_pairs={{0,6},{1,7},{2,4},{3,5},{4,2},{5,3},{6,0},{7,1},{8,14},{9,15},{10,... | collective-permute-start | bytes 786440 | tf_op jit(solution)/shard_map/ppermute | solution.py:211
  27.4 9.2 %collective-permute-start.11 = (bf16[2,128,512]{2,1,0:T(8,128)(2,1)S(1)}, bf16[2,128,512]{2,1,0:T(8,128)(2,1)S(1)}, u32[]{:S(2)}, u32[]{:S(2)}) collective-permute-start(bf16[2,128,512]{2,1,0:T(8,128)(2,1)S(1)} %get-tuple-element.19), channel_id=1, source_target_pairs={{0,8},{1,9},{2,10},{3,11},{4,12},{5,13},{6,14},{7,15},{8,0},{9,1},... | collective-permute-start | bytes 786440 | tf_op jit(solution)/shard_map/ppermute | solution.py:211
  29.0 14.0 %collective-permute-start.12 = (bf16[2,128,512]{2,1,0:T(8,128)(2,1)S(1)}, bf16[2,128,512]{2,1,0:T(8,128)(2,1)S(1)}, u32[]{:S(2)}, u32[]{:S(2)}) collective-permute-start(bf16[2,128,512]{2,1,0:T(8,128)(2,1)S(1)} %get-tuple-element.20), channel_id=1, source_target_pairs={{0,10},{1,13},{2,8},{3,15},{4,14},{5,9},{6,12},{7,11},{8,2},{9,5},... | collective-permute-start | bytes 786440 | tf_op jit(solution)/shard_map/ppermute | solution.py:211
  30.2 24.5 %copy-start.1 = (bf16[2,128,512]{2,1,0:T(8,128)(2,1)}, bf16[2,128,512]{2,1,0:T(8,128)(2,1)S(1)}, u32[]{:S(2)}) copy-start(bf16[2,128,512]{2,1,0:T(8,128)(2,1)S(1)} %collective-permute-done.8.refs_1_) | copy-start | bytes 786436
  30.2 18.6 %collective-permute-start.13 = (bf16[2,128,512]{2,1,0:T(8,128)(2,1)S(1)}, bf16[2,128,512]{2,1,0:T(8,128)(2,1)S(1)}, u32[]{:S(2)}, u32[]{:S(2)}) collective-permute-start(bf16[2,128,512]{2,1,0:T(8,128)(2,1)S(1)} %get-tuple-element.21), channel_id=1, source_target_pairs={{0,12},{1,11},{2,14},{3,9},{4,8},{5,15},{6,10},{7,13},{8,4},{9,3},... | collective-permute-start | bytes 786440 | tf_op jit(solution)/shard_map/ppermute | solution.py:211
  31.7 22.9 %copy-start.3 = (bf16[2,128,512]{2,1,0:T(8,128)(2,1)}, bf16[2,128,512]{2,1,0:T(8,128)(2,1)S(1)}, u32[]{:S(2)}) copy-start(bf16[2,128,512]{2,1,0:T(8,128)(2,1)S(1)} %collective-permute-done.9.refs_2_) | copy-start | bytes 786436
  31.7 22.8 %collective-permute-start.14 = (bf16[2,128,512]{2,1,0:T(8,128)(2,1)S(1)}, bf16[2,128,512]{2,1,0:T(8,128)(2,1)S(1)}, u32[]{:S(2)}, u32[]{:S(2)}) collective-permute-start(bf16[2,128,512]{2,1,0:T(8,128)(2,1)S(1)} %get-tuple-element.22), channel_id=1, source_target_pairs={{0,14},{1,15},{2,12},{3,13},{4,10},{5,11},{6,8},{7,9},{8,6},{9,7},... | collective-permute-start | bytes 786440 | tf_op jit(solution)/shard_map/ppermute | solution.py:211
  33.3 21.3 %copy-start.5 = (bf16[2,128,512]{2,1,0:T(8,128)(2,1)}, bf16[2,128,512]{2,1,0:T(8,128)(2,1)S(1)}, u32[]{:S(2)}) copy-start(bf16[2,128,512]{2,1,0:T(8,128)(2,1)S(1)} %collective-permute-done.10.refs_3_) | copy-start | bytes 786436
  33.3 15.5 %collective-permute-start.36 = (bf16[2,128,256]{2,1,0:T(8,128)(2,1)S(1)}, bf16[2,128,256]{2,1,0:T(8,128)(2,1)S(1)}, u32[]{:S(2)}, u32[]{:S(2)}) collective-permute-start(bf16[2,128,256]{2,1,0:T(8,128)(2,1)S(1)} %pad_maximum_fusion.5.refs_0_), channel_id=1, source_target_pairs={{0,2},{1,5},{2,0},{3,7},{4,6},{5,1},{6,4},{7,3},{8,10},{9,13},{10,... | collective-permute-start | bytes 393224 | tf_op jit(solution)/shard_map/ppermute | solution.py:211
  36.6 18.1 %collective-permute-start.17 = (bf16[128,512]{1,0:T(8,128)(2,1)S(1)}, bf16[128,512]{1,0:T(8,128)(2,1)S(1)}, u32[]{:S(2)}, u32[]{:S(2)}) collective-permute-start(bf16[128,512]{1,0:T(8,128)(2,1)S(1)} %get-tuple-element.30), channel_id=1, source_target_pairs={{0,8},{1,9},{2,10},{3,11},{4,12},{5,13},{6,14},{7,15},{8,0},{9,1},... | collective-permute-start | bytes 393224 | tf_op jit(solution)/shard_map/ppermute | solution.py:211
  43.0 12.9 %collective-permute-start.37 = (bf16[2,128,256]{2,1,0:T(8,128)(2,1)S(1)}, bf16[2,128,256]{2,1,0:T(8,128)(2,1)S(1)}, u32[]{:S(2)}, u32[]{:S(2)}) collective-permute-start(bf16[2,128,256]{2,1,0:T(8,128)(2,1)S(1)} %pad_maximum_fusion.5.refs_0_), channel_id=1, source_target_pairs={{0,4},{1,3},{2,6},{3,1},{4,0},{5,7},{6,2},{7,5},{8,12},{9,11},{10,... | collective-permute-start | bytes 393224 | tf_op jit(solution)/shard_map/ppermute | solution.py:211
  48.8 8.7 %collective-permute-start.39 = (bf16[2,128,256]{2,1,0:T(8,128)(2,1)S(1)}, bf16[2,128,256]{2,1,0:T(8,128)(2,1)S(1)}, u32[]{:S(2)}, u32[]{:S(2)}) collective-permute-start(bf16[2,128,256]{2,1,0:T(8,128)(2,1)S(1)} %pad_maximum_fusion.5.refs_0_), channel_id=1, source_target_pairs={{0,1},{1,0},{2,3},{3,2},{4,5},{5,4},{6,7},{7,6},{8,9},{9,8},{10,11... | collective-permute-start | bytes 393224 | tf_op jit(solution)/shard_map/ppermute | solution.py:211
  48.9 8.7 %collective-permute-start.38 = (bf16[2,128,256]{2,1,0:T(8,128)(2,1)S(1)}, bf16[2,128,256]{2,1,0:T(8,128)(2,1)S(1)}, u32[]{:S(2)}, u32[]{:S(2)}) collective-permute-start(bf16[2,128,256]{2,1,0:T(8,128)(2,1)S(1)} %collective-permute-done.36.refs_1_), channel_id=1, source_target_pairs={{0,4},{1,3},{2,6},{3,1},{4,0},{5,7},{6,2},{7,5},{8,12},{9,11},{10,... | collective-permute-start | bytes 393224 | tf_op jit(solution)/shard_map/ppermute | solution.py:211
  54.5 3.6 %collective-permute-start.40 = (bf16[2,128,256]{2,1,0:T(8,128)(2,1)S(1)}, bf16[2,128,256]{2,1,0:T(8,128)(2,1)S(1)}, u32[]{:S(2)}, u32[]{:S(2)}) collective-permute-start(bf16[2,128,256]{2,1,0:T(8,128)(2,1)S(1)} %collective-permute-done.36.refs_1_), channel_id=1, source_target_pairs={{0,1},{1,0},{2,3},{3,2},{4,5},{5,4},{6,7},{7,6},{8,9},{9,8},{10,11... | collective-permute-start | bytes 393224 | tf_op jit(solution)/shard_map/ppermute | solution.py:211
  54.8 9.1 %collective-permute-start.27 = (bf16[2,128,512]{2,1,0:T(8,128)(2,1)S(1)}, bf16[2,128,512]{2,1,0:T(8,128)(2,1)S(1)}, u32[]{:S(2)}, u32[]{:S(2)}) collective-permute-start(bf16[2,128,512]{2,1,0:T(8,128)(2,1)S(1)} %pad_maximum_fusion.4.refs_0_), channel_id=1, source_target_pairs={{0,2},{1,5},{2,0},{3,7},{4,6},{5,1},{6,4},{7,3},{8,10},{9,13},{10,... | collective-permute-start | bytes 786440 | tf_op jit(solution)/shard_map/ppermute | solution.py:211
  55.9 8.8 %collective-permute-start.28 = (bf16[2,128,512]{2,1,0:T(8,128)(2,1)S(1)}, bf16[2,128,512]{2,1,0:T(8,128)(2,1)S(1)}, u32[]{:S(2)}, u32[]{:S(2)}) collective-permute-start(bf16[2,128,512]{2,1,0:T(8,128)(2,1)S(1)} %pad_maximum_fusion.4.refs_0_), channel_id=1, source_target_pairs={{0,4},{1,3},{2,6},{3,1},{4,0},{5,7},{6,2},{7,5},{8,12},{9,11},{10,... | collective-permute-start | bytes 786440 | tf_op jit(solution)/shard_map/ppermute | solution.py:211
  57.5 1.3 %collective-permute-start.41 = (bf16[2,128,256]{2,1,0:T(8,128)(2,1)S(1)}, bf16[2,128,256]{2,1,0:T(8,128)(2,1)S(1)}, u32[]{:S(2)}, u32[]{:S(2)}) collective-permute-start(bf16[2,128,256]{2,1,0:T(8,128)(2,1)S(1)} %collective-permute-done.37.refs_2_), channel_id=1, source_target_pairs={{0,1},{1,0},{2,3},{3,2},{4,5},{5,4},{6,7},{7,6},{8,9},{9,8},{10,11... | collective-permute-start | bytes 393224 | tf_op jit(solution)/shard_map/ppermute | solution.py:211
  57.6 17.4 %collective-permute-start.15 = (bf16[4,128,512]{2,1,0:T(8,128)(2,1)S(1)}, bf16[4,128,512]{2,1,0:T(8,128)(2,1)S(1)}, u32[]{:S(2)}, u32[]{:S(2)}) collective-permute-start(bf16[4,128,512]{2,1,0:T(8,128)(2,1)S(1)} %pad_maximum_fusion.1), channel_id=1, source_target_pairs={{0,1},{1,0},{2,3},{3,2},{4,5},{5,4},{6,7},{7,6},{8,9},{9,8},{10,11... | collective-permute-start | bytes 1572872 | tf_op jit(solution)/shard_map/ppermute | solution.py:211
  58.2 18.9 %copy-start.27 = (bf16[2,128,256]{2,1,0:T(8,128)(2,1)}, bf16[2,128,256]{2,1,0:T(8,128)(2,1)S(1)}, u32[]{:S(2)}) copy-start(bf16[2,128,256]{2,1,0:T(8,128)(2,1)S(1)} %collective-permute-done.40.refs_5_) | copy-start | bytes 393220
  58.2 18.9 %collective-permute-start.16 = (bf16[4,128,512]{2,1,0:T(8,128)(2,1)S(1)}, bf16[4,128,512]{2,1,0:T(8,128)(2,1)S(1)}, u32[]{:S(2)}, u32[]{:S(2)}) collective-permute-start(bf16[4,128,512]{2,1,0:T(8,128)(2,1)S(1)} %pad_maximum_fusion.2), channel_id=1, source_target_pairs={{0,1},{1,0},{2,3},{3,2},{4,5},{5,4},{6,7},{7,6},{8,9},{9,8},{10,11... | collective-permute-start | bytes 1572872 | tf_op jit(solution)/shard_map/ppermute | solution.py:211
  59.5 6.5 %collective-permute-start.30 = (bf16[2,128,512]{2,1,0:T(8,128)(2,1)S(1)}, bf16[2,128,512]{2,1,0:T(8,128)(2,1)S(1)}, u32[]{:S(2)}, u32[]{:S(2)}) collective-permute-start(bf16[2,128,512]{2,1,0:T(8,128)(2,1)S(1)} %pad_maximum_fusion.4.refs_0_), channel_id=1, source_target_pairs={{0,1},{1,0},{2,3},{3,2},{4,5},{5,4},{6,7},{7,6},{8,9},{9,8},{10,11... | collective-permute-start | bytes 786440 | tf_op jit(solution)/shard_map/ppermute | solution.py:211
  63.9 9.2 %collective-permute-start.18 = (bf16[2,128,512]{2,1,0:T(8,128)(2,1)S(1)}, bf16[2,128,512]{2,1,0:T(8,128)(2,1)S(1)}, u32[]{:S(2)}, u32[]{:S(2)}) collective-permute-start(bf16[2,128,512]{2,1,0:T(8,128)(2,1)S(1)} %pad_maximum_fusion.3.refs_0_), channel_id=1, source_target_pairs={{0,2},{1,5},{2,0},{3,7},{4,6},{5,1},{6,4},{7,3},{8,10},{9,13},{10,... | collective-permute-start | bytes 786440 | tf_op jit(solution)/shard_map/ppermute | solution.py:211
  64.7 9.7 %collective-permute-start.29 = (bf16[2,128,512]{2,1,0:T(8,128)(2,1)S(1)}, bf16[2,128,512]{2,1,0:T(8,128)(2,1)S(1)}, u32[]{:S(2)}, u32[]{:S(2)}) collective-permute-start(bf16[2,128,512]{2,1,0:T(8,128)(2,1)S(1)} %collective-permute-done.27.refs_1_), channel_id=1, source_target_pairs={{0,4},{1,3},{2,6},{3,1},{4,0},{5,7},{6,2},{7,5},{8,12},{9,11},{10,... | collective-permute-start | bytes 786440 | tf_op jit(solution)/shard_map/ppermute | solution.py:211
  65.9 7.8 %collective-permute-start.42 = (bf16[2,128,256]{2,1,0:T(8,128)(2,1)S(1)}, bf16[2,128,256]{2,1,0:T(8,128)(2,1)S(1)}, u32[]{:S(2)}, u32[]{:S(2)}) collective-permute-start(bf16[2,128,256]{2,1,0:T(8,128)(2,1)S(1)} %collective-permute-done.38.refs_3_), channel_id=1, source_target_pairs={{0,1},{1,0},{2,3},{3,2},{4,5},{5,4},{6,7},{7,6},{8,9},{9,8},{10,11... | collective-permute-start | bytes 393224 | tf_op jit(solution)/shard_map/ppermute | solution.py:211
  73.0 15.3 %collective-permute-start.19 = (bf16[2,128,512]{2,1,0:T(8,128)(2,1)S(1)}, bf16[2,128,512]{2,1,0:T(8,128)(2,1)S(1)}, u32[]{:S(2)}, u32[]{:S(2)}) collective-permute-start(bf16[2,128,512]{2,1,0:T(8,128)(2,1)S(1)} %pad_maximum_fusion.3.refs_0_), channel_id=1, source_target_pairs={{0,4},{1,3},{2,6},{3,1},{4,0},{5,7},{6,2},{7,5},{8,12},{9,11},{10,... | collective-permute-start | bytes 786440 | tf_op jit(solution)/shard_map/ppermute | solution.py:211
  74.4 17.1 %collective-permute-start.31 = (bf16[2,128,512]{2,1,0:T(8,128)(2,1)S(1)}, bf16[2,128,512]{2,1,0:T(8,128)(2,1)S(1)}, u32[]{:S(2)}, u32[]{:S(2)}) collective-permute-start(bf16[2,128,512]{2,1,0:T(8,128)(2,1)S(1)} %collective-permute-done.27.refs_1_), channel_id=1, source_target_pairs={{0,1},{1,0},{2,3},{3,2},{4,5},{5,4},{6,7},{7,6},{8,9},{9,8},{10,11... | collective-permute-start | bytes 786440 | tf_op jit(solution)/shard_map/ppermute | solution.py:211
  74.4 17.3 %collective-permute-start.32 = (bf16[2,128,512]{2,1,0:T(8,128)(2,1)S(1)}, bf16[2,128,512]{2,1,0:T(8,128)(2,1)S(1)}, u32[]{:S(2)}, u32[]{:S(2)}) collective-permute-start(bf16[2,128,512]{2,1,0:T(8,128)(2,1)S(1)} %collective-permute-done.28.refs_2_), channel_id=1, source_target_pairs={{0,1},{1,0},{2,3},{3,2},{4,5},{5,4},{6,7},{7,6},{8,9},{9,8},{10,11... | collective-permute-start | bytes 786440 | tf_op jit(solution)/shard_map/ppermute | solution.py:211
  75.8 16.3 %collective-permute-start.20 = (bf16[2,128,512]{2,1,0:T(8,128)(2,1)S(1)}, bf16[2,128,512]{2,1,0:T(8,128)(2,1)S(1)}, u32[]{:S(2)}, u32[]{:S(2)}) collective-permute-start(bf16[2,128,512]{2,1,0:T(8,128)(2,1)S(1)} %collective-permute-done.18.refs_1_), channel_id=1, source_target_pairs={{0,4},{1,3},{2,6},{3,1},{4,0},{5,7},{6,2},{7,5},{8,12},{9,11},{10,... | collective-permute-start | bytes 786440 | tf_op jit(solution)/shard_map/ppermute | solution.py:211
  77.9 14.4 %collective-permute-start.33 = (bf16[2,128,512]{2,1,0:T(8,128)(2,1)S(1)}, bf16[2,128,512]{2,1,0:T(8,128)(2,1)S(1)}, u32[]{:S(2)}, u32[]{:S(2)}) collective-permute-start(bf16[2,128,512]{2,1,0:T(8,128)(2,1)S(1)} %collective-permute-done.29.refs_3_), channel_id=1, source_target_pairs={{0,1},{1,0},{2,3},{3,2},{4,5},{5,4},{6,7},{7,6},{8,9},{9,8},{10,11... | collective-permute-start | bytes 786440 | tf_op jit(solution)/shard_map/ppermute | solution.py:211
  88.3 9.7 %collective-permute-start.43 = (bf16[256,256]{1,0:T(8,128)(2,1)S(1)}, bf16[256,256]{1,0:T(8,128)(2,1)S(1)}, u32[]{:S(2)}, u32[]{:S(2)}) collective-permute-start(bf16[256,256]{1,0:T(8,128)(2,1)S(1)} %fold.11), channel_id=1, source_target_pairs={{0,16},{1,17},{2,18},{3,19},{4,20},{5,21},{6,22},{7,23},{8,24},{9,... | collective-permute-start | bytes 393224 | tf_op jit(solution)/shard_map/ppermute | solution.py:211
  91.5 6.6 %collective-permute-start.21 = (bf16[2,128,512]{2,1,0:T(8,128)(2,1)S(1)}, bf16[2,128,512]{2,1,0:T(8,128)(2,1)S(1)}, u32[]{:S(2)}, u32[]{:S(2)}) collective-permute-start(bf16[2,128,512]{2,1,0:T(8,128)(2,1)S(1)} %pad_maximum_fusion.3.refs_0_), channel_id=1, source_target_pairs={{0,1},{1,0},{2,3},{3,2},{4,5},{5,4},{6,7},{7,6},{8,9},{9,8},{10,11... | collective-permute-start | bytes 786440 | tf_op jit(solution)/shard_map/ppermute | solution.py:211
  91.8 6.3 %collective-permute-start.22 = (bf16[2,128,512]{2,1,0:T(8,128)(2,1)S(1)}, bf16[2,128,512]{2,1,0:T(8,128)(2,1)S(1)}, u32[]{:S(2)}, u32[]{:S(2)}) collective-permute-start(bf16[2,128,512]{2,1,0:T(8,128)(2,1)S(1)} %collective-permute-done.18.refs_1_), channel_id=1, source_target_pairs={{0,1},{1,0},{2,3},{3,2},{4,5},{5,4},{6,7},{7,6},{8,9},{9,8},{10,11... | collective-permute-start | bytes 786440 | tf_op jit(solution)/shard_map/ppermute | solution.py:211
  92.0 6.0 %collective-permute-start.23 = (bf16[2,128,512]{2,1,0:T(8,128)(2,1)S(1)}, bf16[2,128,512]{2,1,0:T(8,128)(2,1)S(1)}, u32[]{:S(2)}, u32[]{:S(2)}) collective-permute-start(bf16[2,128,512]{2,1,0:T(8,128)(2,1)S(1)} %collective-permute-done.19.refs_2_), channel_id=1, source_target_pairs={{0,1},{1,0},{2,3},{3,2},{4,5},{5,4},{6,7},{7,6},{8,9},{9,8},{10,11... | collective-permute-start | bytes 786440 | tf_op jit(solution)/shard_map/ppermute | solution.py:211
  92.3 5.8 %collective-permute-start.24 = (bf16[2,128,512]{2,1,0:T(8,128)(2,1)S(1)}, bf16[2,128,512]{2,1,0:T(8,128)(2,1)S(1)}, u32[]{:S(2)}, u32[]{:S(2)}) collective-permute-start(bf16[2,128,512]{2,1,0:T(8,128)(2,1)S(1)} %collective-permute-done.20.refs_3_), channel_id=1, source_target_pairs={{0,1},{1,0},{2,3},{3,2},{4,5},{5,4},{6,7},{7,6},{8,9},{9,8},{10,11... | collective-permute-start | bytes 786440 | tf_op jit(solution)/shard_map/ppermute | solution.py:211
  98.0 20.2 %collective-permute-start.34 = (bf16[256,512]{1,0:T(8,128)(2,1)S(1)}, bf16[256,512]{1,0:T(8,128)(2,1)S(1)}, u32[]{:S(2)}, u32[]{:S(2)}) collective-permute-start(bf16[256,512]{1,0:T(8,128)(2,1)S(1)} %fold.9), channel_id=1, source_target_pairs={{0,16},{1,17},{2,18},{3,19},{4,20},{5,21},{6,22},{7,23},{8,24},{9,... | collective-permute-start | bytes 786440 | tf_op jit(solution)/shard_map/ppermute | solution.py:211
  98.8 24.9 %collective-permute-start.25 = (bf16[256,512]{1,0:T(8,128)(2,1)S(1)}, bf16[256,512]{1,0:T(8,128)(2,1)S(1)}, u32[]{:S(2)}, u32[]{:S(2)}) collective-permute-start(bf16[256,512]{1,0:T(8,128)(2,1)S(1)} %fold.7), channel_id=1, source_target_pairs={{0,16},{1,17},{2,18},{3,19},{4,20},{5,21},{6,22},{7,23},{8,24},{9,... | collective-permute-start | bytes 786440 | tf_op jit(solution)/shard_map/ppermute | solution.py:211
  (34 other events, 149.9 us)

commit v3 on v2

v3 whole, which is shorter than its diff:
```python
import functools

import jax
import jax.numpy as jnp
from jax import lax
from jax.experimental import pallas as pl
from jax.experimental.pallas import tpu as pltpu
from jax.sharding import PartitionSpec as P

F32 = jnp.float32
BF16 = jnp.bfloat16
VMEM_LIMIT = 16 * 1024 * 1024
LEAD = 4


def dot(a, b, ca, cb):
    return lax.dot_general(a, b, (((ca,), (cb,)), ((), ())), preferred_element_type=F32)


def attention_kernel(own_ref, lens_ref, q_ref, do_ref, *refs, span, head, group, docs, cube):
    kv_refs, (gq_ref, lead_ref), term_refs = refs[:span], refs[span : span + 2], refs[span + 2 :]
    rows = q_ref.shape[0]
    scale = head ** (-0.5)
    own = own_ref[0]
    first = jnp.int32(0)
    start = jnp.int32(0)
    for d in range(docs):
        first = jnp.where(start <= own, jnp.maximum(first, start), first)
        start = start + lens_ref[0, d]
    kv = jnp.concatenate([r[...] for r in kv_refs], axis=0)
    keys, values = kv[:, :head], kv[:, head:]
    keys_t = keys.T
    width = 2 * rows
    key_at = lax.broadcasted_iota(jnp.int32, (span * rows, width), 0)
    query_at = lax.broadcasted_iota(jnp.int32, (span * rows, width), 1) % rows
    low = (first - own + span - 1) * rows
    allowed = (key_at >= low) & (key_at <= query_at + (span - 1) * rows)
    dk = jnp.zeros((span * rows, head), F32)
    dv = jnp.zeros((span * rows, head), F32)
    for pair in range(group // 2):
        at = [2 * pair * head, (2 * pair + 1) * head]
        q2 = jnp.concatenate([q_ref[:, a : a + head] for a in at], axis=0)
        do2 = jnp.concatenate([do_ref[:, a : a + head] for a in at], axis=0)
        scores = jnp.where(allowed, dot(keys, q2, 1, 1) * scale, -1e30)
        exps = jnp.exp(scores - jnp.max(scores, axis=0, keepdims=True))
        probs = exps * (1.0 / jnp.sum(exps, axis=0, keepdims=True))
        probs_half = probs.astype(BF16)
        dprobs = dot(values, do2, 1, 1)
        row_dots = jnp.sum(probs_half.astype(F32) * dprobs, axis=0, keepdims=True)
        dscores_half = (probs * (dprobs - row_dots)).astype(BF16)
        dk = dk + dot(dscores_half, q2, 1, 0)
        dv = dv + dot(probs_half, do2, 1, 0)
        gq_t = dot(keys_t, dscores_half, 1, 0) * scale
        for i, a in enumerate(at):
            gq = gq_t[:, i * rows : (i + 1) * rows].T.astype(BF16)
            gq_ref[:, a : a + head] = gq
            if a < lead_ref.shape[1]:
                lead_ref[:, a : a + head] = gq
    terms = jnp.concatenate([dk * scale, dv], axis=1).astype(BF16).reshape(span, rows, 2 * head)
    if not cube:
        term_refs[0][...] = terms
        term_refs[1][...] = terms[span - 1]
        return
    for ref in term_refs:
        ref[...] = jnp.zeros_like(ref)
    for t in range(span):
        p = cube_place(own, own - (span - 1) + t)
        shown = own >= span - 1 - t

        for chip, ref in enumerate(term_refs):

            @pl.when(shown & (p // 2 == chip))
            def _(t=t, p=p, ref=ref):
                ref[p % 2] = terms[t].astype(ref.dtype)


def cube_place(own, shard):
    gap = jnp.bitwise_xor(own, shard % 8)
    core, across, along = gap % 2, gap // 2 % 2, gap // 4
    first = jnp.where(own % 2 == 0, across, along)
    return core + 2 * first + 4 * (across + along - first)


def shift(value, by):
    ctx = lax.axis_size("ctx")
    return lax.ppermute(value, "ctx", [(i, (i + by) % ctx) for i in range(ctx)])


def attention(own, lens, q, do, own_kv, cube):
    ctx = lax.axis_size("ctx")
    span = ctx // 2 + 1
    slots = [shift(own_kv, d) for d in range(span - 1, 0, -1)] + [own_kv]
    head = own_kv.shape[1] // 2
    rows = q.shape[0]
    group = q.shape[1] // head
    smem = pl.BlockSpec(memory_space=pltpu.SMEM)
    vmem = pl.BlockSpec(memory_space=pltpu.VMEM)
    if cube:
        terms = [jax.ShapeDtypeStruct((2, rows, 2 * head), t) for t in (F32, BF16, BF16, BF16)]
    else:
        terms = [jax.ShapeDtypeStruct(n + (rows, 2 * head), BF16) for n in ((span,), ())]
    return pl.pallas_call(
        functools.partial(
            attention_kernel, span=span, head=head, group=group, docs=lens.shape[1], cube=cube
        ),
        out_shape=(
            jax.ShapeDtypeStruct(q.shape, BF16),
            jax.ShapeDtypeStruct((rows, LEAD * head), BF16),
            *terms,
        ),
        in_specs=[smem, smem] + [vmem] * (2 + len(slots)),
        out_specs=(vmem,) * (2 + len(terms)),
        compiler_params=pltpu.CompilerParams(vmem_limit_bytes=VMEM_LIMIT),
        cost_estimate=pl.CostEstimate(
            flops=12 * group * rows * rows * span * head,
            bytes_accessed=6 * q.size + 4 * span * rows * 2 * head,
            transcendentals=group * rows * rows * span,
        ),
        name="attention",
    )(own, lens, q, do, *slots)


def spread_kernel(place_ref, x_ref, *outs, dp, part):
    z, c = place_ref[0], place_ref[1]
    first = 2 + 2 * (c % 2)
    for far in range(2):
        for at, flip in enumerate((0, first, 6 - first, 6)):
            out = outs[at] if not far else outs[5] if at == 3 else outs[4].at[at]
            for other in range(2):
                for high in range(2):
                    plane = (2 * high + z % 2) ^ far
                    src = pl.multiple_of(((c ^ flip ^ other) * dp + plane) * part, part)
                    out[other, :, high * part : (high + 1) * part] = x_ref[:, pl.ds(src, part)]


def spread(place, x, ctx, dp):
    rows, width = x.shape
    part = width // (ctx * dp)
    piece = (2, rows, 2 * part)
    vmem = pl.BlockSpec(memory_space=pltpu.VMEM)
    return pl.pallas_call(
        functools.partial(spread_kernel, dp=dp, part=part),
        out_shape=[jax.ShapeDtypeStruct(p, BF16) for p in [piece] * 4 + [(3,) + piece, piece]],
        in_specs=[pl.BlockSpec(memory_space=pltpu.SMEM), vmem],
        out_specs=[vmem] * 6,
        compiler_params=pltpu.CompilerParams(vmem_limit_bytes=VMEM_LIMIT),
        cost_estimate=pl.CostEstimate(flops=0, bytes_accessed=4 * x.size, transcendentals=0),
        name="spread",
    )(place, x)


def local_call(kernel, name, out_shape, args, gates=(), smem=0, flops=0):
    vmem = pl.BlockSpec(memory_space=pltpu.VMEM)
    specs = [pl.BlockSpec(memory_space=pltpu.SMEM)] * smem + [vmem] * (len(args) - smem)
    specs += [pl.BlockSpec(memory_space=pl.ANY)] * len(gates)
    return pl.pallas_call(
        kernel,
        out_shape=out_shape,
        in_specs=specs,
        out_specs=jax.tree.map(lambda _: vmem, out_shape),
        compiler_params=pltpu.CompilerParams(vmem_limit_bytes=VMEM_LIMIT),
        cost_estimate=pl.CostEstimate(
            flops=flops,
            bytes_accessed=sum(2 * a.size for a in args) + sum(2 * o.size for o in out_shape),
            transcendentals=0,
        ),
        name=name,
    )(*args, *gates)


def turn_kernel(*refs):
    pieces, outs = refs[:4], refs[-2:]
    rows = pieces[1].shape[1]
    for at, piece in enumerate(pieces):
        piece = piece.at[0] if len(piece.shape) == 4 else piece
        for core in range(2):
            outs[core][:, at * rows : (at + 1) * rows] = piece[core].T


def turn(pieces):
    _, rows, width = pieces[1].shape
    turned = jax.ShapeDtypeStruct((width, 4 * rows), BF16)
    return local_call(turn_kernel, "turn", (turned, turned), pieces)


def pack_kernel(own_ref, moved_ref, *refs):
    n = own_ref.shape[0]
    refs[-1][:n] = own_ref[...]
    refs[-1][n:] = moved_ref[...]


def pack(own, moved, gates=()):
    out = jax.ShapeDtypeStruct((2 * own.shape[0],) + own.shape[1:], BF16)
    return local_call(pack_kernel, "pack", (out,), [own, moved], gates)[0]


def hold_kernel(own_ref, *refs):
    refs[-1][...] = own_ref[...]


def hold(own, gates):
    out = jax.ShapeDtypeStruct(own.shape, own.dtype)
    return local_call(hold_kernel, "hold", (out,), [own], gates)[0]


def merge_kernel(held_ref, *refs):
    moved, (hold_ref, send_ref) = refs[:3], refs[-2:]
    total = held_ref[...]
    for ref in moved:
        total = total + ref[...].astype(F32)
    hold_ref[...] = total[0]
    send_ref[...] = total[1].astype(BF16)


def merge(held, moved, gates=()):
    outs = tuple(jax.ShapeDtypeStruct(held.shape[1:], t) for t in (F32, BF16))
    return local_call(merge_kernel, "merge", outs, [held, *moved], gates)


def settle_kernel(gq_ref, held_ref, *refs):
    moved, (cols_ref, gkv_ref) = refs[:-2], refs[-2:]
    width = cols_ref.shape[1] - gkv_ref.shape[1]
    total = held_ref[...].astype(F32)
    for ref in moved:
        total = total + ref[...].astype(F32)
    gkv = total.astype(BF16)
    gkv_ref[...] = gkv
    cols_ref[:, :width] = gq_ref[:, gq_ref.shape[1] - width :]
    cols_ref[:, width:] = gkv


def settle(gq, lead, held, moved):
    rows, kv_width = held.shape
    outs = (
        jax.ShapeDtypeStruct((rows, gq.shape[1] - lead.shape[1] + kv_width), BF16),
        jax.ShapeDtypeStruct((rows, kv_width), BF16),
    )
    return local_call(settle_kernel, "settle", outs, [gq, held, *moved])


def fold_kernel(side_ref, *refs):
    turned, cols, out = refs[:4], refs[4:10], refs[-1]
    rows = cols[0].shape[1]
    pairs = [(col, at) for col in cols for at in range(0, col.shape[0], 2)]
    half, n = out.shape
    at = pl.multiple_of(side_ref[0] * half, half)
    total = None
    for core in range(2):
        for chip in range(4):
            span = slice(chip * rows, (chip + 1) * rows)
            left = jnp.concatenate(
                [t[pl.ds(at, half), span] for t in turned[2 * core : 2 * core + 2]], axis=1
            )
            col, pair = pairs[4 * core + chip]
            term = dot(left, col[pair : pair + 2].reshape(2 * rows, n), 1, 0)
            total = term if total is None else total + term
    out[...] = total.astype(out.dtype)


def fold(side, turned, cols, dtype, gates=()):
    half = turned[0].shape[0] // 2
    depth = 4 * turned[0].shape[1]
    n = cols[0].shape[2]
    out = jax.ShapeDtypeStruct((half, n), dtype)
    args = [side, *turned, *cols]
    flops = 2 * half * depth * n
    return local_call(fold_kernel, "fold", (out,), args, gates, smem=1, flops=flops)[0]


def fold_rows(features, piece_rows):
    return lax.dot_general(
        features, piece_rows, (((0,), (0,)), ((), ())), preferred_element_type=F32
    )


def hop(value, dz, of_core):
    pairs = [
        (8 * z + c, 8 * (z ^ dz) + (c ^ of_core[c % 2])) for z in range(4) for c in range(8)
    ]
    return lax.ppermute(value, ("dp", "ctx"), pairs)


FIRST, SECOND, DIAGONAL, STAY, SIBLING = (2, 4), (4, 2), (6, 6), (0, 0), (1, 1)


def gather_pairs(cols, gates, late_gates=()):
    both = pack(cols[None], hop(cols, 1, STAY)[None], gates)
    from_first = hop(both, 0, FIRST)
    from_second = hop(both, 0, SECOND)
    from_diagonal = hop(from_first, 0, SECOND)
    near = hop(pack(both, from_first), 0, SIBLING)
    far = hop(pack(from_second, from_diagonal, late_gates), 0, SIBLING)
    return [both, from_first, from_second, from_diagonal, near, far]


def shards_cube(normed_input, queries, keys_values, grad_output, doc_lengths):
    ctx, dp = lax.axis_size("ctx"), lax.axis_size("dp")
    own, z = lax.axis_index("ctx"), lax.axis_index("dp")
    side = (z // 2)[None]
    *pieces, across, corner = spread(jnp.stack([z, own]), normed_input[0], ctx, dp)
    grad_query, lead, held, *send = attention(
        own[None], doc_lengths, queries[0], grad_output[0], keys_values[0], cube=True
    )
    chips = (FIRST, SECOND, DIAGONAL)
    near, near_sib = turn(pieces[:1] + [hop(p, 0, c) for p, c in zip(pieces[1:], chips)])
    across = hop(across, 1, STAY)
    corner = hop(hold(corner, [lead]), 1, DIAGONAL)
    far, far_sib = turn([across, hop(across[1], 0, FIRST), hop(across[2], 0, SECOND), corner])
    turned = [near, far, hop(near_sib, 0, SIBLING), hop(far_sib, 0, SIBLING)]
    first_cols = gather_pairs(lead, [near])
    held, send = merge(held, [hop(t, 0, c) for t, c in zip(send, chips)])
    rest, grad_kv = settle(grad_query, lead, held, [hop(send, 0, SIBLING)])
    first_fold = fold(1 - side, turned, first_cols, BF16)
    rest_cols = gather_pairs(rest, [far], [first_fold])
    first_sent = hop(first_fold, 2, STAY)
    rest_sent = hop(fold(1 - side, turned, rest_cols, BF16), 2, STAY)
    totals = [
        fold(side, turned, cols, F32) + sent.astype(F32)
        for cols, sent in ((first_cols, first_sent), (rest_cols, rest_sent))
    ]
    return grad_query[None], grad_kv[None], jnp.concatenate(totals, axis=1)


def shards(normed_input, queries, keys_values, grad_output, doc_lengths):
    ctx = lax.axis_size("ctx")
    own = lax.axis_index("ctx")
    shard_rows, model_width = normed_input.shape[1:]
    grad_query, lead, terms, held = attention(
        own[None], doc_lengths, queries[0], grad_output[0], keys_values[0], cube=False
    )
    span = terms.shape[0]
    moved = [shift(terms[span - 1 - d], -d) for d in range(1, span)]
    rest, grad_kv = settle(grad_query, lead, held, moved)
    grad_cols = jnp.concatenate([lead, rest], axis=1)
    part = model_width // ctx
    pieces = normed_input[0].reshape(shard_rows, ctx, part)
    my_features = lax.all_to_all(pieces, "ctx", split_axis=1, concat_axis=0, tiled=True)
    my_features = my_features.reshape(ctx * shard_rows, part)
    partial = fold_rows(my_features, lax.all_gather(grad_cols, "ctx", axis=0, tiled=True))
    grad_weights = lax.psum_scatter(
        partial.astype(BF16), "dp", scatter_dimension=0, tiled=True
    ).astype(F32)
    return grad_query[None], grad_kv[None], grad_weights


def solution(mesh):
    cube = mesh.shape["dp"] == 4 and mesh.shape["ctx"] == 8
    spec = P("dp", "ctx", None)
    return jax.shard_map(
        shards_cube if cube else shards,
        mesh=mesh,
        in_specs=(spec, spec, spec, spec, P("dp", None)),
        out_specs=(spec, spec, P(("ctx", "dp"), None)),
        check_vma=False,
    )
```

time: 125 us -> 102 us (0.82)
  local copies, waits for them, and re-layouts: 14.9 us -> 1.67 us
  starting transfers between devices: 41.1 us -> 31.9 us
  waiting for transfers between devices: 56.4 us -> 47.2 us
  Pallas kernels: 9.76 us -> 18.5 us
    unnamed x76 -> x24, local copies, waits for them, and re-layouts: 13.8 us -> 1.63 us
    ppermute x36 -> x27, waiting for transfers between devices: 55.6 us -> 46 us  [hop(): return lax.ppermute(value, ('dp', 'ctx'), pairs)]
    pallas_call x7 -> x15, Pallas kernels: 4.42 us -> 12.9 us  [local_call(): pl.pallas_call(kernel, out_shape=out_shape, in_specs=specs, out_specs=jax...]
    ppermute x8 -> x4, starting transfers between devices: 9.09 us -> 4.42 us  [shift(): return lax.ppermute(value, 'ctx', [(i, (i + by) % ctx) for i in range(ctx)])]
    ppermute x36 -> x27, starting transfers between devices: 32 us -> 27.5 us  [hop(): return lax.ppermute(value, ('dp', 'ctx'), pairs)]
  transfers between devices with their start and end apart: 44 -> 31, of which waited for: 13 -> 13; matrix products, arithmetic and copies ran while one was open for 1% -> 0% of each run, Pallas kernels for 8% -> 17%
where the time goes in v3:
time: 102 us
  waiting for transfers between devices  47.2 us (46%)
  starting transfers between devices  31.9 us (31%)
  Pallas kernels  18.5 us (18%)
  local copies, waits for them, and re-layouts  1.67 us (2%)
  other arithmetic  1.35 us (1%)
    ppermute x27, waiting for transfers between devices, hop(): return lax.ppermute(value, ('dp', 'ctx'), pairs)  46 us
    ppermute x27, starting transfers between devices, hop(): return lax.ppermute(value, ('dp', 'ctx'), pairs)  27.5 us
    pallas_call x15, Pallas kernels, local_call(): pl.pallas_call(kernel, out_shape=out_shape, in_specs=specs, out_specs=jax...  12.9 us
    pallas_call x1, Pallas kernels, attention(): pl.pallas_call(functools.partial(attention_kernel, span=span, head=head,...  4.78 us
    ppermute x4, starting transfers between devices, shift(): return lax.ppermute(value, 'ctx', [(i, (i + by) % ctx) for i in range(ctx)])  4.42 us
  transfers between devices with their start and end apart: 31, of which 13 were waited for; matrix products, arithmetic and copies ran while one was open for 0% of the time, Pallas kernels for 17%

profile of v3, /device:TPU:0, one launch (start us, length us, event | category | flops | bytes accessed | tf_op | source)
XLA Modules:
  0.0 101.5 jit_solution(17447460643643946817)
XLA Ops:
  0.7 1.6 %copy-done.6 = bf16[1,128,8192]{2,1,0:T(8,128)(2,1)S(1)} copy-done((bf16[1,128,8192]{2,1,0:T(8,128)(2,1)S(1)}, bf16[1,128,8192]{2,1,0:T(8,128)(2,1)}, u32[]{:S(2)}) %copy-start.6) | copy-done | bytes 2097176
  2.3 0.8 spread.1
  3.1 3.1 %collective-permute-start.11 = (bf16[3,2,128,512]{3,2,1,0:T(8,128)(2,1)S(1)}, bf16[3,2,128,512]{3,2,1,0:T(8,128)(2,1)S(1)}, u32[]{:S(2)}, u32[]{:S(2)}) collective-permute-start(bf16[3,2,128,512]{3,2,1,0:T(8,128)(2,1)S(1)} %get-tuple-element.36), channel_id=1, source_target_pairs={{0,8},{1,9},{2,10},{3,11},{4,12},{5,13},{6,14},{7,15},{8,0},{9,1},... | collective-permute-start | bytes 2359304 | tf_op jit(solution)/shard_map/ppermute | solution.py:280
  6.2 1.5 %collective-permute-start.2 = (bf16[128,256]{1,0:T(8,128)(2,1)S(1)}, bf16[128,256]{1,0:T(8,128)(2,1)S(1)}, u32[]{:S(2)}, u32[]{:S(2)}) collective-permute-start(bf16[128,256]{1,0:T(8,128)(2,1)S(1)} %bitcast.26), channel_id=1, source_target_pairs={{0,2},{1,3},{2,4},{3,5},{4,6},{5,7},{6,0},{7,1},{8,10},{9,11},{10,... | collective-permute-start | bytes 196616 | tf_op jit(solution)/shard_map/ppermute | solution.py:86
  7.8 2.4 %collective-permute-start.1 = (bf16[128,256]{1,0:T(8,128)(2,1)S(1)}, bf16[128,256]{1,0:T(8,128)(2,1)S(1)}, u32[]{:S(2)}, u32[]{:S(2)}) collective-permute-start(bf16[128,256]{1,0:T(8,128)(2,1)S(1)} %bitcast.27), channel_id=1, source_target_pairs={{0,3},{1,4},{2,5},{3,6},{4,7},{5,0},{6,1},{7,2},{8,11},{9,12},{10,... | collective-permute-start | bytes 196616 | tf_op jit(solution)/shard_map/ppermute | solution.py:86
  10.2 0.5 collective-permute-start
  10.7 0.3 collective-permute-done.3.refs_3_
  11.0 1.2 %collective-permute-start.8 = (bf16[2,128,512]{2,1,0:T(8,128)(2,1)S(1)}, bf16[2,128,512]{2,1,0:T(8,128)(2,1)S(1)}, u32[]{:S(2)}, u32[]{:S(2)}) collective-permute-start(bf16[2,128,512]{2,1,0:T(8,128)(2,1)S(1)} %get-tuple-element.32), channel_id=1, source_target_pairs={{0,2},{1,5},{2,0},{3,7},{4,6},{5,1},{6,4},{7,3},{8,10},{9,13},{10,... | collective-permute-start | bytes 786440 | tf_op jit(solution)/shard_map/ppermute | solution.py:280
  12.2 1.2 %collective-permute-start.9 = (bf16[2,128,512]{2,1,0:T(8,128)(2,1)S(1)}, bf16[2,128,512]{2,1,0:T(8,128)(2,1)S(1)}, u32[]{:S(2)}, u32[]{:S(2)}) collective-permute-start(bf16[2,128,512]{2,1,0:T(8,128)(2,1)S(1)} %get-tuple-element.33), channel_id=1, source_target_pairs={{0,4},{1,3},{2,6},{3,1},{4,0},{5,7},{6,2},{7,5},{8,12},{9,11},{10,... | collective-permute-start | bytes 786440 | tf_op jit(solution)/shard_map/ppermute | solution.py:280
  13.4 1.1 %collective-permute-start.10 = (bf16[2,128,512]{2,1,0:T(8,128)(2,1)S(1)}, bf16[2,128,512]{2,1,0:T(8,128)(2,1)S(1)}, u32[]{:S(2)}, u32[]{:S(2)}) collective-permute-start(bf16[2,128,512]{2,1,0:T(8,128)(2,1)S(1)} %get-tuple-element.34), channel_id=1, source_target_pairs={{0,6},{1,7},{2,4},{3,5},{4,2},{5,3},{6,0},{7,1},{8,14},{9,15},{10,... | collective-permute-start | bytes 786440 | tf_op jit(solution)/shard_map/ppermute | solution.py:280
  14.5 0.9 collective-permute-done.refs_0_
  15.4 4.8 %attention.1 = (bf16[128,1024]{1,0:T(8,128)(2,1)}, bf16[128,512]{1,0:T(8,128)(2,1)S(1)}, f32[2,128,256]{2,1,0:T(8,128)S(1)}, bf16[2,128,256]{2,1,0:T(8,128)(2,1)...) custom-call(s32[1]{0:T(128)} %bitcast.own_ref, s32[1,3]{1,0:T(1,128)S(1)} %copy-done.11, ...), custom_call_target="tpu_custom_call" | custom-call | flops 1006632960 | bytes 1441792 | tf_op jit(solution)/shard_map/attention/pallas_call | solution.py:102
  20.2 0.4 collective-permute-start.17
  20.7 1.9 %collective-permute-start.4 = (bf16[2,128,256]{2,1,0:T(8,128)(2,1)S(1)}, bf16[2,128,256]{2,1,0:T(8,128)(2,1)S(1)}, u32[]{:S(2)}, u32[]{:S(2)}) collective-permute-start(bf16[2,128,256]{2,1,0:T(8,128)(2,1)S(1)} %get-tuple-element.25), channel_id=1, source_target_pairs={{0,2},{1,5},{2,0},{3,7},{4,6},{5,1},{6,4},{7,3},{8,10},{9,13},{10,... | collective-permute-start | bytes 393224 | tf_op jit(solution)/shard_map/ppermute | solution.py:280
  22.6 3.0 %collective-permute-done.9.refs_2_ = bf16[2,128,512]{2,1,0:T(8,128)(2,1)S(1)} collective-permute-done((bf16[2,128,512]{2,1,0:T(8,128)(2,1)S(1)}, bf16[2,128,512]{2,1,0:T(8,128)(2,1)S(1)}, u32[]{:S(2)}, u32[]{:S(2)}) %collective-permute-start.9) | collective-permute-done | bytes 262176 | tf_op jit(solution)/shard_map/ppermute | solution.py:280
  25.5 2.6 %collective-permute-start.5 = (bf16[2,128,256]{2,1,0:T(8,128)(2,1)S(1)}, bf16[2,128,256]{2,1,0:T(8,128)(2,1)S(1)}, u32[]{:S(2)}, u32[]{:S(2)}) collective-permute-start(bf16[2,128,256]{2,1,0:T(8,128)(2,1)S(1)} %get-tuple-element.26), channel_id=1, source_target_pairs={{0,4},{1,3},{2,6},{3,1},{4,0},{5,7},{6,2},{7,5},{8,12},{9,11},{10,... | collective-permute-start | bytes 393224 | tf_op jit(solution)/shard_map/ppermute | solution.py:280
  28.2 0.3 turn.2
  28.5 2.5 %collective-permute-start.14 = (bf16[2,128,512]{2,1,0:T(8,128)(2,1)S(1)}, bf16[2,128,512]{2,1,0:T(8,128)(2,1)S(1)}, u32[]{:S(2)}, u32[]{:S(2)}) collective-permute-start(bf16[2,128,512]{2,1,0:T(8,128)(2,1)S(1)} %hold.1), channel_id=1, source_target_pairs={{0,14},{1,15},{2,12},{3,13},{4,10},{5,11},{6,8},{7,9},{8,6},{9,7},... | collective-permute-start | bytes 786440 | tf_op jit(solution)/shard_map/ppermute | solution.py:280
  31.2 1.1 %collective-permute-start.13 = (bf16[2,128,512]{2,1,0:T(8,128)(2,1)S(1)}, bf16[2,128,512]{2,1,0:T(8,128)(2,1)S(1)}, u32[]{:S(2)}, u32[]{:S(2)}) collective-permute-start(bf16[2,128,512]{2,1,0:T(8,128)(2,1)S(1)} %get-tuple-element.43), channel_id=1, source_target_pairs={{0,4},{1,3},{2,6},{3,1},{4,0},{5,7},{6,2},{7,5},{8,12},{9,11},{10,... | collective-permute-start | bytes 786440 | tf_op jit(solution)/shard_map/ppermute | solution.py:280
  32.3 6.8 %collective-permute-done.5.refs_1_ = bf16[2,128,256]{2,1,0:T(8,128)(2,1)S(1)} collective-permute-done((bf16[2,128,256]{2,1,0:T(8,128)(2,1)S(1)}, bf16[2,128,256]{2,1,0:T(8,128)(2,1)S(1)}, u32[]{:S(2)}, u32[]{:S(2)}) %collective-permute-start.5) | collective-permute-done | bytes 131104 | tf_op jit(solution)/shard_map/ppermute | solution.py:280
  39.1 1.4 %collective-permute-done.6.refs_2_ = bf16[2,128,256]{2,1,0:T(8,128)(2,1)S(1)} collective-permute-done((bf16[2,128,256]{2,1,0:T(8,128)(2,1)S(1)}, bf16[2,128,256]{2,1,0:T(8,128)(2,1)S(1)}, u32[]{:S(2)}, u32[]{:S(2)}) %collective-permute-start.6) | collective-permute-done | bytes 131104 | tf_op jit(solution)/shard_map/ppermute | solution.py:280
  40.7 1.2 %collective-permute-done.7.refs_0_ = bf16[128,256]{1,0:T(8,128)(2,1)S(1)} collective-permute-done((bf16[128,256]{1,0:T(8,128)(2,1)S(1)}, bf16[128,256]{1,0:T(8,128)(2,1)S(1)}, u32[]{:S(2)}, u32[]{:S(2)}) %collective-permute-start.7) | collective-permute-done | bytes 65568 | tf_op jit(solution)/shard_map/ppermute | solution.py:280
  41.9 0.7 settle.1
  42.5 0.2 collective-permute-start.15
  42.7 1.1 %collective-permute-done.18.moved_ref.refs_5_ = bf16[2,128,512]{2,1,0:T(8,128)(2,1)S(1)} collective-permute-done((bf16[2,128,512]{2,1,0:T(8,128)(2,1)S(1)}, bf16[2,128,512]{2,1,0:T(8,128)(2,1)S(1)}, u32[]{:S(2)}, u32[]{:S(2)}) %collective-permute-start.18) | collective-permute-done | bytes 262176 | tf_op jit(solution)/shard_map/ppermute | solution.py:280
  43.8 1.5 %collective-permute-start.19 = (bf16[2,128,512]{2,1,0:T(8,128)(2,1)S(1)}, bf16[2,128,512]{2,1,0:T(8,128)(2,1)S(1)}, u32[]{:S(2)}, u32[]{:S(2)}) collective-permute-start(bf16[2,128,512]{2,1,0:T(8,128)(2,1)S(1)} %pack.6.own_ref.refs_4_), channel_id=1, source_target_pairs={{0,4},{1,3},{2,6},{3,1},{4,0},{5,7},{6,2},{7,5},{8,12},{9,11},{10,... | collective-permute-start | bytes 786440 | tf_op jit(solution)/shard_map/ppermute | solution.py:280
  45.4 1.7 %collective-permute-start.20 = (bf16[2,128,512]{2,1,0:T(8,128)(2,1)S(1)}, bf16[2,128,512]{2,1,0:T(8,128)(2,1)S(1)}, u32[]{:S(2)}, u32[]{:S(2)}) collective-permute-start(bf16[2,128,512]{2,1,0:T(8,128)(2,1)S(1)} %collective-permute-done.18.moved_ref.refs_5_), channel_id=1, source_target_pairs={{0,4},{1,3},{2,6},{3,1},{4,0},{5,7},{6,2},{7,5},{8,12},{9,11},{10,... | collective-permute-start | bytes 786440 | tf_op jit(solution)/shard_map/ppermute | solution.py:280
  47.2 1.1 %turn.3 = (bf16[512,512]{1,0:T(8,128)(2,1)S(1)}, bf16[512,512]{1,0:T(8,128)(2,1)}) custom-call(bf16[3,2,128,512]{3,2,1,0:T(8,128)(2,1)S(1)} %collective-permute-done.11.refs_0_, bf16[2,128,512]{2,1,0:T(8,128)(2,1)S(1)} %collective-permute-done.12.refs_1_, bf16[2,128,512]{2,1,0:T(8,128)(2,1)S(1)} %collective-permute-done.13.refs_2_, ...), custom_call_target="tpu_custom_call" | custom-call | bytes 2621440 | tf_op jit(solution)/shard_map/turn/pallas_call | solution.py:156
  48.3 1.2 %collective-permute-done.24 = bf16[128,768]{1,0:T(8,128)(2,1)S(1)} collective-permute-done((bf16[128,768]{1,0:T(8,128)(2,1)S(1)}, bf16[128,768]{1,0:T(8,128)(2,1)S(1)}, u32[]{:S(2)}, u32[]{:S(2)}) %collective-permute-start.24) | collective-permute-done | bytes 196640 | tf_op jit(solution)/shard_map/ppermute | solution.py:280
  49.6 0.9 pack.7
  50.5 0.6 collective-permute-start.21
  51.1 3.6 %collective-permute-done.20.moved_ref.refs_7_ = bf16[2,128,512]{2,1,0:T(8,128)(2,1)S(1)} collective-permute-done((bf16[2,128,512]{2,1,0:T(8,128)(2,1)S(1)}, bf16[2,128,512]{2,1,0:T(8,128)(2,1)S(1)}, u32[]{:S(2)}, u32[]{:S(2)}) %collective-permute-start.20) | collective-permute-done | bytes 262176 | tf_op jit(solution)/shard_map/ppermute | solution.py:280
  54.7 0.9 pack.8
  55.6 0.5 collective-permute-start.16
  56.1 1.5 %collective-permute-start.26 = (bf16[2,128,768]{2,1,0:T(8,128)(2,1)S(1)}, bf16[2,128,768]{2,1,0:T(8,128)(2,1)S(1)}, u32[]{:S(2)}, u32[]{:S(2)}) collective-permute-start(bf16[2,128,768]{2,1,0:T(8,128)(2,1)S(1)} %pack.9.own_ref.refs_4_), channel_id=1, source_target_pairs={{0,4},{1,3},{2,6},{3,1},{4,0},{5,7},{6,2},{7,5},{8,12},{9,11},{10,... | collective-permute-start | bytes 1179656 | tf_op jit(solution)/shard_map/ppermute | solution.py:280
  57.7 0.9 collective-permute-start.27
  58.5 1.1 %pack.10 = bf16[4,128,768]{2,1,0:T(8,128)(2,1)S(1)} custom-call(bf16[2,128,768]{2,1,0:T(8,128)(2,1)S(1)} %pack.9.own_ref.refs_4_, bf16[2,128,768]{2,1,0:T(8,128)(2,1)} %collective-permute-done.25.moved_ref.refs_5_), custom_call_target="tpu_custom_call" | custom-call | bytes 1572864 | tf_op jit(solution)/shard_map/pack/pallas_call | solution.py:156
  59.8 1.9 %fold.5.refs_0_ = bf16[256,512]{1,0:T(8,128)(2,1)S(1)} custom-call(s32[1]{0:T(128)S(6)} %sub.9.side_ref, bf16[512,512]{1,0:T(8,128)(2,1)S(1)} %get-tuple-element.35.refs_0_, bf16[512,512]{1,0:T(8,128)(2,1)S(1)} %get-tuple-element.39.refs_1_.refs_0_, bf16[512,512]{1,0:T(8,128)(2,1)S(1)} %collective-permute-done.15.refs_2_, ...), custom_call_target="tpu_custom_call" | custom-call | flops 536870912 | bytes 4456450 | tf_op jit(solution)/shard_map/fold/pallas_call | solution.py:156
  61.7 2.2 %collective-permute-done.26.own_ref.refs_6_ = bf16[2,128,768]{2,1,0:T(8,128)(2,1)S(1)} collective-permute-done((bf16[2,128,768]{2,1,0:T(8,128)(2,1)S(1)}, bf16[2,128,768]{2,1,0:T(8,128)(2,1)S(1)}, u32[]{:S(2)}, u32[]{:S(2)}) %collective-permute-start.26) | collective-permute-done | bytes 393248 | tf_op jit(solution)/shard_map/ppermute | solution.py:280
  63.9 4.2 %collective-permute-done.27.moved_ref.refs_7_ = bf16[2,128,768]{2,1,0:T(8,128)(2,1)S(1)} collective-permute-done((bf16[2,128,768]{2,1,0:T(8,128)(2,1)}, bf16[2,128,768]{2,1,0:T(8,128)(2,1)S(1)}, u32[]{:S(2)}, u32[]{:S(2)}) %collective-permute-start.27) | collective-permute-done | bytes 393248 | tf_op jit(solution)/shard_map/ppermute | solution.py:280
  68.2 2.7 %collective-permute-start.23 = (bf16[256,512]{1,0:T(8,128)(2,1)S(1)}, bf16[256,512]{1,0:T(8,128)(2,1)S(1)}, u32[]{:S(2)}, u32[]{:S(2)}) collective-permute-start(bf16[256,512]{1,0:T(8,128)(2,1)S(1)} %fold.5.refs_0_), channel_id=1, source_target_pairs={{0,16},{1,17},{2,18},{3,19},{4,20},{5,21},{6,22},{7,23},{8,24},{9,... | collective-permute-start | bytes 786440 | tf_op jit(solution)/shard_map/ppermute | solution.py:280
  70.9 2.0 %fold.7 = bf16[256,768]{1,0:T(8,128)(2,1)S(1)} custom-call(s32[1]{0:T(128)S(6)} %sub.9.side_ref, bf16[512,512]{1,0:T(8,128)(2,1)S(1)} %get-tuple-element.35.refs_0_, bf16[512,512]{1,0:T(8,128)(2,1)S(1)} %get-tuple-element.39.refs_1_.refs_0_, bf16[512,512]{1,0:T(8,128)(2,1)S(1)} %collective-permute-done.15.refs_2_, ...), custom_call_target="tpu_custom_call" | custom-call | flops 805306368 | bytes 5636098 | tf_op jit(solution)/shard_map/fold/pallas_call | solution.py:156
  72.9 2.3 %collective-permute-start.30 = (bf16[256,768]{1,0:T(8,128)(2,1)S(1)}, bf16[256,768]{1,0:T(8,128)(2,1)S(1)}, u32[]{:S(2)}, u32[]{:S(2)}) collective-permute-start(bf16[256,768]{1,0:T(8,128)(2,1)S(1)} %fold.7), channel_id=1, source_target_pairs={{0,16},{1,17},{2,18},{3,19},{4,20},{5,21},{6,22},{7,23},{8,24},{9,... | collective-permute-start | bytes 1179656 | tf_op jit(solution)/shard_map/ppermute | solution.py:280
  75.1 1.9 %fold.4 = f32[256,512]{1,0:T(8,128)S(1)} custom-call(s32[1]{0:T(128)} %bitcast.6.side_ref, bf16[512,512]{1,0:T(8,128)(2,1)S(1)} %get-tuple-element.35.refs_0_, bf16[512,512]{1,0:T(8,128)(2,1)S(1)} %get-tuple-element.39.refs_1_.refs_0_, bf16[512,512]{1,0:T(8,128)(2,1)S(1)} %collective-permute-done.15.refs_2_, ...), custom_call_target="tpu_custom_call" | custom-call | flops 536870912 | bytes 4456450 | tf_op jit(solution)/shard_map/fold/pallas_call | solution.py:156
  77.0 15.3 %collective-permute-done.23 = bf16[256,512]{1,0:T(8,128)(2,1)S(1)} collective-permute-done((bf16[256,512]{1,0:T(8,128)(2,1)S(1)}, bf16[256,512]{1,0:T(8,128)(2,1)S(1)}, u32[]{:S(2)}, u32[]{:S(2)}) %collective-permute-start.23) | collective-permute-done | bytes 262176 | tf_op jit(solution)/shard_map/ppermute | solution.py:280
  92.4 2.0 %fold.6 = f32[256,768]{1,0:T(8,128)S(1)} custom-call(s32[1]{0:T(128)} %bitcast.6.side_ref, bf16[512,512]{1,0:T(8,128)(2,1)S(1)} %get-tuple-element.35.refs_0_, bf16[512,512]{1,0:T(8,128)(2,1)S(1)} %get-tuple-element.39.refs_1_.refs_0_, bf16[512,512]{1,0:T(8,128)(2,1)S(1)} %collective-permute-done.15.refs_2_, ...), custom_call_target="tpu_custom_call" | custom-call | flops 805306368 | bytes 5636098 | tf_op jit(solution)/shard_map/fold/pallas_call | solution.py:156
  94.4 5.9 %collective-permute-done.30 = bf16[256,768]{1,0:T(8,128)(2,1)S(1)} collective-permute-done((bf16[256,768]{1,0:T(8,128)(2,1)S(1)}, bf16[256,768]{1,0:T(8,128)(2,1)S(1)}, u32[]{:S(2)}, u32[]{:S(2)}) %collective-permute-start.30) | collective-permute-done | bytes 393248 | tf_op jit(solution)/shard_map/ppermute | solution.py:280
  100.4 1.1 %pad_maximum_fusion = f32[256,1280]{1,0:T(8,128)} fusion(f32[256,768]{1,0:T(8,128)S(1)} %convert_add_fusion, f32[256,512]{1,0:T(8,128)S(1)} %convert_add_fusion.1), kind=kLoop, calls=%fused_computation | loop fusion | flops 327680 | bytes 2621440 | tf_op jit(solution)/shard_map/concatenate | solution.py:321
  (60 shorter events, 1.0 us)
Async XLA Ops:
  0.6 14.8 %copy-start.11 = (s32[1,3]{1,0:T(1,128)S(1)}, s32[1,3]{1,0:T(1,128)}, u32[]{:S(2)}) copy-start(s32[1,3]{1,0:T(1,128)} %lens_ref.1) | copy-start | bytes 40
  0.7 1.6 %copy-start.6 = (bf16[1,128,8192]{2,1,0:T(8,128)(2,1)S(1)}, bf16[1,128,8192]{2,1,0:T(8,128)(2,1)}, u32[]{:S(2)}) copy-start(bf16[1,128,8192]{2,1,0:T(8,128)(2,1)} %param.5) | copy-start | bytes 6291460
  2.3 3.9 %copy-start.10 = (bf16[1,128,256]{2,1,0:T(8,128)(2,1)S(1)}, bf16[1,128,256]{2,1,0:T(8,128)(2,1)}, u32[]{:S(2)}) copy-start(bf16[1,128,256]{2,1,0:T(8,128)(2,1)} %param.7) | copy-start | bytes 196612
  2.3 13.1 %copy-start.8 = (bf16[1,128,1024]{2,1,0:T(8,128)(2,1)S(1)}, bf16[1,128,1024]{2,1,0:T(8,128)(2,1)}, u32[]{:S(2)}) copy-start(bf16[1,128,1024]{2,1,0:T(8,128)(2,1)} %param.6) | copy-start | bytes 786436
  2.3 13.1 %copy-start.9 = (bf16[1,128,1024]{2,1,0:T(8,128)(2,1)S(1)}, bf16[1,128,1024]{2,1,0:T(8,128)(2,1)}, u32[]{:S(2)}) copy-start(bf16[1,128,1024]{2,1,0:T(8,128)(2,1)} %param.8) | copy-start | bytes 786436
  3.1 27.9 %collective-permute-start.11 = (bf16[3,2,128,512]{3,2,1,0:T(8,128)(2,1)S(1)}, bf16[3,2,128,512]{3,2,1,0:T(8,128)(2,1)S(1)}, u32[]{:S(2)}, u32[]{:S(2)}) collective-permute-start(bf16[3,2,128,512]{3,2,1,0:T(8,128)(2,1)S(1)} %get-tuple-element.36), channel_id=1, source_target_pairs={{0,8},{1,9},{2,10},{3,11},{4,12},{5,13},{6,14},{7,15},{8,0},{9,1},... | collective-permute-start | bytes 2359304 | tf_op jit(solution)/shard_map/ppermute | solution.py:280
  6.2 4.8 %collective-permute-start.3 = (bf16[128,256]{1,0:T(8,128)(2,1)S(1)}, bf16[128,256]{1,0:T(8,128)(2,1)S(1)}, u32[]{:S(2)}, u32[]{:S(2)}) collective-permute-start(bf16[128,256]{1,0:T(8,128)(2,1)S(1)} %bitcast.25), channel_id=1, source_target_pairs={{0,1},{1,2},{2,3},{3,4},{4,5},{5,6},{6,7},{7,0},{8,9},{9,10},{10,1... | collective-permute-start | bytes 196616 | tf_op jit(solution)/shard_map/ppermute | solution.py:86
  6.2 5.9 %collective-permute-start.2 = (bf16[128,256]{1,0:T(8,128)(2,1)S(1)}, bf16[128,256]{1,0:T(8,128)(2,1)S(1)}, u32[]{:S(2)}, u32[]{:S(2)}) collective-permute-start(bf16[128,256]{1,0:T(8,128)(2,1)S(1)} %bitcast.26), channel_id=1, source_target_pairs={{0,2},{1,3},{2,4},{3,5},{4,6},{5,7},{6,0},{7,1},{8,10},{9,11},{10,... | collective-permute-start | bytes 196616 | tf_op jit(solution)/shard_map/ppermute | solution.py:86
  7.8 5.6 %collective-permute-start.1 = (bf16[128,256]{1,0:T(8,128)(2,1)S(1)}, bf16[128,256]{1,0:T(8,128)(2,1)S(1)}, u32[]{:S(2)}, u32[]{:S(2)}) collective-permute-start(bf16[128,256]{1,0:T(8,128)(2,1)S(1)} %bitcast.27), channel_id=1, source_target_pairs={{0,3},{1,4},{2,5},{3,6},{4,7},{5,0},{6,1},{7,2},{8,11},{9,12},{10,... | collective-permute-start | bytes 196616 | tf_op jit(solution)/shard_map/ppermute | solution.py:86
  10.2 5.2 %collective-permute-start = (bf16[128,256]{1,0:T(8,128)(2,1)S(1)}, bf16[128,256]{1,0:T(8,128)(2,1)S(1)}, u32[]{:S(2)}, u32[]{:S(2)}) collective-permute-start(bf16[128,256]{1,0:T(8,128)(2,1)S(1)} %bitcast.28), channel_id=1, source_target_pairs={{0,4},{1,5},{2,6},{3,7},{4,0},{5,1},{6,2},{7,3},{8,12},{9,13},{10,... | collective-permute-start | bytes 196616 | tf_op jit(solution)/shard_map/ppermute | solution.py:86
  11.0 9.6 %collective-permute-start.8 = (bf16[2,128,512]{2,1,0:T(8,128)(2,1)S(1)}, bf16[2,128,512]{2,1,0:T(8,128)(2,1)S(1)}, u32[]{:S(2)}, u32[]{:S(2)}) collective-permute-start(bf16[2,128,512]{2,1,0:T(8,128)(2,1)S(1)} %get-tuple-element.32), channel_id=1, source_target_pairs={{0,2},{1,5},{2,0},{3,7},{4,6},{5,1},{6,4},{7,3},{8,10},{9,13},{10,... | collective-permute-start | bytes 786440 | tf_op jit(solution)/shard_map/ppermute | solution.py:280
  12.2 13.4 %collective-permute-start.9 = (bf16[2,128,512]{2,1,0:T(8,128)(2,1)S(1)}, bf16[2,128,512]{2,1,0:T(8,128)(2,1)S(1)}, u32[]{:S(2)}, u32[]{:S(2)}) collective-permute-start(bf16[2,128,512]{2,1,0:T(8,128)(2,1)S(1)} %get-tuple-element.33), channel_id=1, source_target_pairs={{0,4},{1,3},{2,6},{3,1},{4,0},{5,7},{6,2},{7,5},{8,12},{9,11},{10,... | collective-permute-start | bytes 786440 | tf_op jit(solution)/shard_map/ppermute | solution.py:280
  13.4 14.8 %collective-permute-start.10 = (bf16[2,128,512]{2,1,0:T(8,128)(2,1)S(1)}, bf16[2,128,512]{2,1,0:T(8,128)(2,1)S(1)}, u32[]{:S(2)}, u32[]{:S(2)}) collective-permute-start(bf16[2,128,512]{2,1,0:T(8,128)(2,1)S(1)} %get-tuple-element.34), channel_id=1, source_target_pairs={{0,6},{1,7},{2,4},{3,5},{4,2},{5,3},{6,0},{7,1},{8,14},{9,15},{10,... | collective-permute-start | bytes 786440 | tf_op jit(solution)/shard_map/ppermute | solution.py:280
  20.2 8.3 %collective-permute-start.17 = (bf16[128,512]{1,0:T(8,128)(2,1)S(1)}, bf16[128,512]{1,0:T(8,128)(2,1)S(1)}, u32[]{:S(2)}, u32[]{:S(2)}) collective-permute-start(bf16[128,512]{1,0:T(8,128)(2,1)S(1)} %get-tuple-element.38.refs_0_), channel_id=1, source_target_pairs={{0,8},{1,9},{2,10},{3,11},{4,12},{5,13},{6,14},{7,15},{8,0},{9,1},... | collective-permute-start | bytes 393224 | tf_op jit(solution)/shard_map/ppermute | solution.py:280
  20.7 10.5 %collective-permute-start.4 = (bf16[2,128,256]{2,1,0:T(8,128)(2,1)S(1)}, bf16[2,128,256]{2,1,0:T(8,128)(2,1)S(1)}, u32[]{:S(2)}, u32[]{:S(2)}) collective-permute-start(bf16[2,128,256]{2,1,0:T(8,128)(2,1)S(1)} %get-tuple-element.25), channel_id=1, source_target_pairs={{0,2},{1,5},{2,0},{3,7},{4,6},{5,1},{6,4},{7,3},{8,10},{9,13},{10,... | collective-permute-start | bytes 393224 | tf_op jit(solution)/shard_map/ppermute | solution.py:280
  25.5 13.5 %collective-permute-start.5 = (bf16[2,128,256]{2,1,0:T(8,128)(2,1)S(1)}, bf16[2,128,256]{2,1,0:T(8,128)(2,1)S(1)}, u32[]{:S(2)}, u32[]{:S(2)}) collective-permute-start(bf16[2,128,256]{2,1,0:T(8,128)(2,1)S(1)} %get-tuple-element.26), channel_id=1, source_target_pairs={{0,4},{1,3},{2,6},{3,1},{4,0},{5,7},{6,2},{7,5},{8,12},{9,11},{10,... | collective-permute-start | bytes 393224 | tf_op jit(solution)/shard_map/ppermute | solution.py:280
  28.2 12.3 %collective-permute-start.6 = (bf16[2,128,256]{2,1,0:T(8,128)(2,1)S(1)}, bf16[2,128,256]{2,1,0:T(8,128)(2,1)S(1)}, u32[]{:S(2)}, u32[]{:S(2)}) collective-permute-start(bf16[2,128,256]{2,1,0:T(8,128)(2,1)S(1)} %get-tuple-element.27), channel_id=1, source_target_pairs={{0,6},{1,7},{2,4},{3,5},{4,2},{5,3},{6,0},{7,1},{8,14},{9,15},{10,... | collective-permute-start | bytes 393224 | tf_op jit(solution)/shard_map/ppermute | solution.py:280
  28.5 14.0 %collective-permute-start.14 = (bf16[2,128,512]{2,1,0:T(8,128)(2,1)S(1)}, bf16[2,128,512]{2,1,0:T(8,128)(2,1)S(1)}, u32[]{:S(2)}, u32[]{:S(2)}) collective-permute-start(bf16[2,128,512]{2,1,0:T(8,128)(2,1)S(1)} %hold.1), channel_id=1, source_target_pairs={{0,14},{1,15},{2,12},{3,13},{4,10},{5,11},{6,8},{7,9},{8,6},{9,7},... | collective-permute-start | bytes 786440 | tf_op jit(solution)/shard_map/ppermute | solution.py:280
  31.0 10.9 %copy-start.7 = (bf16[128,1024]{1,0:T(8,128)(2,1)S(1)}, bf16[128,1024]{1,0:T(8,128)(2,1)}, u32[]{:S(2)}) copy-start(bf16[128,1024]{1,0:T(8,128)(2,1)} %get-tuple-element.23.gq_ref) | copy-start | bytes 786436
  31.0 12.8 %collective-permute-start.18 = (bf16[2,128,512]{2,1,0:T(8,128)(2,1)S(1)}, bf16[2,128,512]{2,1,0:T(8,128)(2,1)S(1)}, u32[]{:S(2)}, u32[]{:S(2)}) collective-permute-start(bf16[2,128,512]{2,1,0:T(8,128)(2,1)S(1)} %pack.6.own_ref.refs_4_), channel_id=1, source_target_pairs={{0,2},{1,5},{2,0},{3,7},{4,6},{5,1},{6,4},{7,3},{8,10},{9,13},{10,... | collective-permute-start | bytes 786440 | tf_op jit(solution)/shard_map/ppermute | solution.py:280
  31.2 14.2 %collective-permute-start.13 = (bf16[2,128,512]{2,1,0:T(8,128)(2,1)S(1)}, bf16[2,128,512]{2,1,0:T(8,128)(2,1)S(1)}, u32[]{:S(2)}, u32[]{:S(2)}) collective-permute-start(bf16[2,128,512]{2,1,0:T(8,128)(2,1)S(1)} %get-tuple-element.43), channel_id=1, source_target_pairs={{0,4},{1,3},{2,6},{3,1},{4,0},{5,7},{6,2},{7,5},{8,12},{9,11},{10,... | collective-permute-start | bytes 786440 | tf_op jit(solution)/shard_map/ppermute | solution.py:280
  40.5 1.3 %collective-permute-start.7 = (bf16[128,256]{1,0:T(8,128)(2,1)S(1)}, bf16[128,256]{1,0:T(8,128)(2,1)S(1)}, u32[]{:S(2)}, u32[]{:S(2)}) collective-permute-start(bf16[128,256]{1,0:T(8,128)(2,1)S(1)} %get-tuple-element.29), channel_id=1, source_target_pairs={{0,1},{1,0},{2,3},{3,2},{4,5},{5,4},{6,7},{7,6},{8,9},{9,8},{10,11... | collective-permute-start | bytes 196616 | tf_op jit(solution)/shard_map/ppermute | solution.py:280
  40.6 6.5 %collective-permute-start.12 = (bf16[2,128,512]{2,1,0:T(8,128)(2,1)S(1)}, bf16[2,128,512]{2,1,0:T(8,128)(2,1)S(1)}, u32[]{:S(2)}, u32[]{:S(2)}) collective-permute-start(bf16[2,128,512]{2,1,0:T(8,128)(2,1)S(1)} %get-tuple-element.44), channel_id=1, source_target_pairs={{0,2},{1,5},{2,0},{3,7},{4,6},{5,1},{6,4},{7,3},{8,10},{9,13},{10,... | collective-permute-start | bytes 786440 | tf_op jit(solution)/shard_map/ppermute | solution.py:280
  42.5 7.0 %collective-permute-start.24 = (bf16[128,768]{1,0:T(8,128)(2,1)S(1)}, bf16[128,768]{1,0:T(8,128)(2,1)S(1)}, u32[]{:S(2)}, u32[]{:S(2)}) collective-permute-start(bf16[128,768]{1,0:T(8,128)(2,1)S(1)} %get-tuple-element.42), channel_id=1, source_target_pairs={{0,8},{1,9},{2,10},{3,11},{4,12},{5,13},{6,14},{7,15},{8,0},{9,1},... | collective-permute-start | bytes 589832 | tf_op jit(solution)/shard_map/ppermute | solution.py:280
  42.5 13.6 %collective-permute-start.15 = (bf16[512,512]{1,0:T(8,128)(2,1)S(1)}, bf16[512,512]{1,0:T(8,128)(2,1)S(1)}, u32[]{:S(2)}, u32[]{:S(2)}) collective-permute-start(bf16[512,512]{1,0:T(8,128)(2,1)S(1)} %get-tuple-element.40), channel_id=1, source_target_pairs={{0,1},{1,0},{2,3},{3,2},{4,5},{5,4},{6,7},{7,6},{8,9},{9,8},{10,11... | collective-permute-start | bytes 1572872 | tf_op jit(solution)/shard_map/ppermute | solution.py:280
  43.8 5.8 %copy-start = (bf16[2,128,512]{2,1,0:T(8,128)(2,1)}, bf16[2,128,512]{2,1,0:T(8,128)(2,1)S(1)}, u32[]{:S(2)}) copy-start(bf16[2,128,512]{2,1,0:T(8,128)(2,1)S(1)} %collective-permute-done.18.moved_ref.refs_5_) | copy-start | bytes 786436
  43.8 7.2 %collective-permute-start.19 = (bf16[2,128,512]{2,1,0:T(8,128)(2,1)S(1)}, bf16[2,128,512]{2,1,0:T(8,128)(2,1)S(1)}, u32[]{:S(2)}, u32[]{:S(2)}) collective-permute-start(bf16[2,128,512]{2,1,0:T(8,128)(2,1)S(1)} %pack.6.own_ref.refs_4_), channel_id=1, source_target_pairs={{0,4},{1,3},{2,6},{3,1},{4,0},{5,7},{6,2},{7,5},{8,12},{9,11},{10,... | collective-permute-start | bytes 786440 | tf_op jit(solution)/shard_map/ppermute | solution.py:280
  45.4 9.3 %collective-permute-start.20 = (bf16[2,128,512]{2,1,0:T(8,128)(2,1)S(1)}, bf16[2,128,512]{2,1,0:T(8,128)(2,1)S(1)}, u32[]{:S(2)}, u32[]{:S(2)}) collective-permute-start(bf16[2,128,512]{2,1,0:T(8,128)(2,1)S(1)} %collective-permute-done.18.moved_ref.refs_5_), channel_id=1, source_target_pairs={{0,4},{1,3},{2,6},{3,1},{4,0},{5,7},{6,2},{7,5},{8,12},{9,11},{10,... | collective-permute-start | bytes 786440 | tf_op jit(solution)/shard_map/ppermute | solution.py:280
  49.5 8.1 %collective-permute-start.25 = (bf16[2,128,768]{2,1,0:T(8,128)(2,1)S(1)}, bf16[2,128,768]{2,1,0:T(8,128)(2,1)}, u32[]{:S(2)}, u32[]{:S(2)}) collective-permute-start(bf16[2,128,768]{2,1,0:T(8,128)(2,1)S(1)} %pack.9.own_ref.refs_4_), channel_id=1, source_target_pairs={{0,2},{1,5},{2,0},{3,7},{4,6},{5,1},{6,4},{7,3},{8,10},{9,13},{10,... | collective-permute-start | bytes 1179656 | tf_op jit(solution)/shard_map/ppermute | solution.py:280
  50.5 9.2 %collective-permute-start.21 = (bf16[4,128,512]{2,1,0:T(8,128)(2,1)}, bf16[4,128,512]{2,1,0:T(8,128)(2,1)}, u32[]{:S(2)}, u32[]{:S(2)}) collective-permute-start(bf16[4,128,512]{2,1,0:T(8,128)(2,1)} %pack.7), channel_id=1, source_target_pairs={{0,1},{1,0},{2,3},{3,2},{4,5},{5,4},{6,7},{7,6},{8,9},{9,8},{10,11... | collective-permute-start | bytes 1572872 | tf_op jit(solution)/shard_map/ppermute | solution.py:280
  51.1 6.6 %copy-start.2 = (bf16[2,128,512]{2,1,0:T(8,128)(2,1)}, bf16[2,128,512]{2,1,0:T(8,128)(2,1)S(1)}, u32[]{:S(2)}) copy-start(bf16[2,128,512]{2,1,0:T(8,128)(2,1)S(1)} %collective-permute-done.19.own_ref.refs_6_) | copy-start | bytes 786436
  54.7 0.9 copy-start.4
  55.6 4.1 %collective-permute-start.22 = (bf16[4,128,512]{2,1,0:T(8,128)(2,1)}, bf16[4,128,512]{2,1,0:T(8,128)(2,1)}, u32[]{:S(2)}, u32[]{:S(2)}) collective-permute-start(bf16[4,128,512]{2,1,0:T(8,128)(2,1)} %pack.8), channel_id=1, source_target_pairs={{0,1},{1,0},{2,3},{3,2},{4,5},{5,4},{6,7},{7,6},{8,9},{9,8},{10,11... | collective-permute-start | bytes 1572872 | tf_op jit(solution)/shard_map/ppermute | solution.py:280
  55.6 4.2 %collective-permute-start.16 = (bf16[512,512]{1,0:T(8,128)(2,1)}, bf16[512,512]{1,0:T(8,128)(2,1)S(1)}, u32[]{:S(2)}, u32[]{:S(2)}) collective-permute-start(bf16[512,512]{1,0:T(8,128)(2,1)} %get-tuple-element.41), channel_id=1, source_target_pairs={{0,1},{1,0},{2,3},{3,2},{4,5},{5,4},{6,7},{7,6},{8,9},{9,8},{10,11... | collective-permute-start | bytes 1572872 | tf_op jit(solution)/shard_map/ppermute | solution.py:280
  56.1 7.8 %collective-permute-start.26 = (bf16[2,128,768]{2,1,0:T(8,128)(2,1)S(1)}, bf16[2,128,768]{2,1,0:T(8,128)(2,1)S(1)}, u32[]{:S(2)}, u32[]{:S(2)}) collective-permute-start(bf16[2,128,768]{2,1,0:T(8,128)(2,1)S(1)} %pack.9.own_ref.refs_4_), channel_id=1, source_target_pairs={{0,4},{1,3},{2,6},{3,1},{4,0},{5,7},{6,2},{7,5},{8,12},{9,11},{10,... | collective-permute-start | bytes 1179656 | tf_op jit(solution)/shard_map/ppermute | solution.py:280
  57.7 10.4 %collective-permute-start.27 = (bf16[2,128,768]{2,1,0:T(8,128)(2,1)}, bf16[2,128,768]{2,1,0:T(8,128)(2,1)S(1)}, u32[]{:S(2)}, u32[]{:S(2)}) collective-permute-start(bf16[2,128,768]{2,1,0:T(8,128)(2,1)} %collective-permute-done.25.moved_ref.refs_5_), channel_id=1, source_target_pairs={{0,4},{1,3},{2,6},{3,1},{4,0},{5,7},{6,2},{7,5},{8,12},{9,11},{10,... | collective-permute-start | bytes 1179656 | tf_op jit(solution)/shard_map/ppermute | solution.py:280
  58.5 1.2 %copy-start.1 = (bf16[2,128,512]{2,1,0:T(8,128)(2,1)S(1)}, bf16[2,128,512]{2,1,0:T(8,128)(2,1)}, u32[]{:S(2)}) copy-start(bf16[2,128,512]{2,1,0:T(8,128)(2,1)} %copy-done) | copy-start | bytes 786436
  58.5 1.2 %copy-start.3 = (bf16[2,128,512]{2,1,0:T(8,128)(2,1)S(1)}, bf16[2,128,512]{2,1,0:T(8,128)(2,1)}, u32[]{:S(2)}) copy-start(bf16[2,128,512]{2,1,0:T(8,128)(2,1)} %copy-done.2) | copy-start | bytes 786436
  58.5 1.3 %copy-start.5 = (bf16[2,128,512]{2,1,0:T(8,128)(2,1)S(1)}, bf16[2,128,512]{2,1,0:T(8,128)(2,1)}, u32[]{:S(2)}) copy-start(bf16[2,128,512]{2,1,0:T(8,128)(2,1)} %copy-done.4) | copy-start | bytes 786436
  59.7 11.2 %collective-permute-start.28 = (bf16[4,128,768]{2,1,0:T(8,128)(2,1)S(1)}, bf16[4,128,768]{2,1,0:T(8,128)(2,1)S(1)}, u32[]{:S(2)}, u32[]{:S(2)}) collective-permute-start(bf16[4,128,768]{2,1,0:T(8,128)(2,1)S(1)} %pack.10), channel_id=1, source_target_pairs={{0,1},{1,0},{2,3},{3,2},{4,5},{5,4},{6,7},{7,6},{8,9},{9,8},{10,11... | collective-permute-start | bytes 2359304 | tf_op jit(solution)/shard_map/ppermute | solution.py:280
  68.2 2.7 %collective-permute-start.29 = (bf16[4,128,768]{2,1,0:T(8,128)(2,1)S(1)}, bf16[4,128,768]{2,1,0:T(8,128)(2,1)S(1)}, u32[]{:S(2)}, u32[]{:S(2)}) collective-permute-start(bf16[4,128,768]{2,1,0:T(8,128)(2,1)S(1)} %pack.11), channel_id=1, source_target_pairs={{0,1},{1,0},{2,3},{3,2},{4,5},{5,4},{6,7},{7,6},{8,9},{9,8},{10,11... | collective-permute-start | bytes 2359304 | tf_op jit(solution)/shard_map/ppermute | solution.py:280
  68.2 24.1 %collective-permute-start.23 = (bf16[256,512]{1,0:T(8,128)(2,1)S(1)}, bf16[256,512]{1,0:T(8,128)(2,1)S(1)}, u32[]{:S(2)}, u32[]{:S(2)}) collective-permute-start(bf16[256,512]{1,0:T(8,128)(2,1)S(1)} %fold.5.refs_0_), channel_id=1, source_target_pairs={{0,16},{1,17},{2,18},{3,19},{4,20},{5,21},{6,22},{7,23},{8,24},{9,... | collective-permute-start | bytes 786440 | tf_op jit(solution)/shard_map/ppermute | solution.py:280
  72.9 27.4 %collective-permute-start.30 = (bf16[256,768]{1,0:T(8,128)(2,1)S(1)}, bf16[256,768]{1,0:T(8,128)(2,1)S(1)}, u32[]{:S(2)}, u32[]{:S(2)}) collective-permute-start(bf16[256,768]{1,0:T(8,128)(2,1)S(1)} %fold.7), channel_id=1, source_target_pairs={{0,16},{1,17},{2,18},{3,19},{4,20},{5,21},{6,22},{7,23},{8,24},{9,... | collective-permute-start | bytes 1179656 | tf_op jit(solution)/shard_map/ppermute | solution.py:280

commit v4 on v3

--- a/solution.py
+++ b/solution.py
@@ -123,26 +123,30 @@
 def spread_kernel(place_ref, x_ref, *outs, dp, part):
     z, c = place_ref[0], place_ref[1]
     first = 2 + 2 * (c % 2)
-    for far in range(2):
-        for at, flip in enumerate((0, first, 6 - first, 6)):
-            out = outs[at] if not far else outs[5] if at == 3 else outs[4].at[at]
-            for other in range(2):
-                for high in range(2):
-                    plane = (2 * high + z % 2) ^ far
+    for home in range(2):
+        for far in range(2):
+            for at, flip in enumerate((0, first, 6 - first, 6)):
+                if home:
+                    out = outs[9].at[at] if far else outs[5 + at]
+                else:
+                    out = outs[4].at[at] if far else outs[at]
+                plane = z ^ far ^ (2 - 2 * home)
+                for other in range(2):
                     src = pl.multiple_of(((c ^ flip ^ other) * dp + plane) * part, part)
-                    out[other, :, high * part : (high + 1) * part] = x_ref[:, pl.ds(src, part)]
+                    out[other] = x_ref[:, pl.ds(src, part)]
 
 
 def spread(place, x, ctx, dp):
     rows, width = x.shape
     part = width // (ctx * dp)
-    piece = (2, rows, 2 * part)
+    piece = (2, rows, part)
     vmem = pl.BlockSpec(memory_space=pltpu.VMEM)
+    shapes = ([piece] * 4 + [(4,) + piece]) * 2
     return pl.pallas_call(
         functools.partial(spread_kernel, dp=dp, part=part),
-        out_shape=[jax.ShapeDtypeStruct(p, BF16) for p in [piece] * 4 + [(3,) + piece, piece]],
+        out_shape=[jax.ShapeDtypeStruct(p, BF16) for p in shapes],
         in_specs=[pl.BlockSpec(memory_space=pltpu.SMEM), vmem],
-        out_specs=[vmem] * 6,
+        out_specs=[vmem] * len(shapes),
         compiler_params=pltpu.CompilerParams(vmem_limit_bytes=VMEM_LIMIT),
         cost_estimate=pl.CostEstimate(flops=0, bytes_accessed=4 * x.size, transcendentals=0),
         name="spread",
@@ -161,7 +165,7 @@
         compiler_params=pltpu.CompilerParams(vmem_limit_bytes=VMEM_LIMIT),
         cost_estimate=pl.CostEstimate(
             flops=flops,
-            bytes_accessed=sum(2 * a.size for a in args) + sum(2 * o.size for o in out_shape),
+            bytes_accessed=0,
             transcendentals=0,
         ),
         name=name,
@@ -177,10 +181,10 @@
             outs[core][:, at * rows : (at + 1) * rows] = piece[core].T
 
 
-def turn(pieces):
+def turn(pieces, gates=()):
     _, rows, width = pieces[1].shape
     turned = jax.ShapeDtypeStruct((width, 4 * rows), BF16)
-    return local_call(turn_kernel, "turn", (turned, turned), pieces)
+    return local_call(turn_kernel, "turn", (turned, turned), pieces, gates)
 
 
 def pack_kernel(own_ref, moved_ref, *refs):
@@ -194,13 +198,15 @@
     return local_call(pack_kernel, "pack", (out,), [own, moved], gates)[0]
 
 
-def hold_kernel(own_ref, *refs):
-    refs[-1][...] = own_ref[...]
+def hold_kernel(*refs, count):
+    for own, out in zip(refs[:count], refs[-count:]):
+        out[...] = own[...]
 
 
 def hold(own, gates):
-    out = jax.ShapeDtypeStruct(own.shape, own.dtype)
-    return local_call(hold_kernel, "hold", (out,), [own], gates)[0]
+    outs = [jax.ShapeDtypeStruct(a.shape, a.dtype) for a in own]
+    kernel = functools.partial(hold_kernel, count=len(own))
+    return local_call(kernel, "hold", outs, own, gates)
 
 
 def merge_kernel(held_ref, *refs):
@@ -238,33 +244,35 @@
     return local_call(settle_kernel, "settle", outs, [gq, held, *moved])
 
 
-def fold_kernel(side_ref, *refs):
-    turned, cols, out = refs[:4], refs[4:10], refs[-1]
+def fold_kernel(*refs, outs, joined):
+    turned, cols, outs = refs[:4], refs[4:10], refs[-outs:]
+    lead = refs[10] if joined else None
     rows = cols[0].shape[1]
     pairs = [(col, at) for col in cols for at in range(0, col.shape[0], 2)]
-    half, n = out.shape
-    at = pl.multiple_of(side_ref[0] * half, half)
     total = None
     for core in range(2):
         for chip in range(4):
             span = slice(chip * rows, (chip + 1) * rows)
-            left = jnp.concatenate(
-                [t[pl.ds(at, half), span] for t in turned[2 * core : 2 * core + 2]], axis=1
-            )
+            left = jnp.concatenate([t[:, span] for t in turned[2 * core : 2 * core + 2]], axis=1)
             col, pair = pairs[4 * core + chip]
-            term = dot(left, col[pair : pair + 2].reshape(2 * rows, n), 1, 0)
+            term = dot(left, col[pair : pair + 2].reshape(2 * rows, col.shape[2]), 1, 0)
             total = term if total is None else total + term
-    out[...] = total.astype(out.dtype)
-
-
-def fold(side, turned, cols, dtype, gates=()):
-    half = turned[0].shape[0] // 2
-    depth = 4 * turned[0].shape[1]
-    n = cols[0].shape[2]
-    out = jax.ShapeDtypeStruct((half, n), dtype)
-    args = [side, *turned, *cols]
-    flops = 2 * half * depth * n
-    return local_call(fold_kernel, "fold", (out,), args, gates, smem=1, flops=flops)[0]
+    total = total.astype(outs[0].dtype)
+    if joined:
+        total = jnp.concatenate([lead[...], total], axis=1)
+    start = 0
+    for out in outs:
+        out[...] = total[:, start : start + out.shape[1]]
+        start += out.shape[1]
+
+
+def fold(turned, cols, dtype, cuts=(), joined=()):
+    half, depth = turned[0].shape
+    n = cols[0].shape[2] + sum(j.shape[1] for j in joined)
+    edges = [0, *cuts, n]
+    outs = [jax.ShapeDtypeStruct((half, b - a), dtype) for a, b in zip(edges, edges[1:])]
+    kernel = functools.partial(fold_kernel, outs=len(outs), joined=bool(joined))
+    return local_call(kernel, "fold", outs, [*turned, *cols, *joined])
 
 
 def fold_rows(features, piece_rows):
@@ -296,29 +304,34 @@
 def shards_cube(normed_input, queries, keys_values, grad_output, doc_lengths):
     ctx, dp = lax.axis_size("ctx"), lax.axis_size("dp")
     own, z = lax.axis_index("ctx"), lax.axis_index("dp")
-    side = (z // 2)[None]
-    *pieces, across, corner = spread(jnp.stack([z, own]), normed_input[0], ctx, dp)
+    pieces = spread(jnp.stack([z, own]), normed_input[0], ctx, dp)
     grad_query, lead, held, *send = attention(
         own[None], doc_lengths, queries[0], grad_output[0], keys_values[0], cube=True
     )
     chips = (FIRST, SECOND, DIAGONAL)
-    near, near_sib = turn(pieces[:1] + [hop(p, 0, c) for p, c in zip(pieces[1:], chips)])
-    across = hop(across, 1, STAY)
-    corner = hop(hold(corner, [lead]), 1, DIAGONAL)
-    far, far_sib = turn([across, hop(across[1], 0, FIRST), hop(across[2], 0, SECOND), corner])
-    turned = [near, far, hop(near_sib, 0, SIBLING), hop(far_sib, 0, SIBLING)]
+    near, near_sib = turn([pieces[0]] + [hop(p, 0, c) for p, c in zip(pieces[1:4], chips)])
+    across = hop(pieces[4], 1, STAY)
+    far, far_sib = turn([across] + [hop(across[i + 1], 0, c) for i, c in enumerate(chips)])
+    away = [near, far, hop(near_sib, 0, SIBLING), hop(far_sib, 0, SIBLING)]
     first_cols = gather_pairs(lead, [near])
+    beyond = hop(hold([pieces[9]], [first_cols[0]])[0], 1, STAY)
     held, send = merge(held, [hop(t, 0, c) for t, c in zip(send, chips)])
     rest, grad_kv = settle(grad_query, lead, held, [hop(send, 0, SIBLING)])
-    first_fold = fold(1 - side, turned, first_cols, BF16)
-    rest_cols = gather_pairs(rest, [far], [first_fold])
-    first_sent = hop(first_fold, 2, STAY)
-    rest_sent = hop(fold(1 - side, turned, rest_cols, BF16), 2, STAY)
-    totals = [
-        fold(side, turned, cols, F32) + sent.astype(F32)
-        for cols, sent in ((first_cols, first_sent), (rest_cols, rest_sent))
-    ]
-    return grad_query[None], grad_kv[None], jnp.concatenate(totals, axis=1)
+    first_folds = fold(away, first_cols, BF16, cuts=[256])
+    sent = [hop(first_folds[0], 2, STAY)]
+    rest_cols = gather_pairs(rest, [far,beyond], [sent[0]])
+    (rest_fold,) = fold(away, rest_cols, BF16, joined=first_folds[1:])
+    sent.append(hop(rest_fold, 2, STAY))
+    home_near, home_near_sib = turn(
+        [pieces[5]] + [hop(p, 0, c) for p, c in zip(pieces[6:9], chips)]
+    )
+    home_far, home_far_sib = turn(
+        [beyond] + [hop(beyond[i + 1], 0, c) for i, c in enumerate(chips)]
+    )
+    home = [home_near, home_far, hop(home_near_sib, 0, SIBLING), hop(home_far_sib, 0, SIBLING)]
+    folds = [fold(home, cols, F32)[0] for cols in (first_cols, rest_cols)]
+    total = jnp.concatenate(folds, axis=1) + jnp.concatenate(sent, axis=1).astype(F32)
+    return grad_query[None], grad_kv[None], total
 
 
 def shards(normed_input, queries, keys_values, grad_output, doc_lengths):

time: 102 us -> 96.5 us (0.946)
  starting transfers between devices: 31.9 us -> 40.7 us
  Pallas kernels: 18.5 us -> 10.7 us
  waiting for transfers between devices: 47.2 us -> 41.2 us
    ppermute x27 -> x36, starting transfers between devices: 27.5 us -> 36.3 us  [hop(): return lax.ppermute(value, ('dp', 'ctx'), pairs)]
    pallas_call x15 -> x17, Pallas kernels: 12.9 us -> 5.07 us  [local_call(): pl.pallas_call(kernel, out_shape=out_shape, in_specs=specs, out_specs=jax...]
    ppermute x27 -> x36, waiting for transfers between devices: 46 us -> 39.9 us  [hop(): return lax.ppermute(value, ('dp', 'ctx'), pairs)]
    concatenate x1 -> x0, other arithmetic: 1.14 us -> none  [shards_cube(): return (grad_query[None], grad_kv[None], jnp.concatenate(totals, axis=1))]
    add x2 -> x1, other arithmetic: 0.13 us -> 1.21 us  [shards_cube(): jnp.concatenate(folds, axis=1) + jnp.concatenate(sent, axis=1).astype(F32)]
  transfers between devices with their start and end apart: 31 -> 40, of which waited for: 13 -> 19; matrix products, arithmetic and copies ran while one was open for 0% -> 0% of each run, Pallas kernels for 17% -> 10%
where the time goes in v4:
time: 96.5 us; the launch traced here: 96.4 us
  waiting for transfers between devices  41.2 us (43%)
  starting transfers between devices  40.7 us (42%)
  Pallas kernels  10.7 us (11%)
  local copies, waits for them, and re-layouts  1.67 us (2%)
  other arithmetic  1.29 us (1%)
    ppermute x36, waiting for transfers between devices, hop(): return lax.ppermute(value, ('dp', 'ctx'), pairs)  39.9 us
    ppermute x36, starting transfers between devices, hop(): return lax.ppermute(value, ('dp', 'ctx'), pairs)  36.3 us
    pallas_call x17, Pallas kernels, local_call(): pl.pallas_call(kernel, out_shape=out_shape, in_specs=specs, out_specs=jax...  5.07 us
    pallas_call x1, Pallas kernels, attention(): pl.pallas_call(functools.partial(attention_kernel, span=span, head=head,...  4.77 us
    ppermute x4, starting transfers between devices, shift(): return lax.ppermute(value, 'ctx', [(i, (i + by) % ctx) for i in range(ctx)])  4.42 us
  transfers between devices with their start and end apart: 40, of which 19 were waited for; matrix products, arithmetic and copies ran while one was open for 0% of the time, Pallas kernels for 10%

profile of v4, /device:TPU:0, one launch (start us, length us, event | category | flops | bytes accessed | tf_op | source)
XLA Modules:
  0.0 96.4 jit_solution(8512662949029158200)
XLA Ops:
  0.7 1.6 %copy-done = bf16[1,128,8192]{2,1,0:T(8,128)(2,1)S(1)} copy-done((bf16[1,128,8192]{2,1,0:T(8,128)(2,1)S(1)}, bf16[1,128,8192]{2,1,0:T(8,128)(2,1)}, u32[]{:S(2)}) %copy-start) | copy-done | bytes 2097176
  2.3 0.8 spread.1
  3.2 3.1 %collective-permute-start.27 = (bf16[4,2,128,256]{3,2,1,0:T(8,128)(2,1)S(1)}, bf16[4,2,128,256]{3,2,1,0:T(8,128)(2,1)S(1)}, u32[]{:S(2)}, u32[]{:S(2)}) collective-permute-start(bf16[4,2,128,256]{3,2,1,0:T(8,128)(2,1)S(1)} %get-tuple-element.57), channel_id=1, source_target_pairs={{0,8},{1,9},{2,10},{3,11},{4,12},{5,13},{6,14},{7,15},{8,0},{9,1},... | collective-permute-start | bytes 1572872 | tf_op jit(solution)/shard_map/ppermute | solution.py:288
  6.3 1.5 %collective-permute-start.2 = (bf16[128,256]{1,0:T(8,128)(2,1)S(1)}, bf16[128,256]{1,0:T(8,128)(2,1)S(1)}, u32[]{:S(2)}, u32[]{:S(2)}) collective-permute-start(bf16[128,256]{1,0:T(8,128)(2,1)S(1)} %bitcast.33), channel_id=1, source_target_pairs={{0,2},{1,3},{2,4},{3,5},{4,6},{5,7},{6,0},{7,1},{8,10},{9,11},{10,... | collective-permute-start | bytes 196616 | tf_op jit(solution)/shard_map/ppermute | solution.py:86
  7.8 2.4 %collective-permute-start.1 = (bf16[128,256]{1,0:T(8,128)(2,1)S(1)}, bf16[128,256]{1,0:T(8,128)(2,1)S(1)}, u32[]{:S(2)}, u32[]{:S(2)}) collective-permute-start(bf16[128,256]{1,0:T(8,128)(2,1)S(1)} %bitcast.34), channel_id=1, source_target_pairs={{0,3},{1,4},{2,5},{3,6},{4,7},{5,0},{6,1},{7,2},{8,11},{9,12},{10,... | collective-permute-start | bytes 196616 | tf_op jit(solution)/shard_map/ppermute | solution.py:86
  10.2 0.5 collective-permute-start
  11.0 1.2 %collective-permute-start.12 = (bf16[2,128,256]{2,1,0:T(8,128)(2,1)S(1)}, bf16[2,128,256]{2,1,0:T(8,128)(2,1)S(1)}, u32[]{:S(2)}, u32[]{:S(2)}) collective-permute-start(bf16[2,128,256]{2,1,0:T(8,128)(2,1)S(1)} %get-tuple-element.49), channel_id=1, source_target_pairs={{0,2},{1,5},{2,0},{3,7},{4,6},{5,1},{6,4},{7,3},{8,10},{9,13},{10,... | collective-permute-start | bytes 393224 | tf_op jit(solution)/shard_map/ppermute | solution.py:288
  12.2 1.2 %collective-permute-start.13 = (bf16[2,128,256]{2,1,0:T(8,128)(2,1)S(1)}, bf16[2,128,256]{2,1,0:T(8,128)(2,1)S(1)}, u32[]{:S(2)}, u32[]{:S(2)}) collective-permute-start(bf16[2,128,256]{2,1,0:T(8,128)(2,1)S(1)} %get-tuple-element.50), channel_id=1, source_target_pairs={{0,4},{1,3},{2,6},{3,1},{4,0},{5,7},{6,2},{7,5},{8,12},{9,11},{10,... | collective-permute-start | bytes 393224 | tf_op jit(solution)/shard_map/ppermute | solution.py:288
  13.4 1.1 %collective-permute-start.14 = (bf16[2,128,256]{2,1,0:T(8,128)(2,1)S(1)}, bf16[2,128,256]{2,1,0:T(8,128)(2,1)S(1)}, u32[]{:S(2)}, u32[]{:S(2)}) collective-permute-start(bf16[2,128,256]{2,1,0:T(8,128)(2,1)S(1)} %get-tuple-element.51), channel_id=1, source_target_pairs={{0,6},{1,7},{2,4},{3,5},{4,2},{5,3},{6,0},{7,1},{8,14},{9,15},{10,... | collective-permute-start | bytes 393224 | tf_op jit(solution)/shard_map/ppermute | solution.py:288
  14.5 0.9 collective-permute-done.refs_0_
  15.4 4.8 %attention.1 = (bf16[128,1024]{1,0:T(8,128)(2,1)}, bf16[128,512]{1,0:T(8,128)(2,1)S(1)}, f32[2,128,256]{2,1,0:T(8,128)S(1)}, bf16[2,128,256]{2,1,0:T(8,128)(2,1)...) custom-call(s32[1]{0:T(128)} %bitcast.own_ref, s32[1,3]{1,0:T(1,128)S(1)} %copy-done.5, ...), custom_call_target="tpu_custom_call" | custom-call | flops 1006632960 | bytes 1441792 | tf_op jit(solution)/shard_map/attention/pallas_call | solution.py:102
  20.6 1.9 %collective-permute-start.4 = (bf16[2,128,256]{2,1,0:T(8,128)(2,1)S(1)}, bf16[2,128,256]{2,1,0:T(8,128)(2,1)S(1)}, u32[]{:S(2)}, u32[]{:S(2)}) collective-permute-start(bf16[2,128,256]{2,1,0:T(8,128)(2,1)S(1)} %get-tuple-element.35), channel_id=1, source_target_pairs={{0,2},{1,5},{2,0},{3,7},{4,6},{5,1},{6,4},{7,3},{8,10},{9,13},{10,... | collective-permute-start | bytes 393224 | tf_op jit(solution)/shard_map/ppermute | solution.py:288
  22.5 1.6 %collective-permute-start.6 = (bf16[2,128,256]{2,1,0:T(8,128)(2,1)S(1)}, bf16[2,128,256]{2,1,0:T(8,128)(2,1)S(1)}, u32[]{:S(2)}, u32[]{:S(2)}) collective-permute-start(bf16[2,128,256]{2,1,0:T(8,128)(2,1)S(1)} %get-tuple-element.37), channel_id=1, source_target_pairs={{0,6},{1,7},{2,4},{3,5},{4,2},{5,3},{6,0},{7,1},{8,14},{9,15},{10,... | collective-permute-start | bytes 393224 | tf_op jit(solution)/shard_map/ppermute | solution.py:288
  24.3 0.8 collective-permute-done.11
  25.2 0.8 collective-permute-start.15
  26.1 0.9 collective-permute-done.4.refs_0_
  27.0 1.5 %collective-permute-start.21 = (bf16[2,128,512]{2,1,0:T(8,128)(2,1)S(1)}, bf16[2,128,512]{2,1,0:T(8,128)(2,1)S(1)}, u32[]{:S(2)}, u32[]{:S(2)}) collective-permute-start(bf16[2,128,512]{2,1,0:T(8,128)(2,1)S(1)} %pack.6.refs_1_.own_ref.refs_4_), channel_id=1, source_target_pairs={{0,2},{1,5},{2,0},{3,7},{4,6},{5,1},{6,4},{7,3},{8,10},{9,13},{10,... | collective-permute-start | bytes 786440 | tf_op jit(solution)/shard_map/ppermute | solution.py:288
  28.5 2.5 %collective-permute-done.5.refs_1_ = bf16[2,128,256]{2,1,0:T(8,128)(2,1)S(1)} collective-permute-done((bf16[2,128,256]{2,1,0:T(8,128)(2,1)S(1)}, bf16[2,128,256]{2,1,0:T(8,128)(2,1)S(1)}, u32[]{:S(2)}, u32[]{:S(2)}) %collective-permute-start.5) | collective-permute-done | bytes 131104 | tf_op jit(solution)/shard_map/ppermute | solution.py:288
  31.3 1.4 %collective-permute-start.29 = (bf16[2,128,256]{2,1,0:T(8,128)(2,1)S(1)}, bf16[2,128,256]{2,1,0:T(8,128)(2,1)S(1)}, u32[]{:S(2)}, u32[]{:S(2)}) collective-permute-start(bf16[2,128,256]{2,1,0:T(8,128)(2,1)S(1)} %get-tuple-element.64), channel_id=1, source_target_pairs={{0,4},{1,3},{2,6},{3,1},{4,0},{5,7},{6,2},{7,5},{8,12},{9,11},{10,... | collective-permute-start | bytes 393224 | tf_op jit(solution)/shard_map/ppermute | solution.py:288
  32.7 0.7 settle.1
  33.3 1.6 %collective-permute-start.26 = (bf16[128,768]{1,0:T(8,128)(2,1)S(1)}, bf16[128,768]{1,0:T(8,128)(2,1)S(1)}, u32[]{:S(2)}, u32[]{:S(2)}) collective-permute-start(bf16[128,768]{1,0:T(8,128)(2,1)S(1)} %get-tuple-element.56), channel_id=1, source_target_pairs={{0,8},{1,9},{2,10},{3,11},{4,12},{5,13},{6,14},{7,15},{8,0},{9,1},... | collective-permute-start | bytes 589832 | tf_op jit(solution)/shard_map/ppermute | solution.py:288
  34.9 2.1 %collective-permute-start.28 = (bf16[2,128,256]{2,1,0:T(8,128)(2,1)S(1)}, bf16[2,128,256]{2,1,0:T(8,128)(2,1)S(1)}, u32[]{:S(2)}, u32[]{:S(2)}) collective-permute-start(bf16[2,128,256]{2,1,0:T(8,128)(2,1)S(1)} %get-tuple-element.65), channel_id=1, source_target_pairs={{0,2},{1,5},{2,0},{3,7},{4,6},{5,1},{6,4},{7,3},{8,10},{9,13},{10,... | collective-permute-start | bytes 393224 | tf_op jit(solution)/shard_map/ppermute | solution.py:288
  37.0 1.5 %collective-permute-done.30.refs_3_ = bf16[2,128,256]{2,1,0:T(8,128)(2,1)S(1)} collective-permute-done((bf16[2,128,256]{2,1,0:T(8,128)(2,1)S(1)}, bf16[2,128,256]{2,1,0:T(8,128)(2,1)S(1)}, u32[]{:S(2)}, u32[]{:S(2)}) %collective-permute-start.30) | collective-permute-done | bytes 131104 | tf_op jit(solution)/shard_map/ppermute | solution.py:288
  38.6 1.4 %collective-permute-done.29.refs_2_ = bf16[2,128,256]{2,1,0:T(8,128)(2,1)S(1)} collective-permute-done((bf16[2,128,256]{2,1,0:T(8,128)(2,1)S(1)}, bf16[2,128,256]{2,1,0:T(8,128)(2,1)S(1)}, u32[]{:S(2)}, u32[]{:S(2)}) %collective-permute-start.29) | collective-permute-done | bytes 131104 | tf_op jit(solution)/shard_map/ppermute | solution.py:288
  40.0 0.5 collective-permute-start.23
  40.9 0.7 collective-permute-done.26
  41.6 1.9 %collective-permute-start.31 = (bf16[2,128,768]{2,1,0:T(8,128)(2,1)S(1)}, bf16[2,128,768]{2,1,0:T(8,128)(2,1)S(1)}, u32[]{:S(2)}, u32[]{:S(2)}) collective-permute-start(bf16[2,128,768]{2,1,0:T(8,128)(2,1)S(1)} %pack.9.own_ref.refs_4_), channel_id=1, source_target_pairs={{0,2},{1,5},{2,0},{3,7},{4,6},{5,1},{6,4},{7,3},{8,10},{9,13},{10,... | collective-permute-start | bytes 1179656 | tf_op jit(solution)/shard_map/ppermute | solution.py:288
  43.7 1.1 %collective-permute-done.22.own_ref.refs_6_ = bf16[2,128,512]{2,1,0:T(8,128)(2,1)S(1)} collective-permute-done((bf16[2,128,512]{2,1,0:T(8,128)(2,1)S(1)}, bf16[2,128,512]{2,1,0:T(8,128)(2,1)S(1)}, u32[]{:S(2)}, u32[]{:S(2)}) %collective-permute-start.22) | collective-permute-done | bytes 262176 | tf_op jit(solution)/shard_map/ppermute | solution.py:288
  44.9 5.6 %collective-permute-done.23.moved_ref.refs_7_ = bf16[2,128,512]{2,1,0:T(8,128)(2,1)S(1)} collective-permute-done((bf16[2,128,512]{2,1,0:T(8,128)(2,1)S(1)}, bf16[2,128,512]{2,1,0:T(8,128)(2,1)S(1)}, u32[]{:S(2)}, u32[]{:S(2)}) %collective-permute-start.23) | collective-permute-done | bytes 262176 | tf_op jit(solution)/shard_map/ppermute | solution.py:288
  51.2 1.7 %collective-permute-done.35.refs_2_ = bf16[256,512]{1,0:T(8,128)(2,1)S(1)} collective-permute-done((bf16[256,512]{1,0:T(8,128)(2,1)S(1)}, bf16[256,512]{1,0:T(8,128)(2,1)S(1)}, u32[]{:S(2)}, u32[]{:S(2)}) %collective-permute-start.35) | collective-permute-done | bytes 262176 | tf_op jit(solution)/shard_map/ppermute | solution.py:288
  52.9 2.0 %collective-permute-start.33 = (bf16[2,128,768]{2,1,0:T(8,128)(2,1)S(1)}, bf16[2,128,768]{2,1,0:T(8,128)(2,1)S(1)}, u32[]{:S(2)}, u32[]{:S(2)}) collective-permute-start(bf16[2,128,768]{2,1,0:T(8,128)(2,1)S(1)} %collective-permute-done.31.moved_ref.refs_5_), channel_id=1, source_target_pairs={{0,4},{1,3},{2,6},{3,1},{4,0},{5,7},{6,2},{7,5},{8,12},{9,11},{10,... | collective-permute-start | bytes 1179656 | tf_op jit(solution)/shard_map/ppermute | solution.py:288
  54.9 0.7 fold.5
  55.6 2.7 %collective-permute-start.37 = (bf16[256,256]{1,0:T(8,128)(2,1)S(1)}, bf16[256,256]{1,0:T(8,128)(2,1)S(1)}, u32[]{:S(2)}, u32[]{:S(2)}) collective-permute-start(bf16[256,256]{1,0:T(8,128)(2,1)S(1)} %get-tuple-element.61), channel_id=1, source_target_pairs={{0,16},{1,17},{2,18},{3,19},{4,20},{5,21},{6,22},{7,23},{8,24},{9,... | collective-permute-start | bytes 393224 | tf_op jit(solution)/shard_map/ppermute | solution.py:288
  58.5 2.2 %collective-permute-done.32.own_ref.refs_6_ = bf16[2,128,768]{2,1,0:T(8,128)(2,1)S(1)} collective-permute-done((bf16[2,128,768]{2,1,0:T(8,128)(2,1)S(1)}, bf16[2,128,768]{2,1,0:T(8,128)(2,1)S(1)}, u32[]{:S(2)}, u32[]{:S(2)}) %collective-permute-start.32) | collective-permute-done | bytes 393248 | tf_op jit(solution)/shard_map/ppermute | solution.py:288
  60.6 3.7 %collective-permute-done.37.refs_0_ = bf16[256,256]{1,0:T(8,128)(2,1)S(1)} collective-permute-done((bf16[256,256]{1,0:T(8,128)(2,1)S(1)}, bf16[256,256]{1,0:T(8,128)(2,1)S(1)}, u32[]{:S(2)}, u32[]{:S(2)}) %collective-permute-start.37) | collective-permute-done | bytes 131104 | tf_op jit(solution)/shard_map/ppermute | solution.py:288
  65.0 0.8 collective-permute-start.8
  65.9 2.6 %collective-permute-start.10 = (bf16[2,128,256]{2,1,0:T(8,128)(2,1)S(1)}, bf16[2,128,256]{2,1,0:T(8,128)(2,1)S(1)}, u32[]{:S(2)}, u32[]{:S(2)}) collective-permute-start(bf16[2,128,256]{2,1,0:T(8,128)(2,1)S(1)} %get-tuple-element.44), channel_id=1, source_target_pairs={{0,6},{1,7},{2,4},{3,5},{4,2},{5,3},{6,0},{7,1},{8,14},{9,15},{10,... | collective-permute-start | bytes 393224 | tf_op jit(solution)/shard_map/ppermute | solution.py:288
  68.5 1.0 %fold.7 = bf16[256,1024]{1,0:T(8,128)(2,1)S(1)} custom-call(bf16[256,512]{1,0:T(8,128)(2,1)S(1)} %get-tuple-element.52.refs_0_, bf16[256,512]{1,0:T(8,128)(2,1)S(1)} %get-tuple-element.58.refs_0_.refs_1_, bf16[256,512]{1,0:T(8,128)(2,1)S(1)} %collective-permute-done.35.refs_2_, bf16[256,512]{1,0:T(8,128)(2,1)S(1)} %collective-permute-done.36.refs_3_, ...), custom_call_target="tpu_custom_call" | custom-call | tf_op jit(solution)/shard_map/fold/pallas_call | solution.py:160
  69.5 2.7 %collective-permute-start.39 = (bf16[256,1024]{1,0:T(8,128)(2,1)S(1)}, bf16[256,1024]{1,0:T(8,128)(2,1)S(1)}, u32[]{:S(2)}, u32[]{:S(2)}) collective-permute-start(bf16[256,1024]{1,0:T(8,128)(2,1)S(1)} %fold.7), channel_id=1, source_target_pairs={{0,16},{1,17},{2,18},{3,19},{4,20},{5,21},{6,22},{7,23},{8,24},{9,... | collective-permute-start | bytes 1572872 | tf_op jit(solution)/shard_map/ppermute | solution.py:288
  72.6 1.9 %collective-permute-start.17 = (bf16[2,128,256]{2,1,0:T(8,128)(2,1)S(1)}, bf16[2,128,256]{2,1,0:T(8,128)(2,1)S(1)}, u32[]{:S(2)}, u32[]{:S(2)}) collective-permute-start(bf16[2,128,256]{2,1,0:T(8,128)(2,1)S(1)} %get-tuple-element.67), channel_id=1, source_target_pairs={{0,4},{1,3},{2,6},{3,1},{4,0},{5,7},{6,2},{7,5},{8,12},{9,11},{10,... | collective-permute-start | bytes 393224 | tf_op jit(solution)/shard_map/ppermute | solution.py:288
  74.5 1.3 %collective-permute-start.16 = (bf16[2,128,256]{2,1,0:T(8,128)(2,1)S(1)}, bf16[2,128,256]{2,1,0:T(8,128)(2,1)S(1)}, u32[]{:S(2)}, u32[]{:S(2)}) collective-permute-start(bf16[2,128,256]{2,1,0:T(8,128)(2,1)S(1)} %get-tuple-element.68), channel_id=1, source_target_pairs={{0,2},{1,5},{2,0},{3,7},{4,6},{5,1},{6,4},{7,3},{8,10},{9,13},{10,... | collective-permute-start | bytes 393224 | tf_op jit(solution)/shard_map/ppermute | solution.py:288
  76.1 3.3 %collective-permute-done.18.refs_3_ = bf16[2,128,256]{2,1,0:T(8,128)(2,1)S(1)} collective-permute-done((bf16[2,128,256]{2,1,0:T(8,128)(2,1)S(1)}, bf16[2,128,256]{2,1,0:T(8,128)(2,1)S(1)}, u32[]{:S(2)}, u32[]{:S(2)}) %collective-permute-start.18) | collective-permute-done | bytes 131104 | tf_op jit(solution)/shard_map/ppermute | solution.py:288
  79.4 1.4 %collective-permute-done.17.refs_2_ = bf16[2,128,256]{2,1,0:T(8,128)(2,1)S(1)} collective-permute-done((bf16[2,128,256]{2,1,0:T(8,128)(2,1)S(1)}, bf16[2,128,256]{2,1,0:T(8,128)(2,1)S(1)}, u32[]{:S(2)}, u32[]{:S(2)}) %collective-permute-start.17) | collective-permute-done | bytes 131104 | tf_op jit(solution)/shard_map/ppermute | solution.py:288
  81.1 1.5 %collective-permute-done.20.refs_3_ = bf16[256,512]{1,0:T(8,128)(2,1)S(1)} collective-permute-done((bf16[256,512]{1,0:T(8,128)(2,1)S(1)}, bf16[256,512]{1,0:T(8,128)(2,1)S(1)}, u32[]{:S(2)}, u32[]{:S(2)}) %collective-permute-start.20) | collective-permute-done | bytes 262176 | tf_op jit(solution)/shard_map/ppermute | solution.py:288
  82.6 0.7 fold.4
  83.3 1.0 %fold.6 = f32[256,768]{1,0:T(8,128)S(1)} custom-call(bf16[256,512]{1,0:T(8,128)(2,1)S(1)} %get-tuple-element.45.refs_0_, bf16[256,512]{1,0:T(8,128)(2,1)S(1)} %get-tuple-element.53.refs_1_, bf16[256,512]{1,0:T(8,128)(2,1)S(1)} %collective-permute-done.19.refs_2_, bf16[256,512]{1,0:T(8,128)(2,1)S(1)} %collective-permute-done.20.refs_3_, ...), custom_call_target="tpu_custom_call" | custom-call | tf_op jit(solution)/shard_map/fold/pallas_call | solution.py:160
  84.3 10.9 %collective-permute-done.39 = bf16[256,1024]{1,0:T(8,128)(2,1)S(1)} collective-permute-done((bf16[256,1024]{1,0:T(8,128)(2,1)S(1)}, bf16[256,1024]{1,0:T(8,128)(2,1)S(1)}, u32[]{:S(2)}, u32[]{:S(2)}) %collective-permute-start.39) | collective-permute-done | bytes 524320 | tf_op jit(solution)/shard_map/ppermute | solution.py:288
  95.2 1.2 %maximum_add_fusion = f32[256,1280]{1,0:T(8,128)} fusion(f32[256,768]{1,0:T(8,128)S(1)} %fold.6, f32[256,512]{1,0:T(8,128)S(1)} %fold.4, bf16[256,1024]{1,0:T(8,128)(2,1)S(1)} %collective-permute-done.39, bf16[256,256]{1,0:T(8,128)(2,1)S(1)} %collective-permute-done.37.refs_0_), kind=kLoop, calls=%fused_computation | loop fusion | flops 1966080 | bytes 3276800 | tf_op jit(solution)/shard_map/add | solution.py:333
  (67 shorter events, 4.7 us)
Async XLA Ops:
  0.6 14.8 %copy-start.5 = (s32[1,3]{1,0:T(1,128)S(1)}, s32[1,3]{1,0:T(1,128)}, u32[]{:S(2)}) copy-start(s32[1,3]{1,0:T(1,128)} %lens_ref.1) | copy-start | bytes 40
  0.7 1.6 %copy-start = (bf16[1,128,8192]{2,1,0:T(8,128)(2,1)S(1)}, bf16[1,128,8192]{2,1,0:T(8,128)(2,1)}, u32[]{:S(2)}) copy-start(bf16[1,128,8192]{2,1,0:T(8,128)(2,1)} %param.5) | copy-start | bytes 6291460
  2.3 3.9 %copy-start.4 = (bf16[1,128,256]{2,1,0:T(8,128)(2,1)S(1)}, bf16[1,128,256]{2,1,0:T(8,128)(2,1)}, u32[]{:S(2)}) copy-start(bf16[1,128,256]{2,1,0:T(8,128)(2,1)} %param.7) | copy-start | bytes 196612
  2.3 13.1 %copy-start.2 = (bf16[1,128,1024]{2,1,0:T(8,128)(2,1)S(1)}, bf16[1,128,1024]{2,1,0:T(8,128)(2,1)}, u32[]{:S(2)}) copy-start(bf16[1,128,1024]{2,1,0:T(8,128)(2,1)} %param.6) | copy-start | bytes 786436
  2.3 13.1 %copy-start.3 = (bf16[1,128,1024]{2,1,0:T(8,128)(2,1)S(1)}, bf16[1,128,1024]{2,1,0:T(8,128)(2,1)}, u32[]{:S(2)}) copy-start(bf16[1,128,1024]{2,1,0:T(8,128)(2,1)} %param.8) | copy-start | bytes 786436
  3.2 28.0 %collective-permute-start.27 = (bf16[4,2,128,256]{3,2,1,0:T(8,128)(2,1)S(1)}, bf16[4,2,128,256]{3,2,1,0:T(8,128)(2,1)S(1)}, u32[]{:S(2)}, u32[]{:S(2)}) collective-permute-start(bf16[4,2,128,256]{3,2,1,0:T(8,128)(2,1)S(1)} %get-tuple-element.57), channel_id=1, source_target_pairs={{0,8},{1,9},{2,10},{3,11},{4,12},{5,13},{6,14},{7,15},{8,0},{9,1},... | collective-permute-start | bytes 1572872 | tf_op jit(solution)/shard_map/ppermute | solution.py:288
  6.2 4.8 %collective-permute-start.3 = (bf16[128,256]{1,0:T(8,128)(2,1)S(1)}, bf16[128,256]{1,0:T(8,128)(2,1)S(1)}, u32[]{:S(2)}, u32[]{:S(2)}) collective-permute-start(bf16[128,256]{1,0:T(8,128)(2,1)S(1)} %bitcast.32), channel_id=1, source_target_pairs={{0,1},{1,2},{2,3},{3,4},{4,5},{5,6},{6,7},{7,0},{8,9},{9,10},{10,1... | collective-permute-start | bytes 196616 | tf_op jit(solution)/shard_map/ppermute | solution.py:86
  6.3 5.9 %collective-permute-start.2 = (bf16[128,256]{1,0:T(8,128)(2,1)S(1)}, bf16[128,256]{1,0:T(8,128)(2,1)S(1)}, u32[]{:S(2)}, u32[]{:S(2)}) collective-permute-start(bf16[128,256]{1,0:T(8,128)(2,1)S(1)} %bitcast.33), channel_id=1, source_target_pairs={{0,2},{1,3},{2,4},{3,5},{4,6},{5,7},{6,0},{7,1},{8,10},{9,11},{10,... | collective-permute-start | bytes 196616 | tf_op jit(solution)/shard_map/ppermute | solution.py:86
  7.8 5.6 %collective-permute-start.1 = (bf16[128,256]{1,0:T(8,128)(2,1)S(1)}, bf16[128,256]{1,0:T(8,128)(2,1)S(1)}, u32[]{:S(2)}, u32[]{:S(2)}) collective-permute-start(bf16[128,256]{1,0:T(8,128)(2,1)S(1)} %bitcast.34), channel_id=1, source_target_pairs={{0,3},{1,4},{2,5},{3,6},{4,7},{5,0},{6,1},{7,2},{8,11},{9,12},{10,... | collective-permute-start | bytes 196616 | tf_op jit(solution)/shard_map/ppermute | solution.py:86
  10.2 5.2 %collective-permute-start = (bf16[128,256]{1,0:T(8,128)(2,1)S(1)}, bf16[128,256]{1,0:T(8,128)(2,1)S(1)}, u32[]{:S(2)}, u32[]{:S(2)}) collective-permute-start(bf16[128,256]{1,0:T(8,128)(2,1)S(1)} %bitcast.35), channel_id=1, source_target_pairs={{0,4},{1,5},{2,6},{3,7},{4,0},{5,1},{6,2},{7,3},{8,12},{9,13},{10,... | collective-permute-start | bytes 196616 | tf_op jit(solution)/shard_map/ppermute | solution.py:86
  11.0 9.6 %collective-permute-start.12 = (bf16[2,128,256]{2,1,0:T(8,128)(2,1)S(1)}, bf16[2,128,256]{2,1,0:T(8,128)(2,1)S(1)}, u32[]{:S(2)}, u32[]{:S(2)}) collective-permute-start(bf16[2,128,256]{2,1,0:T(8,128)(2,1)S(1)} %get-tuple-element.49), channel_id=1, source_target_pairs={{0,2},{1,5},{2,0},{3,7},{4,6},{5,1},{6,4},{7,3},{8,10},{9,13},{10,... | collective-permute-start | bytes 393224 | tf_op jit(solution)/shard_map/ppermute | solution.py:288
  12.2 10.3 %collective-permute-start.13 = (bf16[2,128,256]{2,1,0:T(8,128)(2,1)S(1)}, bf16[2,128,256]{2,1,0:T(8,128)(2,1)S(1)}, u32[]{:S(2)}, u32[]{:S(2)}) collective-permute-start(bf16[2,128,256]{2,1,0:T(8,128)(2,1)S(1)} %get-tuple-element.50), channel_id=1, source_target_pairs={{0,4},{1,3},{2,6},{3,1},{4,0},{5,7},{6,2},{7,5},{8,12},{9,11},{10,... | collective-permute-start | bytes 393224 | tf_op jit(solution)/shard_map/ppermute | solution.py:288
  13.4 9.1 %collective-permute-start.14 = (bf16[2,128,256]{2,1,0:T(8,128)(2,1)S(1)}, bf16[2,128,256]{2,1,0:T(8,128)(2,1)S(1)}, u32[]{:S(2)}, u32[]{:S(2)}) collective-permute-start(bf16[2,128,256]{2,1,0:T(8,128)(2,1)S(1)} %get-tuple-element.51), channel_id=1, source_target_pairs={{0,6},{1,7},{2,4},{3,5},{4,2},{5,3},{6,0},{7,1},{8,14},{9,15},{10,... | collective-permute-start | bytes 393224 | tf_op jit(solution)/shard_map/ppermute | solution.py:288
  20.2 5.0 %collective-permute-start.11 = (bf16[128,512]{1,0:T(8,128)(2,1)S(1)}, bf16[128,512]{1,0:T(8,128)(2,1)S(1)}, u32[]{:S(2)}, u32[]{:S(2)}) collective-permute-start(bf16[128,512]{1,0:T(8,128)(2,1)S(1)} %get-tuple-element.47), channel_id=1, source_target_pairs={{0,8},{1,9},{2,10},{3,11},{4,12},{5,13},{6,14},{7,15},{8,0},{9,1},... | collective-permute-start | bytes 393224 | tf_op jit(solution)/shard_map/ppermute | solution.py:288
  20.6 6.4 %collective-permute-start.4 = (bf16[2,128,256]{2,1,0:T(8,128)(2,1)S(1)}, bf16[2,128,256]{2,1,0:T(8,128)(2,1)S(1)}, u32[]{:S(2)}, u32[]{:S(2)}) collective-permute-start(bf16[2,128,256]{2,1,0:T(8,128)(2,1)S(1)} %get-tuple-element.35), channel_id=1, source_target_pairs={{0,2},{1,5},{2,0},{3,7},{4,6},{5,1},{6,4},{7,3},{8,10},{9,13},{10,... | collective-permute-start | bytes 393224 | tf_op jit(solution)/shard_map/ppermute | solution.py:288
  22.5 8.5 %collective-permute-start.5 = (bf16[2,128,256]{2,1,0:T(8,128)(2,1)S(1)}, bf16[2,128,256]{2,1,0:T(8,128)(2,1)S(1)}, u32[]{:S(2)}, u32[]{:S(2)}) collective-permute-start(bf16[2,128,256]{2,1,0:T(8,128)(2,1)S(1)} %get-tuple-element.36), channel_id=1, source_target_pairs={{0,4},{1,3},{2,6},{3,1},{4,0},{5,7},{6,2},{7,5},{8,12},{9,11},{10,... | collective-permute-start | bytes 393224 | tf_op jit(solution)/shard_map/ppermute | solution.py:288
  22.5 8.5 %collective-permute-start.6 = (bf16[2,128,256]{2,1,0:T(8,128)(2,1)S(1)}, bf16[2,128,256]{2,1,0:T(8,128)(2,1)S(1)}, u32[]{:S(2)}, u32[]{:S(2)}) collective-permute-start(bf16[2,128,256]{2,1,0:T(8,128)(2,1)S(1)} %get-tuple-element.37), channel_id=1, source_target_pairs={{0,6},{1,7},{2,4},{3,5},{4,2},{5,3},{6,0},{7,1},{8,14},{9,15},{10,... | collective-permute-start | bytes 393224 | tf_op jit(solution)/shard_map/ppermute | solution.py:288
  25.2 7.5 %copy-start.1 = (bf16[128,1024]{1,0:T(8,128)(2,1)S(1)}, bf16[128,1024]{1,0:T(8,128)(2,1)}, u32[]{:S(2)}) copy-start(bf16[128,1024]{1,0:T(8,128)(2,1)} %get-tuple-element.33.gq_ref) | copy-start | bytes 786436
  25.2 16.4 %collective-permute-start.15 = (bf16[4,2,128,256]{3,2,1,0:T(8,128)(2,1)S(1)}, bf16[4,2,128,256]{3,2,1,0:T(8,128)(2,1)S(1)}, u32[]{:S(2)}, u32[]{:S(2)}) collective-permute-start(bf16[4,2,128,256]{3,2,1,0:T(8,128)(2,1)S(1)} %hold.1), channel_id=1, source_target_pairs={{0,8},{1,9},{2,10},{3,11},{4,12},{5,13},{6,14},{7,15},{8,0},{9,1},... | collective-permute-start | bytes 1572872 | tf_op jit(solution)/shard_map/ppermute | solution.py:288
  27.0 7.9 %collective-permute-start.21 = (bf16[2,128,512]{2,1,0:T(8,128)(2,1)S(1)}, bf16[2,128,512]{2,1,0:T(8,128)(2,1)S(1)}, u32[]{:S(2)}, u32[]{:S(2)}) collective-permute-start(bf16[2,128,512]{2,1,0:T(8,128)(2,1)S(1)} %pack.6.refs_1_.own_ref.refs_4_), channel_id=1, source_target_pairs={{0,2},{1,5},{2,0},{3,7},{4,6},{5,1},{6,4},{7,3},{8,10},{9,13},{10,... | collective-permute-start | bytes 786440 | tf_op jit(solution)/shard_map/ppermute | solution.py:288
  31.1 1.6 %collective-permute-start.7 = (bf16[128,256]{1,0:T(8,128)(2,1)S(1)}, bf16[128,256]{1,0:T(8,128)(2,1)S(1)}, u32[]{:S(2)}, u32[]{:S(2)}) collective-permute-start(bf16[128,256]{1,0:T(8,128)(2,1)S(1)} %get-tuple-element.39), channel_id=1, source_target_pairs={{0,1},{1,0},{2,3},{3,2},{4,5},{5,4},{6,7},{7,6},{8,9},{9,8},{10,11... | collective-permute-start | bytes 196616 | tf_op jit(solution)/shard_map/ppermute | solution.py:288
  31.2 7.3 %collective-permute-start.30 = (bf16[2,128,256]{2,1,0:T(8,128)(2,1)S(1)}, bf16[2,128,256]{2,1,0:T(8,128)(2,1)S(1)}, u32[]{:S(2)}, u32[]{:S(2)}) collective-permute-start(bf16[2,128,256]{2,1,0:T(8,128)(2,1)S(1)} %get-tuple-element.63), channel_id=1, source_target_pairs={{0,6},{1,7},{2,4},{3,5},{4,2},{5,3},{6,0},{7,1},{8,14},{9,15},{10,... | collective-permute-start | bytes 393224 | tf_op jit(solution)/shard_map/ppermute | solution.py:288
  31.3 8.7 %collective-permute-start.29 = (bf16[2,128,256]{2,1,0:T(8,128)(2,1)S(1)}, bf16[2,128,256]{2,1,0:T(8,128)(2,1)S(1)}, u32[]{:S(2)}, u32[]{:S(2)}) collective-permute-start(bf16[2,128,256]{2,1,0:T(8,128)(2,1)S(1)} %get-tuple-element.64), channel_id=1, source_target_pairs={{0,4},{1,3},{2,6},{3,1},{4,0},{5,7},{6,2},{7,5},{8,12},{9,11},{10,... | collective-permute-start | bytes 393224 | tf_op jit(solution)/shard_map/ppermute | solution.py:288
  33.3 8.3 %collective-permute-start.26 = (bf16[128,768]{1,0:T(8,128)(2,1)S(1)}, bf16[128,768]{1,0:T(8,128)(2,1)S(1)}, u32[]{:S(2)}, u32[]{:S(2)}) collective-permute-start(bf16[128,768]{1,0:T(8,128)(2,1)S(1)} %get-tuple-element.56), channel_id=1, source_target_pairs={{0,8},{1,9},{2,10},{3,11},{4,12},{5,13},{6,14},{7,15},{8,0},{9,1},... | collective-permute-start | bytes 589832 | tf_op jit(solution)/shard_map/ppermute | solution.py:288
  34.9 5.8 %collective-permute-start.28 = (bf16[2,128,256]{2,1,0:T(8,128)(2,1)S(1)}, bf16[2,128,256]{2,1,0:T(8,128)(2,1)S(1)}, u32[]{:S(2)}, u32[]{:S(2)}) collective-permute-start(bf16[2,128,256]{2,1,0:T(8,128)(2,1)S(1)} %get-tuple-element.65), channel_id=1, source_target_pairs={{0,2},{1,5},{2,0},{3,7},{4,6},{5,1},{6,4},{7,3},{8,10},{9,13},{10,... | collective-permute-start | bytes 393224 | tf_op jit(solution)/shard_map/ppermute | solution.py:288
  38.5 6.4 %collective-permute-start.22 = (bf16[2,128,512]{2,1,0:T(8,128)(2,1)S(1)}, bf16[2,128,512]{2,1,0:T(8,128)(2,1)S(1)}, u32[]{:S(2)}, u32[]{:S(2)}) collective-permute-start(bf16[2,128,512]{2,1,0:T(8,128)(2,1)S(1)} %pack.6.refs_1_.own_ref.refs_4_), channel_id=1, source_target_pairs={{0,4},{1,3},{2,6},{3,1},{4,0},{5,7},{6,2},{7,5},{8,12},{9,11},{10,... | collective-permute-start | bytes 786440 | tf_op jit(solution)/shard_map/ppermute | solution.py:288
  40.0 10.5 %collective-permute-start.23 = (bf16[2,128,512]{2,1,0:T(8,128)(2,1)S(1)}, bf16[2,128,512]{2,1,0:T(8,128)(2,1)S(1)}, u32[]{:S(2)}, u32[]{:S(2)}) collective-permute-start(bf16[2,128,512]{2,1,0:T(8,128)(2,1)S(1)} %collective-permute-done.21.moved_ref.refs_5_), channel_id=1, source_target_pairs={{0,4},{1,3},{2,6},{3,1},{4,0},{5,7},{6,2},{7,5},{8,12},{9,11},{10,... | collective-permute-start | bytes 786440 | tf_op jit(solution)/shard_map/ppermute | solution.py:288
  41.6 11.2 %collective-permute-start.31 = (bf16[2,128,768]{2,1,0:T(8,128)(2,1)S(1)}, bf16[2,128,768]{2,1,0:T(8,128)(2,1)S(1)}, u32[]{:S(2)}, u32[]{:S(2)}) collective-permute-start(bf16[2,128,768]{2,1,0:T(8,128)(2,1)S(1)} %pack.9.own_ref.refs_4_), channel_id=1, source_target_pairs={{0,2},{1,5},{2,0},{3,7},{4,6},{5,1},{6,4},{7,3},{8,10},{9,13},{10,... | collective-permute-start | bytes 1179656 | tf_op jit(solution)/shard_map/ppermute | solution.py:288
  43.6 11.3 %collective-permute-start.24 = (bf16[4,128,512]{2,1,0:T(8,128)(2,1)S(1)}, bf16[4,128,512]{2,1,0:T(8,128)(2,1)S(1)}, u32[]{:S(2)}, u32[]{:S(2)}) collective-permute-start(bf16[4,128,512]{2,1,0:T(8,128)(2,1)S(1)} %pack.7), channel_id=1, source_target_pairs={{0,1},{1,0},{2,3},{3,2},{4,5},{5,4},{6,7},{7,6},{8,9},{9,8},{10,11... | collective-permute-start | bytes 1572872 | tf_op jit(solution)/shard_map/ppermute | solution.py:288
  50.5 4.4 %collective-permute-start.25 = (bf16[4,128,512]{2,1,0:T(8,128)(2,1)S(1)}, bf16[4,128,512]{2,1,0:T(8,128)(2,1)S(1)}, u32[]{:S(2)}, u32[]{:S(2)}) collective-permute-start(bf16[4,128,512]{2,1,0:T(8,128)(2,1)S(1)} %pack.8), channel_id=1, source_target_pairs={{0,1},{1,0},{2,3},{3,2},{4,5},{5,4},{6,7},{7,6},{8,9},{9,8},{10,11... | collective-permute-start | bytes 1572872 | tf_op jit(solution)/shard_map/ppermute | solution.py:288
  50.6 2.3 %collective-permute-start.35 = (bf16[256,512]{1,0:T(8,128)(2,1)S(1)}, bf16[256,512]{1,0:T(8,128)(2,1)S(1)}, u32[]{:S(2)}, u32[]{:S(2)}) collective-permute-start(bf16[256,512]{1,0:T(8,128)(2,1)S(1)} %get-tuple-element.59), channel_id=1, source_target_pairs={{0,1},{1,0},{2,3},{3,2},{4,5},{5,4},{6,7},{7,6},{8,9},{9,8},{10,11... | collective-permute-start | bytes 786440 | tf_op jit(solution)/shard_map/ppermute | solution.py:288
  51.1 3.8 %collective-permute-start.36 = (bf16[256,512]{1,0:T(8,128)(2,1)S(1)}, bf16[256,512]{1,0:T(8,128)(2,1)S(1)}, u32[]{:S(2)}, u32[]{:S(2)}) collective-permute-start(bf16[256,512]{1,0:T(8,128)(2,1)S(1)} %get-tuple-element.60), channel_id=1, source_target_pairs={{0,1},{1,0},{2,3},{3,2},{4,5},{5,4},{6,7},{7,6},{8,9},{9,8},{10,11... | collective-permute-start | bytes 786440 | tf_op jit(solution)/shard_map/ppermute | solution.py:288
  52.9 7.8 %collective-permute-start.32 = (bf16[2,128,768]{2,1,0:T(8,128)(2,1)S(1)}, bf16[2,128,768]{2,1,0:T(8,128)(2,1)S(1)}, u32[]{:S(2)}, u32[]{:S(2)}) collective-permute-start(bf16[2,128,768]{2,1,0:T(8,128)(2,1)S(1)} %pack.9.own_ref.refs_4_), channel_id=1, source_target_pairs={{0,4},{1,3},{2,6},{3,1},{4,0},{5,7},{6,2},{7,5},{8,12},{9,11},{10,... | collective-permute-start | bytes 1179656 | tf_op jit(solution)/shard_map/ppermute | solution.py:288
  52.9 12.0 %collective-permute-start.33 = (bf16[2,128,768]{2,1,0:T(8,128)(2,1)S(1)}, bf16[2,128,768]{2,1,0:T(8,128)(2,1)S(1)}, u32[]{:S(2)}, u32[]{:S(2)}) collective-permute-start(bf16[2,128,768]{2,1,0:T(8,128)(2,1)S(1)} %collective-permute-done.31.moved_ref.refs_5_), channel_id=1, source_target_pairs={{0,4},{1,3},{2,6},{3,1},{4,0},{5,7},{6,2},{7,5},{8,12},{9,11},{10,... | collective-permute-start | bytes 1179656 | tf_op jit(solution)/shard_map/ppermute | solution.py:288
  55.6 8.8 %collective-permute-start.37 = (bf16[256,256]{1,0:T(8,128)(2,1)S(1)}, bf16[256,256]{1,0:T(8,128)(2,1)S(1)}, u32[]{:S(2)}, u32[]{:S(2)}) collective-permute-start(bf16[256,256]{1,0:T(8,128)(2,1)S(1)} %get-tuple-element.61), channel_id=1, source_target_pairs={{0,16},{1,17},{2,18},{3,19},{4,20},{5,21},{6,22},{7,23},{8,24},{9,... | collective-permute-start | bytes 393224 | tf_op jit(solution)/shard_map/ppermute | solution.py:288
  58.4 10.2 %collective-permute-start.34 = (bf16[4,128,768]{2,1,0:T(8,128)(2,1)S(1)}, bf16[4,128,768]{2,1,0:T(8,128)(2,1)S(1)}, u32[]{:S(2)}, u32[]{:S(2)}) collective-permute-start(bf16[4,128,768]{2,1,0:T(8,128)(2,1)S(1)} %pack.10), channel_id=1, source_target_pairs={{0,1},{1,0},{2,3},{3,2},{4,5},{5,4},{6,7},{7,6},{8,9},{9,8},{10,11... | collective-permute-start | bytes 2359304 | tf_op jit(solution)/shard_map/ppermute | solution.py:288
  64.9 3.6 %collective-permute-start.38 = (bf16[4,128,768]{2,1,0:T(8,128)(2,1)S(1)}, bf16[4,128,768]{2,1,0:T(8,128)(2,1)S(1)}, u32[]{:S(2)}, u32[]{:S(2)}) collective-permute-start(bf16[4,128,768]{2,1,0:T(8,128)(2,1)S(1)} %pack.11), channel_id=1, source_target_pairs={{0,1},{1,0},{2,3},{3,2},{4,5},{5,4},{6,7},{7,6},{8,9},{9,8},{10,11... | collective-permute-start | bytes 2359304 | tf_op jit(solution)/shard_map/ppermute | solution.py:288
  65.0 7.6 %collective-permute-start.8 = (bf16[2,128,256]{2,1,0:T(8,128)(2,1)S(1)}, bf16[2,128,256]{2,1,0:T(8,128)(2,1)S(1)}, u32[]{:S(2)}, u32[]{:S(2)}) collective-permute-start(bf16[2,128,256]{2,1,0:T(8,128)(2,1)S(1)} %get-tuple-element.42), channel_id=1, source_target_pairs={{0,2},{1,5},{2,0},{3,7},{4,6},{5,1},{6,4},{7,3},{8,10},{9,13},{10,... | collective-permute-start | bytes 393224 | tf_op jit(solution)/shard_map/ppermute | solution.py:288
  65.8 8.7 %collective-permute-start.9 = (bf16[2,128,256]{2,1,0:T(8,128)(2,1)S(1)}, bf16[2,128,256]{2,1,0:T(8,128)(2,1)S(1)}, u32[]{:S(2)}, u32[]{:S(2)}) collective-permute-start(bf16[2,128,256]{2,1,0:T(8,128)(2,1)S(1)} %get-tuple-element.43), channel_id=1, source_target_pairs={{0,4},{1,3},{2,6},{3,1},{4,0},{5,7},{6,2},{7,5},{8,12},{9,11},{10,... | collective-permute-start | bytes 393224 | tf_op jit(solution)/shard_map/ppermute | solution.py:288
  65.9 9.9 %collective-permute-start.10 = (bf16[2,128,256]{2,1,0:T(8,128)(2,1)S(1)}, bf16[2,128,256]{2,1,0:T(8,128)(2,1)S(1)}, u32[]{:S(2)}, u32[]{:S(2)}) collective-permute-start(bf16[2,128,256]{2,1,0:T(8,128)(2,1)S(1)} %get-tuple-element.44), channel_id=1, source_target_pairs={{0,6},{1,7},{2,4},{3,5},{4,2},{5,3},{6,0},{7,1},{8,14},{9,15},{10,... | collective-permute-start | bytes 393224 | tf_op jit(solution)/shard_map/ppermute | solution.py:288
  69.5 25.6 %collective-permute-start.39 = (bf16[256,1024]{1,0:T(8,128)(2,1)S(1)}, bf16[256,1024]{1,0:T(8,128)(2,1)S(1)}, u32[]{:S(2)}, u32[]{:S(2)}) collective-permute-start(bf16[256,1024]{1,0:T(8,128)(2,1)S(1)} %fold.7), channel_id=1, source_target_pairs={{0,16},{1,17},{2,18},{3,19},{4,20},{5,21},{6,22},{7,23},{8,24},{9,... | collective-permute-start | bytes 1572872 | tf_op jit(solution)/shard_map/ppermute | solution.py:288
  72.3 7.1 %collective-permute-start.18 = (bf16[2,128,256]{2,1,0:T(8,128)(2,1)S(1)}, bf16[2,128,256]{2,1,0:T(8,128)(2,1)S(1)}, u32[]{:S(2)}, u32[]{:S(2)}) collective-permute-start(bf16[2,128,256]{2,1,0:T(8,128)(2,1)S(1)} %get-tuple-element.66), channel_id=1, source_target_pairs={{0,6},{1,7},{2,4},{3,5},{4,2},{5,3},{6,0},{7,1},{8,14},{9,15},{10,... | collective-permute-start | bytes 393224 | tf_op jit(solution)/shard_map/ppermute | solution.py:288
  72.6 8.2 %collective-permute-start.17 = (bf16[2,128,256]{2,1,0:T(8,128)(2,1)S(1)}, bf16[2,128,256]{2,1,0:T(8,128)(2,1)S(1)}, u32[]{:S(2)}, u32[]{:S(2)}) collective-permute-start(bf16[2,128,256]{2,1,0:T(8,128)(2,1)S(1)} %get-tuple-element.67), channel_id=1, source_target_pairs={{0,4},{1,3},{2,6},{3,1},{4,0},{5,7},{6,2},{7,5},{8,12},{9,11},{10,... | collective-permute-start | bytes 393224 | tf_op jit(solution)/shard_map/ppermute | solution.py:288
  74.5 6.3 %collective-permute-start.16 = (bf16[2,128,256]{2,1,0:T(8,128)(2,1)S(1)}, bf16[2,128,256]{2,1,0:T(8,128)(2,1)S(1)}, u32[]{:S(2)}, u32[]{:S(2)}) collective-permute-start(bf16[2,128,256]{2,1,0:T(8,128)(2,1)S(1)} %get-tuple-element.68), channel_id=1, source_target_pairs={{0,2},{1,5},{2,0},{3,7},{4,6},{5,1},{6,4},{7,3},{8,10},{9,13},{10,... | collective-permute-start | bytes 393224 | tf_op jit(solution)/shard_map/ppermute | solution.py:288
  76.0 5.0 %collective-permute-start.19 = (bf16[256,512]{1,0:T(8,128)(2,1)S(1)}, bf16[256,512]{1,0:T(8,128)(2,1)S(1)}, u32[]{:S(2)}, u32[]{:S(2)}) collective-permute-start(bf16[256,512]{1,0:T(8,128)(2,1)S(1)} %get-tuple-element.54), channel_id=1, source_target_pairs={{0,1},{1,0},{2,3},{3,2},{4,5},{5,4},{6,7},{7,6},{8,9},{9,8},{10,11... | collective-permute-start | bytes 786440 | tf_op jit(solution)/shard_map/ppermute | solution.py:288
  81.0 1.6 %collective-permute-start.20 = (bf16[256,512]{1,0:T(8,128)(2,1)S(1)}, bf16[256,512]{1,0:T(8,128)(2,1)S(1)}, u32[]{:S(2)}, u32[]{:S(2)}) collective-permute-start(bf16[256,512]{1,0:T(8,128)(2,1)S(1)} %get-tuple-element.55), channel_id=1, source_target_pairs={{0,1},{1,0},{2,3},{3,2},{4,5},{5,4},{6,7},{7,6},{8,9},{9,8},{10,11... | collective-permute-start | bytes 786440 | tf_op jit(solution)/shard_map/ppermute | solution.py:288

commit v5 on v4

--- a/solution.py
+++ b/solution.py
@@ -317,13 +317,14 @@
     beyond = hop(hold([pieces[9]], [first_cols[0]])[0], 1, STAY)
     held, send = merge(held, [hop(t, 0, c) for t, c in zip(send, chips)])
     rest, grad_kv = settle(grad_query, lead, held, [hop(send, 0, SIBLING)])
-    first_folds = fold(away, first_cols, BF16, cuts=[256])
+    first_folds = fold(away, first_cols, BF16, cuts=[384])
     sent = [hop(first_folds[0], 2, STAY)]
     rest_cols = gather_pairs(rest, [far,beyond], [sent[0]])
     (rest_fold,) = fold(away, rest_cols, BF16, joined=first_folds[1:])
     sent.append(hop(rest_fold, 2, STAY))
+    held_pieces = hold(pieces[6:9], [rest_fold])
     home_near, home_near_sib = turn(
-        [pieces[5]] + [hop(p, 0, c) for p, c in zip(pieces[6:9], chips)]
+        [pieces[5]] + [hop(p, 0, c) for p, c in zip(held_pieces, chips)]
     )
     home_far, home_far_sib = turn(
         [beyond] + [hop(beyond[i + 1], 0, c) for i, c in enumerate(chips)]

time: 96.5 us -> 92.6 us (0.960)
  starting transfers between devices: 40.7 us -> 35 us
  waiting for transfers between devices: 41.2 us -> 42.8 us
    ppermute x36, starting transfers between devices: 36.3 us -> 30.6 us  [hop(): return lax.ppermute(value, ('dp', 'ctx'), pairs)]
    ppermute x36, waiting for transfers between devices: 39.9 us -> 41.6 us  [hop(): return lax.ppermute(value, ('dp', 'ctx'), pairs)]
    pallas_call x17 -> x18, Pallas kernels: 5.07 us -> 5.1 us  [local_call(): pl.pallas_call(kernel, out_shape=out_shape, in_specs=specs, out_specs=jax...]
  transfers between devices with their start and end apart: 40 -> 40, of which waited for: 19 -> 18; matrix products, arithmetic and copies ran while one was open for 0% -> 0% of each run, Pallas kernels for 10% -> 11%
where the time goes in v5:
time: 92.6 us; the launch traced here: 92.4 us
  waiting for transfers between devices  42.8 us (46%)
  starting transfers between devices  35 us (38%)
  Pallas kernels  10.7 us (12%)
  local copies, waits for them, and re-layouts  1.66 us (2%)
  other arithmetic  1.26 us (1%)
    ppermute x36, waiting for transfers between devices, hop(): return lax.ppermute(value, ('dp', 'ctx'), pairs)  41.6 us
    ppermute x36, starting transfers between devices, hop(): return lax.ppermute(value, ('dp', 'ctx'), pairs)  30.6 us
    pallas_call x18, Pallas kernels, local_call(): pl.pallas_call(kernel, out_shape=out_shape, in_specs=specs, out_specs=jax...  5.1 us
    pallas_call x1, Pallas kernels, attention(): pl.pallas_call(functools.partial(attention_kernel, span=span, head=head,...  4.78 us
    ppermute x4, starting transfers between devices, shift(): return lax.ppermute(value, 'ctx', [(i, (i + by) % ctx) for i in range(ctx)])  4.42 us
  transfers between devices with their start and end apart: 40, of which 18 were waited for; matrix products, arithmetic and copies ran while one was open for 0% of the time, Pallas kernels for 11%

profile of v5, /device:TPU:0, one launch (start us, length us, event | category | flops | bytes accessed | tf_op | source)
XLA Modules:
  0.0 92.4 jit_solution(2494021800718272268)
XLA Ops:
  0.7 1.6 %copy-done = bf16[1,128,8192]{2,1,0:T(8,128)(2,1)S(1)} copy-done((bf16[1,128,8192]{2,1,0:T(8,128)(2,1)S(1)}, bf16[1,128,8192]{2,1,0:T(8,128)(2,1)}, u32[]{:S(2)}) %copy-start) | copy-done | bytes 2097176
  2.3 0.8 spread.1
  3.2 3.1 %collective-permute-start.11 = (bf16[4,2,128,256]{3,2,1,0:T(8,128)(2,1)S(1)}, bf16[4,2,128,256]{3,2,1,0:T(8,128)(2,1)S(1)}, u32[]{:S(2)}, u32[]{:S(2)}) collective-permute-start(bf16[4,2,128,256]{3,2,1,0:T(8,128)(2,1)S(1)} %get-tuple-element.53), channel_id=1, source_target_pairs={{0,8},{1,9},{2,10},{3,11},{4,12},{5,13},{6,14},{7,15},{8,0},{9,1},... | collective-permute-start | bytes 1572872 | tf_op jit(solution)/shard_map/ppermute | solution.py:288
  6.3 1.5 %collective-permute-start.2 = (bf16[128,256]{1,0:T(8,128)(2,1)S(1)}, bf16[128,256]{1,0:T(8,128)(2,1)S(1)}, u32[]{:S(2)}, u32[]{:S(2)}) collective-permute-start(bf16[128,256]{1,0:T(8,128)(2,1)S(1)} %bitcast.33), channel_id=1, source_target_pairs={{0,2},{1,3},{2,4},{3,5},{4,6},{5,7},{6,0},{7,1},{8,10},{9,11},{10,... | collective-permute-start | bytes 196616 | tf_op jit(solution)/shard_map/ppermute | solution.py:86
  7.8 2.4 %collective-permute-start.1 = (bf16[128,256]{1,0:T(8,128)(2,1)S(1)}, bf16[128,256]{1,0:T(8,128)(2,1)S(1)}, u32[]{:S(2)}, u32[]{:S(2)}) collective-permute-start(bf16[128,256]{1,0:T(8,128)(2,1)S(1)} %bitcast.34), channel_id=1, source_target_pairs={{0,3},{1,4},{2,5},{3,6},{4,7},{5,0},{6,1},{7,2},{8,11},{9,12},{10,... | collective-permute-start | bytes 196616 | tf_op jit(solution)/shard_map/ppermute | solution.py:86
  10.2 0.5 collective-permute-start
  11.0 1.2 %collective-permute-start.8 = (bf16[2,128,256]{2,1,0:T(8,128)(2,1)S(1)}, bf16[2,128,256]{2,1,0:T(8,128)(2,1)S(1)}, u32[]{:S(2)}, u32[]{:S(2)}) collective-permute-start(bf16[2,128,256]{2,1,0:T(8,128)(2,1)S(1)} %get-tuple-element.49), channel_id=1, source_target_pairs={{0,2},{1,5},{2,0},{3,7},{4,6},{5,1},{6,4},{7,3},{8,10},{9,13},{10,... | collective-permute-start | bytes 393224 | tf_op jit(solution)/shard_map/ppermute | solution.py:288
  12.2 1.2 %collective-permute-start.9 = (bf16[2,128,256]{2,1,0:T(8,128)(2,1)S(1)}, bf16[2,128,256]{2,1,0:T(8,128)(2,1)S(1)}, u32[]{:S(2)}, u32[]{:S(2)}) collective-permute-start(bf16[2,128,256]{2,1,0:T(8,128)(2,1)S(1)} %get-tuple-element.50), channel_id=1, source_target_pairs={{0,4},{1,3},{2,6},{3,1},{4,0},{5,7},{6,2},{7,5},{8,12},{9,11},{10,... | collective-permute-start | bytes 393224 | tf_op jit(solution)/shard_map/ppermute | solution.py:288
  13.4 1.1 %collective-permute-start.10 = (bf16[2,128,256]{2,1,0:T(8,128)(2,1)S(1)}, bf16[2,128,256]{2,1,0:T(8,128)(2,1)S(1)}, u32[]{:S(2)}, u32[]{:S(2)}) collective-permute-start(bf16[2,128,256]{2,1,0:T(8,128)(2,1)S(1)} %get-tuple-element.51), channel_id=1, source_target_pairs={{0,6},{1,7},{2,4},{3,5},{4,2},{5,3},{6,0},{7,1},{8,14},{9,15},{10,... | collective-permute-start | bytes 393224 | tf_op jit(solution)/shard_map/ppermute | solution.py:288
  14.5 0.9 collective-permute-done.refs_0_
  15.4 4.8 %attention.1 = (bf16[128,1024]{1,0:T(8,128)(2,1)}, bf16[128,512]{1,0:T(8,128)(2,1)S(1)}, f32[2,128,256]{2,1,0:T(8,128)S(1)}, bf16[2,128,256]{2,1,0:T(8,128)(2,1)...) custom-call(s32[1]{0:T(128)} %bitcast.own_ref, s32[1,3]{1,0:T(1,128)S(1)} %copy-done.5, ...), custom_call_target="tpu_custom_call" | custom-call | flops 1006632960 | bytes 1441792 | tf_op jit(solution)/shard_map/attention/pallas_call | solution.py:102
  20.2 0.4 collective-permute-start.18
  20.6 1.8 %collective-permute-start.4 = (bf16[2,128,256]{2,1,0:T(8,128)(2,1)S(1)}, bf16[2,128,256]{2,1,0:T(8,128)(2,1)S(1)}, u32[]{:S(2)}, u32[]{:S(2)}) collective-permute-start(bf16[2,128,256]{2,1,0:T(8,128)(2,1)S(1)} %get-tuple-element.38), channel_id=1, source_target_pairs={{0,2},{1,5},{2,0},{3,7},{4,6},{5,1},{6,4},{7,3},{8,10},{9,13},{10,... | collective-permute-start | bytes 393224 | tf_op jit(solution)/shard_map/ppermute | solution.py:288
  22.5 1.6 %collective-permute-start.6 = (bf16[2,128,256]{2,1,0:T(8,128)(2,1)S(1)}, bf16[2,128,256]{2,1,0:T(8,128)(2,1)S(1)}, u32[]{:S(2)}, u32[]{:S(2)}) collective-permute-start(bf16[2,128,256]{2,1,0:T(8,128)(2,1)S(1)} %get-tuple-element.40), channel_id=1, source_target_pairs={{0,6},{1,7},{2,4},{3,5},{4,2},{5,3},{6,0},{7,1},{8,14},{9,15},{10,... | collective-permute-start | bytes 393224 | tf_op jit(solution)/shard_map/ppermute | solution.py:288
  24.3 0.8 collective-permute-done.18
  25.2 1.9 %collective-permute-start.24 = (bf16[2,128,512]{2,1,0:T(8,128)(2,1)S(1)}, bf16[2,128,512]{2,1,0:T(8,128)(2,1)S(1)}, u32[]{:S(2)}, u32[]{:S(2)}) collective-permute-start(bf16[2,128,512]{2,1,0:T(8,128)(2,1)S(1)} %pack.6.refs_1_.own_ref.refs_4_), channel_id=1, source_target_pairs={{0,2},{1,5},{2,0},{3,7},{4,6},{5,1},{6,4},{7,3},{8,10},{9,13},{10,... | collective-permute-start | bytes 786440 | tf_op jit(solution)/shard_map/ppermute | solution.py:288
  27.1 0.8 collective-permute-start.19
  28.0 1.1 %collective-permute-start.14 = (bf16[2,128,256]{2,1,0:T(8,128)(2,1)S(1)}, bf16[2,128,256]{2,1,0:T(8,128)(2,1)S(1)}, u32[]{:S(2)}, u32[]{:S(2)}) collective-permute-start(bf16[2,128,256]{2,1,0:T(8,128)(2,1)S(1)} %get-tuple-element.72), channel_id=1, source_target_pairs={{0,6},{1,7},{2,4},{3,5},{4,2},{5,3},{6,0},{7,1},{8,14},{9,15},{10,... | collective-permute-start | bytes 393224 | tf_op jit(solution)/shard_map/ppermute | solution.py:288
  29.1 2.5 %collective-permute-done.5.refs_1_ = bf16[2,128,256]{2,1,0:T(8,128)(2,1)S(1)} collective-permute-done((bf16[2,128,256]{2,1,0:T(8,128)(2,1)S(1)}, bf16[2,128,256]{2,1,0:T(8,128)(2,1)S(1)}, u32[]{:S(2)}, u32[]{:S(2)}) %collective-permute-start.5) | collective-permute-done | bytes 131104 | tf_op jit(solution)/shard_map/ppermute | solution.py:288
  31.9 1.2 %collective-permute-done.7.refs_0_ = bf16[128,256]{1,0:T(8,128)(2,1)S(1)} collective-permute-done((bf16[128,256]{1,0:T(8,128)(2,1)S(1)}, bf16[128,256]{1,0:T(8,128)(2,1)S(1)}, u32[]{:S(2)}, u32[]{:S(2)}) %collective-permute-start.7) | collective-permute-done | bytes 65568 | tf_op jit(solution)/shard_map/ppermute | solution.py:288
  33.0 0.9 collective-permute-start.25
  33.9 0.7 settle.1
  34.5 2.3 %collective-permute-start.17 = (bf16[128,768]{1,0:T(8,128)(2,1)S(1)}, bf16[128,768]{1,0:T(8,128)(2,1)S(1)}, u32[]{:S(2)}, u32[]{:S(2)}) collective-permute-start(bf16[128,768]{1,0:T(8,128)(2,1)S(1)} %get-tuple-element.57), channel_id=1, source_target_pairs={{0,8},{1,9},{2,10},{3,11},{4,12},{5,13},{6,14},{7,15},{8,0},{9,1},... | collective-permute-start | bytes 589832 | tf_op jit(solution)/shard_map/ppermute | solution.py:288
  37.0 1.0 %collective-permute-start.26 = (bf16[2,128,512]{2,1,0:T(8,128)(2,1)S(1)}, bf16[2,128,512]{2,1,0:T(8,128)(2,1)S(1)}, u32[]{:S(2)}, u32[]{:S(2)}) collective-permute-start(bf16[2,128,512]{2,1,0:T(8,128)(2,1)S(1)} %collective-permute-done.24.moved_ref.refs_5_), channel_id=1, source_target_pairs={{0,4},{1,3},{2,6},{3,1},{4,0},{5,7},{6,2},{7,5},{8,12},{9,11},{10,... | collective-permute-start | bytes 786440 | tf_op jit(solution)/shard_map/ppermute | solution.py:288
  38.0 0.9 collective-permute-start.12
  38.9 5.2 %collective-permute-done.12.refs_1_ = bf16[2,128,256]{2,1,0:T(8,128)(2,1)S(1)} collective-permute-done((bf16[2,128,256]{2,1,0:T(8,128)(2,1)S(1)}, bf16[2,128,256]{2,1,0:T(8,128)(2,1)S(1)}, u32[]{:S(2)}, u32[]{:S(2)}) %collective-permute-start.12) | collective-permute-done | bytes 131104 | tf_op jit(solution)/shard_map/ppermute | solution.py:288
  45.0 0.5 collective-permute-start.28
  46.0 1.9 %collective-permute-done.15.refs_2_ = bf16[256,512]{1,0:T(8,128)(2,1)S(1)} collective-permute-done((bf16[256,512]{1,0:T(8,128)(2,1)S(1)}, bf16[256,512]{1,0:T(8,128)(2,1)S(1)}, u32[]{:S(2)}, u32[]{:S(2)}) %collective-permute-start.15) | collective-permute-done | bytes 262176 | tf_op jit(solution)/shard_map/ppermute | solution.py:288
  48.2 5.9 %collective-permute-done.20.moved_ref.refs_5_ = bf16[2,128,768]{2,1,0:T(8,128)(2,1)S(1)} collective-permute-done((bf16[2,128,768]{2,1,0:T(8,128)(2,1)S(1)}, bf16[2,128,768]{2,1,0:T(8,128)(2,1)S(1)}, u32[]{:S(2)}, u32[]{:S(2)}) %collective-permute-start.20) | collective-permute-done | bytes 393248 | tf_op jit(solution)/shard_map/ppermute | solution.py:288
  54.4 0.7 fold.4
  55.1 2.7 %collective-permute-start.29 = (bf16[256,384]{1,0:T(8,128)(2,1)S(1)}, bf16[256,384]{1,0:T(8,128)(2,1)S(1)}, u32[]{:S(2)}, u32[]{:S(2)}) collective-permute-start(bf16[256,384]{1,0:T(8,128)(2,1)S(1)} %get-tuple-element.60), channel_id=1, source_target_pairs={{0,16},{1,17},{2,18},{3,19},{4,20},{5,21},{6,22},{7,23},{8,24},{9,... | collective-permute-start | bytes 589832 | tf_op jit(solution)/shard_map/ppermute | solution.py:288
  57.9 6.2 %collective-permute-done.29.refs_0_ = bf16[256,384]{1,0:T(8,128)(2,1)S(1)} collective-permute-done((bf16[256,384]{1,0:T(8,128)(2,1)S(1)}, bf16[256,384]{1,0:T(8,128)(2,1)S(1)}, u32[]{:S(2)}, u32[]{:S(2)}) %collective-permute-start.29) | collective-permute-done | bytes 196640 | tf_op jit(solution)/shard_map/ppermute | solution.py:288
  64.3 0.5 collective-permute-start.36
  64.8 1.5 %collective-permute-start.35 = (bf16[2,128,256]{2,1,0:T(8,128)(2,1)S(1)}, bf16[2,128,256]{2,1,0:T(8,128)(2,1)S(1)}, u32[]{:S(2)}, u32[]{:S(2)}) collective-permute-start(bf16[2,128,256]{2,1,0:T(8,128)(2,1)S(1)} %get-tuple-element.70), channel_id=1, source_target_pairs={{0,4},{1,3},{2,6},{3,1},{4,0},{5,7},{6,2},{7,5},{8,12},{9,11},{10,... | collective-permute-start | bytes 393224 | tf_op jit(solution)/shard_map/ppermute | solution.py:288
  66.6 1.0 %fold.5.refs_3_ = bf16[256,896]{1,0:T(8,128)(2,1)S(1)} custom-call(bf16[256,512]{1,0:T(8,128)(2,1)S(1)} %get-tuple-element.52.refs_0_, bf16[256,512]{1,0:T(8,128)(2,1)S(1)} %get-tuple-element.54.refs_0_.refs_1_, bf16[256,512]{1,0:T(8,128)(2,1)S(1)} %collective-permute-done.15.refs_2_, bf16[256,512]{1,0:T(8,128)(2,1)S(1)} %collective-permute-done.16.refs_3_, ...), custom_call_target="tpu_custom_call" | custom-call | tf_op jit(solution)/shard_map/fold/pallas_call | solution.py:160
  67.9 1.3 %collective-permute-start.34 = (bf16[2,128,256]{2,1,0:T(8,128)(2,1)S(1)}, bf16[2,128,256]{2,1,0:T(8,128)(2,1)S(1)}, u32[]{:S(2)}, u32[]{:S(2)}) collective-permute-start(bf16[2,128,256]{2,1,0:T(8,128)(2,1)S(1)} %get-tuple-element.71), channel_id=1, source_target_pairs={{0,2},{1,5},{2,0},{3,7},{4,6},{5,1},{6,4},{7,3},{8,10},{9,13},{10,... | collective-permute-start | bytes 393224 | tf_op jit(solution)/shard_map/ppermute | solution.py:288
  69.3 0.8 collective-permute-start.31
  70.1 1.6 %collective-permute-done.36.refs_3_ = bf16[2,128,256]{2,1,0:T(8,128)(2,1)S(1)} collective-permute-done((bf16[2,128,256]{2,1,0:T(8,128)(2,1)S(1)}, bf16[2,128,256]{2,1,0:T(8,128)(2,1)S(1)}, u32[]{:S(2)}, u32[]{:S(2)}) %collective-permute-start.36) | collective-permute-done | bytes 131104 | tf_op jit(solution)/shard_map/ppermute | solution.py:288
  71.6 1.3 %collective-permute-start.32 = (bf16[2,128,256]{2,1,0:T(8,128)(2,1)S(1)}, bf16[2,128,256]{2,1,0:T(8,128)(2,1)S(1)}, u32[]{:S(2)}, u32[]{:S(2)}) collective-permute-start(bf16[2,128,256]{2,1,0:T(8,128)(2,1)S(1)} %get-tuple-element.63), channel_id=1, source_target_pairs={{0,4},{1,3},{2,6},{3,1},{4,0},{5,7},{6,2},{7,5},{8,12},{9,11},{10,... | collective-permute-start | bytes 393224 | tf_op jit(solution)/shard_map/ppermute | solution.py:288
  72.9 0.8 collective-permute-done.35.refs_2_
  73.8 0.5 collective-permute-start.33
  74.5 2.5 %collective-permute-done.31.refs_1_ = bf16[2,128,256]{2,1,0:T(8,128)(2,1)S(1)} collective-permute-done((bf16[2,128,256]{2,1,0:T(8,128)(2,1)S(1)}, bf16[2,128,256]{2,1,0:T(8,128)(2,1)S(1)}, u32[]{:S(2)}, u32[]{:S(2)}) %collective-permute-start.31) | collective-permute-done | bytes 131104 | tf_op jit(solution)/shard_map/ppermute | solution.py:288
  77.0 2.8 %collective-permute-done.33.refs_3_ = bf16[2,128,256]{2,1,0:T(8,128)(2,1)S(1)} collective-permute-done((bf16[2,128,256]{2,1,0:T(8,128)(2,1)S(1)}, bf16[2,128,256]{2,1,0:T(8,128)(2,1)S(1)}, u32[]{:S(2)}, u32[]{:S(2)}) %collective-permute-start.33) | collective-permute-done | bytes 131104 | tf_op jit(solution)/shard_map/ppermute | solution.py:288
  80.1 1.5 %collective-permute-done.37.refs_2_ = bf16[256,512]{1,0:T(8,128)(2,1)S(1)} collective-permute-done((bf16[256,512]{1,0:T(8,128)(2,1)S(1)}, bf16[256,512]{1,0:T(8,128)(2,1)S(1)}, u32[]{:S(2)}, u32[]{:S(2)}) %collective-permute-start.37) | collective-permute-done | bytes 262176 | tf_op jit(solution)/shard_map/ppermute | solution.py:288
  81.6 1.0 %fold.7 = f32[256,768]{1,0:T(8,128)S(1)} custom-call(bf16[256,512]{1,0:T(8,128)(2,1)S(1)} %get-tuple-element.65.refs_0_, bf16[256,512]{1,0:T(8,128)(2,1)S(1)} %get-tuple-element.66.refs_1_, bf16[256,512]{1,0:T(8,128)(2,1)S(1)} %collective-permute-done.37.refs_2_, bf16[256,512]{1,0:T(8,128)(2,1)S(1)} %collective-permute-done.38.refs_3_, ...), custom_call_target="tpu_custom_call" | custom-call | tf_op jit(solution)/shard_map/fold/pallas_call | solution.py:160
  82.6 0.7 fold.6
  83.3 8.0 %collective-permute-done.39 = bf16[256,896]{1,0:T(8,128)(2,1)S(1)} collective-permute-done((bf16[256,896]{1,0:T(8,128)(2,1)S(1)}, bf16[256,896]{1,0:T(8,128)(2,1)S(1)}, u32[]{:S(2)}, u32[]{:S(2)}) %collective-permute-start.39) | collective-permute-done | bytes 458784 | tf_op jit(solution)/shard_map/ppermute | solution.py:288
  91.3 1.2 %maximum_add_fusion = f32[256,1280]{1,0:T(8,128)} fusion(f32[256,768]{1,0:T(8,128)S(1)} %fold.7, f32[256,512]{1,0:T(8,128)S(1)} %fold.6, bf16[256,896]{1,0:T(8,128)(2,1)S(1)} %collective-permute-done.39, bf16[256,384]{1,0:T(8,128)(2,1)S(1)} %collective-permute-done.29.refs_0_), kind=kLoop, calls=%fused_computation | loop fusion | flops 1966080 | bytes 3276800 | tf_op jit(solution)/shard_map/add | solution.py:334
  (68 shorter events, 4.5 us)
Async XLA Ops:
  0.6 14.8 %copy-start.5 = (s32[1,3]{1,0:T(1,128)S(1)}, s32[1,3]{1,0:T(1,128)}, u32[]{:S(2)}) copy-start(s32[1,3]{1,0:T(1,128)} %lens_ref.1) | copy-start | bytes 40
  0.7 1.6 %copy-start = (bf16[1,128,8192]{2,1,0:T(8,128)(2,1)S(1)}, bf16[1,128,8192]{2,1,0:T(8,128)(2,1)}, u32[]{:S(2)}) copy-start(bf16[1,128,8192]{2,1,0:T(8,128)(2,1)} %param.5) | copy-start | bytes 6291460
  2.3 3.9 %copy-start.4 = (bf16[1,128,256]{2,1,0:T(8,128)(2,1)S(1)}, bf16[1,128,256]{2,1,0:T(8,128)(2,1)}, u32[]{:S(2)}) copy-start(bf16[1,128,256]{2,1,0:T(8,128)(2,1)} %param.7) | copy-start | bytes 196612
  2.3 13.1 %copy-start.2 = (bf16[1,128,1024]{2,1,0:T(8,128)(2,1)S(1)}, bf16[1,128,1024]{2,1,0:T(8,128)(2,1)}, u32[]{:S(2)}) copy-start(bf16[1,128,1024]{2,1,0:T(8,128)(2,1)} %param.6) | copy-start | bytes 786436
  2.3 13.1 %copy-start.3 = (bf16[1,128,1024]{2,1,0:T(8,128)(2,1)S(1)}, bf16[1,128,1024]{2,1,0:T(8,128)(2,1)}, u32[]{:S(2)}) copy-start(bf16[1,128,1024]{2,1,0:T(8,128)(2,1)} %param.8) | copy-start | bytes 786436
  3.2 24.0 %collective-permute-start.11 = (bf16[4,2,128,256]{3,2,1,0:T(8,128)(2,1)S(1)}, bf16[4,2,128,256]{3,2,1,0:T(8,128)(2,1)S(1)}, u32[]{:S(2)}, u32[]{:S(2)}) collective-permute-start(bf16[4,2,128,256]{3,2,1,0:T(8,128)(2,1)S(1)} %get-tuple-element.53), channel_id=1, source_target_pairs={{0,8},{1,9},{2,10},{3,11},{4,12},{5,13},{6,14},{7,15},{8,0},{9,1},... | collective-permute-start | bytes 1572872 | tf_op jit(solution)/shard_map/ppermute | solution.py:288
  6.2 4.8 %collective-permute-start.3 = (bf16[128,256]{1,0:T(8,128)(2,1)S(1)}, bf16[128,256]{1,0:T(8,128)(2,1)S(1)}, u32[]{:S(2)}, u32[]{:S(2)}) collective-permute-start(bf16[128,256]{1,0:T(8,128)(2,1)S(1)} %bitcast.32), channel_id=1, source_target_pairs={{0,1},{1,2},{2,3},{3,4},{4,5},{5,6},{6,7},{7,0},{8,9},{9,10},{10,1... | collective-permute-start | bytes 196616 | tf_op jit(solution)/shard_map/ppermute | solution.py:86
  6.3 5.9 %collective-permute-start.2 = (bf16[128,256]{1,0:T(8,128)(2,1)S(1)}, bf16[128,256]{1,0:T(8,128)(2,1)S(1)}, u32[]{:S(2)}, u32[]{:S(2)}) collective-permute-start(bf16[128,256]{1,0:T(8,128)(2,1)S(1)} %bitcast.33), channel_id=1, source_target_pairs={{0,2},{1,3},{2,4},{3,5},{4,6},{5,7},{6,0},{7,1},{8,10},{9,11},{10,... | collective-permute-start | bytes 196616 | tf_op jit(solution)/shard_map/ppermute | solution.py:86
  7.8 5.6 %collective-permute-start.1 = (bf16[128,256]{1,0:T(8,128)(2,1)S(1)}, bf16[128,256]{1,0:T(8,128)(2,1)S(1)}, u32[]{:S(2)}, u32[]{:S(2)}) collective-permute-start(bf16[128,256]{1,0:T(8,128)(2,1)S(1)} %bitcast.34), channel_id=1, source_target_pairs={{0,3},{1,4},{2,5},{3,6},{4,7},{5,0},{6,1},{7,2},{8,11},{9,12},{10,... | collective-permute-start | bytes 196616 | tf_op jit(solution)/shard_map/ppermute | solution.py:86
  10.2 5.2 %collective-permute-start = (bf16[128,256]{1,0:T(8,128)(2,1)S(1)}, bf16[128,256]{1,0:T(8,128)(2,1)S(1)}, u32[]{:S(2)}, u32[]{:S(2)}) collective-permute-start(bf16[128,256]{1,0:T(8,128)(2,1)S(1)} %bitcast.35), channel_id=1, source_target_pairs={{0,4},{1,5},{2,6},{3,7},{4,0},{5,1},{6,2},{7,3},{8,12},{9,13},{10,... | collective-permute-start | bytes 196616 | tf_op jit(solution)/shard_map/ppermute | solution.py:86
  11.0 9.6 %collective-permute-start.8 = (bf16[2,128,256]{2,1,0:T(8,128)(2,1)S(1)}, bf16[2,128,256]{2,1,0:T(8,128)(2,1)S(1)}, u32[]{:S(2)}, u32[]{:S(2)}) collective-permute-start(bf16[2,128,256]{2,1,0:T(8,128)(2,1)S(1)} %get-tuple-element.49), channel_id=1, source_target_pairs={{0,2},{1,5},{2,0},{3,7},{4,6},{5,1},{6,4},{7,3},{8,10},{9,13},{10,... | collective-permute-start | bytes 393224 | tf_op jit(solution)/shard_map/ppermute | solution.py:288
  12.2 10.3 %collective-permute-start.9 = (bf16[2,128,256]{2,1,0:T(8,128)(2,1)S(1)}, bf16[2,128,256]{2,1,0:T(8,128)(2,1)S(1)}, u32[]{:S(2)}, u32[]{:S(2)}) collective-permute-start(bf16[2,128,256]{2,1,0:T(8,128)(2,1)S(1)} %get-tuple-element.50), channel_id=1, source_target_pairs={{0,4},{1,3},{2,6},{3,1},{4,0},{5,7},{6,2},{7,5},{8,12},{9,11},{10,... | collective-permute-start | bytes 393224 | tf_op jit(solution)/shard_map/ppermute | solution.py:288
  13.4 9.1 %collective-permute-start.10 = (bf16[2,128,256]{2,1,0:T(8,128)(2,1)S(1)}, bf16[2,128,256]{2,1,0:T(8,128)(2,1)S(1)}, u32[]{:S(2)}, u32[]{:S(2)}) collective-permute-start(bf16[2,128,256]{2,1,0:T(8,128)(2,1)S(1)} %get-tuple-element.51), channel_id=1, source_target_pairs={{0,6},{1,7},{2,4},{3,5},{4,2},{5,3},{6,0},{7,1},{8,14},{9,15},{10,... | collective-permute-start | bytes 393224 | tf_op jit(solution)/shard_map/ppermute | solution.py:288
  20.2 5.0 %collective-permute-start.18 = (bf16[128,512]{1,0:T(8,128)(2,1)S(1)}, bf16[128,512]{1,0:T(8,128)(2,1)S(1)}, u32[]{:S(2)}, u32[]{:S(2)}) collective-permute-start(bf16[128,512]{1,0:T(8,128)(2,1)S(1)} %get-tuple-element.59), channel_id=1, source_target_pairs={{0,8},{1,9},{2,10},{3,11},{4,12},{5,13},{6,14},{7,15},{8,0},{9,1},... | collective-permute-start | bytes 393224 | tf_op jit(solution)/shard_map/ppermute | solution.py:288
  20.6 7.4 %collective-permute-start.4 = (bf16[2,128,256]{2,1,0:T(8,128)(2,1)S(1)}, bf16[2,128,256]{2,1,0:T(8,128)(2,1)S(1)}, u32[]{:S(2)}, u32[]{:S(2)}) collective-permute-start(bf16[2,128,256]{2,1,0:T(8,128)(2,1)S(1)} %get-tuple-element.38), channel_id=1, source_target_pairs={{0,2},{1,5},{2,0},{3,7},{4,6},{5,1},{6,4},{7,3},{8,10},{9,13},{10,... | collective-permute-start | bytes 393224 | tf_op jit(solution)/shard_map/ppermute | solution.py:288
  22.5 9.1 %collective-permute-start.5 = (bf16[2,128,256]{2,1,0:T(8,128)(2,1)S(1)}, bf16[2,128,256]{2,1,0:T(8,128)(2,1)S(1)}, u32[]{:S(2)}, u32[]{:S(2)}) collective-permute-start(bf16[2,128,256]{2,1,0:T(8,128)(2,1)S(1)} %get-tuple-element.39), channel_id=1, source_target_pairs={{0,4},{1,3},{2,6},{3,1},{4,0},{5,7},{6,2},{7,5},{8,12},{9,11},{10,... | collective-permute-start | bytes 393224 | tf_op jit(solution)/shard_map/ppermute | solution.py:288
  22.5 9.1 %collective-permute-start.6 = (bf16[2,128,256]{2,1,0:T(8,128)(2,1)S(1)}, bf16[2,128,256]{2,1,0:T(8,128)(2,1)S(1)}, u32[]{:S(2)}, u32[]{:S(2)}) collective-permute-start(bf16[2,128,256]{2,1,0:T(8,128)(2,1)S(1)} %get-tuple-element.40), channel_id=1, source_target_pairs={{0,6},{1,7},{2,4},{3,5},{4,2},{5,3},{6,0},{7,1},{8,14},{9,15},{10,... | collective-permute-start | bytes 393224 | tf_op jit(solution)/shard_map/ppermute | solution.py:288
  25.2 9.4 %collective-permute-start.24 = (bf16[2,128,512]{2,1,0:T(8,128)(2,1)S(1)}, bf16[2,128,512]{2,1,0:T(8,128)(2,1)S(1)}, u32[]{:S(2)}, u32[]{:S(2)}) collective-permute-start(bf16[2,128,512]{2,1,0:T(8,128)(2,1)S(1)} %pack.6.refs_1_.own_ref.refs_4_), channel_id=1, source_target_pairs={{0,2},{1,5},{2,0},{3,7},{4,6},{5,1},{6,4},{7,3},{8,10},{9,13},{10,... | collective-permute-start | bytes 786440 | tf_op jit(solution)/shard_map/ppermute | solution.py:288
  27.1 6.8 %copy-start.1 = (bf16[128,1024]{1,0:T(8,128)(2,1)S(1)}, bf16[128,1024]{1,0:T(8,128)(2,1)}, u32[]{:S(2)}) copy-start(bf16[128,1024]{1,0:T(8,128)(2,1)} %get-tuple-element.36.gq_ref) | copy-start | bytes 786436
  27.1 17.5 %collective-permute-start.19 = (bf16[4,2,128,256]{3,2,1,0:T(8,128)(2,1)S(1)}, bf16[4,2,128,256]{3,2,1,0:T(8,128)(2,1)S(1)}, u32[]{:S(2)}, u32[]{:S(2)}) collective-permute-start(bf16[4,2,128,256]{3,2,1,0:T(8,128)(2,1)S(1)} %hold.2), channel_id=1, source_target_pairs={{0,8},{1,9},{2,10},{3,11},{4,12},{5,13},{6,14},{7,15},{8,0},{9,1},... | collective-permute-start | bytes 1572872 | tf_op jit(solution)/shard_map/ppermute | solution.py:288
  28.0 9.0 %collective-permute-start.14 = (bf16[2,128,256]{2,1,0:T(8,128)(2,1)S(1)}, bf16[2,128,256]{2,1,0:T(8,128)(2,1)S(1)}, u32[]{:S(2)}, u32[]{:S(2)}) collective-permute-start(bf16[2,128,256]{2,1,0:T(8,128)(2,1)S(1)} %get-tuple-element.72), channel_id=1, source_target_pairs={{0,6},{1,7},{2,4},{3,5},{4,2},{5,3},{6,0},{7,1},{8,14},{9,15},{10,... | collective-permute-start | bytes 393224 | tf_op jit(solution)/shard_map/ppermute | solution.py:288
  31.7 1.3 %collective-permute-start.7 = (bf16[128,256]{1,0:T(8,128)(2,1)S(1)}, bf16[128,256]{1,0:T(8,128)(2,1)S(1)}, u32[]{:S(2)}, u32[]{:S(2)}) collective-permute-start(bf16[128,256]{1,0:T(8,128)(2,1)S(1)} %get-tuple-element.42), channel_id=1, source_target_pairs={{0,1},{1,0},{2,3},{3,2},{4,5},{5,4},{6,7},{7,6},{8,9},{9,8},{10,11... | collective-permute-start | bytes 196616 | tf_op jit(solution)/shard_map/ppermute | solution.py:288
  31.8 6.2 %collective-permute-start.13 = (bf16[2,128,256]{2,1,0:T(8,128)(2,1)S(1)}, bf16[2,128,256]{2,1,0:T(8,128)(2,1)S(1)}, u32[]{:S(2)}, u32[]{:S(2)}) collective-permute-start(bf16[2,128,256]{2,1,0:T(8,128)(2,1)S(1)} %get-tuple-element.73), channel_id=1, source_target_pairs={{0,4},{1,3},{2,6},{3,1},{4,0},{5,7},{6,2},{7,5},{8,12},{9,11},{10,... | collective-permute-start | bytes 393224 | tf_op jit(solution)/shard_map/ppermute | solution.py:288
  33.0 11.9 %collective-permute-start.25 = (bf16[2,128,512]{2,1,0:T(8,128)(2,1)S(1)}, bf16[2,128,512]{2,1,0:T(8,128)(2,1)S(1)}, u32[]{:S(2)}, u32[]{:S(2)}) collective-permute-start(bf16[2,128,512]{2,1,0:T(8,128)(2,1)S(1)} %pack.6.refs_1_.own_ref.refs_4_), channel_id=1, source_target_pairs={{0,4},{1,3},{2,6},{3,1},{4,0},{5,7},{6,2},{7,5},{8,12},{9,11},{10,... | collective-permute-start | bytes 786440 | tf_op jit(solution)/shard_map/ppermute | solution.py:288
  34.5 10.1 %collective-permute-start.17 = (bf16[128,768]{1,0:T(8,128)(2,1)S(1)}, bf16[128,768]{1,0:T(8,128)(2,1)S(1)}, u32[]{:S(2)}, u32[]{:S(2)}) collective-permute-start(bf16[128,768]{1,0:T(8,128)(2,1)S(1)} %get-tuple-element.57), channel_id=1, source_target_pairs={{0,8},{1,9},{2,10},{3,11},{4,12},{5,13},{6,14},{7,15},{8,0},{9,1},... | collective-permute-start | bytes 589832 | tf_op jit(solution)/shard_map/ppermute | solution.py:288
  37.0 7.9 %collective-permute-start.26 = (bf16[2,128,512]{2,1,0:T(8,128)(2,1)S(1)}, bf16[2,128,512]{2,1,0:T(8,128)(2,1)S(1)}, u32[]{:S(2)}, u32[]{:S(2)}) collective-permute-start(bf16[2,128,512]{2,1,0:T(8,128)(2,1)S(1)} %collective-permute-done.24.moved_ref.refs_5_), channel_id=1, source_target_pairs={{0,4},{1,3},{2,6},{3,1},{4,0},{5,7},{6,2},{7,5},{8,12},{9,11},{10,... | collective-permute-start | bytes 786440 | tf_op jit(solution)/shard_map/ppermute | solution.py:288
  38.0 6.1 %collective-permute-start.12 = (bf16[2,128,256]{2,1,0:T(8,128)(2,1)S(1)}, bf16[2,128,256]{2,1,0:T(8,128)(2,1)S(1)}, u32[]{:S(2)}, u32[]{:S(2)}) collective-permute-start(bf16[2,128,256]{2,1,0:T(8,128)(2,1)S(1)} %get-tuple-element.74), channel_id=1, source_target_pairs={{0,2},{1,5},{2,0},{3,7},{4,6},{5,1},{6,4},{7,3},{8,10},{9,13},{10,... | collective-permute-start | bytes 393224 | tf_op jit(solution)/shard_map/ppermute | solution.py:288
  44.7 9.4 %collective-permute-start.20 = (bf16[2,128,768]{2,1,0:T(8,128)(2,1)S(1)}, bf16[2,128,768]{2,1,0:T(8,128)(2,1)S(1)}, u32[]{:S(2)}, u32[]{:S(2)}) collective-permute-start(bf16[2,128,768]{2,1,0:T(8,128)(2,1)S(1)} %pack.7.own_ref.refs_4_), channel_id=1, source_target_pairs={{0,2},{1,5},{2,0},{3,7},{4,6},{5,1},{6,4},{7,3},{8,10},{9,13},{10,... | collective-permute-start | bytes 1179656 | tf_op jit(solution)/shard_map/ppermute | solution.py:288
  44.8 9.6 %collective-permute-start.27 = (bf16[4,128,512]{2,1,0:T(8,128)(2,1)S(1)}, bf16[4,128,512]{2,1,0:T(8,128)(2,1)S(1)}, u32[]{:S(2)}, u32[]{:S(2)}) collective-permute-start(bf16[4,128,512]{2,1,0:T(8,128)(2,1)S(1)} %pack.9), channel_id=1, source_target_pairs={{0,1},{1,0},{2,3},{3,2},{4,5},{5,4},{6,7},{7,6},{8,9},{9,8},{10,11... | collective-permute-start | bytes 1572872 | tf_op jit(solution)/shard_map/ppermute | solution.py:288
  45.0 9.5 %collective-permute-start.28 = (bf16[4,128,512]{2,1,0:T(8,128)(2,1)S(1)}, bf16[4,128,512]{2,1,0:T(8,128)(2,1)S(1)}, u32[]{:S(2)}, u32[]{:S(2)}) collective-permute-start(bf16[4,128,512]{2,1,0:T(8,128)(2,1)S(1)} %pack.10), channel_id=1, source_target_pairs={{0,1},{1,0},{2,3},{3,2},{4,5},{5,4},{6,7},{7,6},{8,9},{9,8},{10,11... | collective-permute-start | bytes 1572872 | tf_op jit(solution)/shard_map/ppermute | solution.py:288
  45.5 2.4 %collective-permute-start.15 = (bf16[256,512]{1,0:T(8,128)(2,1)S(1)}, bf16[256,512]{1,0:T(8,128)(2,1)S(1)}, u32[]{:S(2)}, u32[]{:S(2)}) collective-permute-start(bf16[256,512]{1,0:T(8,128)(2,1)S(1)} %get-tuple-element.55), channel_id=1, source_target_pairs={{0,1},{1,0},{2,3},{3,2},{4,5},{5,4},{6,7},{7,6},{8,9},{9,8},{10,11... | collective-permute-start | bytes 786440 | tf_op jit(solution)/shard_map/ppermute | solution.py:288
  45.6 8.8 %collective-permute-start.16 = (bf16[256,512]{1,0:T(8,128)(2,1)S(1)}, bf16[256,512]{1,0:T(8,128)(2,1)S(1)}, u32[]{:S(2)}, u32[]{:S(2)}) collective-permute-start(bf16[256,512]{1,0:T(8,128)(2,1)S(1)} %get-tuple-element.56), channel_id=1, source_target_pairs={{0,1},{1,0},{2,3},{3,2},{4,5},{5,4},{6,7},{7,6},{8,9},{9,8},{10,11... | collective-permute-start | bytes 786440 | tf_op jit(solution)/shard_map/ppermute | solution.py:288
  47.9 10.0 %collective-permute-start.21 = (bf16[2,128,768]{2,1,0:T(8,128)(2,1)S(1)}, bf16[2,128,768]{2,1,0:T(8,128)(2,1)S(1)}, u32[]{:S(2)}, u32[]{:S(2)}) collective-permute-start(bf16[2,128,768]{2,1,0:T(8,128)(2,1)S(1)} %pack.7.own_ref.refs_4_), channel_id=1, source_target_pairs={{0,4},{1,3},{2,6},{3,1},{4,0},{5,7},{6,2},{7,5},{8,12},{9,11},{10,... | collective-permute-start | bytes 1179656 | tf_op jit(solution)/shard_map/ppermute | solution.py:288
  54.1 10.0 %collective-permute-start.22 = (bf16[2,128,768]{2,1,0:T(8,128)(2,1)S(1)}, bf16[2,128,768]{2,1,0:T(8,128)(2,1)S(1)}, u32[]{:S(2)}, u32[]{:S(2)}) collective-permute-start(bf16[2,128,768]{2,1,0:T(8,128)(2,1)S(1)} %collective-permute-done.20.moved_ref.refs_5_), channel_id=1, source_target_pairs={{0,4},{1,3},{2,6},{3,1},{4,0},{5,7},{6,2},{7,5},{8,12},{9,11},{10,... | collective-permute-start | bytes 1179656 | tf_op jit(solution)/shard_map/ppermute | solution.py:288
  55.1 9.0 %collective-permute-start.29 = (bf16[256,384]{1,0:T(8,128)(2,1)S(1)}, bf16[256,384]{1,0:T(8,128)(2,1)S(1)}, u32[]{:S(2)}, u32[]{:S(2)}) collective-permute-start(bf16[256,384]{1,0:T(8,128)(2,1)S(1)} %get-tuple-element.60), channel_id=1, source_target_pairs={{0,16},{1,17},{2,18},{3,19},{4,20},{5,21},{6,22},{7,23},{8,24},{9,... | collective-permute-start | bytes 589832 | tf_op jit(solution)/shard_map/ppermute | solution.py:288
  57.9 8.5 %collective-permute-start.23 = (bf16[4,128,768]{2,1,0:T(8,128)(2,1)S(1)}, bf16[4,128,768]{2,1,0:T(8,128)(2,1)S(1)}, u32[]{:S(2)}, u32[]{:S(2)}) collective-permute-start(bf16[4,128,768]{2,1,0:T(8,128)(2,1)S(1)} %pack.8), channel_id=1, source_target_pairs={{0,1},{1,0},{2,3},{3,2},{4,5},{5,4},{6,7},{7,6},{8,9},{9,8},{10,11... | collective-permute-start | bytes 2359304 | tf_op jit(solution)/shard_map/ppermute | solution.py:288
  64.2 2.4 %collective-permute-start.30 = (bf16[4,128,768]{2,1,0:T(8,128)(2,1)S(1)}, bf16[4,128,768]{2,1,0:T(8,128)(2,1)S(1)}, u32[]{:S(2)}, u32[]{:S(2)}) collective-permute-start(bf16[4,128,768]{2,1,0:T(8,128)(2,1)S(1)} %pack.11), channel_id=1, source_target_pairs={{0,1},{1,0},{2,3},{3,2},{4,5},{5,4},{6,7},{7,6},{8,9},{9,8},{10,11... | collective-permute-start | bytes 2359304 | tf_op jit(solution)/shard_map/ppermute | solution.py:288
  64.3 7.3 %collective-permute-start.36 = (bf16[2,128,256]{2,1,0:T(8,128)(2,1)S(1)}, bf16[2,128,256]{2,1,0:T(8,128)(2,1)S(1)}, u32[]{:S(2)}, u32[]{:S(2)}) collective-permute-start(bf16[2,128,256]{2,1,0:T(8,128)(2,1)S(1)} %get-tuple-element.69), channel_id=1, source_target_pairs={{0,6},{1,7},{2,4},{3,5},{4,2},{5,3},{6,0},{7,1},{8,14},{9,15},{10,... | collective-permute-start | bytes 393224 | tf_op jit(solution)/shard_map/ppermute | solution.py:288
  64.8 8.9 %collective-permute-start.35 = (bf16[2,128,256]{2,1,0:T(8,128)(2,1)S(1)}, bf16[2,128,256]{2,1,0:T(8,128)(2,1)S(1)}, u32[]{:S(2)}, u32[]{:S(2)}) collective-permute-start(bf16[2,128,256]{2,1,0:T(8,128)(2,1)S(1)} %get-tuple-element.70), channel_id=1, source_target_pairs={{0,4},{1,3},{2,6},{3,1},{4,0},{5,7},{6,2},{7,5},{8,12},{9,11},{10,... | collective-permute-start | bytes 393224 | tf_op jit(solution)/shard_map/ppermute | solution.py:288
  67.5 23.7 %collective-permute-start.39 = (bf16[256,896]{1,0:T(8,128)(2,1)S(1)}, bf16[256,896]{1,0:T(8,128)(2,1)S(1)}, u32[]{:S(2)}, u32[]{:S(2)}) collective-permute-start(bf16[256,896]{1,0:T(8,128)(2,1)S(1)} %fold.5.refs_3_), channel_id=1, source_target_pairs={{0,16},{1,17},{2,18},{3,19},{4,20},{5,21},{6,22},{7,23},{8,24},{9,... | collective-permute-start | bytes 1376264 | tf_op jit(solution)/shard_map/ppermute | solution.py:288
  67.9 6.3 %collective-permute-start.34 = (bf16[2,128,256]{2,1,0:T(8,128)(2,1)S(1)}, bf16[2,128,256]{2,1,0:T(8,128)(2,1)S(1)}, u32[]{:S(2)}, u32[]{:S(2)}) collective-permute-start(bf16[2,128,256]{2,1,0:T(8,128)(2,1)S(1)} %get-tuple-element.71), channel_id=1, source_target_pairs={{0,2},{1,5},{2,0},{3,7},{4,6},{5,1},{6,4},{7,3},{8,10},{9,13},{10,... | collective-permute-start | bytes 393224 | tf_op jit(solution)/shard_map/ppermute | solution.py:288
  69.3 7.7 %collective-permute-start.31 = (bf16[2,128,256]{2,1,0:T(8,128)(2,1)S(1)}, bf16[2,128,256]{2,1,0:T(8,128)(2,1)S(1)}, u32[]{:S(2)}, u32[]{:S(2)}) collective-permute-start(bf16[2,128,256]{2,1,0:T(8,128)(2,1)S(1)} %get-tuple-element.62), channel_id=1, source_target_pairs={{0,2},{1,5},{2,0},{3,7},{4,6},{5,1},{6,4},{7,3},{8,10},{9,13},{10,... | collective-permute-start | bytes 393224 | tf_op jit(solution)/shard_map/ppermute | solution.py:288
  71.6 5.4 %collective-permute-start.32 = (bf16[2,128,256]{2,1,0:T(8,128)(2,1)S(1)}, bf16[2,128,256]{2,1,0:T(8,128)(2,1)S(1)}, u32[]{:S(2)}, u32[]{:S(2)}) collective-permute-start(bf16[2,128,256]{2,1,0:T(8,128)(2,1)S(1)} %get-tuple-element.63), channel_id=1, source_target_pairs={{0,4},{1,3},{2,6},{3,1},{4,0},{5,7},{6,2},{7,5},{8,12},{9,11},{10,... | collective-permute-start | bytes 393224 | tf_op jit(solution)/shard_map/ppermute | solution.py:288
  73.8 6.1 %collective-permute-start.33 = (bf16[2,128,256]{2,1,0:T(8,128)(2,1)S(1)}, bf16[2,128,256]{2,1,0:T(8,128)(2,1)S(1)}, u32[]{:S(2)}, u32[]{:S(2)}) collective-permute-start(bf16[2,128,256]{2,1,0:T(8,128)(2,1)S(1)} %get-tuple-element.64), channel_id=1, source_target_pairs={{0,6},{1,7},{2,4},{3,5},{4,2},{5,3},{6,0},{7,1},{8,14},{9,15},{10,... | collective-permute-start | bytes 393224 | tf_op jit(solution)/shard_map/ppermute | solution.py:288
  74.4 5.7 %collective-permute-start.38 = (bf16[256,512]{1,0:T(8,128)(2,1)S(1)}, bf16[256,512]{1,0:T(8,128)(2,1)S(1)}, u32[]{:S(2)}, u32[]{:S(2)}) collective-permute-start(bf16[256,512]{1,0:T(8,128)(2,1)S(1)} %get-tuple-element.68), channel_id=1, source_target_pairs={{0,1},{1,0},{2,3},{3,2},{4,5},{5,4},{6,7},{7,6},{8,9},{9,8},{10,11... | collective-permute-start | bytes 786440 | tf_op jit(solution)/shard_map/ppermute | solution.py:288
  80.0 1.6 %collective-permute-start.37 = (bf16[256,512]{1,0:T(8,128)(2,1)S(1)}, bf16[256,512]{1,0:T(8,128)(2,1)S(1)}, u32[]{:S(2)}, u32[]{:S(2)}) collective-permute-start(bf16[256,512]{1,0:T(8,128)(2,1)S(1)} %get-tuple-element.67), channel_id=1, source_target_pairs={{0,1},{1,0},{2,3},{3,2},{4,5},{5,4},{6,7},{7,6},{8,9},{9,8},{10,11... | collective-permute-start | bytes 786440 | tf_op jit(solution)/shard_map/ppermute | solution.py:288

commit v6 on v5

--- a/solution.py
+++ b/solution.py
@@ -314,7 +314,7 @@
     far, far_sib = turn([across] + [hop(across[i + 1], 0, c) for i, c in enumerate(chips)])
     away = [near, far, hop(near_sib, 0, SIBLING), hop(far_sib, 0, SIBLING)]
     first_cols = gather_pairs(lead, [near])
-    beyond = hop(hold([pieces[9]], [first_cols[0]])[0], 1, STAY)
+    beyond = hop(hold([pieces[9]], [near])[0], 1, STAY)
     held, send = merge(held, [hop(t, 0, c) for t, c in zip(send, chips)])
     rest, grad_kv = settle(grad_query, lead, held, [hop(send, 0, SIBLING)])
     first_folds = fold(away, first_cols, BF16, cuts=[384])

time: 92.6 us -> 92.1 us (level)
  starting transfers between devices: 35 us -> 33.4 us
  waiting for transfers between devices: 42.8 us -> 44 us
    ppermute x36, starting transfers between devices: 30.6 us -> 28.9 us  [hop(): return lax.ppermute(value, ('dp', 'ctx'), pairs)]
    ppermute x36, waiting for transfers between devices: 41.6 us -> 42.8 us  [hop(): return lax.ppermute(value, ('dp', 'ctx'), pairs)]
  transfers between devices with their start and end apart: 40 -> 40, of which waited for: 18 -> 20; matrix products, arithmetic and copies ran while one was open for 0% -> 0% of each run, Pallas kernels for 11% -> 11%
where the time goes in v6:
time: 92.1 us; the launch traced here: 92 us
  waiting for transfers between devices  44 us (48%)
  starting transfers between devices  33.4 us (36%)
  Pallas kernels  10.7 us (12%)
  local copies, waits for them, and re-layouts  1.67 us (2%)
  other arithmetic  1.26 us (1%)
    ppermute x36, waiting for transfers between devices, hop(): return lax.ppermute(value, ('dp', 'ctx'), pairs)  42.8 us
    ppermute x36, starting transfers between devices, hop(): return lax.ppermute(value, ('dp', 'ctx'), pairs)  28.9 us
    pallas_call x18, Pallas kernels, local_call(): pl.pallas_call(kernel, out_shape=out_shape, in_specs=specs, out_specs=jax...  5.11 us
    pallas_call x1, Pallas kernels, attention(): pl.pallas_call(functools.partial(attention_kernel, span=span, head=head,...  4.77 us
    ppermute x4, starting transfers between devices, shift(): return lax.ppermute(value, 'ctx', [(i, (i + by) % ctx) for i in range(ctx)])  4.42 us
  transfers between devices with their start and end apart: 40, of which 20 were waited for; matrix products, arithmetic and copies ran while one was open for 0% of the time, Pallas kernels for 11%

profile of v6, /device:TPU:0, one launch (start us, length us, event | category | flops | bytes accessed | tf_op | source)
XLA Modules:
  0.0 92.0 jit_solution(2989525328414416311)
XLA Ops:
  0.7 1.6 %copy-done = bf16[1,128,8192]{2,1,0:T(8,128)(2,1)S(1)} copy-done((bf16[1,128,8192]{2,1,0:T(8,128)(2,1)S(1)}, bf16[1,128,8192]{2,1,0:T(8,128)(2,1)}, u32[]{:S(2)}) %copy-start) | copy-done | bytes 2097176
  2.3 0.8 spread.1
  3.2 3.1 %collective-permute-start.11 = (bf16[4,2,128,256]{3,2,1,0:T(8,128)(2,1)S(1)}, bf16[4,2,128,256]{3,2,1,0:T(8,128)(2,1)S(1)}, u32[]{:S(2)}, u32[]{:S(2)}) collective-permute-start(bf16[4,2,128,256]{3,2,1,0:T(8,128)(2,1)S(1)} %get-tuple-element.53), channel_id=1, source_target_pairs={{0,8},{1,9},{2,10},{3,11},{4,12},{5,13},{6,14},{7,15},{8,0},{9,1},... | collective-permute-start | bytes 1572872 | tf_op jit(solution)/shard_map/ppermute | solution.py:288
  6.3 1.5 %collective-permute-start.2 = (bf16[128,256]{1,0:T(8,128)(2,1)S(1)}, bf16[128,256]{1,0:T(8,128)(2,1)S(1)}, u32[]{:S(2)}, u32[]{:S(2)}) collective-permute-start(bf16[128,256]{1,0:T(8,128)(2,1)S(1)} %bitcast.33), channel_id=1, source_target_pairs={{0,2},{1,3},{2,4},{3,5},{4,6},{5,7},{6,0},{7,1},{8,10},{9,11},{10,... | collective-permute-start | bytes 196616 | tf_op jit(solution)/shard_map/ppermute | solution.py:86
  7.8 2.4 %collective-permute-start.1 = (bf16[128,256]{1,0:T(8,128)(2,1)S(1)}, bf16[128,256]{1,0:T(8,128)(2,1)S(1)}, u32[]{:S(2)}, u32[]{:S(2)}) collective-permute-start(bf16[128,256]{1,0:T(8,128)(2,1)S(1)} %bitcast.34), channel_id=1, source_target_pairs={{0,3},{1,4},{2,5},{3,6},{4,7},{5,0},{6,1},{7,2},{8,11},{9,12},{10,... | collective-permute-start | bytes 196616 | tf_op jit(solution)/shard_map/ppermute | solution.py:86
  11.0 1.2 %collective-permute-start.8 = (bf16[2,128,256]{2,1,0:T(8,128)(2,1)S(1)}, bf16[2,128,256]{2,1,0:T(8,128)(2,1)S(1)}, u32[]{:S(2)}, u32[]{:S(2)}) collective-permute-start(bf16[2,128,256]{2,1,0:T(8,128)(2,1)S(1)} %get-tuple-element.49), channel_id=1, source_target_pairs={{0,2},{1,5},{2,0},{3,7},{4,6},{5,1},{6,4},{7,3},{8,10},{9,13},{10,... | collective-permute-start | bytes 393224 | tf_op jit(solution)/shard_map/ppermute | solution.py:288
  12.2 1.2 %collective-permute-start.9 = (bf16[2,128,256]{2,1,0:T(8,128)(2,1)S(1)}, bf16[2,128,256]{2,1,0:T(8,128)(2,1)S(1)}, u32[]{:S(2)}, u32[]{:S(2)}) collective-permute-start(bf16[2,128,256]{2,1,0:T(8,128)(2,1)S(1)} %get-tuple-element.50), channel_id=1, source_target_pairs={{0,4},{1,3},{2,6},{3,1},{4,0},{5,7},{6,2},{7,5},{8,12},{9,11},{10,... | collective-permute-start | bytes 393224 | tf_op jit(solution)/shard_map/ppermute | solution.py:288
  13.4 1.1 %collective-permute-start.10 = (bf16[2,128,256]{2,1,0:T(8,128)(2,1)S(1)}, bf16[2,128,256]{2,1,0:T(8,128)(2,1)S(1)}, u32[]{:S(2)}, u32[]{:S(2)}) collective-permute-start(bf16[2,128,256]{2,1,0:T(8,128)(2,1)S(1)} %get-tuple-element.51), channel_id=1, source_target_pairs={{0,6},{1,7},{2,4},{3,5},{4,2},{5,3},{6,0},{7,1},{8,14},{9,15},{10,... | collective-permute-start | bytes 393224 | tf_op jit(solution)/shard_map/ppermute | solution.py:288
  14.5 0.9 collective-permute-done.refs_0_
  15.4 4.8 %attention.1 = (bf16[128,1024]{1,0:T(8,128)(2,1)}, bf16[128,512]{1,0:T(8,128)(2,1)S(1)}, f32[2,128,256]{2,1,0:T(8,128)S(1)}, bf16[2,128,256]{2,1,0:T(8,128)(2,1)...) custom-call(s32[1]{0:T(128)} %bitcast.own_ref, s32[1,3]{1,0:T(1,128)S(1)} %copy-done.5, ...), custom_call_target="tpu_custom_call" | custom-call | flops 1006632960 | bytes 1441792 | tf_op jit(solution)/shard_map/attention/pallas_call | solution.py:102
  20.6 1.9 %collective-permute-start.4 = (bf16[2,128,256]{2,1,0:T(8,128)(2,1)S(1)}, bf16[2,128,256]{2,1,0:T(8,128)(2,1)S(1)}, u32[]{:S(2)}, u32[]{:S(2)}) collective-permute-start(bf16[2,128,256]{2,1,0:T(8,128)(2,1)S(1)} %get-tuple-element.38), channel_id=1, source_target_pairs={{0,2},{1,5},{2,0},{3,7},{4,6},{5,1},{6,4},{7,3},{8,10},{9,13},{10,... | collective-permute-start | bytes 393224 | tf_op jit(solution)/shard_map/ppermute | solution.py:288
  22.5 1.6 %collective-permute-start.6 = (bf16[2,128,256]{2,1,0:T(8,128)(2,1)S(1)}, bf16[2,128,256]{2,1,0:T(8,128)(2,1)S(1)}, u32[]{:S(2)}, u32[]{:S(2)}) collective-permute-start(bf16[2,128,256]{2,1,0:T(8,128)(2,1)S(1)} %get-tuple-element.40), channel_id=1, source_target_pairs={{0,6},{1,7},{2,4},{3,5},{4,2},{5,3},{6,0},{7,1},{8,14},{9,15},{10,... | collective-permute-start | bytes 393224 | tf_op jit(solution)/shard_map/ppermute | solution.py:288
  24.4 0.8 collective-permute-done.23
  25.2 0.9 collective-permute-start.18
  26.1 1.9 %collective-permute-start.24 = (bf16[2,128,512]{2,1,0:T(8,128)(2,1)S(1)}, bf16[2,128,512]{2,1,0:T(8,128)(2,1)S(1)}, u32[]{:S(2)}, u32[]{:S(2)}) collective-permute-start(bf16[2,128,512]{2,1,0:T(8,128)(2,1)S(1)} %pack.8.own_ref.refs_4_), channel_id=1, source_target_pairs={{0,2},{1,5},{2,0},{3,7},{4,6},{5,1},{6,4},{7,3},{8,10},{9,13},{10,... | collective-permute-start | bytes 786440 | tf_op jit(solution)/shard_map/ppermute | solution.py:288
  28.0 1.0 %collective-permute-start.14 = (bf16[2,128,256]{2,1,0:T(8,128)(2,1)S(1)}, bf16[2,128,256]{2,1,0:T(8,128)(2,1)S(1)}, u32[]{:S(2)}, u32[]{:S(2)}) collective-permute-start(bf16[2,128,256]{2,1,0:T(8,128)(2,1)S(1)} %get-tuple-element.72), channel_id=1, source_target_pairs={{0,6},{1,7},{2,4},{3,5},{4,2},{5,3},{6,0},{7,1},{8,14},{9,15},{10,... | collective-permute-start | bytes 393224 | tf_op jit(solution)/shard_map/ppermute | solution.py:288
  29.0 2.8 %collective-permute-done.5.refs_1_ = bf16[2,128,256]{2,1,0:T(8,128)(2,1)S(1)} collective-permute-done((bf16[2,128,256]{2,1,0:T(8,128)(2,1)S(1)}, bf16[2,128,256]{2,1,0:T(8,128)(2,1)S(1)}, u32[]{:S(2)}, u32[]{:S(2)}) %collective-permute-start.5) | collective-permute-done | bytes 131104 | tf_op jit(solution)/shard_map/ppermute | solution.py:288
  32.0 1.2 %collective-permute-done.7.refs_0_ = bf16[128,256]{1,0:T(8,128)(2,1)S(1)} collective-permute-done((bf16[128,256]{1,0:T(8,128)(2,1)S(1)}, bf16[128,256]{1,0:T(8,128)(2,1)S(1)}, u32[]{:S(2)}, u32[]{:S(2)}) %collective-permute-start.7) | collective-permute-done | bytes 65568 | tf_op jit(solution)/shard_map/ppermute | solution.py:288
  33.2 0.9 collective-permute-start.25
  34.1 0.7 settle.1
  34.7 1.6 %collective-permute-start.17 = (bf16[128,768]{1,0:T(8,128)(2,1)S(1)}, bf16[128,768]{1,0:T(8,128)(2,1)S(1)}, u32[]{:S(2)}, u32[]{:S(2)}) collective-permute-start(bf16[128,768]{1,0:T(8,128)(2,1)S(1)} %get-tuple-element.57), channel_id=1, source_target_pairs={{0,8},{1,9},{2,10},{3,11},{4,12},{5,13},{6,14},{7,15},{8,0},{9,1},... | collective-permute-start | bytes 589832 | tf_op jit(solution)/shard_map/ppermute | solution.py:288
  36.3 1.2 %collective-permute-done.14.refs_3_ = bf16[2,128,256]{2,1,0:T(8,128)(2,1)S(1)} collective-permute-done((bf16[2,128,256]{2,1,0:T(8,128)(2,1)S(1)}, bf16[2,128,256]{2,1,0:T(8,128)(2,1)S(1)}, u32[]{:S(2)}, u32[]{:S(2)}) %collective-permute-start.14) | collective-permute-done | bytes 131104 | tf_op jit(solution)/shard_map/ppermute | solution.py:288
  38.0 5.7 %collective-permute-done.12.refs_1_ = bf16[2,128,256]{2,1,0:T(8,128)(2,1)S(1)} collective-permute-done((bf16[2,128,256]{2,1,0:T(8,128)(2,1)S(1)}, bf16[2,128,256]{2,1,0:T(8,128)(2,1)S(1)}, u32[]{:S(2)}, u32[]{:S(2)}) %collective-permute-start.12) | collective-permute-done | bytes 131104 | tf_op jit(solution)/shard_map/ppermute | solution.py:288
  45.7 1.9 %collective-permute-done.15.refs_2_ = bf16[256,512]{1,0:T(8,128)(2,1)S(1)} collective-permute-done((bf16[256,512]{1,0:T(8,128)(2,1)S(1)}, bf16[256,512]{1,0:T(8,128)(2,1)S(1)}, u32[]{:S(2)}, u32[]{:S(2)}) %collective-permute-start.15) | collective-permute-done | bytes 262176 | tf_op jit(solution)/shard_map/ppermute | solution.py:288
  47.6 0.7 collective-permute-start.20
  48.4 4.8 %collective-permute-done.19.moved_ref.refs_5_ = bf16[2,128,768]{2,1,0:T(8,128)(2,1)S(1)} collective-permute-done((bf16[2,128,768]{2,1,0:T(8,128)(2,1)S(1)}, bf16[2,128,768]{2,1,0:T(8,128)(2,1)S(1)}, u32[]{:S(2)}, u32[]{:S(2)}) %collective-permute-start.19) | collective-permute-done | bytes 393248 | tf_op jit(solution)/shard_map/ppermute | solution.py:288
  53.1 1.4 %collective-permute-start.21 = (bf16[2,128,768]{2,1,0:T(8,128)(2,1)S(1)}, bf16[2,128,768]{2,1,0:T(8,128)(2,1)S(1)}, u32[]{:S(2)}, u32[]{:S(2)}) collective-permute-start(bf16[2,128,768]{2,1,0:T(8,128)(2,1)S(1)} %collective-permute-done.19.moved_ref.refs_5_), channel_id=1, source_target_pairs={{0,4},{1,3},{2,6},{3,1},{4,0},{5,7},{6,2},{7,5},{8,12},{9,11},{10,... | collective-permute-start | bytes 1179656 | tf_op jit(solution)/shard_map/ppermute | solution.py:288
  54.6 0.7 fold.4
  55.3 2.6 %collective-permute-start.29 = (bf16[256,384]{1,0:T(8,128)(2,1)S(1)}, bf16[256,384]{1,0:T(8,128)(2,1)S(1)}, u32[]{:S(2)}, u32[]{:S(2)}) collective-permute-start(bf16[256,384]{1,0:T(8,128)(2,1)S(1)} %get-tuple-element.60), channel_id=1, source_target_pairs={{0,16},{1,17},{2,18},{3,19},{4,20},{5,21},{6,22},{7,23},{8,24},{9,... | collective-permute-start | bytes 589832 | tf_op jit(solution)/shard_map/ppermute | solution.py:288
  58.1 5.9 %collective-permute-done.29.refs_0_ = bf16[256,384]{1,0:T(8,128)(2,1)S(1)} collective-permute-done((bf16[256,384]{1,0:T(8,128)(2,1)S(1)}, bf16[256,384]{1,0:T(8,128)(2,1)S(1)}, u32[]{:S(2)}, u32[]{:S(2)}) %collective-permute-start.29) | collective-permute-done | bytes 196640 | tf_op jit(solution)/shard_map/ppermute | solution.py:288
  64.2 0.6 collective-permute-start.36
  64.8 0.9 %collective-permute-start.35 = (bf16[2,128,256]{2,1,0:T(8,128)(2,1)S(1)}, bf16[2,128,256]{2,1,0:T(8,128)(2,1)S(1)}, u32[]{:S(2)}, u32[]{:S(2)}) collective-permute-start(bf16[2,128,256]{2,1,0:T(8,128)(2,1)S(1)} %get-tuple-element.70), channel_id=1, source_target_pairs={{0,4},{1,3},{2,6},{3,1},{4,0},{5,7},{6,2},{7,5},{8,12},{9,11},{10,... | collective-permute-start | bytes 393224 | tf_op jit(solution)/shard_map/ppermute | solution.py:288
  65.8 0.7 collective-permute-done.30.refs_9_
  66.4 1.0 %fold.5.refs_3_ = bf16[256,896]{1,0:T(8,128)(2,1)S(1)} custom-call(bf16[256,512]{1,0:T(8,128)(2,1)S(1)} %get-tuple-element.52.refs_1_.refs_0_, bf16[256,512]{1,0:T(8,128)(2,1)S(1)} %get-tuple-element.54.refs_0_.refs_1_, bf16[256,512]{1,0:T(8,128)(2,1)S(1)} %collective-permute-done.15.refs_2_, bf16[256,512]{1,0:T(8,128)(2,1)S(1)} %collective-permute-done.16.refs_3_, ...), custom_call_target="tpu_custom_call" | custom-call | tf_op jit(solution)/shard_map/fold/pallas_call | solution.py:160
  67.4 0.6 collective-permute-start.39
  68.1 1.3 %collective-permute-start.34 = (bf16[2,128,256]{2,1,0:T(8,128)(2,1)S(1)}, bf16[2,128,256]{2,1,0:T(8,128)(2,1)S(1)}, u32[]{:S(2)}, u32[]{:S(2)}) collective-permute-start(bf16[2,128,256]{2,1,0:T(8,128)(2,1)S(1)} %get-tuple-element.71), channel_id=1, source_target_pairs={{0,2},{1,5},{2,0},{3,7},{4,6},{5,1},{6,4},{7,3},{8,10},{9,13},{10,... | collective-permute-start | bytes 393224 | tf_op jit(solution)/shard_map/ppermute | solution.py:288
  69.4 0.8 collective-permute-start.31
  70.2 1.3 %collective-permute-done.36.refs_3_ = bf16[2,128,256]{2,1,0:T(8,128)(2,1)S(1)} collective-permute-done((bf16[2,128,256]{2,1,0:T(8,128)(2,1)S(1)}, bf16[2,128,256]{2,1,0:T(8,128)(2,1)S(1)}, u32[]{:S(2)}, u32[]{:S(2)}) %collective-permute-start.36) | collective-permute-done | bytes 131104 | tf_op jit(solution)/shard_map/ppermute | solution.py:288
  71.5 0.6 collective-permute-start.32
  72.1 1.6 %collective-permute-done.35.refs_2_ = bf16[2,128,256]{2,1,0:T(8,128)(2,1)S(1)} collective-permute-done((bf16[2,128,256]{2,1,0:T(8,128)(2,1)S(1)}, bf16[2,128,256]{2,1,0:T(8,128)(2,1)S(1)}, u32[]{:S(2)}, u32[]{:S(2)}) %collective-permute-start.35) | collective-permute-done | bytes 131104 | tf_op jit(solution)/shard_map/ppermute | solution.py:288
  74.6 0.8 collective-permute-done.31.refs_1_
  75.5 1.6 %collective-permute-done.32.refs_2_ = bf16[2,128,256]{2,1,0:T(8,128)(2,1)S(1)} collective-permute-done((bf16[2,128,256]{2,1,0:T(8,128)(2,1)S(1)}, bf16[2,128,256]{2,1,0:T(8,128)(2,1)S(1)}, u32[]{:S(2)}, u32[]{:S(2)}) %collective-permute-start.32) | collective-permute-done | bytes 131104 | tf_op jit(solution)/shard_map/ppermute | solution.py:288
  77.0 2.6 %collective-permute-done.33.refs_3_ = bf16[2,128,256]{2,1,0:T(8,128)(2,1)S(1)} collective-permute-done((bf16[2,128,256]{2,1,0:T(8,128)(2,1)S(1)}, bf16[2,128,256]{2,1,0:T(8,128)(2,1)S(1)}, u32[]{:S(2)}, u32[]{:S(2)}) %collective-permute-start.33) | collective-permute-done | bytes 131104 | tf_op jit(solution)/shard_map/ppermute | solution.py:288
  79.9 1.5 %collective-permute-done.37.refs_2_ = bf16[256,512]{1,0:T(8,128)(2,1)S(1)} collective-permute-done((bf16[256,512]{1,0:T(8,128)(2,1)S(1)}, bf16[256,512]{1,0:T(8,128)(2,1)S(1)}, u32[]{:S(2)}, u32[]{:S(2)}) %collective-permute-start.37) | collective-permute-done | bytes 262176 | tf_op jit(solution)/shard_map/ppermute | solution.py:288
  81.4 1.0 %fold.7 = f32[256,768]{1,0:T(8,128)S(1)} custom-call(bf16[256,512]{1,0:T(8,128)(2,1)S(1)} %get-tuple-element.65.refs_0_, bf16[256,512]{1,0:T(8,128)(2,1)S(1)} %get-tuple-element.66.refs_1_, bf16[256,512]{1,0:T(8,128)(2,1)S(1)} %collective-permute-done.37.refs_2_, bf16[256,512]{1,0:T(8,128)(2,1)S(1)} %collective-permute-done.38.refs_3_, ...), custom_call_target="tpu_custom_call" | custom-call | tf_op jit(solution)/shard_map/fold/pallas_call | solution.py:160
  82.4 0.7 fold.6
  83.1 7.7 %collective-permute-done.39 = bf16[256,896]{1,0:T(8,128)(2,1)S(1)} collective-permute-done((bf16[256,896]{1,0:T(8,128)(2,1)S(1)}, bf16[256,896]{1,0:T(8,128)(2,1)S(1)}, u32[]{:S(2)}, u32[]{:S(2)}) %collective-permute-start.39) | collective-permute-done | bytes 458784 | tf_op jit(solution)/shard_map/ppermute | solution.py:288
  90.8 1.2 %maximum_add_fusion = f32[256,1280]{1,0:T(8,128)} fusion(f32[256,768]{1,0:T(8,128)S(1)} %fold.7, f32[256,512]{1,0:T(8,128)S(1)} %fold.6, bf16[256,896]{1,0:T(8,128)(2,1)S(1)} %collective-permute-done.39, bf16[256,384]{1,0:T(8,128)(2,1)S(1)} %collective-permute-done.29.refs_0_), kind=kLoop, calls=%fused_computation | loop fusion | flops 1966080 | bytes 3276800 | tf_op jit(solution)/shard_map/add | solution.py:334
  (68 shorter events, 5.9 us)
Async XLA Ops:
  0.6 14.8 %copy-start.5 = (s32[1,3]{1,0:T(1,128)S(1)}, s32[1,3]{1,0:T(1,128)}, u32[]{:S(2)}) copy-start(s32[1,3]{1,0:T(1,128)} %lens_ref.1) | copy-start | bytes 40
  0.7 1.6 %copy-start = (bf16[1,128,8192]{2,1,0:T(8,128)(2,1)S(1)}, bf16[1,128,8192]{2,1,0:T(8,128)(2,1)}, u32[]{:S(2)}) copy-start(bf16[1,128,8192]{2,1,0:T(8,128)(2,1)} %param.5) | copy-start | bytes 6291460
  2.3 3.9 %copy-start.4 = (bf16[1,128,256]{2,1,0:T(8,128)(2,1)S(1)}, bf16[1,128,256]{2,1,0:T(8,128)(2,1)}, u32[]{:S(2)}) copy-start(bf16[1,128,256]{2,1,0:T(8,128)(2,1)} %param.7) | copy-start | bytes 196612
  2.3 13.1 %copy-start.2 = (bf16[1,128,1024]{2,1,0:T(8,128)(2,1)S(1)}, bf16[1,128,1024]{2,1,0:T(8,128)(2,1)}, u32[]{:S(2)}) copy-start(bf16[1,128,1024]{2,1,0:T(8,128)(2,1)} %param.6) | copy-start | bytes 786436
  2.3 13.1 %copy-start.3 = (bf16[1,128,1024]{2,1,0:T(8,128)(2,1)S(1)}, bf16[1,128,1024]{2,1,0:T(8,128)(2,1)}, u32[]{:S(2)}) copy-start(bf16[1,128,1024]{2,1,0:T(8,128)(2,1)} %param.8) | copy-start | bytes 786436
  3.2 22.9 %collective-permute-start.11 = (bf16[4,2,128,256]{3,2,1,0:T(8,128)(2,1)S(1)}, bf16[4,2,128,256]{3,2,1,0:T(8,128)(2,1)S(1)}, u32[]{:S(2)}, u32[]{:S(2)}) collective-permute-start(bf16[4,2,128,256]{3,2,1,0:T(8,128)(2,1)S(1)} %get-tuple-element.53), channel_id=1, source_target_pairs={{0,8},{1,9},{2,10},{3,11},{4,12},{5,13},{6,14},{7,15},{8,0},{9,1},... | collective-permute-start | bytes 1572872 | tf_op jit(solution)/shard_map/ppermute | solution.py:288
  6.3 4.8 %collective-permute-start.3 = (bf16[128,256]{1,0:T(8,128)(2,1)S(1)}, bf16[128,256]{1,0:T(8,128)(2,1)S(1)}, u32[]{:S(2)}, u32[]{:S(2)}) collective-permute-start(bf16[128,256]{1,0:T(8,128)(2,1)S(1)} %bitcast.32), channel_id=1, source_target_pairs={{0,1},{1,2},{2,3},{3,4},{4,5},{5,6},{6,7},{7,0},{8,9},{9,10},{10,1... | collective-permute-start | bytes 196616 | tf_op jit(solution)/shard_map/ppermute | solution.py:86
  6.3 5.9 %collective-permute-start.2 = (bf16[128,256]{1,0:T(8,128)(2,1)S(1)}, bf16[128,256]{1,0:T(8,128)(2,1)S(1)}, u32[]{:S(2)}, u32[]{:S(2)}) collective-permute-start(bf16[128,256]{1,0:T(8,128)(2,1)S(1)} %bitcast.33), channel_id=1, source_target_pairs={{0,2},{1,3},{2,4},{3,5},{4,6},{5,7},{6,0},{7,1},{8,10},{9,11},{10,... | collective-permute-start | bytes 196616 | tf_op jit(solution)/shard_map/ppermute | solution.py:86
  7.8 5.6 %collective-permute-start.1 = (bf16[128,256]{1,0:T(8,128)(2,1)S(1)}, bf16[128,256]{1,0:T(8,128)(2,1)S(1)}, u32[]{:S(2)}, u32[]{:S(2)}) collective-permute-start(bf16[128,256]{1,0:T(8,128)(2,1)S(1)} %bitcast.34), channel_id=1, source_target_pairs={{0,3},{1,4},{2,5},{3,6},{4,7},{5,0},{6,1},{7,2},{8,11},{9,12},{10,... | collective-permute-start | bytes 196616 | tf_op jit(solution)/shard_map/ppermute | solution.py:86
  10.2 5.2 %collective-permute-start = (bf16[128,256]{1,0:T(8,128)(2,1)S(1)}, bf16[128,256]{1,0:T(8,128)(2,1)S(1)}, u32[]{:S(2)}, u32[]{:S(2)}) collective-permute-start(bf16[128,256]{1,0:T(8,128)(2,1)S(1)} %bitcast.35), channel_id=1, source_target_pairs={{0,4},{1,5},{2,6},{3,7},{4,0},{5,1},{6,2},{7,3},{8,12},{9,13},{10,... | collective-permute-start | bytes 196616 | tf_op jit(solution)/shard_map/ppermute | solution.py:86
  11.0 9.6 %collective-permute-start.8 = (bf16[2,128,256]{2,1,0:T(8,128)(2,1)S(1)}, bf16[2,128,256]{2,1,0:T(8,128)(2,1)S(1)}, u32[]{:S(2)}, u32[]{:S(2)}) collective-permute-start(bf16[2,128,256]{2,1,0:T(8,128)(2,1)S(1)} %get-tuple-element.49), channel_id=1, source_target_pairs={{0,2},{1,5},{2,0},{3,7},{4,6},{5,1},{6,4},{7,3},{8,10},{9,13},{10,... | collective-permute-start | bytes 393224 | tf_op jit(solution)/shard_map/ppermute | solution.py:288
  12.2 10.3 %collective-permute-start.9 = (bf16[2,128,256]{2,1,0:T(8,128)(2,1)S(1)}, bf16[2,128,256]{2,1,0:T(8,128)(2,1)S(1)}, u32[]{:S(2)}, u32[]{:S(2)}) collective-permute-start(bf16[2,128,256]{2,1,0:T(8,128)(2,1)S(1)} %get-tuple-element.50), channel_id=1, source_target_pairs={{0,4},{1,3},{2,6},{3,1},{4,0},{5,7},{6,2},{7,5},{8,12},{9,11},{10,... | collective-permute-start | bytes 393224 | tf_op jit(solution)/shard_map/ppermute | solution.py:288
  13.4 9.1 %collective-permute-start.10 = (bf16[2,128,256]{2,1,0:T(8,128)(2,1)S(1)}, bf16[2,128,256]{2,1,0:T(8,128)(2,1)S(1)}, u32[]{:S(2)}, u32[]{:S(2)}) collective-permute-start(bf16[2,128,256]{2,1,0:T(8,128)(2,1)S(1)} %get-tuple-element.51), channel_id=1, source_target_pairs={{0,6},{1,7},{2,4},{3,5},{4,2},{5,3},{6,0},{7,1},{8,14},{9,15},{10,... | collective-permute-start | bytes 393224 | tf_op jit(solution)/shard_map/ppermute | solution.py:288
  20.2 5.0 %collective-permute-start.23 = (bf16[128,512]{1,0:T(8,128)(2,1)S(1)}, bf16[128,512]{1,0:T(8,128)(2,1)S(1)}, u32[]{:S(2)}, u32[]{:S(2)}) collective-permute-start(bf16[128,512]{1,0:T(8,128)(2,1)S(1)} %get-tuple-element.59), channel_id=1, source_target_pairs={{0,8},{1,9},{2,10},{3,11},{4,12},{5,13},{6,14},{7,15},{8,0},{9,1},... | collective-permute-start | bytes 393224 | tf_op jit(solution)/shard_map/ppermute | solution.py:288
  20.6 7.4 %collective-permute-start.4 = (bf16[2,128,256]{2,1,0:T(8,128)(2,1)S(1)}, bf16[2,128,256]{2,1,0:T(8,128)(2,1)S(1)}, u32[]{:S(2)}, u32[]{:S(2)}) collective-permute-start(bf16[2,128,256]{2,1,0:T(8,128)(2,1)S(1)} %get-tuple-element.38), channel_id=1, source_target_pairs={{0,2},{1,5},{2,0},{3,7},{4,6},{5,1},{6,4},{7,3},{8,10},{9,13},{10,... | collective-permute-start | bytes 393224 | tf_op jit(solution)/shard_map/ppermute | solution.py:288
  22.5 9.3 %collective-permute-start.5 = (bf16[2,128,256]{2,1,0:T(8,128)(2,1)S(1)}, bf16[2,128,256]{2,1,0:T(8,128)(2,1)S(1)}, u32[]{:S(2)}, u32[]{:S(2)}) collective-permute-start(bf16[2,128,256]{2,1,0:T(8,128)(2,1)S(1)} %get-tuple-element.39), channel_id=1, source_target_pairs={{0,4},{1,3},{2,6},{3,1},{4,0},{5,7},{6,2},{7,5},{8,12},{9,11},{10,... | collective-permute-start | bytes 393224 | tf_op jit(solution)/shard_map/ppermute | solution.py:288
  22.5 9.3 %collective-permute-start.6 = (bf16[2,128,256]{2,1,0:T(8,128)(2,1)S(1)}, bf16[2,128,256]{2,1,0:T(8,128)(2,1)S(1)}, u32[]{:S(2)}, u32[]{:S(2)}) collective-permute-start(bf16[2,128,256]{2,1,0:T(8,128)(2,1)S(1)} %get-tuple-element.40), channel_id=1, source_target_pairs={{0,6},{1,7},{2,4},{3,5},{4,2},{5,3},{6,0},{7,1},{8,14},{9,15},{10,... | collective-permute-start | bytes 393224 | tf_op jit(solution)/shard_map/ppermute | solution.py:288
  24.4 9.7 %copy-start.1 = (bf16[128,1024]{1,0:T(8,128)(2,1)S(1)}, bf16[128,1024]{1,0:T(8,128)(2,1)}, u32[]{:S(2)}) copy-start(bf16[128,1024]{1,0:T(8,128)(2,1)} %get-tuple-element.36.gq_ref) | copy-start | bytes 786436
  25.2 18.8 %collective-permute-start.18 = (bf16[4,2,128,256]{3,2,1,0:T(8,128)(2,1)S(1)}, bf16[4,2,128,256]{3,2,1,0:T(8,128)(2,1)S(1)}, u32[]{:S(2)}, u32[]{:S(2)}) collective-permute-start(bf16[4,2,128,256]{3,2,1,0:T(8,128)(2,1)S(1)} %hold.2), channel_id=1, source_target_pairs={{0,8},{1,9},{2,10},{3,11},{4,12},{5,13},{6,14},{7,15},{8,0},{9,1},... | collective-permute-start | bytes 1572872 | tf_op jit(solution)/shard_map/ppermute | solution.py:288
  26.1 8.7 %collective-permute-start.24 = (bf16[2,128,512]{2,1,0:T(8,128)(2,1)S(1)}, bf16[2,128,512]{2,1,0:T(8,128)(2,1)S(1)}, u32[]{:S(2)}, u32[]{:S(2)}) collective-permute-start(bf16[2,128,512]{2,1,0:T(8,128)(2,1)S(1)} %pack.8.own_ref.refs_4_), channel_id=1, source_target_pairs={{0,2},{1,5},{2,0},{3,7},{4,6},{5,1},{6,4},{7,3},{8,10},{9,13},{10,... | collective-permute-start | bytes 786440 | tf_op jit(solution)/shard_map/ppermute | solution.py:288
  28.0 9.5 %collective-permute-start.14 = (bf16[2,128,256]{2,1,0:T(8,128)(2,1)S(1)}, bf16[2,128,256]{2,1,0:T(8,128)(2,1)S(1)}, u32[]{:S(2)}, u32[]{:S(2)}) collective-permute-start(bf16[2,128,256]{2,1,0:T(8,128)(2,1)S(1)} %get-tuple-element.72), channel_id=1, source_target_pairs={{0,6},{1,7},{2,4},{3,5},{4,2},{5,3},{6,0},{7,1},{8,14},{9,15},{10,... | collective-permute-start | bytes 393224 | tf_op jit(solution)/shard_map/ppermute | solution.py:288
  31.9 1.3 %collective-permute-start.7 = (bf16[128,256]{1,0:T(8,128)(2,1)S(1)}, bf16[128,256]{1,0:T(8,128)(2,1)S(1)}, u32[]{:S(2)}, u32[]{:S(2)}) collective-permute-start(bf16[128,256]{1,0:T(8,128)(2,1)S(1)} %get-tuple-element.42), channel_id=1, source_target_pairs={{0,1},{1,0},{2,3},{3,2},{4,5},{5,4},{6,7},{7,6},{8,9},{9,8},{10,11... | collective-permute-start | bytes 196616 | tf_op jit(solution)/shard_map/ppermute | solution.py:288
  32.0 6.0 %collective-permute-start.13 = (bf16[2,128,256]{2,1,0:T(8,128)(2,1)S(1)}, bf16[2,128,256]{2,1,0:T(8,128)(2,1)S(1)}, u32[]{:S(2)}, u32[]{:S(2)}) collective-permute-start(bf16[2,128,256]{2,1,0:T(8,128)(2,1)S(1)} %get-tuple-element.73), channel_id=1, source_target_pairs={{0,4},{1,3},{2,6},{3,1},{4,0},{5,7},{6,2},{7,5},{8,12},{9,11},{10,... | collective-permute-start | bytes 393224 | tf_op jit(solution)/shard_map/ppermute | solution.py:288
  33.2 11.4 %collective-permute-start.25 = (bf16[2,128,512]{2,1,0:T(8,128)(2,1)S(1)}, bf16[2,128,512]{2,1,0:T(8,128)(2,1)S(1)}, u32[]{:S(2)}, u32[]{:S(2)}) collective-permute-start(bf16[2,128,512]{2,1,0:T(8,128)(2,1)S(1)} %pack.8.own_ref.refs_4_), channel_id=1, source_target_pairs={{0,4},{1,3},{2,6},{3,1},{4,0},{5,7},{6,2},{7,5},{8,12},{9,11},{10,... | collective-permute-start | bytes 786440 | tf_op jit(solution)/shard_map/ppermute | solution.py:288
  34.7 9.2 %collective-permute-start.17 = (bf16[128,768]{1,0:T(8,128)(2,1)S(1)}, bf16[128,768]{1,0:T(8,128)(2,1)S(1)}, u32[]{:S(2)}, u32[]{:S(2)}) collective-permute-start(bf16[128,768]{1,0:T(8,128)(2,1)S(1)} %get-tuple-element.57), channel_id=1, source_target_pairs={{0,8},{1,9},{2,10},{3,11},{4,12},{5,13},{6,14},{7,15},{8,0},{9,1},... | collective-permute-start | bytes 589832 | tf_op jit(solution)/shard_map/ppermute | solution.py:288
  37.5 7.5 %collective-permute-start.26 = (bf16[2,128,512]{2,1,0:T(8,128)(2,1)S(1)}, bf16[2,128,512]{2,1,0:T(8,128)(2,1)S(1)}, u32[]{:S(2)}, u32[]{:S(2)}) collective-permute-start(bf16[2,128,512]{2,1,0:T(8,128)(2,1)S(1)} %collective-permute-done.24.moved_ref.refs_5_), channel_id=1, source_target_pairs={{0,4},{1,3},{2,6},{3,1},{4,0},{5,7},{6,2},{7,5},{8,12},{9,11},{10,... | collective-permute-start | bytes 786440 | tf_op jit(solution)/shard_map/ppermute | solution.py:288
  38.0 5.7 %collective-permute-start.12 = (bf16[2,128,256]{2,1,0:T(8,128)(2,1)S(1)}, bf16[2,128,256]{2,1,0:T(8,128)(2,1)S(1)}, u32[]{:S(2)}, u32[]{:S(2)}) collective-permute-start(bf16[2,128,256]{2,1,0:T(8,128)(2,1)S(1)} %get-tuple-element.74), channel_id=1, source_target_pairs={{0,2},{1,5},{2,0},{3,7},{4,6},{5,1},{6,4},{7,3},{8,10},{9,13},{10,... | collective-permute-start | bytes 393224 | tf_op jit(solution)/shard_map/ppermute | solution.py:288
  44.0 9.2 %collective-permute-start.19 = (bf16[2,128,768]{2,1,0:T(8,128)(2,1)S(1)}, bf16[2,128,768]{2,1,0:T(8,128)(2,1)S(1)}, u32[]{:S(2)}, u32[]{:S(2)}) collective-permute-start(bf16[2,128,768]{2,1,0:T(8,128)(2,1)S(1)} %pack.6.own_ref.refs_4_), channel_id=1, source_target_pairs={{0,2},{1,5},{2,0},{3,7},{4,6},{5,1},{6,4},{7,3},{8,10},{9,13},{10,... | collective-permute-start | bytes 1179656 | tf_op jit(solution)/shard_map/ppermute | solution.py:288
  44.5 10.0 %collective-permute-start.27 = (bf16[4,128,512]{2,1,0:T(8,128)(2,1)S(1)}, bf16[4,128,512]{2,1,0:T(8,128)(2,1)S(1)}, u32[]{:S(2)}, u32[]{:S(2)}) collective-permute-start(bf16[4,128,512]{2,1,0:T(8,128)(2,1)S(1)} %pack.9), channel_id=1, source_target_pairs={{0,1},{1,0},{2,3},{3,2},{4,5},{5,4},{6,7},{7,6},{8,9},{9,8},{10,11... | collective-permute-start | bytes 1572872 | tf_op jit(solution)/shard_map/ppermute | solution.py:288
  45.0 9.5 %collective-permute-start.28 = (bf16[4,128,512]{2,1,0:T(8,128)(2,1)S(1)}, bf16[4,128,512]{2,1,0:T(8,128)(2,1)S(1)}, u32[]{:S(2)}, u32[]{:S(2)}) collective-permute-start(bf16[4,128,512]{2,1,0:T(8,128)(2,1)S(1)} %pack.10), channel_id=1, source_target_pairs={{0,1},{1,0},{2,3},{3,2},{4,5},{5,4},{6,7},{7,6},{8,9},{9,8},{10,11... | collective-permute-start | bytes 1572872 | tf_op jit(solution)/shard_map/ppermute | solution.py:288
  45.2 2.4 %collective-permute-start.15 = (bf16[256,512]{1,0:T(8,128)(2,1)S(1)}, bf16[256,512]{1,0:T(8,128)(2,1)S(1)}, u32[]{:S(2)}, u32[]{:S(2)}) collective-permute-start(bf16[256,512]{1,0:T(8,128)(2,1)S(1)} %get-tuple-element.55), channel_id=1, source_target_pairs={{0,1},{1,0},{2,3},{3,2},{4,5},{5,4},{6,7},{7,6},{8,9},{9,8},{10,11... | collective-permute-start | bytes 786440 | tf_op jit(solution)/shard_map/ppermute | solution.py:288
  45.6 9.0 %collective-permute-start.16 = (bf16[256,512]{1,0:T(8,128)(2,1)S(1)}, bf16[256,512]{1,0:T(8,128)(2,1)S(1)}, u32[]{:S(2)}, u32[]{:S(2)}) collective-permute-start(bf16[256,512]{1,0:T(8,128)(2,1)S(1)} %get-tuple-element.56), channel_id=1, source_target_pairs={{0,1},{1,0},{2,3},{3,2},{4,5},{5,4},{6,7},{7,6},{8,9},{9,8},{10,11... | collective-permute-start | bytes 786440 | tf_op jit(solution)/shard_map/ppermute | solution.py:288
  47.6 10.4 %collective-permute-start.20 = (bf16[2,128,768]{2,1,0:T(8,128)(2,1)S(1)}, bf16[2,128,768]{2,1,0:T(8,128)(2,1)S(1)}, u32[]{:S(2)}, u32[]{:S(2)}) collective-permute-start(bf16[2,128,768]{2,1,0:T(8,128)(2,1)S(1)} %pack.6.own_ref.refs_4_), channel_id=1, source_target_pairs={{0,4},{1,3},{2,6},{3,1},{4,0},{5,7},{6,2},{7,5},{8,12},{9,11},{10,... | collective-permute-start | bytes 1179656 | tf_op jit(solution)/shard_map/ppermute | solution.py:288
  53.1 10.9 %collective-permute-start.21 = (bf16[2,128,768]{2,1,0:T(8,128)(2,1)S(1)}, bf16[2,128,768]{2,1,0:T(8,128)(2,1)S(1)}, u32[]{:S(2)}, u32[]{:S(2)}) collective-permute-start(bf16[2,128,768]{2,1,0:T(8,128)(2,1)S(1)} %collective-permute-done.19.moved_ref.refs_5_), channel_id=1, source_target_pairs={{0,4},{1,3},{2,6},{3,1},{4,0},{5,7},{6,2},{7,5},{8,12},{9,11},{10,... | collective-permute-start | bytes 1179656 | tf_op jit(solution)/shard_map/ppermute | solution.py:288
  55.3 8.7 %collective-permute-start.29 = (bf16[256,384]{1,0:T(8,128)(2,1)S(1)}, bf16[256,384]{1,0:T(8,128)(2,1)S(1)}, u32[]{:S(2)}, u32[]{:S(2)}) collective-permute-start(bf16[256,384]{1,0:T(8,128)(2,1)S(1)} %get-tuple-element.60), channel_id=1, source_target_pairs={{0,16},{1,17},{2,18},{3,19},{4,20},{5,21},{6,22},{7,23},{8,24},{9,... | collective-permute-start | bytes 589832 | tf_op jit(solution)/shard_map/ppermute | solution.py:288
  58.0 7.8 %collective-permute-start.22 = (bf16[4,128,768]{2,1,0:T(8,128)(2,1)S(1)}, bf16[4,128,768]{2,1,0:T(8,128)(2,1)S(1)}, u32[]{:S(2)}, u32[]{:S(2)}) collective-permute-start(bf16[4,128,768]{2,1,0:T(8,128)(2,1)S(1)} %pack.7), channel_id=1, source_target_pairs={{0,1},{1,0},{2,3},{3,2},{4,5},{5,4},{6,7},{7,6},{8,9},{9,8},{10,11... | collective-permute-start | bytes 2359304 | tf_op jit(solution)/shard_map/ppermute | solution.py:288
  64.1 2.4 %collective-permute-start.30 = (bf16[4,128,768]{2,1,0:T(8,128)(2,1)S(1)}, bf16[4,128,768]{2,1,0:T(8,128)(2,1)S(1)}, u32[]{:S(2)}, u32[]{:S(2)}) collective-permute-start(bf16[4,128,768]{2,1,0:T(8,128)(2,1)S(1)} %pack.11), channel_id=1, source_target_pairs={{0,1},{1,0},{2,3},{3,2},{4,5},{5,4},{6,7},{7,6},{8,9},{9,8},{10,11... | collective-permute-start | bytes 2359304 | tf_op jit(solution)/shard_map/ppermute | solution.py:288
  64.2 7.3 %collective-permute-start.36 = (bf16[2,128,256]{2,1,0:T(8,128)(2,1)S(1)}, bf16[2,128,256]{2,1,0:T(8,128)(2,1)S(1)}, u32[]{:S(2)}, u32[]{:S(2)}) collective-permute-start(bf16[2,128,256]{2,1,0:T(8,128)(2,1)S(1)} %get-tuple-element.69), channel_id=1, source_target_pairs={{0,6},{1,7},{2,4},{3,5},{4,2},{5,3},{6,0},{7,1},{8,14},{9,15},{10,... | collective-permute-start | bytes 393224 | tf_op jit(solution)/shard_map/ppermute | solution.py:288
  64.8 8.9 %collective-permute-start.35 = (bf16[2,128,256]{2,1,0:T(8,128)(2,1)S(1)}, bf16[2,128,256]{2,1,0:T(8,128)(2,1)S(1)}, u32[]{:S(2)}, u32[]{:S(2)}) collective-permute-start(bf16[2,128,256]{2,1,0:T(8,128)(2,1)S(1)} %get-tuple-element.70), channel_id=1, source_target_pairs={{0,4},{1,3},{2,6},{3,1},{4,0},{5,7},{6,2},{7,5},{8,12},{9,11},{10,... | collective-permute-start | bytes 393224 | tf_op jit(solution)/shard_map/ppermute | solution.py:288
  67.4 23.4 %collective-permute-start.39 = (bf16[256,896]{1,0:T(8,128)(2,1)S(1)}, bf16[256,896]{1,0:T(8,128)(2,1)S(1)}, u32[]{:S(2)}, u32[]{:S(2)}) collective-permute-start(bf16[256,896]{1,0:T(8,128)(2,1)S(1)} %fold.5.refs_3_), channel_id=1, source_target_pairs={{0,16},{1,17},{2,18},{3,19},{4,20},{5,21},{6,22},{7,23},{8,24},{9,... | collective-permute-start | bytes 1376264 | tf_op jit(solution)/shard_map/ppermute | solution.py:288
  68.1 6.3 %collective-permute-start.34 = (bf16[2,128,256]{2,1,0:T(8,128)(2,1)S(1)}, bf16[2,128,256]{2,1,0:T(8,128)(2,1)S(1)}, u32[]{:S(2)}, u32[]{:S(2)}) collective-permute-start(bf16[2,128,256]{2,1,0:T(8,128)(2,1)S(1)} %get-tuple-element.71), channel_id=1, source_target_pairs={{0,2},{1,5},{2,0},{3,7},{4,6},{5,1},{6,4},{7,3},{8,10},{9,13},{10,... | collective-permute-start | bytes 393224 | tf_op jit(solution)/shard_map/ppermute | solution.py:288
  69.4 6.0 %collective-permute-start.31 = (bf16[2,128,256]{2,1,0:T(8,128)(2,1)S(1)}, bf16[2,128,256]{2,1,0:T(8,128)(2,1)S(1)}, u32[]{:S(2)}, u32[]{:S(2)}) collective-permute-start(bf16[2,128,256]{2,1,0:T(8,128)(2,1)S(1)} %get-tuple-element.62), channel_id=1, source_target_pairs={{0,2},{1,5},{2,0},{3,7},{4,6},{5,1},{6,4},{7,3},{8,10},{9,13},{10,... | collective-permute-start | bytes 393224 | tf_op jit(solution)/shard_map/ppermute | solution.py:288
  71.5 5.5 %collective-permute-start.32 = (bf16[2,128,256]{2,1,0:T(8,128)(2,1)S(1)}, bf16[2,128,256]{2,1,0:T(8,128)(2,1)S(1)}, u32[]{:S(2)}, u32[]{:S(2)}) collective-permute-start(bf16[2,128,256]{2,1,0:T(8,128)(2,1)S(1)} %get-tuple-element.63), channel_id=1, source_target_pairs={{0,4},{1,3},{2,6},{3,1},{4,0},{5,7},{6,2},{7,5},{8,12},{9,11},{10,... | collective-permute-start | bytes 393224 | tf_op jit(solution)/shard_map/ppermute | solution.py:288
  73.8 5.9 %collective-permute-start.33 = (bf16[2,128,256]{2,1,0:T(8,128)(2,1)S(1)}, bf16[2,128,256]{2,1,0:T(8,128)(2,1)S(1)}, u32[]{:S(2)}, u32[]{:S(2)}) collective-permute-start(bf16[2,128,256]{2,1,0:T(8,128)(2,1)S(1)} %get-tuple-element.64), channel_id=1, source_target_pairs={{0,6},{1,7},{2,4},{3,5},{4,2},{5,3},{6,0},{7,1},{8,14},{9,15},{10,... | collective-permute-start | bytes 393224 | tf_op jit(solution)/shard_map/ppermute | solution.py:288
  74.6 5.3 %collective-permute-start.38 = (bf16[256,512]{1,0:T(8,128)(2,1)S(1)}, bf16[256,512]{1,0:T(8,128)(2,1)S(1)}, u32[]{:S(2)}, u32[]{:S(2)}) collective-permute-start(bf16[256,512]{1,0:T(8,128)(2,1)S(1)} %get-tuple-element.68), channel_id=1, source_target_pairs={{0,1},{1,0},{2,3},{3,2},{4,5},{5,4},{6,7},{7,6},{8,9},{9,8},{10,11... | collective-permute-start | bytes 786440 | tf_op jit(solution)/shard_map/ppermute | solution.py:288
  79.8 1.6 %collective-permute-start.37 = (bf16[256,512]{1,0:T(8,128)(2,1)S(1)}, bf16[256,512]{1,0:T(8,128)(2,1)S(1)}, u32[]{:S(2)}, u32[]{:S(2)}) collective-permute-start(bf16[256,512]{1,0:T(8,128)(2,1)S(1)} %get-tuple-element.67), channel_id=1, source_target_pairs={{0,1},{1,0},{2,3},{3,2},{4,5},{5,4},{6,7},{7,6},{8,9},{9,8},{10,11... | collective-permute-start | bytes 786440 | tf_op jit(solution)/shard_map/ppermute | solution.py:288

commit v7 on v6

--- a/solution.py
+++ b/solution.py
@@ -11,6 +11,7 @@
 BF16 = jnp.bfloat16
 VMEM_LIMIT = 16 * 1024 * 1024
 LEAD = 4
+LOG2_E = 1.4426950408889634
 
 
 def dot(a, b, ca, cb):
@@ -34,16 +35,24 @@
     key_at = lax.broadcasted_iota(jnp.int32, (span * rows, width), 0)
     query_at = lax.broadcasted_iota(jnp.int32, (span * rows, width), 1) % rows
     low = (first - own + span - 1) * rows
-    allowed = (key_at >= low) & (key_at <= query_at + (span - 1) * rows)
+    last = (span - 1) * rows
     dk = jnp.zeros((span * rows, head), F32)
     dv = jnp.zeros((span * rows, head), F32)
     for pair in range(group // 2):
         at = [2 * pair * head, (2 * pair + 1) * head]
         q2 = jnp.concatenate([q_ref[:, a : a + head] for a in at], axis=0)
         do2 = jnp.concatenate([do_ref[:, a : a + head] for a in at], axis=0)
-        scores = jnp.where(allowed, dot(keys, q2, 1, 1) * scale, -1e30)
-        exps = jnp.exp(scores - jnp.max(scores, axis=0, keepdims=True))
-        probs = exps * (1.0 / jnp.sum(exps, axis=0, keepdims=True))
+        scores = dot(keys, q2, 1, 1)
+        scores = jnp.concatenate(
+            [
+                jnp.where(key_at[:last] >= low, scores[:last], -1e30),
+                jnp.where(key_at[:rows] <= query_at[:rows], scores[last:], -1e30),
+            ],
+            axis=0,
+        )
+        exps = jnp.exp2((scores - jnp.max(scores, axis=0, keepdims=True)) * (scale * LOG2_E))
+        inverse = 1.0 / jnp.sum(exps, axis=0, keepdims=True)
+        probs = exps * inverse
         probs_half = probs.astype(BF16)
         dprobs = dot(values, do2, 1, 1)
         row_dots = jnp.sum(probs_half.astype(F32) * dprobs, axis=0, keepdims=True)

time: 92.1 us -> 92.1 us (level)
  no operation moved by 1% of the time
where the time goes in v7:
time: 92.1 us; the launch traced here: 91.9 us
  waiting for transfers between devices  44 us (48%)
  starting transfers between devices  33.4 us (36%)
  Pallas kernels  10.7 us (12%)
  local copies, waits for them, and re-layouts  1.67 us (2%)
  other arithmetic  1.26 us (1%)
    ppermute x36, waiting for transfers between devices, hop(): return lax.ppermute(value, ('dp', 'ctx'), pairs)  42.8 us
    ppermute x36, starting transfers between devices, hop(): return lax.ppermute(value, ('dp', 'ctx'), pairs)  29 us
    pallas_call x18, Pallas kernels, local_call(): pl.pallas_call(kernel, out_shape=out_shape, in_specs=specs, out_specs=jax...  5.11 us
    pallas_call x1, Pallas kernels, attention(): pl.pallas_call(functools.partial(attention_kernel, span=span, head=head,...  4.73 us
    ppermute x4, starting transfers between devices, shift(): return lax.ppermute(value, 'ctx', [(i, (i + by) % ctx) for i in range(ctx)])  4.42 us
  transfers between devices with their start and end apart: 40, of which 20 were waited for; matrix products, arithmetic and copies ran while one was open for 0% of the time, Pallas kernels for 11%

profile of v7, /device:TPU:0, one launch (start us, length us, event | category | flops | bytes accessed | tf_op | source)
XLA Modules:
  0.0 91.9 jit_solution(4675481496121577285)
XLA Ops:
  0.7 1.6 %copy-done = bf16[1,128,8192]{2,1,0:T(8,128)(2,1)S(1)} copy-done((bf16[1,128,8192]{2,1,0:T(8,128)(2,1)S(1)}, bf16[1,128,8192]{2,1,0:T(8,128)(2,1)}, u32[]{:S(2)}) %copy-start) | copy-done | bytes 2097176
  2.3 0.8 spread.1
  3.2 3.1 %collective-permute-start.11 = (bf16[4,2,128,256]{3,2,1,0:T(8,128)(2,1)S(1)}, bf16[4,2,128,256]{3,2,1,0:T(8,128)(2,1)S(1)}, u32[]{:S(2)}, u32[]{:S(2)}) collective-permute-start(bf16[4,2,128,256]{3,2,1,0:T(8,128)(2,1)S(1)} %get-tuple-element.53), channel_id=1, source_target_pairs={{0,8},{1,9},{2,10},{3,11},{4,12},{5,13},{6,14},{7,15},{8,0},{9,1},... | collective-permute-start | bytes 1572872 | tf_op jit(solution)/shard_map/ppermute | solution.py:297
  6.3 1.5 %collective-permute-start.2 = (bf16[128,256]{1,0:T(8,128)(2,1)S(1)}, bf16[128,256]{1,0:T(8,128)(2,1)S(1)}, u32[]{:S(2)}, u32[]{:S(2)}) collective-permute-start(bf16[128,256]{1,0:T(8,128)(2,1)S(1)} %bitcast.33), channel_id=1, source_target_pairs={{0,2},{1,3},{2,4},{3,5},{4,6},{5,7},{6,0},{7,1},{8,10},{9,11},{10,... | collective-permute-start | bytes 196616 | tf_op jit(solution)/shard_map/ppermute | solution.py:95
  7.8 2.4 %collective-permute-start.1 = (bf16[128,256]{1,0:T(8,128)(2,1)S(1)}, bf16[128,256]{1,0:T(8,128)(2,1)S(1)}, u32[]{:S(2)}, u32[]{:S(2)}) collective-permute-start(bf16[128,256]{1,0:T(8,128)(2,1)S(1)} %bitcast.34), channel_id=1, source_target_pairs={{0,3},{1,4},{2,5},{3,6},{4,7},{5,0},{6,1},{7,2},{8,11},{9,12},{10,... | collective-permute-start | bytes 196616 | tf_op jit(solution)/shard_map/ppermute | solution.py:95
  11.0 1.2 %collective-permute-start.8 = (bf16[2,128,256]{2,1,0:T(8,128)(2,1)S(1)}, bf16[2,128,256]{2,1,0:T(8,128)(2,1)S(1)}, u32[]{:S(2)}, u32[]{:S(2)}) collective-permute-start(bf16[2,128,256]{2,1,0:T(8,128)(2,1)S(1)} %get-tuple-element.49), channel_id=1, source_target_pairs={{0,2},{1,5},{2,0},{3,7},{4,6},{5,1},{6,4},{7,3},{8,10},{9,13},{10,... | collective-permute-start | bytes 393224 | tf_op jit(solution)/shard_map/ppermute | solution.py:297
  12.2 1.2 %collective-permute-start.9 = (bf16[2,128,256]{2,1,0:T(8,128)(2,1)S(1)}, bf16[2,128,256]{2,1,0:T(8,128)(2,1)S(1)}, u32[]{:S(2)}, u32[]{:S(2)}) collective-permute-start(bf16[2,128,256]{2,1,0:T(8,128)(2,1)S(1)} %get-tuple-element.50), channel_id=1, source_target_pairs={{0,4},{1,3},{2,6},{3,1},{4,0},{5,7},{6,2},{7,5},{8,12},{9,11},{10,... | collective-permute-start | bytes 393224 | tf_op jit(solution)/shard_map/ppermute | solution.py:297
  13.4 1.1 %collective-permute-start.10 = (bf16[2,128,256]{2,1,0:T(8,128)(2,1)S(1)}, bf16[2,128,256]{2,1,0:T(8,128)(2,1)S(1)}, u32[]{:S(2)}, u32[]{:S(2)}) collective-permute-start(bf16[2,128,256]{2,1,0:T(8,128)(2,1)S(1)} %get-tuple-element.51), channel_id=1, source_target_pairs={{0,6},{1,7},{2,4},{3,5},{4,2},{5,3},{6,0},{7,1},{8,14},{9,15},{10,... | collective-permute-start | bytes 393224 | tf_op jit(solution)/shard_map/ppermute | solution.py:297
  14.5 0.9 collective-permute-done.refs_0_
  15.4 4.7 %attention.1 = (bf16[128,1024]{1,0:T(8,128)(2,1)}, bf16[128,512]{1,0:T(8,128)(2,1)S(1)}, f32[2,128,256]{2,1,0:T(8,128)S(1)}, bf16[2,128,256]{2,1,0:T(8,128)(2,1)...) custom-call(s32[1]{0:T(128)} %bitcast.own_ref, s32[1,3]{1,0:T(1,128)S(1)} %copy-done.5, ...), custom_call_target="tpu_custom_call" | custom-call | flops 1006632960 | bytes 1441792 | tf_op jit(solution)/shard_map/attention/pallas_call | solution.py:111
  20.6 1.9 %collective-permute-start.4 = (bf16[2,128,256]{2,1,0:T(8,128)(2,1)S(1)}, bf16[2,128,256]{2,1,0:T(8,128)(2,1)S(1)}, u32[]{:S(2)}, u32[]{:S(2)}) collective-permute-start(bf16[2,128,256]{2,1,0:T(8,128)(2,1)S(1)} %get-tuple-element.38), channel_id=1, source_target_pairs={{0,2},{1,5},{2,0},{3,7},{4,6},{5,1},{6,4},{7,3},{8,10},{9,13},{10,... | collective-permute-start | bytes 393224 | tf_op jit(solution)/shard_map/ppermute | solution.py:297
  22.5 1.6 %collective-permute-start.6 = (bf16[2,128,256]{2,1,0:T(8,128)(2,1)S(1)}, bf16[2,128,256]{2,1,0:T(8,128)(2,1)S(1)}, u32[]{:S(2)}, u32[]{:S(2)}) collective-permute-start(bf16[2,128,256]{2,1,0:T(8,128)(2,1)S(1)} %get-tuple-element.40), channel_id=1, source_target_pairs={{0,6},{1,7},{2,4},{3,5},{4,2},{5,3},{6,0},{7,1},{8,14},{9,15},{10,... | collective-permute-start | bytes 393224 | tf_op jit(solution)/shard_map/ppermute | solution.py:297
  24.3 0.8 collective-permute-done.23
  25.1 0.9 collective-permute-start.18
  26.0 1.9 %collective-permute-start.24 = (bf16[2,128,512]{2,1,0:T(8,128)(2,1)S(1)}, bf16[2,128,512]{2,1,0:T(8,128)(2,1)S(1)}, u32[]{:S(2)}, u32[]{:S(2)}) collective-permute-start(bf16[2,128,512]{2,1,0:T(8,128)(2,1)S(1)} %pack.8.own_ref.refs_4_), channel_id=1, source_target_pairs={{0,2},{1,5},{2,0},{3,7},{4,6},{5,1},{6,4},{7,3},{8,10},{9,13},{10,... | collective-permute-start | bytes 786440 | tf_op jit(solution)/shard_map/ppermute | solution.py:297
  28.0 1.0 %collective-permute-start.14 = (bf16[2,128,256]{2,1,0:T(8,128)(2,1)S(1)}, bf16[2,128,256]{2,1,0:T(8,128)(2,1)S(1)}, u32[]{:S(2)}, u32[]{:S(2)}) collective-permute-start(bf16[2,128,256]{2,1,0:T(8,128)(2,1)S(1)} %get-tuple-element.72), channel_id=1, source_target_pairs={{0,6},{1,7},{2,4},{3,5},{4,2},{5,3},{6,0},{7,1},{8,14},{9,15},{10,... | collective-permute-start | bytes 393224 | tf_op jit(solution)/shard_map/ppermute | solution.py:297
  29.0 2.8 %collective-permute-done.5.refs_1_ = bf16[2,128,256]{2,1,0:T(8,128)(2,1)S(1)} collective-permute-done((bf16[2,128,256]{2,1,0:T(8,128)(2,1)S(1)}, bf16[2,128,256]{2,1,0:T(8,128)(2,1)S(1)}, u32[]{:S(2)}, u32[]{:S(2)}) %collective-permute-start.5) | collective-permute-done | bytes 131104 | tf_op jit(solution)/shard_map/ppermute | solution.py:297
  32.0 1.2 %collective-permute-done.7.refs_0_ = bf16[128,256]{1,0:T(8,128)(2,1)S(1)} collective-permute-done((bf16[128,256]{1,0:T(8,128)(2,1)S(1)}, bf16[128,256]{1,0:T(8,128)(2,1)S(1)}, u32[]{:S(2)}, u32[]{:S(2)}) %collective-permute-start.7) | collective-permute-done | bytes 65568 | tf_op jit(solution)/shard_map/ppermute | solution.py:297
  33.2 0.9 collective-permute-start.25
  34.0 0.7 settle.1
  34.7 1.6 %collective-permute-start.17 = (bf16[128,768]{1,0:T(8,128)(2,1)S(1)}, bf16[128,768]{1,0:T(8,128)(2,1)S(1)}, u32[]{:S(2)}, u32[]{:S(2)}) collective-permute-start(bf16[128,768]{1,0:T(8,128)(2,1)S(1)} %get-tuple-element.57), channel_id=1, source_target_pairs={{0,8},{1,9},{2,10},{3,11},{4,12},{5,13},{6,14},{7,15},{8,0},{9,1},... | collective-permute-start | bytes 589832 | tf_op jit(solution)/shard_map/ppermute | solution.py:297
  36.3 1.2 %collective-permute-done.14.refs_3_ = bf16[2,128,256]{2,1,0:T(8,128)(2,1)S(1)} collective-permute-done((bf16[2,128,256]{2,1,0:T(8,128)(2,1)S(1)}, bf16[2,128,256]{2,1,0:T(8,128)(2,1)S(1)}, u32[]{:S(2)}, u32[]{:S(2)}) %collective-permute-start.14) | collective-permute-done | bytes 131104 | tf_op jit(solution)/shard_map/ppermute | solution.py:297
  38.0 5.6 %collective-permute-done.12.refs_1_ = bf16[2,128,256]{2,1,0:T(8,128)(2,1)S(1)} collective-permute-done((bf16[2,128,256]{2,1,0:T(8,128)(2,1)S(1)}, bf16[2,128,256]{2,1,0:T(8,128)(2,1)S(1)}, u32[]{:S(2)}, u32[]{:S(2)}) %collective-permute-start.12) | collective-permute-done | bytes 131104 | tf_op jit(solution)/shard_map/ppermute | solution.py:297
  45.7 1.9 %collective-permute-done.15.refs_2_ = bf16[256,512]{1,0:T(8,128)(2,1)S(1)} collective-permute-done((bf16[256,512]{1,0:T(8,128)(2,1)S(1)}, bf16[256,512]{1,0:T(8,128)(2,1)S(1)}, u32[]{:S(2)}, u32[]{:S(2)}) %collective-permute-start.15) | collective-permute-done | bytes 262176 | tf_op jit(solution)/shard_map/ppermute | solution.py:297
  47.6 0.7 collective-permute-start.20
  48.3 4.8 %collective-permute-done.19.moved_ref.refs_5_ = bf16[2,128,768]{2,1,0:T(8,128)(2,1)S(1)} collective-permute-done((bf16[2,128,768]{2,1,0:T(8,128)(2,1)S(1)}, bf16[2,128,768]{2,1,0:T(8,128)(2,1)S(1)}, u32[]{:S(2)}, u32[]{:S(2)}) %collective-permute-start.19) | collective-permute-done | bytes 393248 | tf_op jit(solution)/shard_map/ppermute | solution.py:297
  53.1 1.4 %collective-permute-start.21 = (bf16[2,128,768]{2,1,0:T(8,128)(2,1)S(1)}, bf16[2,128,768]{2,1,0:T(8,128)(2,1)S(1)}, u32[]{:S(2)}, u32[]{:S(2)}) collective-permute-start(bf16[2,128,768]{2,1,0:T(8,128)(2,1)S(1)} %collective-permute-done.19.moved_ref.refs_5_), channel_id=1, source_target_pairs={{0,4},{1,3},{2,6},{3,1},{4,0},{5,7},{6,2},{7,5},{8,12},{9,11},{10,... | collective-permute-start | bytes 1179656 | tf_op jit(solution)/shard_map/ppermute | solution.py:297
  54.5 0.7 fold.4
  55.2 2.6 %collective-permute-start.29 = (bf16[256,384]{1,0:T(8,128)(2,1)S(1)}, bf16[256,384]{1,0:T(8,128)(2,1)S(1)}, u32[]{:S(2)}, u32[]{:S(2)}) collective-permute-start(bf16[256,384]{1,0:T(8,128)(2,1)S(1)} %get-tuple-element.60), channel_id=1, source_target_pairs={{0,16},{1,17},{2,18},{3,19},{4,20},{5,21},{6,22},{7,23},{8,24},{9,... | collective-permute-start | bytes 589832 | tf_op jit(solution)/shard_map/ppermute | solution.py:297
  58.0 5.9 %collective-permute-done.29.refs_0_ = bf16[256,384]{1,0:T(8,128)(2,1)S(1)} collective-permute-done((bf16[256,384]{1,0:T(8,128)(2,1)S(1)}, bf16[256,384]{1,0:T(8,128)(2,1)S(1)}, u32[]{:S(2)}, u32[]{:S(2)}) %collective-permute-start.29) | collective-permute-done | bytes 196640 | tf_op jit(solution)/shard_map/ppermute | solution.py:297
  64.2 0.6 collective-permute-start.36
  64.8 1.0 %collective-permute-start.35 = (bf16[2,128,256]{2,1,0:T(8,128)(2,1)S(1)}, bf16[2,128,256]{2,1,0:T(8,128)(2,1)S(1)}, u32[]{:S(2)}, u32[]{:S(2)}) collective-permute-start(bf16[2,128,256]{2,1,0:T(8,128)(2,1)S(1)} %get-tuple-element.70), channel_id=1, source_target_pairs={{0,4},{1,3},{2,6},{3,1},{4,0},{5,7},{6,2},{7,5},{8,12},{9,11},{10,... | collective-permute-start | bytes 393224 | tf_op jit(solution)/shard_map/ppermute | solution.py:297
  65.8 0.6 collective-permute-done.30.refs_9_
  66.4 1.0 %fold.5.refs_3_ = bf16[256,896]{1,0:T(8,128)(2,1)S(1)} custom-call(bf16[256,512]{1,0:T(8,128)(2,1)S(1)} %get-tuple-element.52.refs_1_.refs_0_, bf16[256,512]{1,0:T(8,128)(2,1)S(1)} %get-tuple-element.54.refs_0_.refs_1_, bf16[256,512]{1,0:T(8,128)(2,1)S(1)} %collective-permute-done.15.refs_2_, bf16[256,512]{1,0:T(8,128)(2,1)S(1)} %collective-permute-done.16.refs_3_, ...), custom_call_target="tpu_custom_call" | custom-call | tf_op jit(solution)/shard_map/fold/pallas_call | solution.py:169
  67.4 0.6 collective-permute-start.39
  68.0 1.3 %collective-permute-start.34 = (bf16[2,128,256]{2,1,0:T(8,128)(2,1)S(1)}, bf16[2,128,256]{2,1,0:T(8,128)(2,1)S(1)}, u32[]{:S(2)}, u32[]{:S(2)}) collective-permute-start(bf16[2,128,256]{2,1,0:T(8,128)(2,1)S(1)} %get-tuple-element.71), channel_id=1, source_target_pairs={{0,2},{1,5},{2,0},{3,7},{4,6},{5,1},{6,4},{7,3},{8,10},{9,13},{10,... | collective-permute-start | bytes 393224 | tf_op jit(solution)/shard_map/ppermute | solution.py:297
  69.4 0.8 collective-permute-start.31
  70.1 1.3 %collective-permute-done.36.refs_3_ = bf16[2,128,256]{2,1,0:T(8,128)(2,1)S(1)} collective-permute-done((bf16[2,128,256]{2,1,0:T(8,128)(2,1)S(1)}, bf16[2,128,256]{2,1,0:T(8,128)(2,1)S(1)}, u32[]{:S(2)}, u32[]{:S(2)}) %collective-permute-start.36) | collective-permute-done | bytes 131104 | tf_op jit(solution)/shard_map/ppermute | solution.py:297
  71.5 0.6 collective-permute-start.32
  72.1 1.7 %collective-permute-done.35.refs_2_ = bf16[2,128,256]{2,1,0:T(8,128)(2,1)S(1)} collective-permute-done((bf16[2,128,256]{2,1,0:T(8,128)(2,1)S(1)}, bf16[2,128,256]{2,1,0:T(8,128)(2,1)S(1)}, u32[]{:S(2)}, u32[]{:S(2)}) %collective-permute-start.35) | collective-permute-done | bytes 131104 | tf_op jit(solution)/shard_map/ppermute | solution.py:297
  74.6 0.8 collective-permute-done.31.refs_1_
  75.4 1.6 %collective-permute-done.32.refs_2_ = bf16[2,128,256]{2,1,0:T(8,128)(2,1)S(1)} collective-permute-done((bf16[2,128,256]{2,1,0:T(8,128)(2,1)S(1)}, bf16[2,128,256]{2,1,0:T(8,128)(2,1)S(1)}, u32[]{:S(2)}, u32[]{:S(2)}) %collective-permute-start.32) | collective-permute-done | bytes 131104 | tf_op jit(solution)/shard_map/ppermute | solution.py:297
  77.0 2.6 %collective-permute-done.33.refs_3_ = bf16[2,128,256]{2,1,0:T(8,128)(2,1)S(1)} collective-permute-done((bf16[2,128,256]{2,1,0:T(8,128)(2,1)S(1)}, bf16[2,128,256]{2,1,0:T(8,128)(2,1)S(1)}, u32[]{:S(2)}, u32[]{:S(2)}) %collective-permute-start.33) | collective-permute-done | bytes 131104 | tf_op jit(solution)/shard_map/ppermute | solution.py:297
  79.9 1.5 %collective-permute-done.37.refs_2_ = bf16[256,512]{1,0:T(8,128)(2,1)S(1)} collective-permute-done((bf16[256,512]{1,0:T(8,128)(2,1)S(1)}, bf16[256,512]{1,0:T(8,128)(2,1)S(1)}, u32[]{:S(2)}, u32[]{:S(2)}) %collective-permute-start.37) | collective-permute-done | bytes 262176 | tf_op jit(solution)/shard_map/ppermute | solution.py:297
  81.4 1.0 %fold.7 = f32[256,768]{1,0:T(8,128)S(1)} custom-call(bf16[256,512]{1,0:T(8,128)(2,1)S(1)} %get-tuple-element.65.refs_0_, bf16[256,512]{1,0:T(8,128)(2,1)S(1)} %get-tuple-element.66.refs_1_, bf16[256,512]{1,0:T(8,128)(2,1)S(1)} %collective-permute-done.37.refs_2_, bf16[256,512]{1,0:T(8,128)(2,1)S(1)} %collective-permute-done.38.refs_3_, ...), custom_call_target="tpu_custom_call" | custom-call | tf_op jit(solution)/shard_map/fold/pallas_call | solution.py:169
  82.4 0.7 fold.6
  83.1 7.7 %collective-permute-done.39 = bf16[256,896]{1,0:T(8,128)(2,1)S(1)} collective-permute-done((bf16[256,896]{1,0:T(8,128)(2,1)S(1)}, bf16[256,896]{1,0:T(8,128)(2,1)S(1)}, u32[]{:S(2)}, u32[]{:S(2)}) %collective-permute-start.39) | collective-permute-done | bytes 458784 | tf_op jit(solution)/shard_map/ppermute | solution.py:297
  90.7 1.2 %maximum_add_fusion = f32[256,1280]{1,0:T(8,128)} fusion(f32[256,768]{1,0:T(8,128)S(1)} %fold.7, f32[256,512]{1,0:T(8,128)S(1)} %fold.6, bf16[256,896]{1,0:T(8,128)(2,1)S(1)} %collective-permute-done.39, bf16[256,384]{1,0:T(8,128)(2,1)S(1)} %collective-permute-done.29.refs_0_), kind=kLoop, calls=%fused_computation | loop fusion | flops 1966080 | bytes 3276800 | tf_op jit(solution)/shard_map/add | solution.py:343
  (68 shorter events, 5.9 us)
Async XLA Ops:
  0.6 14.8 %copy-start.5 = (s32[1,3]{1,0:T(1,128)S(1)}, s32[1,3]{1,0:T(1,128)}, u32[]{:S(2)}) copy-start(s32[1,3]{1,0:T(1,128)} %lens_ref.1) | copy-start | bytes 40
  0.7 1.6 %copy-start = (bf16[1,128,8192]{2,1,0:T(8,128)(2,1)S(1)}, bf16[1,128,8192]{2,1,0:T(8,128)(2,1)}, u32[]{:S(2)}) copy-start(bf16[1,128,8192]{2,1,0:T(8,128)(2,1)} %param.5) | copy-start | bytes 6291460
  2.3 3.9 %copy-start.4 = (bf16[1,128,256]{2,1,0:T(8,128)(2,1)S(1)}, bf16[1,128,256]{2,1,0:T(8,128)(2,1)}, u32[]{:S(2)}) copy-start(bf16[1,128,256]{2,1,0:T(8,128)(2,1)} %param.7) | copy-start | bytes 196612
  2.3 13.1 %copy-start.2 = (bf16[1,128,1024]{2,1,0:T(8,128)(2,1)S(1)}, bf16[1,128,1024]{2,1,0:T(8,128)(2,1)}, u32[]{:S(2)}) copy-start(bf16[1,128,1024]{2,1,0:T(8,128)(2,1)} %param.6) | copy-start | bytes 786436
  2.3 13.1 %copy-start.3 = (bf16[1,128,1024]{2,1,0:T(8,128)(2,1)S(1)}, bf16[1,128,1024]{2,1,0:T(8,128)(2,1)}, u32[]{:S(2)}) copy-start(bf16[1,128,1024]{2,1,0:T(8,128)(2,1)} %param.8) | copy-start | bytes 786436
  3.2 22.9 %collective-permute-start.11 = (bf16[4,2,128,256]{3,2,1,0:T(8,128)(2,1)S(1)}, bf16[4,2,128,256]{3,2,1,0:T(8,128)(2,1)S(1)}, u32[]{:S(2)}, u32[]{:S(2)}) collective-permute-start(bf16[4,2,128,256]{3,2,1,0:T(8,128)(2,1)S(1)} %get-tuple-element.53), channel_id=1, source_target_pairs={{0,8},{1,9},{2,10},{3,11},{4,12},{5,13},{6,14},{7,15},{8,0},{9,1},... | collective-permute-start | bytes 1572872 | tf_op jit(solution)/shard_map/ppermute | solution.py:297
  6.3 4.8 %collective-permute-start.3 = (bf16[128,256]{1,0:T(8,128)(2,1)S(1)}, bf16[128,256]{1,0:T(8,128)(2,1)S(1)}, u32[]{:S(2)}, u32[]{:S(2)}) collective-permute-start(bf16[128,256]{1,0:T(8,128)(2,1)S(1)} %bitcast.32), channel_id=1, source_target_pairs={{0,1},{1,2},{2,3},{3,4},{4,5},{5,6},{6,7},{7,0},{8,9},{9,10},{10,1... | collective-permute-start | bytes 196616 | tf_op jit(solution)/shard_map/ppermute | solution.py:95
  6.3 5.9 %collective-permute-start.2 = (bf16[128,256]{1,0:T(8,128)(2,1)S(1)}, bf16[128,256]{1,0:T(8,128)(2,1)S(1)}, u32[]{:S(2)}, u32[]{:S(2)}) collective-permute-start(bf16[128,256]{1,0:T(8,128)(2,1)S(1)} %bitcast.33), channel_id=1, source_target_pairs={{0,2},{1,3},{2,4},{3,5},{4,6},{5,7},{6,0},{7,1},{8,10},{9,11},{10,... | collective-permute-start | bytes 196616 | tf_op jit(solution)/shard_map/ppermute | solution.py:95
  7.8 5.6 %collective-permute-start.1 = (bf16[128,256]{1,0:T(8,128)(2,1)S(1)}, bf16[128,256]{1,0:T(8,128)(2,1)S(1)}, u32[]{:S(2)}, u32[]{:S(2)}) collective-permute-start(bf16[128,256]{1,0:T(8,128)(2,1)S(1)} %bitcast.34), channel_id=1, source_target_pairs={{0,3},{1,4},{2,5},{3,6},{4,7},{5,0},{6,1},{7,2},{8,11},{9,12},{10,... | collective-permute-start | bytes 196616 | tf_op jit(solution)/shard_map/ppermute | solution.py:95
  10.2 5.2 %collective-permute-start = (bf16[128,256]{1,0:T(8,128)(2,1)S(1)}, bf16[128,256]{1,0:T(8,128)(2,1)S(1)}, u32[]{:S(2)}, u32[]{:S(2)}) collective-permute-start(bf16[128,256]{1,0:T(8,128)(2,1)S(1)} %bitcast.35), channel_id=1, source_target_pairs={{0,4},{1,5},{2,6},{3,7},{4,0},{5,1},{6,2},{7,3},{8,12},{9,13},{10,... | collective-permute-start | bytes 196616 | tf_op jit(solution)/shard_map/ppermute | solution.py:95
  11.0 9.6 %collective-permute-start.8 = (bf16[2,128,256]{2,1,0:T(8,128)(2,1)S(1)}, bf16[2,128,256]{2,1,0:T(8,128)(2,1)S(1)}, u32[]{:S(2)}, u32[]{:S(2)}) collective-permute-start(bf16[2,128,256]{2,1,0:T(8,128)(2,1)S(1)} %get-tuple-element.49), channel_id=1, source_target_pairs={{0,2},{1,5},{2,0},{3,7},{4,6},{5,1},{6,4},{7,3},{8,10},{9,13},{10,... | collective-permute-start | bytes 393224 | tf_op jit(solution)/shard_map/ppermute | solution.py:297
  12.2 10.3 %collective-permute-start.9 = (bf16[2,128,256]{2,1,0:T(8,128)(2,1)S(1)}, bf16[2,128,256]{2,1,0:T(8,128)(2,1)S(1)}, u32[]{:S(2)}, u32[]{:S(2)}) collective-permute-start(bf16[2,128,256]{2,1,0:T(8,128)(2,1)S(1)} %get-tuple-element.50), channel_id=1, source_target_pairs={{0,4},{1,3},{2,6},{3,1},{4,0},{5,7},{6,2},{7,5},{8,12},{9,11},{10,... | collective-permute-start | bytes 393224 | tf_op jit(solution)/shard_map/ppermute | solution.py:297
  13.4 9.0 %collective-permute-start.10 = (bf16[2,128,256]{2,1,0:T(8,128)(2,1)S(1)}, bf16[2,128,256]{2,1,0:T(8,128)(2,1)S(1)}, u32[]{:S(2)}, u32[]{:S(2)}) collective-permute-start(bf16[2,128,256]{2,1,0:T(8,128)(2,1)S(1)} %get-tuple-element.51), channel_id=1, source_target_pairs={{0,6},{1,7},{2,4},{3,5},{4,2},{5,3},{6,0},{7,1},{8,14},{9,15},{10,... | collective-permute-start | bytes 393224 | tf_op jit(solution)/shard_map/ppermute | solution.py:297
  20.1 5.0 %collective-permute-start.23 = (bf16[128,512]{1,0:T(8,128)(2,1)S(1)}, bf16[128,512]{1,0:T(8,128)(2,1)S(1)}, u32[]{:S(2)}, u32[]{:S(2)}) collective-permute-start(bf16[128,512]{1,0:T(8,128)(2,1)S(1)} %get-tuple-element.59), channel_id=1, source_target_pairs={{0,8},{1,9},{2,10},{3,11},{4,12},{5,13},{6,14},{7,15},{8,0},{9,1},... | collective-permute-start | bytes 393224 | tf_op jit(solution)/shard_map/ppermute | solution.py:297
  20.6 7.4 %collective-permute-start.4 = (bf16[2,128,256]{2,1,0:T(8,128)(2,1)S(1)}, bf16[2,128,256]{2,1,0:T(8,128)(2,1)S(1)}, u32[]{:S(2)}, u32[]{:S(2)}) collective-permute-start(bf16[2,128,256]{2,1,0:T(8,128)(2,1)S(1)} %get-tuple-element.38), channel_id=1, source_target_pairs={{0,2},{1,5},{2,0},{3,7},{4,6},{5,1},{6,4},{7,3},{8,10},{9,13},{10,... | collective-permute-start | bytes 393224 | tf_op jit(solution)/shard_map/ppermute | solution.py:297
  22.5 9.3 %collective-permute-start.5 = (bf16[2,128,256]{2,1,0:T(8,128)(2,1)S(1)}, bf16[2,128,256]{2,1,0:T(8,128)(2,1)S(1)}, u32[]{:S(2)}, u32[]{:S(2)}) collective-permute-start(bf16[2,128,256]{2,1,0:T(8,128)(2,1)S(1)} %get-tuple-element.39), channel_id=1, source_target_pairs={{0,4},{1,3},{2,6},{3,1},{4,0},{5,7},{6,2},{7,5},{8,12},{9,11},{10,... | collective-permute-start | bytes 393224 | tf_op jit(solution)/shard_map/ppermute | solution.py:297
  22.5 9.3 %collective-permute-start.6 = (bf16[2,128,256]{2,1,0:T(8,128)(2,1)S(1)}, bf16[2,128,256]{2,1,0:T(8,128)(2,1)S(1)}, u32[]{:S(2)}, u32[]{:S(2)}) collective-permute-start(bf16[2,128,256]{2,1,0:T(8,128)(2,1)S(1)} %get-tuple-element.40), channel_id=1, source_target_pairs={{0,6},{1,7},{2,4},{3,5},{4,2},{5,3},{6,0},{7,1},{8,14},{9,15},{10,... | collective-permute-start | bytes 393224 | tf_op jit(solution)/shard_map/ppermute | solution.py:297
  24.3 9.7 %copy-start.1 = (bf16[128,1024]{1,0:T(8,128)(2,1)S(1)}, bf16[128,1024]{1,0:T(8,128)(2,1)}, u32[]{:S(2)}) copy-start(bf16[128,1024]{1,0:T(8,128)(2,1)} %get-tuple-element.36.gq_ref) | copy-start | bytes 786436
  25.1 18.7 %collective-permute-start.18 = (bf16[4,2,128,256]{3,2,1,0:T(8,128)(2,1)S(1)}, bf16[4,2,128,256]{3,2,1,0:T(8,128)(2,1)S(1)}, u32[]{:S(2)}, u32[]{:S(2)}) collective-permute-start(bf16[4,2,128,256]{3,2,1,0:T(8,128)(2,1)S(1)} %hold.2), channel_id=1, source_target_pairs={{0,8},{1,9},{2,10},{3,11},{4,12},{5,13},{6,14},{7,15},{8,0},{9,1},... | collective-permute-start | bytes 1572872 | tf_op jit(solution)/shard_map/ppermute | solution.py:297
  26.0 8.7 %collective-permute-start.24 = (bf16[2,128,512]{2,1,0:T(8,128)(2,1)S(1)}, bf16[2,128,512]{2,1,0:T(8,128)(2,1)S(1)}, u32[]{:S(2)}, u32[]{:S(2)}) collective-permute-start(bf16[2,128,512]{2,1,0:T(8,128)(2,1)S(1)} %pack.8.own_ref.refs_4_), channel_id=1, source_target_pairs={{0,2},{1,5},{2,0},{3,7},{4,6},{5,1},{6,4},{7,3},{8,10},{9,13},{10,... | collective-permute-start | bytes 786440 | tf_op jit(solution)/shard_map/ppermute | solution.py:297
  28.0 9.5 %collective-permute-start.14 = (bf16[2,128,256]{2,1,0:T(8,128)(2,1)S(1)}, bf16[2,128,256]{2,1,0:T(8,128)(2,1)S(1)}, u32[]{:S(2)}, u32[]{:S(2)}) collective-permute-start(bf16[2,128,256]{2,1,0:T(8,128)(2,1)S(1)} %get-tuple-element.72), channel_id=1, source_target_pairs={{0,6},{1,7},{2,4},{3,5},{4,2},{5,3},{6,0},{7,1},{8,14},{9,15},{10,... | collective-permute-start | bytes 393224 | tf_op jit(solution)/shard_map/ppermute | solution.py:297
  31.9 1.3 %collective-permute-start.7 = (bf16[128,256]{1,0:T(8,128)(2,1)S(1)}, bf16[128,256]{1,0:T(8,128)(2,1)S(1)}, u32[]{:S(2)}, u32[]{:S(2)}) collective-permute-start(bf16[128,256]{1,0:T(8,128)(2,1)S(1)} %get-tuple-element.42), channel_id=1, source_target_pairs={{0,1},{1,0},{2,3},{3,2},{4,5},{5,4},{6,7},{7,6},{8,9},{9,8},{10,11... | collective-permute-start | bytes 196616 | tf_op jit(solution)/shard_map/ppermute | solution.py:297
  31.9 6.0 %collective-permute-start.13 = (bf16[2,128,256]{2,1,0:T(8,128)(2,1)S(1)}, bf16[2,128,256]{2,1,0:T(8,128)(2,1)S(1)}, u32[]{:S(2)}, u32[]{:S(2)}) collective-permute-start(bf16[2,128,256]{2,1,0:T(8,128)(2,1)S(1)} %get-tuple-element.73), channel_id=1, source_target_pairs={{0,4},{1,3},{2,6},{3,1},{4,0},{5,7},{6,2},{7,5},{8,12},{9,11},{10,... | collective-permute-start | bytes 393224 | tf_op jit(solution)/shard_map/ppermute | solution.py:297
  33.2 11.4 %collective-permute-start.25 = (bf16[2,128,512]{2,1,0:T(8,128)(2,1)S(1)}, bf16[2,128,512]{2,1,0:T(8,128)(2,1)S(1)}, u32[]{:S(2)}, u32[]{:S(2)}) collective-permute-start(bf16[2,128,512]{2,1,0:T(8,128)(2,1)S(1)} %pack.8.own_ref.refs_4_), channel_id=1, source_target_pairs={{0,4},{1,3},{2,6},{3,1},{4,0},{5,7},{6,2},{7,5},{8,12},{9,11},{10,... | collective-permute-start | bytes 786440 | tf_op jit(solution)/shard_map/ppermute | solution.py:297
  34.7 9.2 %collective-permute-start.17 = (bf16[128,768]{1,0:T(8,128)(2,1)S(1)}, bf16[128,768]{1,0:T(8,128)(2,1)S(1)}, u32[]{:S(2)}, u32[]{:S(2)}) collective-permute-start(bf16[128,768]{1,0:T(8,128)(2,1)S(1)} %get-tuple-element.57), channel_id=1, source_target_pairs={{0,8},{1,9},{2,10},{3,11},{4,12},{5,13},{6,14},{7,15},{8,0},{9,1},... | collective-permute-start | bytes 589832 | tf_op jit(solution)/shard_map/ppermute | solution.py:297
  37.5 7.5 %collective-permute-start.26 = (bf16[2,128,512]{2,1,0:T(8,128)(2,1)S(1)}, bf16[2,128,512]{2,1,0:T(8,128)(2,1)S(1)}, u32[]{:S(2)}, u32[]{:S(2)}) collective-permute-start(bf16[2,128,512]{2,1,0:T(8,128)(2,1)S(1)} %collective-permute-done.24.moved_ref.refs_5_), channel_id=1, source_target_pairs={{0,4},{1,3},{2,6},{3,1},{4,0},{5,7},{6,2},{7,5},{8,12},{9,11},{10,... | collective-permute-start | bytes 786440 | tf_op jit(solution)/shard_map/ppermute | solution.py:297
  37.9 5.7 %collective-permute-start.12 = (bf16[2,128,256]{2,1,0:T(8,128)(2,1)S(1)}, bf16[2,128,256]{2,1,0:T(8,128)(2,1)S(1)}, u32[]{:S(2)}, u32[]{:S(2)}) collective-permute-start(bf16[2,128,256]{2,1,0:T(8,128)(2,1)S(1)} %get-tuple-element.74), channel_id=1, source_target_pairs={{0,2},{1,5},{2,0},{3,7},{4,6},{5,1},{6,4},{7,3},{8,10},{9,13},{10,... | collective-permute-start | bytes 393224 | tf_op jit(solution)/shard_map/ppermute | solution.py:297
  43.9 9.2 %collective-permute-start.19 = (bf16[2,128,768]{2,1,0:T(8,128)(2,1)S(1)}, bf16[2,128,768]{2,1,0:T(8,128)(2,1)S(1)}, u32[]{:S(2)}, u32[]{:S(2)}) collective-permute-start(bf16[2,128,768]{2,1,0:T(8,128)(2,1)S(1)} %pack.6.own_ref.refs_4_), channel_id=1, source_target_pairs={{0,2},{1,5},{2,0},{3,7},{4,6},{5,1},{6,4},{7,3},{8,10},{9,13},{10,... | collective-permute-start | bytes 1179656 | tf_op jit(solution)/shard_map/ppermute | solution.py:297
  44.5 10.0 %collective-permute-start.27 = (bf16[4,128,512]{2,1,0:T(8,128)(2,1)S(1)}, bf16[4,128,512]{2,1,0:T(8,128)(2,1)S(1)}, u32[]{:S(2)}, u32[]{:S(2)}) collective-permute-start(bf16[4,128,512]{2,1,0:T(8,128)(2,1)S(1)} %pack.9), channel_id=1, source_target_pairs={{0,1},{1,0},{2,3},{3,2},{4,5},{5,4},{6,7},{7,6},{8,9},{9,8},{10,11... | collective-permute-start | bytes 1572872 | tf_op jit(solution)/shard_map/ppermute | solution.py:297
  45.0 9.5 %collective-permute-start.28 = (bf16[4,128,512]{2,1,0:T(8,128)(2,1)S(1)}, bf16[4,128,512]{2,1,0:T(8,128)(2,1)S(1)}, u32[]{:S(2)}, u32[]{:S(2)}) collective-permute-start(bf16[4,128,512]{2,1,0:T(8,128)(2,1)S(1)} %pack.10), channel_id=1, source_target_pairs={{0,1},{1,0},{2,3},{3,2},{4,5},{5,4},{6,7},{7,6},{8,9},{9,8},{10,11... | collective-permute-start | bytes 1572872 | tf_op jit(solution)/shard_map/ppermute | solution.py:297
  45.2 2.4 %collective-permute-start.15 = (bf16[256,512]{1,0:T(8,128)(2,1)S(1)}, bf16[256,512]{1,0:T(8,128)(2,1)S(1)}, u32[]{:S(2)}, u32[]{:S(2)}) collective-permute-start(bf16[256,512]{1,0:T(8,128)(2,1)S(1)} %get-tuple-element.55), channel_id=1, source_target_pairs={{0,1},{1,0},{2,3},{3,2},{4,5},{5,4},{6,7},{7,6},{8,9},{9,8},{10,11... | collective-permute-start | bytes 786440 | tf_op jit(solution)/shard_map/ppermute | solution.py:297
  45.6 9.0 %collective-permute-start.16 = (bf16[256,512]{1,0:T(8,128)(2,1)S(1)}, bf16[256,512]{1,0:T(8,128)(2,1)S(1)}, u32[]{:S(2)}, u32[]{:S(2)}) collective-permute-start(bf16[256,512]{1,0:T(8,128)(2,1)S(1)} %get-tuple-element.56), channel_id=1, source_target_pairs={{0,1},{1,0},{2,3},{3,2},{4,5},{5,4},{6,7},{7,6},{8,9},{9,8},{10,11... | collective-permute-start | bytes 786440 | tf_op jit(solution)/shard_map/ppermute | solution.py:297
  47.6 10.4 %collective-permute-start.20 = (bf16[2,128,768]{2,1,0:T(8,128)(2,1)S(1)}, bf16[2,128,768]{2,1,0:T(8,128)(2,1)S(1)}, u32[]{:S(2)}, u32[]{:S(2)}) collective-permute-start(bf16[2,128,768]{2,1,0:T(8,128)(2,1)S(1)} %pack.6.own_ref.refs_4_), channel_id=1, source_target_pairs={{0,4},{1,3},{2,6},{3,1},{4,0},{5,7},{6,2},{7,5},{8,12},{9,11},{10,... | collective-permute-start | bytes 1179656 | tf_op jit(solution)/shard_map/ppermute | solution.py:297
  53.1 10.9 %collective-permute-start.21 = (bf16[2,128,768]{2,1,0:T(8,128)(2,1)S(1)}, bf16[2,128,768]{2,1,0:T(8,128)(2,1)S(1)}, u32[]{:S(2)}, u32[]{:S(2)}) collective-permute-start(bf16[2,128,768]{2,1,0:T(8,128)(2,1)S(1)} %collective-permute-done.19.moved_ref.refs_5_), channel_id=1, source_target_pairs={{0,4},{1,3},{2,6},{3,1},{4,0},{5,7},{6,2},{7,5},{8,12},{9,11},{10,... | collective-permute-start | bytes 1179656 | tf_op jit(solution)/shard_map/ppermute | solution.py:297
  55.2 8.7 %collective-permute-start.29 = (bf16[256,384]{1,0:T(8,128)(2,1)S(1)}, bf16[256,384]{1,0:T(8,128)(2,1)S(1)}, u32[]{:S(2)}, u32[]{:S(2)}) collective-permute-start(bf16[256,384]{1,0:T(8,128)(2,1)S(1)} %get-tuple-element.60), channel_id=1, source_target_pairs={{0,16},{1,17},{2,18},{3,19},{4,20},{5,21},{6,22},{7,23},{8,24},{9,... | collective-permute-start | bytes 589832 | tf_op jit(solution)/shard_map/ppermute | solution.py:297
  57.9 7.8 %collective-permute-start.22 = (bf16[4,128,768]{2,1,0:T(8,128)(2,1)S(1)}, bf16[4,128,768]{2,1,0:T(8,128)(2,1)S(1)}, u32[]{:S(2)}, u32[]{:S(2)}) collective-permute-start(bf16[4,128,768]{2,1,0:T(8,128)(2,1)S(1)} %pack.7), channel_id=1, source_target_pairs={{0,1},{1,0},{2,3},{3,2},{4,5},{5,4},{6,7},{7,6},{8,9},{9,8},{10,11... | collective-permute-start | bytes 2359304 | tf_op jit(solution)/shard_map/ppermute | solution.py:297
  64.0 2.4 %collective-permute-start.30 = (bf16[4,128,768]{2,1,0:T(8,128)(2,1)S(1)}, bf16[4,128,768]{2,1,0:T(8,128)(2,1)S(1)}, u32[]{:S(2)}, u32[]{:S(2)}) collective-permute-start(bf16[4,128,768]{2,1,0:T(8,128)(2,1)S(1)} %pack.11), channel_id=1, source_target_pairs={{0,1},{1,0},{2,3},{3,2},{4,5},{5,4},{6,7},{7,6},{8,9},{9,8},{10,11... | collective-permute-start | bytes 2359304 | tf_op jit(solution)/shard_map/ppermute | solution.py:297
  64.2 7.3 %collective-permute-start.36 = (bf16[2,128,256]{2,1,0:T(8,128)(2,1)S(1)}, bf16[2,128,256]{2,1,0:T(8,128)(2,1)S(1)}, u32[]{:S(2)}, u32[]{:S(2)}) collective-permute-start(bf16[2,128,256]{2,1,0:T(8,128)(2,1)S(1)} %get-tuple-element.69), channel_id=1, source_target_pairs={{0,6},{1,7},{2,4},{3,5},{4,2},{5,3},{6,0},{7,1},{8,14},{9,15},{10,... | collective-permute-start | bytes 393224 | tf_op jit(solution)/shard_map/ppermute | solution.py:297
  64.8 8.9 %collective-permute-start.35 = (bf16[2,128,256]{2,1,0:T(8,128)(2,1)S(1)}, bf16[2,128,256]{2,1,0:T(8,128)(2,1)S(1)}, u32[]{:S(2)}, u32[]{:S(2)}) collective-permute-start(bf16[2,128,256]{2,1,0:T(8,128)(2,1)S(1)} %get-tuple-element.70), channel_id=1, source_target_pairs={{0,4},{1,3},{2,6},{3,1},{4,0},{5,7},{6,2},{7,5},{8,12},{9,11},{10,... | collective-permute-start | bytes 393224 | tf_op jit(solution)/shard_map/ppermute | solution.py:297
  67.4 23.4 %collective-permute-start.39 = (bf16[256,896]{1,0:T(8,128)(2,1)S(1)}, bf16[256,896]{1,0:T(8,128)(2,1)S(1)}, u32[]{:S(2)}, u32[]{:S(2)}) collective-permute-start(bf16[256,896]{1,0:T(8,128)(2,1)S(1)} %fold.5.refs_3_), channel_id=1, source_target_pairs={{0,16},{1,17},{2,18},{3,19},{4,20},{5,21},{6,22},{7,23},{8,24},{9,... | collective-permute-start | bytes 1376264 | tf_op jit(solution)/shard_map/ppermute | solution.py:297
  68.0 6.3 %collective-permute-start.34 = (bf16[2,128,256]{2,1,0:T(8,128)(2,1)S(1)}, bf16[2,128,256]{2,1,0:T(8,128)(2,1)S(1)}, u32[]{:S(2)}, u32[]{:S(2)}) collective-permute-start(bf16[2,128,256]{2,1,0:T(8,128)(2,1)S(1)} %get-tuple-element.71), channel_id=1, source_target_pairs={{0,2},{1,5},{2,0},{3,7},{4,6},{5,1},{6,4},{7,3},{8,10},{9,13},{10,... | collective-permute-start | bytes 393224 | tf_op jit(solution)/shard_map/ppermute | solution.py:297
  69.4 6.0 %collective-permute-start.31 = (bf16[2,128,256]{2,1,0:T(8,128)(2,1)S(1)}, bf16[2,128,256]{2,1,0:T(8,128)(2,1)S(1)}, u32[]{:S(2)}, u32[]{:S(2)}) collective-permute-start(bf16[2,128,256]{2,1,0:T(8,128)(2,1)S(1)} %get-tuple-element.62), channel_id=1, source_target_pairs={{0,2},{1,5},{2,0},{3,7},{4,6},{5,1},{6,4},{7,3},{8,10},{9,13},{10,... | collective-permute-start | bytes 393224 | tf_op jit(solution)/shard_map/ppermute | solution.py:297
  71.5 5.5 %collective-permute-start.32 = (bf16[2,128,256]{2,1,0:T(8,128)(2,1)S(1)}, bf16[2,128,256]{2,1,0:T(8,128)(2,1)S(1)}, u32[]{:S(2)}, u32[]{:S(2)}) collective-permute-start(bf16[2,128,256]{2,1,0:T(8,128)(2,1)S(1)} %get-tuple-element.63), channel_id=1, source_target_pairs={{0,4},{1,3},{2,6},{3,1},{4,0},{5,7},{6,2},{7,5},{8,12},{9,11},{10,... | collective-permute-start | bytes 393224 | tf_op jit(solution)/shard_map/ppermute | solution.py:297
  73.7 5.9 %collective-permute-start.33 = (bf16[2,128,256]{2,1,0:T(8,128)(2,1)S(1)}, bf16[2,128,256]{2,1,0:T(8,128)(2,1)S(1)}, u32[]{:S(2)}, u32[]{:S(2)}) collective-permute-start(bf16[2,128,256]{2,1,0:T(8,128)(2,1)S(1)} %get-tuple-element.64), channel_id=1, source_target_pairs={{0,6},{1,7},{2,4},{3,5},{4,2},{5,3},{6,0},{7,1},{8,14},{9,15},{10,... | collective-permute-start | bytes 393224 | tf_op jit(solution)/shard_map/ppermute | solution.py:297
  74.5 5.4 %collective-permute-start.38 = (bf16[256,512]{1,0:T(8,128)(2,1)S(1)}, bf16[256,512]{1,0:T(8,128)(2,1)S(1)}, u32[]{:S(2)}, u32[]{:S(2)}) collective-permute-start(bf16[256,512]{1,0:T(8,128)(2,1)S(1)} %get-tuple-element.68), channel_id=1, source_target_pairs={{0,1},{1,0},{2,3},{3,2},{4,5},{5,4},{6,7},{7,6},{8,9},{9,8},{10,11... | collective-permute-start | bytes 786440 | tf_op jit(solution)/shard_map/ppermute | solution.py:297
  79.8 1.6 %collective-permute-start.37 = (bf16[256,512]{1,0:T(8,128)(2,1)S(1)}, bf16[256,512]{1,0:T(8,128)(2,1)S(1)}, u32[]{:S(2)}, u32[]{:S(2)}) collective-permute-start(bf16[256,512]{1,0:T(8,128)(2,1)S(1)} %get-tuple-element.67), channel_id=1, source_target_pairs={{0,1},{1,0},{2,3},{3,2},{4,5},{5,4},{6,7},{7,6},{8,9},{9,8},{10,11... | collective-permute-start | bytes 786440 | tf_op jit(solution)/shard_map/ppermute | solution.py:297
